TPU v7x, 32 devices: a whole 2x2x4 slice. The times are simulated.
32 devices in a mesh: period: 4 (over x, core), bus: 8 (over z, y).
Axes of the slice: x: 2, y: 2, z: 4, core: 2. Of those that a mesh axis runs over, the one named last changes fastest.
Arguments:
- gain: bfloat16 [4, 2048, 2048], P('period', 'bus'), may hold values from -0.15 to 1.15
- schur: bfloat16 [4, 2048, 2048], P('period', 'bus'), may hold values from -0.0625 to 0.0625
- inverse_blocks: bfloat16 [4, 10240, 1280], P('period', 'bus'), may hold values from -0.15625 to 0.15625
- sensitivity: bfloat16 [10240, 2048], P('bus'), may hold values from -0.078125 to 0.078125
- residual_bus: float32 [4, 10240, 512], P('period', 'bus'), may hold values from -6 to 6
- unit_rhs: float32 [4, 2048, 512], P('period', 'bus'), may hold values from -6 to 6
- start_state: float32 [2048, 512], P('bus'), may hold values from -6 to 6
- active_set: int32 [4, 10240], P('period', 'bus'), may hold values 0 or 1
- unit_bus: int32 [2048], replicated, may hold values from 0 to 10239
Outputs:
- storage_path: float32 [4, 2048, 512], P('period', 'bus')
- costate: float32 [4, 2048, 512], P('period', 'bus')
- bus_update: float32 [4, 10240, 512], P('period', 'bus')
All inputs are finite; a program needn't handle non-finite values. No bound on the sum of `active_set` on one device may be relied on, other than what follows from the above.
Results may differ from a plain program's by a relative error of at most 0.008.
Values may be sent and summed in bfloat16 or wider, within the bound.
No kernel may reach another device: no remote copies, remote signals or barrier semaphores. Data moves between devices by JAX's collectives and lax.ppermute only.
A program may use at most 64 MiB of HBM per device.

v0:
```python
import functools

import jax
import jax.numpy as jnp
from jax import lax
from jax.experimental import pallas as pl
from jax.experimental.pallas import tpu as pltpu
from jax.sharding import PartitionSpec as P

BOTH = ("period", "bus")
F32 = jnp.float32
BF16 = jnp.bfloat16
EVEN = (0, 2, 4, 6)
MIB = 1 << 20


def bus_send(block, flip, periods):
    size = lax.axis_size("bus")
    route = [(p * size + b, p * size + (b ^ flip)) for p in periods for b in range(size)]
    return lax.ppermute(block, BOTH, route)


def period_send(block, source, target):
    size = lax.axis_size("bus")
    route = [(source * size + b, target * size + b) for b in range(size)]
    return lax.ppermute(block, BOTH, route)


def times(left, right):
    return jnp.dot(left, right, preferred_element_type=F32)


def times_t(left, right):
    return lax.dot_general(left, right, (((1,), (1,)), ((), ())), preferred_element_type=F32)


def gather_parts(block, periods):
    parts = {0: block}
    for flip in (6, 4, 2):
        parts[flip] = bus_send(block, flip, periods)
    for flip in EVEN:
        parts[flip ^ 1] = bus_send(parts[flip], 1, periods)
    return [parts[flip] for flip in range(8)]


def reduce_parts(parts, periods):
    total = None
    for flip in (6, 4, 2, 0):
        here = parts[flip] + bus_send(parts[flip ^ 1], 1, periods).astype(F32)
        if flip:
            here = bus_send(here.astype(BF16), flip, periods).astype(F32)
        total = here if total is None else total + here
    return total


def swap_parts(keep, send, periods):
    there = bus_send(send, 1, periods)
    parts = {}
    for place, flip in enumerate(EVEN):
        pair = jnp.stack([keep[place], there[place]])
        if flip:
            pair = bus_send(pair, flip, periods)
        parts[flip], parts[flip ^ 1] = pair[0], pair[1]
    return [parts[flip] for flip in range(8)]


def in_vmem():
    return pl.BlockSpec(memory_space=pltpu.VMEM)


def anywhere():
    return pl.BlockSpec(memory_space=pl.ANY)


def in_smem():
    return pl.BlockSpec(memory_space=pltpu.SMEM)


def kernel_call(kernel, out_shape, in_specs, scratch, flops, bytes_accessed):
    return pl.pallas_call(
        kernel,
        out_shape=out_shape,
        in_specs=in_specs,
        out_specs=jax.tree.map(lambda _: in_vmem(), out_shape),
        scratch_shapes=scratch,
        compiler_params=pltpu.CompilerParams(vmem_limit_bytes=48 * MIB),
        cost_estimate=pl.CostEstimate(
            flops=flops, bytes_accessed=bytes_accessed, transcendentals=0
        ),
    )


def front_kernel(
    rank_ref, active, rhs, residual_hbm, inverse_hbm, sens_hbm,
    k0, s0, k1, s1, k2, s2, k3, s3,
    residual, inverse, sens, net, solve_t, partial, sems,
):
    rank = rank_ref[0]
    loads = [
        pltpu.make_async_copy(residual_hbm, residual, sems.at[0]),
        pltpu.make_async_copy(inverse_hbm, inverse, sems.at[1]),
        pltpu.make_async_copy(sens_hbm, sens, sems.at[2]),
    ]
    for load in loads:
        load.start()
    loads[0].wait()
    net[...] = (residual[...] * (1.0 + 3.0 * active[...].astype(F32))).astype(BF16)
    loads[1].wait()
    blocks = inverse.shape[0] // 256

    @pl.loop(0, blocks)
    def _(i):
        rows = pl.ds(pl.multiple_of(i * 256, 256), 256)
        solve_t[:, rows] = times(inverse[rows, :], net[...]).T.astype(BF16)

    loads[2].wait()

    @pl.loop(0, sens.shape[1] // 256)
    def _(i):
        columns = pl.ds(pl.multiple_of(i * 256, 256), 256)
        partial[:, columns] = times(solve_t[...], sens[:, columns])

    units = rhs.shape[0]
    own = pl.ds(pl.multiple_of(rank * units, units), units)
    partial[:, own] += rhs[...].T
    rows = k0.shape[0]
    for flip, out in enumerate((k0, s0, k1, s1, k2, s2, k3, s3)):
        owner = pl.multiple_of((rank ^ flip) * rows, rows)
        out[...] = partial[pl.ds(owner, rows), :].astype(out.dtype)


def front(rank, active, rhs, residual, inverse, sens):
    buses, columns = residual.shape
    units = sens.shape[1]
    rows = columns // 8
    keep = jax.ShapeDtypeStruct((rows, units), F32)
    send = jax.ShapeDtypeStruct((rows, units), BF16)
    return kernel_call(
        front_kernel,
        [keep, send] * 4,
        [in_smem(), in_vmem(), in_vmem(), anywhere(), anywhere(), anywhere()],
        [
            pltpu.VMEM((buses, columns), F32),
            pltpu.VMEM((buses, buses), BF16),
            pltpu.VMEM((buses, units), BF16),
            pltpu.VMEM((buses, columns), BF16),
            pltpu.VMEM((columns, buses), BF16),
            pltpu.VMEM((columns, units), F32),
            pltpu.SemaphoreType.DMA((3,)),
        ],
        2 * buses * columns * (buses + units),
        24 * MIB,
    )(rank, active, rhs, residual, inverse, sens)


def weight_loads(rank, weights, held, sems):
    units = held.shape[1]
    loads = []
    for flip in range(8):
        owner = pl.multiple_of((rank ^ flip) * units, units)
        source = weights.at[pl.ds(owner, units)]
        loads.append(pltpu.make_async_copy(source, held.at[flip], sems.at[flip]))
    return loads


def backward_kernel(rank_ref, vector, base, *refs):
    weights, out, held, total, sems = refs
    rank = rank_ref[0]
    loads = weight_loads(rank, weights, held, sems)
    for load in loads:
        load.start()
    units = held.shape[1]
    total[...] = base[...]
    for flip, load in enumerate(loads):
        load.wait()
        own = pl.ds(pl.multiple_of((rank ^ flip) * units, units), units)
        total[...] += times(vector[:, own], held[flip])
    out[...] = total[...].astype(out.dtype)


def forward_kernel(subtract, rank_ref, vector, *refs):
    weights, refs = refs[0], refs[1:]
    terms, (out, held, sems) = (refs[:8], refs[8:]) if subtract else (None, refs)
    rank = rank_ref[0]
    loads = weight_loads(rank, weights, held, sems)
    for load in loads:
        load.start()
    units = held.shape[1]
    for flip, load in enumerate(loads):
        load.wait()
        own = pl.ds(pl.multiple_of((rank ^ flip) * units, units), units)
        product = times_t(vector[...], held[flip])
        if subtract:
            product = product - terms[flip][...].astype(F32)
        out[:, own] = product.astype(out.dtype)


def backward(rank, vector, base, weights):
    rows, whole = vector.shape
    units = weights.shape[0] // 8
    return kernel_call(
        backward_kernel,
        jax.ShapeDtypeStruct((rows, whole), BF16),
        [in_smem(), in_vmem(), in_vmem()] + [anywhere()],
        [
            pltpu.VMEM((8, units, whole), BF16),
            pltpu.VMEM((rows, whole), F32),
            pltpu.SemaphoreType.DMA((8,)),
        ],
        2 * rows * whole * whole,
        2 * whole * whole,
    )(rank, vector, base, weights)


def forward(rank, vector, weights, terms=()):
    rows, whole = vector.shape
    units = weights.shape[0] // 8
    return kernel_call(
        functools.partial(forward_kernel, bool(terms)),
        jax.ShapeDtypeStruct((rows, whole), BF16),
        [in_smem(), in_vmem()] + [anywhere()] + [in_vmem()] * len(terms),
        [pltpu.VMEM((8, units, whole), BF16), pltpu.SemaphoreType.DMA((8,))],
        2 * rows * whole * whole,
        2 * whole * whole,
    )(rank, vector, weights, *terms)


def assemble(rank, first, second, whole):
    rows = first[0].shape[0]
    for flip in range(8):
        owner = pl.multiple_of((rank ^ flip) * rows, rows)
        block = first[flip][...]
        if flip and second:
            block = block + second[flip - 1][...]
        whole[pl.ds(owner, rows), :] = block


def couple_kernel(rank_ref, schur, *refs):
    parts, (keep, send, product, whole) = refs[:8], refs[8:]
    rank = rank_ref[0]
    assemble(rank, parts, (), whole)
    product[...] = times_t(whole[...], schur[...])
    rows = keep.shape[1]
    for place, flip in enumerate(EVEN):
        keep[place] = product[pl.ds(pl.multiple_of((rank ^ flip) * rows, rows), rows), :].astype(BF16)
        send[place] = product[pl.ds(pl.multiple_of((rank ^ flip ^ 1) * rows, rows), rows), :].astype(BF16)


def couple(rank, schur, parts):
    units, whole = schur.shape
    rows = parts[0].shape[0]
    piece = jax.ShapeDtypeStruct((4, rows, units), BF16)
    return kernel_call(
        couple_kernel,
        [piece, piece],
        [in_smem(), in_vmem()] + [in_vmem()] * 8,
        [pltpu.VMEM((8 * rows, units), F32), pltpu.VMEM((8 * rows, whole), BF16)],
        16 * rows * whole * units,
        4 * MIB,
    )(rank, schur, *parts)


def costate_kernel(rank_ref, schur, *refs):
    first, second, (costate, coupling, whole) = refs[:8], refs[8:15], refs[15:]
    rank = rank_ref[0]
    assemble(rank, first, second, whole)
    coupling[...] = times_t(schur[...], whole[...])
    units = schur.shape[0]
    own = pl.ds(pl.multiple_of(rank * units, units), units)
    costate[...] = whole[:, own].astype(F32).T


def costate_out(rank, schur, first, second):
    units, whole = schur.shape
    rows = first[0].shape[0]
    out = jax.ShapeDtypeStruct((units, 8 * rows), F32)
    return kernel_call(
        costate_kernel,
        [out, out],
        [in_smem(), in_vmem()] + [in_vmem()] * 15,
        [pltpu.VMEM((8 * rows, whole), BF16)],
        16 * rows * whole * units,
        6 * MIB,
    )(rank, schur, *first, *second[1:])


def final_kernel(rank_ref, unit_bus, active, coupling, gain, residual_hbm, inverse_hbm, *refs):
    first, second = refs[:8], refs[8:15]
    storage, update, residual, inverse, whole, network, sems = refs[15:]
    rank = rank_ref[0]
    loads = [
        pltpu.make_async_copy(residual_hbm, residual, sems.at[0]),
        pltpu.make_async_copy(inverse_hbm, inverse, sems.at[1]),
    ]
    for load in loads:
        load.start()
    assemble(rank, first, second, whole)
    loads[0].wait()
    buses = inverse.shape[0]

    @pl.loop(0, buses // 256)
    def _(i):
        rows = pl.ds(pl.multiple_of(i * 256, 256), 256)
        ids = rank * buses + i * 256 + lax.broadcasted_iota(jnp.int32, (256, 1), 0)
        placed = (unit_bus[...] == ids).astype(BF16)
        injection = times_t(placed, whole[...])
        weighted = residual[rows, :] * (1.0 + 3.0 * active[rows, :].astype(F32))
        network[rows, :] = (weighted - injection).astype(BF16)

    storage[...] = times_t(gain[...], whole[...]) - coupling[...]
    loads[1].wait()

    @pl.loop(0, buses // 256)
    def _(i):
        rows = pl.ds(pl.multiple_of(i * 256, 256), 256)
        update[rows, :] = times(inverse[rows, :], network[...])


def final(rank, unit_bus, active, coupling, gain, residual, inverse, first, second):
    buses, columns = residual.shape
    units, whole = gain.shape
    return kernel_call(
        final_kernel,
        [
            jax.ShapeDtypeStruct((units, columns), F32),
            jax.ShapeDtypeStruct((buses, columns), F32),
        ],
        [in_smem()] + [in_vmem()] * 4 + [anywhere()] * 2 + [in_vmem()] * 15,
        [
            pltpu.VMEM((buses, columns), F32),
            pltpu.VMEM((buses, buses), BF16),
            pltpu.VMEM((columns, whole), BF16),
            pltpu.VMEM((buses, columns), BF16),
            pltpu.SemaphoreType.DMA((2,)),
        ],
        2 * columns * (buses * buses + (buses + units) * whole),
        24 * MIB,
    )(rank, unit_bus, active, coupling, gain, residual, inverse, *first, *second[1:])


def plane_body(
    gain, schur, inverse, sens, residual, unit_rhs, start_state, active, unit_bus
):
    period = lax.axis_index("period")
    rank = lax.axis_index("bus").reshape(1)
    last = lax.axis_size("period") - 1
    everyone = tuple(range(last + 1))
    inner = tuple(range(1, last))
    outer = (0, last)
    rows = residual.shape[1] // 8

    first_schur = period_send(schur, 0, last)
    outer_block = jnp.where(period == last, first_schur, gain)
    gain_inner = matrix_outer = lax.all_gather(outer_block, "bus", axis=0, tiled=True)
    terms = front(rank, active, unit_rhs, residual, inverse, sens)
    unit_right = reduce_parts(terms, everyone)

    start_t = start_state.T.astype(BF16)

    def start_piece(owner):
        return lax.dynamic_slice_in_dim(start_t, owner * rows, rows, 0)

    keep = jnp.stack([start_piece(rank[0] ^ flip) for flip in EVEN])
    send = jnp.stack([start_piece(rank[0] ^ flip ^ 1) for flip in EVEN])
    pieces = jnp.stack(swap_parts(keep, send, everyone))
    ordered = jnp.take(pieces, jnp.arange(8, dtype=jnp.int32) ^ rank[0], axis=0)
    start = jnp.transpose(ordered, (1, 0, 2)).reshape(rows, -1)

    costate = unit_right.astype(BF16)
    for target in range(last - 1, 0, -1):
        later = period_send(costate, target + 1, target)
        costate = jnp.where(period == target, backward(rank, later, unit_right, gain_inner), costate)
    inner_costates = gather_parts(costate, inner)
    keep, send = couple(rank, schur, inner_costates)
    coupled_inner = swap_parts(keep, send, inner)
    later = period_send(costate, 1, 0)
    costate = jnp.where(period == 0, backward(rank, later, unit_right, matrix_outer), costate)

    at_last = period_send(costate, 0, last)
    coupled = period_send(forward(rank, at_last, matrix_outer), last, 0)
    outer_costates = gather_parts(costate, outer)
    costate_rows, coupling = costate_out(rank, schur, outer_costates, inner_costates)

    state = start
    driven = forward(rank, start, matrix_outer)
    advanced = (driven.astype(F32) - coupled.astype(F32)).astype(BF16)
    for target in range(1, last + 1):
        arrived = period_send(advanced, target - 1, target)
        state = jnp.where(period == target, arrived, state)
        if target == last - 1:
            early_states = gather_parts(state, everyone[:-1])
        if target < last:
            advanced = forward(rank, arrived, gain_inner, coupled_inner)
    last_states = gather_parts(state, (last,))
    storage, update = final(
        rank, unit_bus, active, coupling, gain, residual, inverse, last_states, early_states
    )
    return storage, costate_rows, update


def plain_body(
    gain, schur, inverse, sens, residual, unit_rhs, start_state, active, unit_bus
):
    period = lax.axis_index("period")
    rank = lax.axis_index("bus")
    size = lax.axis_size("bus")
    groups = lax.axis_size("period")
    units, whole = gain.shape
    buses, columns = residual.shape
    rows = columns // size

    def gathered(block):
        return lax.all_gather(block, "bus", axis=0, tiled=True)

    def to_columns(block):
        swapped = lax.all_to_all(block.reshape(size, rows, units), "bus", 0, 0)
        return jnp.transpose(swapped, (1, 0, 2)).reshape(rows, whole)

    weighted = residual * (1.0 + 3.0 * active.astype(F32))
    solve = times(inverse, weighted.astype(BF16)).astype(BF16)
    partial = lax.dot_general(solve, sens, (((0,), (0,)), ((), ())), preferred_element_type=F32)
    place = (0, rank * units)
    own = lax.dynamic_slice(partial, place, (columns, units)) + unit_rhs.T
    partial = lax.dynamic_update_slice(partial, own, place).astype(BF16)
    unit_right = lax.psum_scatter(partial, "bus", scatter_dimension=0, tiled=True).astype(F32)
    gain_whole = gathered(gain)
    costate = unit_right.astype(BF16)
    for target in range(groups - 2, -1, -1):
        later = period_send(costate, target + 1, target)
        current = (unit_right + times(later, gain_whole)).astype(BF16)
        costate = jnp.where(period == target, current, costate)
    costate_whole = gathered(costate)
    coupling = times_t(costate_whole, schur)
    coupled = to_columns(coupling.astype(BF16)).astype(F32)
    state = to_columns(start_state.T.astype(BF16))
    advanced = times_t(state, gain_whole) - coupled
    for target in range(1, groups):
        arrived = period_send(advanced.astype(BF16), target - 1, target)
        state = jnp.where(period == target, arrived, state)
        advanced = times_t(arrived, gain_whole) - coupled
    state_whole = gathered(state)
    storage = times_t(gain, state_whole) - coupling.T
    costate_rows = lax.dynamic_slice_in_dim(costate_whole, rank * units, units, 1).T.astype(F32)
    ids = rank * buses + jnp.arange(buses, dtype=jnp.int32)
    placement = (unit_bus == ids[:, None]).astype(BF16)
    network = (weighted - times_t(placement, state_whole)).astype(BF16)
    return storage, costate_rows, times(inverse, network)


def body(
    gain, schur, inverse_blocks, sensitivity, residual_bus, unit_rhs, start_state, active_set, unit_bus
):
    in_planes = lax.axis_size("bus") == 8 and lax.axis_size("period") > 2
    storage, costate, update = (plane_body if in_planes else plain_body)(
        gain[0],
        schur[0],
        inverse_blocks[0],
        sensitivity,
        residual_bus[0],
        unit_rhs[0],
        start_state,
        active_set[0][:, None],
        unit_bus[None, :],
    )
    return storage[None], costate[None], update[None]


def solution(mesh):
    by_period = P("period", "bus", None)
    placed = (
        by_period,
        by_period,
        by_period,
        P("bus", None),
        by_period,
        by_period,
        P("bus", None),
        P("period", "bus"),
        P(),
    )
    return jax.shard_map(
        body,
        mesh=mesh,
        in_specs=placed,
        out_specs=(by_period, by_period, by_period),
        check_vma=False,
    )
```

profile of v0, /device:TPU:15, one launch (start us, length us, event | category | flops | bytes accessed | tf_op | source)
XLA Modules:
  0.0 348.9 jit_solution(16887130439217405830)
XLA Ops:
  7.2 1.4 collective-permute-start.8
  8.7 15.0 %collective-permute-done.8 = bf16[256,2048]{1,0:T(8,128)(2,1)S(1)} collective-permute-done((bf16[256,2048]{1,0:T(8,128)(2,1)}, bf16[256,2048]{1,0:T(8,128)(2,1)S(1)}, u32[]{:S(2)}, u32[]{:S(2)}) %collective-permute-start.8) | collective-permute-done | bytes 1048608 | tf_op jit(solution)/shard_map/ppermute | solution.py:26
  23.7 2.3 broadcast_select_fusion
  26.3 10.9 %shard_map.112 = (f32[64,2048]{1,0:T(8,128)S(1)}, bf16[64,2048]{1,0:T(8,128)(2,1)S(1)}, f32[64,2048]{1,0:T(8,128)S(1)}, bf16[64,2048]{1,0:T(8,128)(2,1)S(1)}, f3...) custom-call(s32[1]{0:T(128)} %bitcast.rank_ref, ...), custom_call_target="tpu_custom_call" | custom-call | flops 4362076160 | bytes 25165824 | tf_op jit(solution)/shard_map/pallas_call | solution.py:138
  38.6 5.6 %collective-permute-start = (bf16[64,2048]{1,0:T(8,128)(2,1)}, bf16[64,2048]{1,0:T(8,128)(2,1)}, u32[]{:S(2)}, u32[]{:S(2)}) collective-permute-start(bf16[64,2048]{1,0:T(8,128)(2,1)} %get-tuple-element.18), channel_id=1, source_target_pairs={{0,1},{1,0},{2,3},{3,2},{4,5},{5,4},{6,7},{7,6},{8,9},{9,8},{10,11... | collective-permute-start | bytes 786440 | tf_op jit(solution)/shard_map/ppermute | solution.py:20
  47.0 5.7 %collective-permute-start.25 = (bf16[4,64,256]{1,2,0:T(8,128)(2,1)}, bf16[4,64,256]{1,2,0:T(8,128)(2,1)}, u32[]{:S(2)}, u32[]{:S(2)}) collective-permute-start(bf16[4,64,256]{1,2,0:T(8,128)(2,1)} %pad_maximum_fusion), channel_id=1, source_target_pairs={{0,1},{1,0},{2,3},{3,2},{4,5},{5,4},{6,7},{7,6},{8,9},{9,8},{10,11... | collective-permute-start | bytes 393224 | tf_op jit(solution)/shard_map/ppermute | solution.py:20
  52.8 5.7 %collective-permute-start.2 = (bf16[64,2048]{1,0:T(8,128)(2,1)}, bf16[64,2048]{1,0:T(8,128)(2,1)S(1)}, u32[]{:S(2)}, u32[]{:S(2)}) collective-permute-start(bf16[64,2048]{1,0:T(8,128)(2,1)} %copy-done.4), channel_id=1, source_target_pairs={{0,1},{1,0},{2,3},{3,2},{4,5},{5,4},{6,7},{7,6},{8,9},{9,8},{10,11... | collective-permute-start | bytes 786440 | tf_op jit(solution)/shard_map/ppermute | solution.py:20
  58.5 5.7 %collective-permute-start.4 = (bf16[64,2048]{1,0:T(8,128)(2,1)}, bf16[64,2048]{1,0:T(8,128)(2,1)S(1)}, u32[]{:S(2)}, u32[]{:S(2)}) collective-permute-start(bf16[64,2048]{1,0:T(8,128)(2,1)} %copy-done.3), channel_id=1, source_target_pairs={{0,1},{1,0},{2,3},{3,2},{4,5},{5,4},{6,7},{7,6},{8,9},{9,8},{10,11... | collective-permute-start | bytes 786440 | tf_op jit(solution)/shard_map/ppermute | solution.py:20
  64.2 5.7 %collective-permute-start.6 = (bf16[64,2048]{1,0:T(8,128)(2,1)S(1)}, bf16[64,2048]{1,0:T(8,128)(2,1)S(1)}, u32[]{:S(2)}, u32[]{:S(2)}) collective-permute-start(bf16[64,2048]{1,0:T(8,128)(2,1)S(1)} %get-tuple-element.24), channel_id=1, source_target_pairs={{0,1},{1,0},{2,3},{3,2},{4,5},{5,4},{6,7},{7,6},{8,9},{9,8},{10,11... | collective-permute-start | bytes 786440 | tf_op jit(solution)/shard_map/ppermute | solution.py:20
  69.9 1.7 add_convert_fusion.2
  76.8 23.3 %collective-permute-done.1 = bf16[64,2048]{1,0:T(8,128)(2,1)S(1)} collective-permute-done((bf16[64,2048]{1,0:T(8,128)(2,1)}, bf16[64,2048]{1,0:T(8,128)(2,1)S(1)}, u32[]{:S(2)}, u32[]{:S(2)}) %collective-permute-start.1) | collective-permute-done | bytes 262176 | tf_op jit(solution)/shard_map/ppermute | solution.py:20
  100.1 14.7 %collective-permute-done.3 = bf16[64,2048]{1,0:T(8,128)(2,1)S(1)} collective-permute-done((bf16[64,2048]{1,0:T(8,128)(2,1)S(1)}, bf16[64,2048]{1,0:T(8,128)(2,1)S(1)}, u32[]{:S(2)}, u32[]{:S(2)}) %collective-permute-start.3) | collective-permute-done | bytes 262176 | tf_op jit(solution)/shard_map/ppermute | solution.py:20
  115.0 7.6 %collective-permute-start.7 = (bf16[64,2048]{1,0:T(8,128)(2,1)S(1)}, bf16[64,2048]{1,0:T(8,128)(2,1)S(1)}, u32[]{:S(2)}, u32[]{:S(2)}) collective-permute-start(bf16[64,2048]{1,0:T(8,128)(2,1)S(1)} %get-tuple-element.33), channel_id=1, source_target_pairs={{24,16},{25,17},{26,18},{27,19},{28,20},{29,21},{30,22},{31,23}} | collective-permute-start | bytes 786440 | tf_op jit(solution)/shard_map/ppermute | solution.py:26
  122.6 1.6 fusion.2
  124.2 39.7 %all-gather.2.cloned.1.call-done.refs_0_ = bf16[2048,2048]{1,0:T(8,128)(2,1)} async-done(((bf16[256,2048]{1,0:T(8,128)(2,1)}), bf16[2048,2048]{1,0:T(8,128)(2,1)}) %all-gather.2.cloned.1.call-update) | async-done | bytes 8388624 | tf_op jit(solution)/shard_map/all_gather | solution.py:354
  163.9 3.8 %shard_map.113 = bf16[64,2048]{1,0:T(8,128)(2,1)S(1)} custom-call(s32[1]{0:T(128)} %bitcast.rank_ref, bf16[64,2048]{1,0:T(8,128)(2,1)S(1)} %collective-permute-done.7.vector, f32[64,2048]{1,0:T(8,128)S(1)} %get-tuple-element.34.base, bf16[2048,2048]{1,0:T(8,128)(2,1)} %all-gather.2.cloned.1.call-done.refs_0_), custom_call_target="tpu_custom_call" | custom-call | flops 536870912 | bytes 8388608 | tf_op jit(solution)/shard_map/pallas_call | solution.py:201
  168.5 2.6 collective-permute-start.26
  172.5 3.8 %shard_map.114 = bf16[64,2048]{1,0:T(8,128)(2,1)S(1)} custom-call(s32[1]{0:T(128)} %bitcast.rank_ref, bf16[64,2048]{1,0:T(8,128)(2,1)S(1)} %collective-permute-done.9.vector, f32[64,2048]{1,0:T(8,128)S(1)} %get-tuple-element.34.base, bf16[2048,2048]{1,0:T(8,128)(2,1)} %all-gather.2.cloned.1.call-done.refs_0_), custom_call_target="tpu_custom_call" | custom-call | flops 536870912 | bytes 8388608 | tf_op jit(solution)/shard_map/pallas_call | solution.py:201
  177.1 5.9 %collective-permute-done.28 = bf16[2,64,256]{1,2,0:T(8,128)(2,1)S(1)} collective-permute-done((bf16[2,64,256]{1,2,0:T(8,128)(2,1)S(1)}, bf16[2,64,256]{1,2,0:T(8,128)(2,1)S(1)}, u32[]{:S(2)}, u32[]{:S(2)}) %collective-permute-start.28) | collective-permute-done | bytes 65568 | tf_op jit(solution)/shard_map/ppermute | solution.py:20
  183.1 1.4 gather_fusion
  187.4 3.8 %shard_map.115 = bf16[64,2048]{1,0:T(8,128)(2,1)S(1)} custom-call(s32[1]{0:T(128)} %bitcast.rank_ref, bf16[64,2048]{1,0:T(8,128)(2,1)S(1)} %collective-permute-done.10.vector, f32[64,2048]{1,0:T(8,128)S(1)} %get-tuple-element.34.base, bf16[2048,2048]{1,0:T(8,128)(2,1)} %all-gather.2.cloned.1.call-done.refs_0_), custom_call_target="tpu_custom_call" | custom-call | flops 536870912 | bytes 8388608 | tf_op jit(solution)/shard_map/pallas_call | solution.py:201
  196.7 6.8 %shard_map.117 = bf16[64,2048]{1,0:T(8,128)(2,1)S(1)} custom-call(s32[1]{0:T(128)} %bitcast.rank_ref, bf16[64,2048]{1,0:T(8,128)(2,1)S(1)} %copy.16.vector, bf16[2048,2048]{1,0:T(8,128)(2,1)} %all-gather.2.cloned.1.call-done.refs_0_), custom_call_target="tpu_custom_call" | custom-call | flops 536870912 | bytes 8388608 | tf_op jit(solution)/shard_map/pallas_call | solution.py:218
  205.3 6.7 %shard_map.118 = bf16[64,2048]{1,0:T(8,128)(2,1)S(1)} custom-call(s32[1]{0:T(128)} %bitcast.rank_ref, bf16[64,2048]{1,0:T(8,128)(2,1)S(1)} %collective-permute-done.29.vector, bf16[2048,2048]{1,0:T(8,128)(2,1)} %all-gather.2.cloned.1.call-done.refs_0_), custom_call_target="tpu_custom_call" | custom-call | flops 536870912 | bytes 8388608 | tf_op jit(solution)/shard_map/pallas_call | solution.py:218
  212.0 5.0 %collective-permute-start.30 = (bf16[64,2048]{1,0:T(8,128)(2,1)S(1)}, bf16[64,2048]{1,0:T(8,128)(2,1)S(1)}, u32[]{:S(2)}, u32[]{:S(2)}) collective-permute-start(bf16[64,2048]{1,0:T(8,128)(2,1)S(1)} %shard_map.118), channel_id=1, source_target_pairs={{24,0},{25,1},{26,2},{27,3},{28,4},{29,5},{30,6},{31,7}} | collective-permute-start | bytes 786440 | tf_op jit(solution)/shard_map/ppermute | solution.py:26
  221.1 6.7 %shard_map.120 = bf16[64,2048]{1,0:T(8,128)(2,1)S(1)} custom-call(s32[1]{0:T(128)} %bitcast.rank_ref, bf16[64,2048]{1,0:T(8,128)(2,1)S(1)} %collective-permute-done.31.vector, bf16[2048,2048]{1,0:T(8,128)(2,1)} %all-gather.2.cloned.1.call-done.refs_0_, bf16[64,256]{1,0:T(8,128)(2,1)S(1)} %get-tuple-element.49.refs_1_, ...), custom_call_target="tpu_custom_call" | custom-call | flops 536870912 | bytes 8388608 | tf_op jit(solution)/shard_map/pallas_call | solution.py:218
  228.5 3.0 collective-permute-start.16
  231.5 1.9 collective-permute-start.14
  233.5 3.4 collective-permute-start.12
  236.9 6.7 %shard_map.121 = bf16[64,2048]{1,0:T(8,128)(2,1)S(1)} custom-call(s32[1]{0:T(128)} %bitcast.rank_ref, bf16[64,2048]{1,0:T(8,128)(2,1)S(1)} %collective-permute-done.36.vector, bf16[2048,2048]{1,0:T(8,128)(2,1)} %all-gather.2.cloned.1.call-done.refs_0_, bf16[64,256]{1,0:T(8,128)(2,1)S(1)} %get-tuple-element.49.refs_1_, ...), custom_call_target="tpu_custom_call" | custom-call | flops 536870912 | bytes 8388608 | tf_op jit(solution)/shard_map/pallas_call | solution.py:218
  243.6 1.4 collective-permute-start.37
  245.1 2.2 collective-permute-start.11
  247.3 3.1 collective-permute-start.17
  250.4 2.2 collective-permute-start.15
  252.6 3.1 collective-permute-start.13
  255.7 14.6 %collective-permute-done.37 = bf16[64,2048]{1,0:T(8,128)(2,1)S(1)} collective-permute-done((bf16[64,2048]{1,0:T(8,128)(2,1)S(1)}, bf16[64,2048]{1,0:T(8,128)(2,1)S(1)}, u32[]{:S(2)}, u32[]{:S(2)}) %collective-permute-start.37) | collective-permute-done | bytes 262176 | tf_op jit(solution)/shard_map/ppermute | solution.py:26
  272.4 20.7 %collective-permute-start.50 = (bf16[64,2048]{1,0:T(8,128)(2,1)S(1)}, bf16[64,2048]{1,0:T(8,128)(2,1)S(1)}, u32[]{:S(2)}, u32[]{:S(2)}) collective-permute-start(bf16[64,2048]{1,0:T(8,128)(2,1)S(1)} %get-tuple-element.32), channel_id=1, source_target_pairs={{0,6},{1,7},{2,4},{3,5},{4,2},{5,3},{6,0},{7,1},{8,14},{9,15},{10,... | collective-permute-start | bytes 786440 | tf_op jit(solution)/shard_map/ppermute | solution.py:20
  293.1 3.1 collective-permute-start.43
  296.3 3.1 collective-permute-start.41
  299.3 2.9 collective-permute-start.39
  302.3 2.2 collective-permute-start.38
  305.1 5.3 %collective-permute-done.43.refs_6_ = bf16[64,2048]{1,0:T(8,128)(2,1)S(1)} collective-permute-done((bf16[64,2048]{1,0:T(8,128)(2,1)S(1)}, bf16[64,2048]{1,0:T(8,128)(2,1)S(1)}, u32[]{:S(2)}, u32[]{:S(2)}) %collective-permute-start.43) | collective-permute-done | bytes 262176 | tf_op jit(solution)/shard_map/ppermute | solution.py:20
  312.3 2.2 collective-permute-start.44
  314.5 3.1 collective-permute-start.42
  317.6 2.2 collective-permute-start.40
  319.8 1.7 shard_map.116
  322.6 5.6 %collective-permute-done.42.refs_5_ = bf16[64,2048]{1,0:T(8,128)(2,1)S(1)} collective-permute-done((bf16[64,2048]{1,0:T(8,128)(2,1)S(1)}, bf16[64,2048]{1,0:T(8,128)(2,1)S(1)}, u32[]{:S(2)}, u32[]{:S(2)}) %collective-permute-start.42) | collective-permute-done | bytes 262176 | tf_op jit(solution)/shard_map/ppermute | solution.py:20
  328.2 3.6 %collective-permute-done.40.refs_3_ = bf16[64,2048]{1,0:T(8,128)(2,1)S(1)} collective-permute-done((bf16[64,2048]{1,0:T(8,128)(2,1)S(1)}, bf16[64,2048]{1,0:T(8,128)(2,1)S(1)}, u32[]{:S(2)}, u32[]{:S(2)}) %collective-permute-start.40) | collective-permute-done | bytes 262176 | tf_op jit(solution)/shard_map/ppermute | solution.py:20
  331.8 10.3 %shard_map.122 = (f32[256,512]{1,0:T(8,128)}, f32[1280,512]{1,0:T(8,128)}) custom-call(s32[1]{0:T(128)} %bitcast.rank_ref, s32[1,2048]{1,0:T(1,128)S(1)} %bitcast.70, s32[1280,1]{1,0:T(8,128)S(1)} %copy.15.active, f32[256,512]{1,0:T(8,128)S(1)} %get-tuple-element.25.coupling, bf16[256,2048]{1,0:T(8,128)(2,1)S(1)} %bitcast.68, f32[1280,512]{1,0:T(8,128)} %bitcast.76, ...), custom_call_target="tpu_custom_call" | custom-call | flops 4898947072 | bytes 25165824 | tf_op jit(solution)/shard_map/pallas_call | solution.py:322
  (130 shorter events, 33.1 us)
Async XLA Ops:
  7.2 156.7 %all-gather.2.cloned.1.call-start = ((), (), s32[]{:S(2)}) async-start(), calls=%async_computation | async-start | bytes 9437184 | tf_op jit(solution)/shard_map/all_gather | solution.py:354
  7.2 16.5 %collective-permute-start.8 = (bf16[256,2048]{1,0:T(8,128)(2,1)}, bf16[256,2048]{1,0:T(8,128)(2,1)S(1)}, u32[]{:S(2)}, u32[]{:S(2)}) collective-permute-start(bf16[256,2048]{1,0:T(8,128)(2,1)} %bitcast.65), channel_id=1, source_target_pairs={{0,24},{1,25},{2,26},{3,27},{4,28},{5,29},{6,30},{7,31}} | collective-permute-start | bytes 3145736 | tf_op jit(solution)/shard_map/ppermute | solution.py:26
  38.6 31.3 %collective-permute-start = (bf16[64,2048]{1,0:T(8,128)(2,1)}, bf16[64,2048]{1,0:T(8,128)(2,1)}, u32[]{:S(2)}, u32[]{:S(2)}) collective-permute-start(bf16[64,2048]{1,0:T(8,128)(2,1)} %get-tuple-element.18), channel_id=1, source_target_pairs={{0,1},{1,0},{2,3},{3,2},{4,5},{5,4},{6,7},{7,6},{8,9},{9,8},{10,11... | collective-permute-start | bytes 786440 | tf_op jit(solution)/shard_map/ppermute | solution.py:20
  47.0 75.5 %collective-permute-start.25 = (bf16[4,64,256]{1,2,0:T(8,128)(2,1)}, bf16[4,64,256]{1,2,0:T(8,128)(2,1)}, u32[]{:S(2)}, u32[]{:S(2)}) collective-permute-start(bf16[4,64,256]{1,2,0:T(8,128)(2,1)} %pad_maximum_fusion), channel_id=1, source_target_pairs={{0,1},{1,0},{2,3},{3,2},{4,5},{5,4},{6,7},{7,6},{8,9},{9,8},{10,11... | collective-permute-start | bytes 393224 | tf_op jit(solution)/shard_map/ppermute | solution.py:20
  52.8 20.1 %collective-permute-start.2 = (bf16[64,2048]{1,0:T(8,128)(2,1)}, bf16[64,2048]{1,0:T(8,128)(2,1)S(1)}, u32[]{:S(2)}, u32[]{:S(2)}) collective-permute-start(bf16[64,2048]{1,0:T(8,128)(2,1)} %copy-done.4), channel_id=1, source_target_pairs={{0,1},{1,0},{2,3},{3,2},{4,5},{5,4},{6,7},{7,6},{8,9},{9,8},{10,11... | collective-permute-start | bytes 786440 | tf_op jit(solution)/shard_map/ppermute | solution.py:20
  58.5 15.7 %collective-permute-start.4 = (bf16[64,2048]{1,0:T(8,128)(2,1)}, bf16[64,2048]{1,0:T(8,128)(2,1)S(1)}, u32[]{:S(2)}, u32[]{:S(2)}) collective-permute-start(bf16[64,2048]{1,0:T(8,128)(2,1)} %copy-done.3), channel_id=1, source_target_pairs={{0,1},{1,0},{2,3},{3,2},{4,5},{5,4},{6,7},{7,6},{8,9},{9,8},{10,11... | collective-permute-start | bytes 786440 | tf_op jit(solution)/shard_map/ppermute | solution.py:20
  64.2 12.6 %collective-permute-start.6 = (bf16[64,2048]{1,0:T(8,128)(2,1)S(1)}, bf16[64,2048]{1,0:T(8,128)(2,1)S(1)}, u32[]{:S(2)}, u32[]{:S(2)}) collective-permute-start(bf16[64,2048]{1,0:T(8,128)(2,1)S(1)} %get-tuple-element.24), channel_id=1, source_target_pairs={{0,1},{1,0},{2,3},{3,2},{4,5},{5,4},{6,7},{7,6},{8,9},{9,8},{10,11... | collective-permute-start | bytes 786440 | tf_op jit(solution)/shard_map/ppermute | solution.py:20
  71.7 28.5 %collective-permute-start.1 = (bf16[64,2048]{1,0:T(8,128)(2,1)}, bf16[64,2048]{1,0:T(8,128)(2,1)S(1)}, u32[]{:S(2)}, u32[]{:S(2)}) collective-permute-start(bf16[64,2048]{1,0:T(8,128)(2,1)} %add_convert_fusion.2), channel_id=1, source_target_pairs={{0,6},{1,7},{2,4},{3,5},{4,2},{5,3},{6,0},{7,1},{8,14},{9,15},{10,... | collective-permute-start | bytes 786440 | tf_op jit(solution)/shard_map/ppermute | solution.py:20
  72.9 41.9 %collective-permute-start.3 = (bf16[64,2048]{1,0:T(8,128)(2,1)S(1)}, bf16[64,2048]{1,0:T(8,128)(2,1)S(1)}, u32[]{:S(2)}, u32[]{:S(2)}) collective-permute-start(bf16[64,2048]{1,0:T(8,128)(2,1)S(1)} %add_convert_fusion.1), channel_id=1, source_target_pairs={{0,4},{1,5},{2,6},{3,7},{4,0},{5,1},{6,2},{7,3},{8,12},{9,13},{10,... | collective-permute-start | bytes 786440 | tf_op jit(solution)/shard_map/ppermute | solution.py:20
  74.2 40.6 %collective-permute-start.5 = (bf16[64,2048]{1,0:T(8,128)(2,1)S(1)}, bf16[64,2048]{1,0:T(8,128)(2,1)S(1)}, u32[]{:S(2)}, u32[]{:S(2)}) collective-permute-start(bf16[64,2048]{1,0:T(8,128)(2,1)S(1)} %add_convert_fusion), channel_id=1, source_target_pairs={{0,2},{1,3},{2,0},{3,1},{4,6},{5,7},{6,4},{7,5},{8,10},{9,11},{10,... | collective-permute-start | bytes 786440 | tf_op jit(solution)/shard_map/ppermute | solution.py:20
  115.0 9.2 %collective-permute-start.7 = (bf16[64,2048]{1,0:T(8,128)(2,1)S(1)}, bf16[64,2048]{1,0:T(8,128)(2,1)S(1)}, u32[]{:S(2)}, u32[]{:S(2)}) collective-permute-start(bf16[64,2048]{1,0:T(8,128)(2,1)S(1)} %get-tuple-element.33), channel_id=1, source_target_pairs={{24,16},{25,17},{26,18},{27,19},{28,20},{29,21},{30,22},{31,23}} | collective-permute-start | bytes 786440 | tf_op jit(solution)/shard_map/ppermute | solution.py:26
  168.5 8.6 %collective-permute-start.26 = (bf16[2,64,256]{1,2,0:T(8,128)(2,1)S(1)}, bf16[2,64,256]{1,2,0:T(8,128)(2,1)S(1)}, u32[]{:S(2)}, u32[]{:S(2)}) collective-permute-start(bf16[2,64,256]{1,2,0:T(8,128)(2,1)S(1)} %pad_maximum_fusion.1), channel_id=1, source_target_pairs={{0,2},{1,3},{2,0},{3,1},{4,6},{5,7},{6,4},{7,5},{8,10},{9,11},{10,... | collective-permute-start | bytes 196616 | tf_op jit(solution)/shard_map/ppermute | solution.py:20
  171.1 6.0 %collective-permute-start.27 = (bf16[2,64,256]{1,2,0:T(8,128)(2,1)S(1)}, bf16[2,64,256]{1,2,0:T(8,128)(2,1)S(1)}, u32[]{:S(2)}, u32[]{:S(2)}) collective-permute-start(bf16[2,64,256]{1,2,0:T(8,128)(2,1)S(1)} %pad_maximum_fusion.2), channel_id=1, source_target_pairs={{0,4},{1,5},{2,6},{3,7},{4,0},{5,1},{6,2},{7,3},{8,12},{9,13},{10,... | collective-permute-start | bytes 196616 | tf_op jit(solution)/shard_map/ppermute | solution.py:20
  172.1 10.9 %collective-permute-start.28 = (bf16[2,64,256]{1,2,0:T(8,128)(2,1)S(1)}, bf16[2,64,256]{1,2,0:T(8,128)(2,1)S(1)}, u32[]{:S(2)}, u32[]{:S(2)}) collective-permute-start(bf16[2,64,256]{1,2,0:T(8,128)(2,1)S(1)} %pad_maximum_fusion.3), channel_id=1, source_target_pairs={{0,6},{1,7},{2,4},{3,5},{4,2},{5,3},{6,0},{7,1},{8,14},{9,15},{10,... | collective-permute-start | bytes 196616 | tf_op jit(solution)/shard_map/ppermute | solution.py:20
  176.4 11.0 %collective-permute-start.10 = (bf16[64,2048]{1,0:T(8,128)(2,1)S(1)}, bf16[64,2048]{1,0:T(8,128)(2,1)S(1)}, u32[]{:S(2)}, u32[]{:S(2)}) collective-permute-start(bf16[64,2048]{1,0:T(8,128)(2,1)S(1)} %broadcast_select_fusion.4.refs_0_), channel_id=1, source_target_pairs={{8,0},{9,1},{10,2},{11,3},{12,4},{13,5},{14,6},{15,7}} | collective-permute-start | bytes 786440 | tf_op jit(solution)/shard_map/ppermute | solution.py:26
  184.5 8.0 %collective-permute-start.23 = (bf16[64,2048]{1,0:T(8,128)(2,1)S(1)}, bf16[64,2048]{1,0:T(8,128)(2,1)S(1)}, u32[]{:S(2)}, u32[]{:S(2)}) collective-permute-start(bf16[64,2048]{1,0:T(8,128)(2,1)S(1)} %broadcast_select_fusion.4.refs_0_), channel_id=1, source_target_pairs={{8,14},{9,15},{10,12},{11,13},{12,10},{13,11},{14,8},{15,9},{16,22... | collective-permute-start | bytes 786440 | tf_op jit(solution)/shard_map/ppermute | solution.py:20
  185.3 7.9 %collective-permute-start.21 = (bf16[64,2048]{1,0:T(8,128)(2,1)S(1)}, bf16[64,2048]{1,0:T(8,128)(2,1)S(1)}, u32[]{:S(2)}, u32[]{:S(2)}) collective-permute-start(bf16[64,2048]{1,0:T(8,128)(2,1)S(1)} %broadcast_select_fusion.4.refs_0_), channel_id=1, source_target_pairs={{8,12},{9,13},{10,14},{11,15},{12,8},{13,9},{14,10},{15,11},{16,20... | collective-permute-start | bytes 786440 | tf_op jit(solution)/shard_map/ppermute | solution.py:20
  186.0 7.9 %collective-permute-start.19 = (bf16[64,2048]{1,0:T(8,128)(2,1)S(1)}, bf16[64,2048]{1,0:T(8,128)(2,1)S(1)}, u32[]{:S(2)}, u32[]{:S(2)}) collective-permute-start(bf16[64,2048]{1,0:T(8,128)(2,1)S(1)} %broadcast_select_fusion.4.refs_0_), channel_id=1, source_target_pairs={{8,10},{9,11},{10,8},{11,9},{12,14},{13,15},{14,12},{15,13},{16,18... | collective-permute-start | bytes 786440 | tf_op jit(solution)/shard_map/ppermute | solution.py:20
  186.7 16.9 %collective-permute-start.18 = (bf16[64,2048]{1,0:T(8,128)(2,1)S(1)}, bf16[64,2048]{1,0:T(8,128)(2,1)S(1)}, u32[]{:S(2)}, u32[]{:S(2)}) collective-permute-start(bf16[64,2048]{1,0:T(8,128)(2,1)S(1)} %broadcast_select_fusion.4.refs_0_), channel_id=1, source_target_pairs={{8,9},{9,8},{10,11},{11,10},{12,13},{13,12},{14,15},{15,14},{16,17... | collective-permute-start | bytes 786440 | tf_op jit(solution)/shard_map/ppermute | solution.py:20
  191.2 14.1 %collective-permute-start.29 = (bf16[64,2048]{1,0:T(8,128)(2,1)S(1)}, bf16[64,2048]{1,0:T(8,128)(2,1)S(1)}, u32[]{:S(2)}, u32[]{:S(2)}) collective-permute-start(bf16[64,2048]{1,0:T(8,128)(2,1)S(1)} %broadcast_select_fusion.5.refs_0_), channel_id=1, source_target_pairs={{0,24},{1,25},{2,26},{3,27},{4,28},{5,29},{6,30},{7,31}} | collective-permute-start | bytes 786440 | tf_op jit(solution)/shard_map/ppermute | solution.py:26
  192.5 11.0 %collective-permute-start.24 = (bf16[64,2048]{1,0:T(8,128)(2,1)S(1)}, bf16[64,2048]{1,0:T(8,128)(2,1)S(1)}, u32[]{:S(2)}, u32[]{:S(2)}) collective-permute-start(bf16[64,2048]{1,0:T(8,128)(2,1)S(1)} %collective-permute-done.23.refs_13_.refs_6_), channel_id=1, source_target_pairs={{8,9},{9,8},{10,11},{11,10},{12,13},{13,12},{14,15},{15,14},{16,17... | collective-permute-start | bytes 786440 | tf_op jit(solution)/shard_map/ppermute | solution.py:20
  193.2 10.4 %collective-permute-start.22 = (bf16[64,2048]{1,0:T(8,128)(2,1)S(1)}, bf16[64,2048]{1,0:T(8,128)(2,1)S(1)}, u32[]{:S(2)}, u32[]{:S(2)}) collective-permute-start(bf16[64,2048]{1,0:T(8,128)(2,1)S(1)} %collective-permute-done.21.refs_11_.refs_4_), channel_id=1, source_target_pairs={{8,9},{9,8},{10,11},{11,10},{12,13},{13,12},{14,15},{15,14},{16,17... | collective-permute-start | bytes 786440 | tf_op jit(solution)/shard_map/ppermute | solution.py:20
  193.9 9.7 %collective-permute-start.20 = (bf16[64,2048]{1,0:T(8,128)(2,1)S(1)}, bf16[64,2048]{1,0:T(8,128)(2,1)S(1)}, u32[]{:S(2)}, u32[]{:S(2)}) collective-permute-start(bf16[64,2048]{1,0:T(8,128)(2,1)S(1)} %collective-permute-done.19.refs_9_.refs_2_), channel_id=1, source_target_pairs={{8,9},{9,8},{10,11},{11,10},{12,13},{13,12},{14,15},{15,14},{16,17... | collective-permute-start | bytes 786440 | tf_op jit(solution)/shard_map/ppermute | solution.py:20
  204.4 12.6 %collective-permute-start.32 = (bf16[4,64,256]{2,1,0:T(8,128)(2,1)S(1)}, bf16[4,64,256]{2,1,0:T(8,128)(2,1)S(1)}, u32[]{:S(2)}, u32[]{:S(2)}) collective-permute-start(bf16[4,64,256]{2,1,0:T(8,128)(2,1)S(1)} %get-tuple-element.27), channel_id=1, source_target_pairs={{8,9},{9,8},{10,11},{11,10},{12,13},{13,12},{14,15},{15,14},{16,17... | collective-permute-start | bytes 393224 | tf_op jit(solution)/shard_map/ppermute | solution.py:20
  212.0 8.3 %collective-permute-start.30 = (bf16[64,2048]{1,0:T(8,128)(2,1)S(1)}, bf16[64,2048]{1,0:T(8,128)(2,1)S(1)}, u32[]{:S(2)}, u32[]{:S(2)}) collective-permute-start(bf16[64,2048]{1,0:T(8,128)(2,1)S(1)} %shard_map.118), channel_id=1, source_target_pairs={{24,0},{25,1},{26,2},{27,3},{28,4},{29,5},{30,6},{31,7}} | collective-permute-start | bytes 786440 | tf_op jit(solution)/shard_map/ppermute | solution.py:26
  227.8 9.1 %collective-permute-start.36 = (bf16[64,2048]{1,0:T(8,128)(2,1)S(1)}, bf16[64,2048]{1,0:T(8,128)(2,1)S(1)}, u32[]{:S(2)}, u32[]{:S(2)}) collective-permute-start(bf16[64,2048]{1,0:T(8,128)(2,1)S(1)} %shard_map.120), channel_id=1, source_target_pairs={{8,16},{9,17},{10,18},{11,19},{12,20},{13,21},{14,22},{15,23}} | collective-permute-start | bytes 786440 | tf_op jit(solution)/shard_map/ppermute | solution.py:26
  228.5 18.8 %collective-permute-start.16 = (bf16[64,2048]{1,0:T(8,128)(2,1)S(1)}, bf16[64,2048]{1,0:T(8,128)(2,1)S(1)}, u32[]{:S(2)}, u32[]{:S(2)}) collective-permute-start(bf16[64,2048]{1,0:T(8,128)(2,1)S(1)} %broadcast_select_fusion.5.refs_0_), channel_id=1, source_target_pairs={{0,6},{1,7},{2,4},{3,5},{4,2},{5,3},{6,0},{7,1},{24,30},{25,31},{2... | collective-permute-start | bytes 786440 | tf_op jit(solution)/shard_map/ppermute | solution.py:20
  231.5 18.8 %collective-permute-start.14 = (bf16[64,2048]{1,0:T(8,128)(2,1)S(1)}, bf16[64,2048]{1,0:T(8,128)(2,1)S(1)}, u32[]{:S(2)}, u32[]{:S(2)}) collective-permute-start(bf16[64,2048]{1,0:T(8,128)(2,1)S(1)} %broadcast_select_fusion.5.refs_0_), channel_id=1, source_target_pairs={{0,4},{1,5},{2,6},{3,7},{4,0},{5,1},{6,2},{7,3},{24,28},{25,29},{2... | collective-permute-start | bytes 786440 | tf_op jit(solution)/shard_map/ppermute | solution.py:20
  233.5 19.1 %collective-permute-start.12 = (bf16[64,2048]{1,0:T(8,128)(2,1)S(1)}, bf16[64,2048]{1,0:T(8,128)(2,1)S(1)}, u32[]{:S(2)}, u32[]{:S(2)}) collective-permute-start(bf16[64,2048]{1,0:T(8,128)(2,1)S(1)} %broadcast_select_fusion.5.refs_0_), channel_id=1, source_target_pairs={{0,2},{1,3},{2,0},{3,1},{4,6},{5,7},{6,4},{7,5},{24,26},{25,27},{2... | collective-permute-start | bytes 786440 | tf_op jit(solution)/shard_map/ppermute | solution.py:20
  243.6 26.6 %collective-permute-start.37 = (bf16[64,2048]{1,0:T(8,128)(2,1)S(1)}, bf16[64,2048]{1,0:T(8,128)(2,1)S(1)}, u32[]{:S(2)}, u32[]{:S(2)}) collective-permute-start(bf16[64,2048]{1,0:T(8,128)(2,1)S(1)} %shard_map.121), channel_id=1, source_target_pairs={{16,24},{17,25},{18,26},{19,27},{20,28},{21,29},{22,30},{23,31}} | collective-permute-start | bytes 786440 | tf_op jit(solution)/shard_map/ppermute | solution.py:26
  245.1 26.0 %collective-permute-start.11 = (bf16[64,2048]{1,0:T(8,128)(2,1)S(1)}, bf16[64,2048]{1,0:T(8,128)(2,1)S(1)}, u32[]{:S(2)}, u32[]{:S(2)}) collective-permute-start(bf16[64,2048]{1,0:T(8,128)(2,1)S(1)} %broadcast_select_fusion.5.refs_0_), channel_id=1, source_target_pairs={{0,1},{1,0},{2,3},{3,2},{4,5},{5,4},{6,7},{7,6},{24,25},{25,24},{2... | collective-permute-start | bytes 786440 | tf_op jit(solution)/shard_map/ppermute | solution.py:20
  247.3 24.5 %collective-permute-start.17 = (bf16[64,2048]{1,0:T(8,128)(2,1)S(1)}, bf16[64,2048]{1,0:T(8,128)(2,1)S(1)}, u32[]{:S(2)}, u32[]{:S(2)}) collective-permute-start(bf16[64,2048]{1,0:T(8,128)(2,1)S(1)} %collective-permute-done.16.refs_6_), channel_id=1, source_target_pairs={{0,1},{1,0},{2,3},{3,2},{4,5},{5,4},{6,7},{7,6},{24,25},{25,24},{2... | collective-permute-start | bytes 786440 | tf_op jit(solution)/shard_map/ppermute | solution.py:20
  250.4 22.0 %collective-permute-start.15 = (bf16[64,2048]{1,0:T(8,128)(2,1)S(1)}, bf16[64,2048]{1,0:T(8,128)(2,1)S(1)}, u32[]{:S(2)}, u32[]{:S(2)}) collective-permute-start(bf16[64,2048]{1,0:T(8,128)(2,1)S(1)} %collective-permute-done.14.refs_4_), channel_id=1, source_target_pairs={{0,1},{1,0},{2,3},{3,2},{4,5},{5,4},{6,7},{7,6},{24,25},{25,24},{2... | collective-permute-start | bytes 786440 | tf_op jit(solution)/shard_map/ppermute | solution.py:20
  252.6 40.5 %collective-permute-start.13 = (bf16[64,2048]{1,0:T(8,128)(2,1)S(1)}, bf16[64,2048]{1,0:T(8,128)(2,1)S(1)}, u32[]{:S(2)}, u32[]{:S(2)}) collective-permute-start(bf16[64,2048]{1,0:T(8,128)(2,1)S(1)} %collective-permute-done.12.refs_2_), channel_id=1, source_target_pairs={{0,1},{1,0},{2,3},{3,2},{4,5},{5,4},{6,7},{7,6},{24,25},{25,24},{2... | collective-permute-start | bytes 786440 | tf_op jit(solution)/shard_map/ppermute | solution.py:20
  270.3 25.9 %collective-permute-start.48 = (bf16[64,2048]{1,0:T(8,128)(2,1)S(1)}, bf16[64,2048]{1,0:T(8,128)(2,1)S(1)}, u32[]{:S(2)}, u32[]{:S(2)}) collective-permute-start(bf16[64,2048]{1,0:T(8,128)(2,1)S(1)} %get-tuple-element.32), channel_id=1, source_target_pairs={{0,4},{1,5},{2,6},{3,7},{4,0},{5,1},{6,2},{7,3},{8,12},{9,13},{10,... | collective-permute-start | bytes 786440 | tf_op jit(solution)/shard_map/ppermute | solution.py:20
  271.0 28.3 %collective-permute-start.46 = (bf16[64,2048]{1,0:T(8,128)(2,1)S(1)}, bf16[64,2048]{1,0:T(8,128)(2,1)S(1)}, u32[]{:S(2)}, u32[]{:S(2)}) collective-permute-start(bf16[64,2048]{1,0:T(8,128)(2,1)S(1)} %get-tuple-element.32), channel_id=1, source_target_pairs={{0,2},{1,3},{2,0},{3,1},{4,6},{5,7},{6,4},{7,5},{8,10},{9,11},{10,... | collective-permute-start | bytes 786440 | tf_op jit(solution)/shard_map/ppermute | solution.py:20
  271.7 30.5 %collective-permute-start.45 = (bf16[64,2048]{1,0:T(8,128)(2,1)S(1)}, bf16[64,2048]{1,0:T(8,128)(2,1)S(1)}, u32[]{:S(2)}, u32[]{:S(2)}) collective-permute-start(bf16[64,2048]{1,0:T(8,128)(2,1)S(1)} %get-tuple-element.32), channel_id=1, source_target_pairs={{0,1},{1,0},{2,3},{3,2},{4,5},{5,4},{6,7},{7,6},{8,9},{9,8},{10,11... | collective-permute-start | bytes 786440 | tf_op jit(solution)/shard_map/ppermute | solution.py:20
  272.4 32.0 %collective-permute-start.50 = (bf16[64,2048]{1,0:T(8,128)(2,1)S(1)}, bf16[64,2048]{1,0:T(8,128)(2,1)S(1)}, u32[]{:S(2)}, u32[]{:S(2)}) collective-permute-start(bf16[64,2048]{1,0:T(8,128)(2,1)S(1)} %get-tuple-element.32), channel_id=1, source_target_pairs={{0,6},{1,7},{2,4},{3,5},{4,2},{5,3},{6,0},{7,1},{8,14},{9,15},{10,... | collective-permute-start | bytes 786440 | tf_op jit(solution)/shard_map/ppermute | solution.py:20
  293.1 17.3 %collective-permute-start.43 = (bf16[64,2048]{1,0:T(8,128)(2,1)S(1)}, bf16[64,2048]{1,0:T(8,128)(2,1)S(1)}, u32[]{:S(2)}, u32[]{:S(2)}) collective-permute-start(bf16[64,2048]{1,0:T(8,128)(2,1)S(1)} %get-tuple-element.31.refs_0_), channel_id=1, source_target_pairs={{24,30},{25,31},{26,28},{27,29},{28,26},{29,27},{30,24},{31,25}} | collective-permute-start | bytes 786440 | tf_op jit(solution)/shard_map/ppermute | solution.py:20
  296.3 15.4 %collective-permute-start.41 = (bf16[64,2048]{1,0:T(8,128)(2,1)S(1)}, bf16[64,2048]{1,0:T(8,128)(2,1)S(1)}, u32[]{:S(2)}, u32[]{:S(2)}) collective-permute-start(bf16[64,2048]{1,0:T(8,128)(2,1)S(1)} %get-tuple-element.31.refs_0_), channel_id=1, source_target_pairs={{24,28},{25,29},{26,30},{27,31},{28,24},{29,25},{30,26},{31,27}} | collective-permute-start | bytes 786440 | tf_op jit(solution)/shard_map/ppermute | solution.py:20
  299.3 13.0 %collective-permute-start.39 = (bf16[64,2048]{1,0:T(8,128)(2,1)S(1)}, bf16[64,2048]{1,0:T(8,128)(2,1)S(1)}, u32[]{:S(2)}, u32[]{:S(2)}) collective-permute-start(bf16[64,2048]{1,0:T(8,128)(2,1)S(1)} %get-tuple-element.31.refs_0_), channel_id=1, source_target_pairs={{24,26},{25,27},{26,24},{27,25},{28,30},{29,31},{30,28},{31,29}} | collective-permute-start | bytes 786440 | tf_op jit(solution)/shard_map/ppermute | solution.py:20
  302.3 12.2 %collective-permute-start.38 = (bf16[64,2048]{1,0:T(8,128)(2,1)S(1)}, bf16[64,2048]{1,0:T(8,128)(2,1)S(1)}, u32[]{:S(2)}, u32[]{:S(2)}) collective-permute-start(bf16[64,2048]{1,0:T(8,128)(2,1)S(1)} %get-tuple-element.31.refs_0_), channel_id=1, source_target_pairs={{24,25},{25,24},{26,27},{27,26},{28,29},{29,28},{30,31},{31,30}} | collective-permute-start | bytes 786440 | tf_op jit(solution)/shard_map/ppermute | solution.py:20
  304.4 13.2 %collective-permute-start.49 = (bf16[64,2048]{1,0:T(8,128)(2,1)S(1)}, bf16[64,2048]{1,0:T(8,128)(2,1)S(1)}, u32[]{:S(2)}, u32[]{:S(2)}) collective-permute-start(bf16[64,2048]{1,0:T(8,128)(2,1)S(1)} %collective-permute-done.48.refs_11_), channel_id=1, source_target_pairs={{0,1},{1,0},{2,3},{3,2},{4,5},{5,4},{6,7},{7,6},{8,9},{9,8},{10,11... | collective-permute-start | bytes 786440 | tf_op jit(solution)/shard_map/ppermute | solution.py:20
  310.5 11.1 %collective-permute-start.47 = (bf16[64,2048]{1,0:T(8,128)(2,1)S(1)}, bf16[64,2048]{1,0:T(8,128)(2,1)S(1)}, u32[]{:S(2)}, u32[]{:S(2)}) collective-permute-start(bf16[64,2048]{1,0:T(8,128)(2,1)S(1)} %collective-permute-done.46.refs_9_), channel_id=1, source_target_pairs={{0,1},{1,0},{2,3},{3,2},{4,5},{5,4},{6,7},{7,6},{8,9},{9,8},{10,11... | collective-permute-start | bytes 786440 | tf_op jit(solution)/shard_map/ppermute | solution.py:20
  311.6 9.9 %collective-permute-start.51 = (bf16[64,2048]{1,0:T(8,128)(2,1)S(1)}, bf16[64,2048]{1,0:T(8,128)(2,1)S(1)}, u32[]{:S(2)}, u32[]{:S(2)}) collective-permute-start(bf16[64,2048]{1,0:T(8,128)(2,1)S(1)} %collective-permute-done.50.refs_13_), channel_id=1, source_target_pairs={{0,1},{1,0},{2,3},{3,2},{4,5},{5,4},{6,7},{7,6},{8,9},{9,8},{10,11... | collective-permute-start | bytes 786440 | tf_op jit(solution)/shard_map/ppermute | solution.py:20
  312.3 10.3 %collective-permute-start.44 = (bf16[64,2048]{1,0:T(8,128)(2,1)S(1)}, bf16[64,2048]{1,0:T(8,128)(2,1)S(1)}, u32[]{:S(2)}, u32[]{:S(2)}) collective-permute-start(bf16[64,2048]{1,0:T(8,128)(2,1)S(1)} %collective-permute-done.43.refs_6_), channel_id=1, source_target_pairs={{24,25},{25,24},{26,27},{27,26},{28,29},{29,28},{30,31},{31,30}} | collective-permute-start | bytes 786440 | tf_op jit(solution)/shard_map/ppermute | solution.py:20
  314.5 13.7 %collective-permute-start.42 = (bf16[64,2048]{1,0:T(8,128)(2,1)S(1)}, bf16[64,2048]{1,0:T(8,128)(2,1)S(1)}, u32[]{:S(2)}, u32[]{:S(2)}) collective-permute-start(bf16[64,2048]{1,0:T(8,128)(2,1)S(1)} %collective-permute-done.41.refs_4_), channel_id=1, source_target_pairs={{24,25},{25,24},{26,27},{27,26},{28,29},{29,28},{30,31},{31,30}} | collective-permute-start | bytes 786440 | tf_op jit(solution)/shard_map/ppermute | solution.py:20
  317.6 14.1 %collective-permute-start.40 = (bf16[64,2048]{1,0:T(8,128)(2,1)S(1)}, bf16[64,2048]{1,0:T(8,128)(2,1)S(1)}, u32[]{:S(2)}, u32[]{:S(2)}) collective-permute-start(bf16[64,2048]{1,0:T(8,128)(2,1)S(1)} %collective-permute-done.39.refs_2_), channel_id=1, source_target_pairs={{24,25},{25,24},{26,27},{27,26},{28,29},{29,28},{30,31},{31,30}} | collective-permute-start | bytes 786440 | tf_op jit(solution)/shard_map/ppermute | solution.py:20
  (17 other events, 271.0 us)
Sparse Core Ops, SparseCore 0:
  26.1 137.6 all-gather.1
where the time goes:
time: 350 us; the launch traced here: 349 us
  waiting for transfers between devices  131 us (37%)
  starting transfers between devices  126 us (36%)
  Pallas kernels  62 us (18%)
  between operations  15 us (4%)
  local copies, waits for them, and re-layouts  7.65 us (2%)
  other arithmetic  7.43 us (2%)
    ppermute x43, starting transfers between devices, bus_send(): return lax.ppermute(block, BOTH, route)  106 us
    ppermute x43, waiting for transfers between devices, bus_send(): return lax.ppermute(block, BOTH, route)  60.8 us
    all_gather x1, waiting for transfers between devices, plane_body(): lax.all_gather(outer_block, 'bus', axis=0, tiled=True)  39.7 us
    ppermute x9, waiting for transfers between devices, period_send(): return lax.ppermute(block, BOTH, route)  30.8 us
    pallas_call x4, Pallas kernels, forward(): kernel_call(functools.partial(forward_kernel, bool(terms)), jax.ShapeDtyp...  26.9 us
    ppermute x9, starting transfers between devices, period_send(): return lax.ppermute(block, BOTH, route)  19.4 us
    pallas_call x3, Pallas kernels, backward(): kernel_call(backward_kernel, jax.ShapeDtypeStruct((rows, whole), BF16), [...  11.4 us
    pallas_call x1, Pallas kernels, front(): kernel_call(front_kernel, [keep, send] * 4, [in_smem(), in_vmem(), in_vme...  10.9 us
  transfers between devices with their start and end apart: 53, of which 13 were waited for; matrix products, arithmetic and copies ran while one was open for 3% of the time, Pallas kernels for 12%

commit v1 on v0

--- a/solution.py
+++ b/solution.py
@@ -43,10 +43,11 @@
     return [parts[flip] for flip in range(8)]
 
 
-def reduce_parts(parts, periods):
+def reduce_parts(keep, send, periods):
+    there = bus_send(send, 1, periods)
     total = None
-    for flip in (6, 4, 2, 0):
-        here = parts[flip] + bus_send(parts[flip ^ 1], 1, periods).astype(F32)
+    for place, flip in ((3, 6), (2, 4), (1, 2), (0, 0)):
+        here = keep[place] + there[place].astype(F32)
         if flip:
             here = bus_send(here.astype(BF16), flip, periods).astype(F32)
         total = here if total is None else total + here
@@ -90,9 +91,18 @@
     )
 
 
+def deal(rank, whole, keep, send):
+    rows = keep.shape[1]
+    for place, flip in enumerate(EVEN):
+        owner = pl.multiple_of((rank ^ flip) * rows, rows)
+        keep[place] = whole[pl.ds(owner, rows), :].astype(keep.dtype)
+        owner = pl.multiple_of((rank ^ flip ^ 1) * rows, rows)
+        send[place] = whole[pl.ds(owner, rows), :].astype(send.dtype)
+
+
 def front_kernel(
     rank_ref, active, rhs, residual_hbm, inverse_hbm, sens_hbm,
-    k0, s0, k1, s1, k2, s2, k3, s3,
+    keep, send,
     residual, inverse, sens, net, solve_t, partial, sems,
 ):
     rank = rank_ref[0]
@@ -123,21 +133,18 @@
     units = rhs.shape[0]
     own = pl.ds(pl.multiple_of(rank * units, units), units)
     partial[:, own] += rhs[...].T
-    rows = k0.shape[0]
-    for flip, out in enumerate((k0, s0, k1, s1, k2, s2, k3, s3)):
-        owner = pl.multiple_of((rank ^ flip) * rows, rows)
-        out[...] = partial[pl.ds(owner, rows), :].astype(out.dtype)
+    deal(rank, partial, keep, send)
 
 
 def front(rank, active, rhs, residual, inverse, sens):
     buses, columns = residual.shape
     units = sens.shape[1]
     rows = columns // 8
-    keep = jax.ShapeDtypeStruct((rows, units), F32)
-    send = jax.ShapeDtypeStruct((rows, units), BF16)
+    keep = jax.ShapeDtypeStruct((4, rows, units), F32)
+    send = jax.ShapeDtypeStruct((4, rows, units), BF16)
     return kernel_call(
         front_kernel,
-        [keep, send] * 4,
+        [keep, send],
         [in_smem(), in_vmem(), in_vmem(), anywhere(), anywhere(), anywhere()],
         [
             pltpu.VMEM((buses, columns), F32),
@@ -217,7 +224,7 @@
     units = weights.shape[0] // 8
     return kernel_call(
         functools.partial(forward_kernel, bool(terms)),
-        jax.ShapeDtypeStruct((rows, whole), BF16),
+        jax.ShapeDtypeStruct((rows, whole), BF16 if terms else F32),
         [in_smem(), in_vmem()] + [anywhere()] + [in_vmem()] * len(terms),
         [pltpu.VMEM((8, units, whole), BF16), pltpu.SemaphoreType.DMA((8,))],
         2 * rows * whole * whole,
@@ -236,23 +243,25 @@
 
 
 def couple_kernel(rank_ref, schur, *refs):
-    parts, (keep, send, product, whole) = refs[:8], refs[8:]
+    parts, (keep, send, costate, coupling, product, whole) = refs[:8], refs[8:]
     rank = rank_ref[0]
     assemble(rank, parts, (), whole)
     product[...] = times_t(whole[...], schur[...])
-    rows = keep.shape[1]
-    for place, flip in enumerate(EVEN):
-        keep[place] = product[pl.ds(pl.multiple_of((rank ^ flip) * rows, rows), rows), :].astype(BF16)
-        send[place] = product[pl.ds(pl.multiple_of((rank ^ flip ^ 1) * rows, rows), rows), :].astype(BF16)
+    deal(rank, product, keep, send)
+    coupling[...] = product[...].T
+    units = schur.shape[0]
+    own = pl.ds(pl.multiple_of(rank * units, units), units)
+    costate[...] = whole[:, own].astype(F32).T
 
 
 def couple(rank, schur, parts):
     units, whole = schur.shape
     rows = parts[0].shape[0]
     piece = jax.ShapeDtypeStruct((4, rows, units), BF16)
+    out = jax.ShapeDtypeStruct((units, 8 * rows), F32)
     return kernel_call(
         couple_kernel,
-        [piece, piece],
+        [piece, piece, out, out],
         [in_smem(), in_vmem()] + [in_vmem()] * 8,
         [pltpu.VMEM((8 * rows, units), F32), pltpu.VMEM((8 * rows, whole), BF16)],
         16 * rows * whole * units,
@@ -260,28 +269,24 @@
     )(rank, schur, *parts)
 
 
-def costate_kernel(rank_ref, schur, *refs):
-    first, second, (costate, coupling, whole) = refs[:8], refs[8:15], refs[15:]
-    rank = rank_ref[0]
-    assemble(rank, first, second, whole)
-    coupling[...] = times_t(schur[...], whole[...])
-    units = schur.shape[0]
-    own = pl.ds(pl.multiple_of(rank * units, units), units)
-    costate[...] = whole[:, own].astype(F32).T
-
-
-def costate_out(rank, schur, first, second):
-    units, whole = schur.shape
-    rows = first[0].shape[0]
-    out = jax.ShapeDtypeStruct((units, 8 * rows), F32)
-    return kernel_call(
-        costate_kernel,
-        [out, out],
-        [in_smem(), in_vmem()] + [in_vmem()] * 15,
-        [pltpu.VMEM((8 * rows, whole), BF16)],
-        16 * rows * whole * units,
-        6 * MIB,
-    )(rank, schur, *first, *second[1:])
+def finish_kernel(rank_ref, driven, *refs):
+    terms, out = refs[:8], refs[8]
+    rank = rank_ref[0]
+    units = terms[0].shape[1]
+    for flip in range(8):
+        own = pl.ds(pl.multiple_of((rank ^ flip) * units, units), units)
+        out[:, own] = (driven[:, own] - terms[flip][...].astype(F32)).astype(out.dtype)
+
+
+def finish(rank, driven, terms):
+    return kernel_call(
+        finish_kernel,
+        jax.ShapeDtypeStruct(driven.shape, BF16),
+        [in_smem(), in_vmem()] + [in_vmem()] * 8,
+        [],
+        driven.size,
+        8 * driven.size,
+    )(rank, driven, *terms)
 
 
 def final_kernel(rank_ref, unit_bus, active, coupling, gain, residual_hbm, inverse_hbm, *refs):
@@ -345,15 +350,11 @@
     rank = lax.axis_index("bus").reshape(1)
     last = lax.axis_size("period") - 1
     everyone = tuple(range(last + 1))
-    inner = tuple(range(1, last))
-    outer = (0, last)
     rows = residual.shape[1] // 8
 
-    first_schur = period_send(schur, 0, last)
-    outer_block = jnp.where(period == last, first_schur, gain)
-    gain_inner = matrix_outer = lax.all_gather(outer_block, "bus", axis=0, tiled=True)
-    terms = front(rank, active, unit_rhs, residual, inverse, sens)
-    unit_right = reduce_parts(terms, everyone)
+    gain_whole = lax.all_gather(gain, "bus", axis=0, tiled=True)
+    keep, send = front(rank, active, unit_rhs, residual, inverse, sens)
+    unit_right = reduce_parts(keep, send, everyone)
 
     start_t = start_state.T.astype(BF16)
 
@@ -367,31 +368,24 @@
     start = jnp.transpose(ordered, (1, 0, 2)).reshape(rows, -1)
 
     costate = unit_right.astype(BF16)
-    for target in range(last - 1, 0, -1):
+    for target in range(last - 1, -1, -1):
         later = period_send(costate, target + 1, target)
-        costate = jnp.where(period == target, backward(rank, later, unit_right, gain_inner), costate)
-    inner_costates = gather_parts(costate, inner)
-    keep, send = couple(rank, schur, inner_costates)
-    coupled_inner = swap_parts(keep, send, inner)
-    later = period_send(costate, 1, 0)
-    costate = jnp.where(period == 0, backward(rank, later, unit_right, matrix_outer), costate)
-
-    at_last = period_send(costate, 0, last)
-    coupled = period_send(forward(rank, at_last, matrix_outer), last, 0)
-    outer_costates = gather_parts(costate, outer)
-    costate_rows, coupling = costate_out(rank, schur, outer_costates, inner_costates)
+        costate = jnp.where(period == target, backward(rank, later, unit_right, gain_whole), costate)
+    costates = gather_parts(costate, everyone)
+    keep, send, costate_rows, coupling = couple(rank, schur, costates)
+    coupled = swap_parts(keep, send, everyone)
 
     state = start
-    driven = forward(rank, start, matrix_outer)
-    advanced = (driven.astype(F32) - coupled.astype(F32)).astype(BF16)
+    advanced = finish(rank, forward(rank, start, gain_whole), coupled)
     for target in range(1, last + 1):
         arrived = period_send(advanced, target - 1, target)
         state = jnp.where(period == target, arrived, state)
-        if target == last - 1:
-            early_states = gather_parts(state, everyone[:-1])
         if target < last:
-            advanced = forward(rank, arrived, gain_inner, coupled_inner)
+            early = state
+            advanced = forward(rank, arrived, gain_whole, coupled)
+    early, state = lax.optimization_barrier((early, state))
     last_states = gather_parts(state, (last,))
+    early_states = gather_parts(early, everyone[:-1])
     storage, update = final(
         rank, unit_bus, active, coupling, gain, residual, inverse, last_states, early_states
     )

time: 350 us -> 323 us (0.923)
  the two profiles are of different devices: /device:TPU:15 before, /device:TPU:2 now
where the time goes in v1:
time: 323 us; the launch traced here: 321 us
  waiting for transfers between devices  184 us (57%)
  starting transfers between devices  56 us (17%)
  Pallas kernels  53.7 us (17%)
  between operations  14.7 us (5%)
  local copies, waits for them, and re-layouts  6.63 us (2%)
  other arithmetic  5.29 us (2%)
    ppermute x33, waiting for transfers between devices, bus_send(): return lax.ppermute(block, BOTH, route)  134 us
    ppermute x33, starting transfers between devices, bus_send(): return lax.ppermute(block, BOTH, route)  47.3 us
    all_gather x1, waiting for transfers between devices, plane_body(): gain_whole = lax.all_gather(gain, 'bus', axis=0, tiled=True)  34.2 us
    pallas_call x3, Pallas kernels, forward(): kernel_call(functools.partial(forward_kernel, bool(terms)), jax.ShapeDtyp...  20.2 us
    ppermute x6, waiting for transfers between devices, period_send(): return lax.ppermute(block, BOTH, route)  15.5 us
    pallas_call x3, Pallas kernels, backward(): kernel_call(backward_kernel, jax.ShapeDtypeStruct((rows, whole), BF16), [...  11.3 us
    pallas_call x1, Pallas kernels, final(): kernel_call(final_kernel, [jax.ShapeDtypeStruct((units, columns), F32), j...  10.3 us
    pallas_call x1, Pallas kernels, front(): kernel_call(front_kernel, [keep, send], [in_smem(), in_vmem(), in_vmem(),...  10.2 us
  transfers between devices with their start and end apart: 40, of which 19 were waited for; matrix products, arithmetic and copies ran while one was open for 3% of the time, Pallas kernels for 8%

profile of v1, /device:TPU:2, one launch (start us, length us, event | category | flops | bytes accessed | tf_op | source)
XLA Modules:
  0.0 320.6 jit_solution(9007499471309028589)
XLA Ops:
  9.9 10.2 %shard_map.112 = (f32[4,64,2048]{2,1,0:T(8,128)S(1)}, bf16[4,64,2048]{2,1,0:T(8,128)(2,1)S(1)}) custom-call(s32[1]{0:T(128)} %bitcast.rank_ref, s32[1280,1]{1,0:T(8,128)S(1)} %copy.15.active, f32[256,512]{1,0:T(8,128)S(1)} %bitcast.76, f32[1280,512]{1,0:T(8,128)} %bitcast.88, bf16[1280,1280]{1,0:T(8,128)(2,1)} %bitcast.86, bf16[1280,2048]{1,0:T(8,128)(2,1)} %sens_hbm.1), custom_call_target="tpu_custom_call" | custom-call | flops 4362076160 | bytes 25165824 | tf_op jit(solution)/shard_map/pallas_call | solution.py:145
  20.1 1.6 collective-permute-start
  21.7 34.5 %collective-permute-done = bf16[4,64,2048]{2,1,0:T(8,128)(2,1)S(1)} collective-permute-done((bf16[4,64,2048]{2,1,0:T(8,128)(2,1)S(1)}, bf16[4,64,2048]{2,1,0:T(8,128)(2,1)S(1)}, u32[]{:S(2)}, u32[]{:S(2)}) %collective-permute-start) | collective-permute-done | bytes 1048608 | tf_op jit(solution)/shard_map/ppermute | solution.py:20
  58.1 3.3 %collective-permute-start.1 = (bf16[64,2048]{1,0:T(8,128)(2,1)}, bf16[64,2048]{1,0:T(8,128)(2,1)}, u32[]{:S(2)}, u32[]{:S(2)}) collective-permute-start(bf16[64,2048]{1,0:T(8,128)(2,1)} %get-tuple-element.27), channel_id=1, source_target_pairs={{0,6},{1,7},{2,4},{3,5},{4,2},{5,3},{6,0},{7,1},{8,14},{9,15},{10,... | collective-permute-start | bytes 786440 | tf_op jit(solution)/shard_map/ppermute | solution.py:20
  64.8 5.6 %collective-permute-done.1 = bf16[64,2048]{1,0:T(8,128)(2,1)} collective-permute-done((bf16[64,2048]{1,0:T(8,128)(2,1)}, bf16[64,2048]{1,0:T(8,128)(2,1)}, u32[]{:S(2)}, u32[]{:S(2)}) %collective-permute-start.1) | collective-permute-done | bytes 262176 | tf_op jit(solution)/shard_map/ppermute | solution.py:20
  70.4 42.5 %collective-permute-done.2 = bf16[64,2048]{1,0:T(8,128)(2,1)} collective-permute-done((bf16[64,2048]{1,0:T(8,128)(2,1)}, bf16[64,2048]{1,0:T(8,128)(2,1)}, u32[]{:S(2)}, u32[]{:S(2)}) %collective-permute-start.2) | collective-permute-done | bytes 262176 | tf_op jit(solution)/shard_map/ppermute | solution.py:20
  112.9 2.0 fusion.4
  116.3 2.2 collective-permute-done.4.vector
  118.5 34.2 %all-gather.3.cloned.1.call-done = bf16[1,2048,2048]{2,1,0:T(8,128)(2,1)} async-done(((bf16[1,256,2048]{2,1,0:T(8,128)(2,1)}), bf16[1,2048,2048]{2,1,0:T(8,128)(2,1)}) %all-gather.3.cloned.1.call-update) | async-done | bytes 8388624 | tf_op jit(solution)/shard_map/all_gather | solution.py:355
  152.7 3.8 %shard_map.113 = bf16[64,2048]{1,0:T(8,128)(2,1)S(1)} custom-call(s32[1]{0:T(128)} %bitcast.rank_ref, bf16[64,2048]{1,0:T(8,128)(2,1)S(1)} %collective-permute-done.4.vector, f32[64,2048]{1,0:T(8,128)S(1)} %get-tuple-element.26.base, bf16[2048,2048]{1,0:T(8,128)(2,1)} %bitcast.78), custom_call_target="tpu_custom_call" | custom-call | flops 536870912 | bytes 8388608 | tf_op jit(solution)/shard_map/pallas_call | solution.py:208
  156.5 3.2 collective-permute-start.5
  160.7 2.8 collective-permute-done.5.vector
  163.6 3.8 %shard_map.114 = bf16[64,2048]{1,0:T(8,128)(2,1)S(1)} custom-call(s32[1]{0:T(128)} %bitcast.rank_ref, bf16[64,2048]{1,0:T(8,128)(2,1)S(1)} %collective-permute-done.5.vector, f32[64,2048]{1,0:T(8,128)S(1)} %get-tuple-element.26.base, bf16[2048,2048]{1,0:T(8,128)(2,1)} %bitcast.79), custom_call_target="tpu_custom_call" | custom-call | flops 536870912 | bytes 8388608 | tf_op jit(solution)/shard_map/pallas_call | solution.py:208
  168.2 2.5 collective-permute-start.16
  170.8 2.0 collective-permute-start.17
  172.8 3.8 %shard_map.115 = bf16[64,2048]{1,0:T(8,128)(2,1)S(1)} custom-call(s32[1]{0:T(128)} %bitcast.rank_ref, bf16[64,2048]{1,0:T(8,128)(2,1)S(1)} %collective-permute-done.6.vector, f32[64,2048]{1,0:T(8,128)S(1)} %get-tuple-element.26.base, bf16[2048,2048]{1,0:T(8,128)(2,1)} %bitcast.80), custom_call_target="tpu_custom_call" | custom-call | flops 536870912 | bytes 8388608 | tf_op jit(solution)/shard_map/pallas_call | solution.py:208
  176.7 2.0 collective-permute-start.12
  178.7 1.5 collective-permute-start.8
  180.2 6.2 %collective-permute-done.16 = bf16[2,64,256]{1,2,0:T(8,128)(2,1)S(1)} collective-permute-done((bf16[2,64,256]{1,2,0:T(8,128)(2,1)S(1)}, bf16[2,64,256]{1,2,0:T(8,128)(2,1)S(1)}, u32[]{:S(2)}, u32[]{:S(2)}) %collective-permute-start.16) | collective-permute-done | bytes 65568 | tf_op jit(solution)/shard_map/ppermute | solution.py:20
  186.4 1.4 gather_fusion
  187.8 9.5 %collective-permute-done.10.refs_4_ = bf16[64,2048]{1,0:T(8,128)(2,1)S(1)} collective-permute-done((bf16[64,2048]{1,0:T(8,128)(2,1)S(1)}, bf16[64,2048]{1,0:T(8,128)(2,1)S(1)}, u32[]{:S(2)}, u32[]{:S(2)}) %collective-permute-start.10) | collective-permute-done | bytes 262176 | tf_op jit(solution)/shard_map/ppermute | solution.py:20
  197.4 1.9 collective-permute-start.13
  200.8 6.8 %shard_map.117.driven = f32[64,2048]{1,0:T(8,128)S(1)} custom-call(s32[1]{0:T(128)} %bitcast.rank_ref, bf16[64,2048]{1,0:T(8,128)(2,1)S(1)} %copy.16.vector, bf16[2048,2048]{1,0:T(8,128)(2,1)} %bitcast.81), custom_call_target="tpu_custom_call" | custom-call | flops 536870912 | bytes 8388608 | tf_op jit(solution)/shard_map/pallas_call | solution.py:225
  207.6 3.2 collective-permute-done.13.refs_7_
  210.8 2.8 collective-permute-done.9.refs_3_
  213.6 1.7 shard_map.116
  215.6 4.7 %collective-permute-done.18 = bf16[4,64,256]{2,1,0:T(8,128)(2,1)S(1)} collective-permute-done((bf16[4,64,256]{2,1,0:T(8,128)(2,1)S(1)}, bf16[4,64,256]{2,1,0:T(8,128)(2,1)S(1)}, u32[]{:S(2)}, u32[]{:S(2)}) %collective-permute-start.18) | collective-permute-done | bytes 131104 | tf_op jit(solution)/shard_map/ppermute | solution.py:20
  220.3 2.0 collective-permute-start.21
  222.3 1.5 collective-permute-start.20
  224.9 1.6 collective-permute-done.21
  226.6 1.8 collective-permute-done.20
  229.4 6.7 %shard_map.119 = bf16[64,2048]{1,0:T(8,128)(2,1)S(1)} custom-call(s32[1]{0:T(128)} %bitcast.rank_ref, bf16[64,2048]{1,0:T(8,128)(2,1)S(1)} %collective-permute-done.22.vector, bf16[2048,2048]{1,0:T(8,128)(2,1)} %bitcast.82, bf16[64,256]{1,0:T(8,128)(2,1)S(1)} %get-tuple-element.44.refs_0_.refs_1_, bf16[64,256]{1,0:T(8,128)(2,1)S(1)} %get-tuple-element.48.refs_1_.refs_2_, ...), custom_call_target="tpu_custom_call" | custom-call | flops 536870912 | bytes 8388608 | tf_op jit(solution)/shard_map/pallas_call | solution.py:225
  236.1 1.4 collective-permute-start.23
  237.5 9.3 %collective-permute-done.23.vector = bf16[64,2048]{1,0:T(8,128)(2,1)S(1)} collective-permute-done((bf16[64,2048]{1,0:T(8,128)(2,1)S(1)}, bf16[64,2048]{1,0:T(8,128)(2,1)S(1)}, u32[]{:S(2)}, u32[]{:S(2)}) %collective-permute-start.23) | collective-permute-done | bytes 262176 | tf_op jit(solution)/shard_map/ppermute | solution.py:26
  246.9 6.7 %shard_map.120 = bf16[64,2048]{1,0:T(8,128)(2,1)S(1)} custom-call(s32[1]{0:T(128)} %bitcast.rank_ref, bf16[64,2048]{1,0:T(8,128)(2,1)S(1)} %collective-permute-done.23.vector, bf16[2048,2048]{1,0:T(8,128)(2,1)} %bitcast.83, bf16[64,256]{1,0:T(8,128)(2,1)S(1)} %get-tuple-element.44.refs_0_.refs_1_, bf16[64,256]{1,0:T(8,128)(2,1)S(1)} %get-tuple-element.48.refs_1_.refs_2_, ...), custom_call_target="tpu_custom_call" | custom-call | flops 536870912 | bytes 8388608 | tf_op jit(solution)/shard_map/pallas_call | solution.py:225
  253.6 1.3 collective-permute-start.24
  258.1 1.9 collective-permute-start.33
  260.1 4.6 %collective-permute-start.35 = (bf16[64,2048]{1,0:T(8,128)(2,1)S(1)}, bf16[64,2048]{1,0:T(8,128)(2,1)S(1)}, u32[]{:S(2)}, u32[]{:S(2)}) collective-permute-start(bf16[64,2048]{1,0:T(8,128)(2,1)S(1)} %get-tuple-element.19), channel_id=1, source_target_pairs={{0,4},{1,5},{2,6},{3,7},{4,0},{5,1},{6,2},{7,3},{8,12},{9,13},{10,... | collective-permute-start | bytes 786440 | tf_op jit(solution)/shard_map/ppermute | solution.py:20
  264.7 3.6 %collective-permute-start.37 = (bf16[64,2048]{1,0:T(8,128)(2,1)S(1)}, bf16[64,2048]{1,0:T(8,128)(2,1)S(1)}, u32[]{:S(2)}, u32[]{:S(2)}) collective-permute-start(bf16[64,2048]{1,0:T(8,128)(2,1)S(1)} %get-tuple-element.19), channel_id=1, source_target_pairs={{0,6},{1,7},{2,4},{3,5},{4,2},{5,3},{6,0},{7,1},{8,14},{9,15},{10,... | collective-permute-start | bytes 786440 | tf_op jit(solution)/shard_map/ppermute | solution.py:20
  269.0 2.4 collective-permute-start.32
  272.1 10.5 %collective-permute-done.35.refs_11_ = bf16[64,2048]{1,0:T(8,128)(2,1)S(1)} collective-permute-done((bf16[64,2048]{1,0:T(8,128)(2,1)S(1)}, bf16[64,2048]{1,0:T(8,128)(2,1)S(1)}, u32[]{:S(2)}, u32[]{:S(2)}) %collective-permute-start.35) | collective-permute-done | bytes 262176 | tf_op jit(solution)/shard_map/ppermute | solution.py:20
  284.0 2.6 collective-permute-start.34
  286.6 3.2 %collective-permute-start.36 = (bf16[64,2048]{1,0:T(8,128)(2,1)S(1)}, bf16[64,2048]{1,0:T(8,128)(2,1)S(1)}, u32[]{:S(2)}, u32[]{:S(2)}) collective-permute-start(bf16[64,2048]{1,0:T(8,128)(2,1)S(1)} %collective-permute-done.35.refs_11_), channel_id=1, source_target_pairs={{0,1},{1,0},{2,3},{3,2},{4,5},{5,4},{6,7},{7,6},{8,9},{9,8},{10,11... | collective-permute-start | bytes 786440 | tf_op jit(solution)/shard_map/ppermute | solution.py:20
  289.9 2.6 collective-permute-start.38
  292.5 2.6 collective-permute-done.34.refs_10_
  295.1 5.5 %collective-permute-done.36.refs_12_ = bf16[64,2048]{1,0:T(8,128)(2,1)S(1)} collective-permute-done((bf16[64,2048]{1,0:T(8,128)(2,1)S(1)}, bf16[64,2048]{1,0:T(8,128)(2,1)S(1)}, u32[]{:S(2)}, u32[]{:S(2)}) %collective-permute-start.36) | collective-permute-done | bytes 262176 | tf_op jit(solution)/shard_map/ppermute | solution.py:20
  300.6 2.8 collective-permute-done.38.refs_14_
  303.4 10.3 %shard_map.121 = (f32[256,512]{1,0:T(8,128)}, f32[1280,512]{1,0:T(8,128)}) custom-call(s32[1]{0:T(128)} %bitcast.rank_ref, s32[1,2048]{1,0:T(1,128)S(1)} %bitcast.77, s32[1280,1]{1,0:T(8,128)S(1)} %copy.15.active, f32[256,512]{1,0:T(8,128)S(1)} %copy-done.4, bf16[256,2048]{1,0:T(8,128)(2,1)S(1)} %bitcast.75, f32[1280,512]{1,0:T(8,128)} %bitcast.89, ...), custom_call_target="tpu_custom_call" | custom-call | flops 4898947072 | bytes 25165824 | tf_op jit(solution)/shard_map/pallas_call | solution.py:327
  (97 shorter events, 21.3 us)
Async XLA Ops:
  7.2 145.5 %all-gather.3.cloned.1.call-start = ((), (), s32[]{:S(2)}) async-start(), calls=%async_computation | async-start | bytes 9437184 | tf_op jit(solution)/shard_map/all_gather | solution.py:355
  20.1 42.4 %copy-start.7 = (f32[256,512]{1,0:T(8,128)S(1)}, f32[256,512]{1,0:T(8,128)}, u32[]{:S(2)}) copy-start(f32[256,512]{1,0:T(8,128)} %param.15) | copy-start | bytes 1572868
  20.1 36.1 %collective-permute-start = (bf16[4,64,2048]{2,1,0:T(8,128)(2,1)S(1)}, bf16[4,64,2048]{2,1,0:T(8,128)(2,1)S(1)}, u32[]{:S(2)}, u32[]{:S(2)}) collective-permute-start(bf16[4,64,2048]{2,1,0:T(8,128)(2,1)S(1)} %get-tuple-element.14), channel_id=1, source_target_pairs={{0,1},{1,0},{2,3},{3,2},{4,5},{5,4},{6,7},{7,6},{8,9},{9,8},{10,11... | collective-permute-start | bytes 3145736 | tf_op jit(solution)/shard_map/ppermute | solution.py:20
  58.1 12.3 %collective-permute-start.1 = (bf16[64,2048]{1,0:T(8,128)(2,1)}, bf16[64,2048]{1,0:T(8,128)(2,1)}, u32[]{:S(2)}, u32[]{:S(2)}) collective-permute-start(bf16[64,2048]{1,0:T(8,128)(2,1)} %get-tuple-element.27), channel_id=1, source_target_pairs={{0,6},{1,7},{2,4},{3,5},{4,2},{5,3},{6,0},{7,1},{8,14},{9,15},{10,... | collective-permute-start | bytes 786440 | tf_op jit(solution)/shard_map/ppermute | solution.py:20
  61.4 51.5 %collective-permute-start.2 = (bf16[64,2048]{1,0:T(8,128)(2,1)}, bf16[64,2048]{1,0:T(8,128)(2,1)}, u32[]{:S(2)}, u32[]{:S(2)}) collective-permute-start(bf16[64,2048]{1,0:T(8,128)(2,1)} %get-tuple-element.29), channel_id=1, source_target_pairs={{0,4},{1,5},{2,6},{3,7},{4,0},{5,1},{6,2},{7,3},{8,12},{9,13},{10,... | collective-permute-start | bytes 786440 | tf_op jit(solution)/shard_map/ppermute | solution.py:20
  61.4 51.5 %collective-permute-start.3 = (bf16[64,2048]{1,0:T(8,128)(2,1)}, bf16[64,2048]{1,0:T(8,128)(2,1)}, u32[]{:S(2)}, u32[]{:S(2)}) collective-permute-start(bf16[64,2048]{1,0:T(8,128)(2,1)} %get-tuple-element.28), channel_id=1, source_target_pairs={{0,2},{1,3},{2,0},{3,1},{4,6},{5,7},{6,4},{7,5},{8,10},{9,11},{10,... | collective-permute-start | bytes 786440 | tf_op jit(solution)/shard_map/ppermute | solution.py:20
  64.2 95.5 %collective-permute-start.14 = (bf16[4,64,256]{1,2,0:T(8,128)(2,1)}, bf16[4,64,256]{1,2,0:T(8,128)(2,1)}, u32[]{:S(2)}, u32[]{:S(2)}) collective-permute-start(bf16[4,64,256]{1,2,0:T(8,128)(2,1)} %pad_maximum_fusion), channel_id=1, source_target_pairs={{0,1},{1,0},{2,3},{3,2},{4,5},{5,4},{6,7},{7,6},{8,9},{9,8},{10,11... | collective-permute-start | bytes 393224 | tf_op jit(solution)/shard_map/ppermute | solution.py:20
  114.9 3.6 %collective-permute-start.4 = (bf16[64,2048]{1,0:T(8,128)(2,1)}, bf16[64,2048]{1,0:T(8,128)(2,1)S(1)}, u32[]{:S(2)}, u32[]{:S(2)}) collective-permute-start(bf16[64,2048]{1,0:T(8,128)(2,1)} %get-tuple-element.25), channel_id=1, source_target_pairs={{24,16},{25,17},{26,18},{27,19},{28,20},{29,21},{30,22},{31,23}} | collective-permute-start | bytes 786440 | tf_op jit(solution)/shard_map/ppermute | solution.py:26
  156.5 7.0 %collective-permute-start.5 = (bf16[64,2048]{1,0:T(8,128)(2,1)S(1)}, bf16[64,2048]{1,0:T(8,128)(2,1)S(1)}, u32[]{:S(2)}, u32[]{:S(2)}) collective-permute-start(bf16[64,2048]{1,0:T(8,128)(2,1)S(1)} %broadcast_select_fusion.2), channel_id=1, source_target_pairs={{16,8},{17,9},{18,10},{19,11},{20,12},{21,13},{22,14},{23,15}} | collective-permute-start | bytes 786440 | tf_op jit(solution)/shard_map/ppermute | solution.py:26
  160.7 7.5 %copy-start.9 = (bf16[1,64,256]{1,2,0:T(8,128)(2,1)S(1)}, bf16[1,64,256]{1,2,0:T(8,128)(2,1)}, u32[]{:S(2)}) copy-start(bf16[1,64,256]{1,2,0:T(8,128)(2,1)} %get-tuple-element.31) | copy-start | bytes 98308
  160.7 10.1 %copy-start.8 = (bf16[1,64,256]{1,2,0:T(8,128)(2,1)S(1)}, bf16[1,64,256]{1,2,0:T(8,128)(2,1)}, u32[]{:S(2)}) copy-start(bf16[1,64,256]{1,2,0:T(8,128)(2,1)} %get-tuple-element.30) | copy-start | bytes 98308
  167.4 5.4 %collective-permute-start.6 = (bf16[64,2048]{1,0:T(8,128)(2,1)S(1)}, bf16[64,2048]{1,0:T(8,128)(2,1)S(1)}, u32[]{:S(2)}, u32[]{:S(2)}) collective-permute-start(bf16[64,2048]{1,0:T(8,128)(2,1)S(1)} %broadcast_select_fusion.3), channel_id=1, source_target_pairs={{8,0},{9,1},{10,2},{11,3},{12,4},{13,5},{14,6},{15,7}} | collective-permute-start | bytes 786440 | tf_op jit(solution)/shard_map/ppermute | solution.py:26
  168.1 10.6 %collective-permute-start.15 = (bf16[2,64,256]{1,2,0:T(8,128)(2,1)S(1)}, bf16[2,64,256]{1,2,0:T(8,128)(2,1)S(1)}, u32[]{:S(2)}, u32[]{:S(2)}) collective-permute-start(bf16[2,64,256]{1,2,0:T(8,128)(2,1)S(1)} %pad_maximum_fusion.1), channel_id=1, source_target_pairs={{0,2},{1,3},{2,0},{3,1},{4,6},{5,7},{6,4},{7,5},{8,10},{9,11},{10,... | collective-permute-start | bytes 196616 | tf_op jit(solution)/shard_map/ppermute | solution.py:20
  168.2 18.1 %collective-permute-start.16 = (bf16[2,64,256]{1,2,0:T(8,128)(2,1)S(1)}, bf16[2,64,256]{1,2,0:T(8,128)(2,1)S(1)}, u32[]{:S(2)}, u32[]{:S(2)}) collective-permute-start(bf16[2,64,256]{1,2,0:T(8,128)(2,1)S(1)} %pad_maximum_fusion.2), channel_id=1, source_target_pairs={{0,4},{1,5},{2,6},{3,7},{4,0},{5,1},{6,2},{7,3},{8,12},{9,13},{10,... | collective-permute-start | bytes 196616 | tf_op jit(solution)/shard_map/ppermute | solution.py:20
  170.8 15.6 %collective-permute-start.17 = (bf16[2,64,256]{1,2,0:T(8,128)(2,1)S(1)}, bf16[2,64,256]{1,2,0:T(8,128)(2,1)S(1)}, u32[]{:S(2)}, u32[]{:S(2)}) collective-permute-start(bf16[2,64,256]{1,2,0:T(8,128)(2,1)S(1)} %pad_maximum_fusion.3), channel_id=1, source_target_pairs={{0,6},{1,7},{2,4},{3,5},{4,2},{5,3},{6,0},{7,1},{8,14},{9,15},{10,... | collective-permute-start | bytes 196616 | tf_op jit(solution)/shard_map/ppermute | solution.py:20
  176.6 20.7 %collective-permute-start.10 = (bf16[64,2048]{1,0:T(8,128)(2,1)S(1)}, bf16[64,2048]{1,0:T(8,128)(2,1)S(1)}, u32[]{:S(2)}, u32[]{:S(2)}) collective-permute-start(bf16[64,2048]{1,0:T(8,128)(2,1)S(1)} %broadcast_select_fusion.4.refs_0_), channel_id=1, source_target_pairs={{0,4},{1,5},{2,6},{3,7},{4,0},{5,1},{6,2},{7,3},{8,12},{9,13},{10,... | collective-permute-start | bytes 786440 | tf_op jit(solution)/shard_map/ppermute | solution.py:20
  176.7 20.7 %collective-permute-start.12 = (bf16[64,2048]{1,0:T(8,128)(2,1)S(1)}, bf16[64,2048]{1,0:T(8,128)(2,1)S(1)}, u32[]{:S(2)}, u32[]{:S(2)}) collective-permute-start(bf16[64,2048]{1,0:T(8,128)(2,1)S(1)} %broadcast_select_fusion.4.refs_0_), channel_id=1, source_target_pairs={{0,6},{1,7},{2,4},{3,5},{4,2},{5,3},{6,0},{7,1},{8,14},{9,15},{10,... | collective-permute-start | bytes 786440 | tf_op jit(solution)/shard_map/ppermute | solution.py:20
  178.7 20.7 %collective-permute-start.8 = (bf16[64,2048]{1,0:T(8,128)(2,1)S(1)}, bf16[64,2048]{1,0:T(8,128)(2,1)S(1)}, u32[]{:S(2)}, u32[]{:S(2)}) collective-permute-start(bf16[64,2048]{1,0:T(8,128)(2,1)S(1)} %broadcast_select_fusion.4.refs_0_), channel_id=1, source_target_pairs={{0,2},{1,3},{2,0},{3,1},{4,6},{5,7},{6,4},{7,5},{8,10},{9,11},{10,... | collective-permute-start | bytes 786440 | tf_op jit(solution)/shard_map/ppermute | solution.py:20
  187.8 19.8 %collective-permute-start.7 = (bf16[64,2048]{1,0:T(8,128)(2,1)S(1)}, bf16[64,2048]{1,0:T(8,128)(2,1)S(1)}, u32[]{:S(2)}, u32[]{:S(2)}) collective-permute-start(bf16[64,2048]{1,0:T(8,128)(2,1)S(1)} %broadcast_select_fusion.4.refs_0_), channel_id=1, source_target_pairs={{0,1},{1,0},{2,3},{3,2},{4,5},{5,4},{6,7},{7,6},{8,9},{9,8},{10,11... | collective-permute-start | bytes 786440 | tf_op jit(solution)/shard_map/ppermute | solution.py:20
  197.3 10.3 %collective-permute-start.11 = (bf16[64,2048]{1,0:T(8,128)(2,1)S(1)}, bf16[64,2048]{1,0:T(8,128)(2,1)S(1)}, u32[]{:S(2)}, u32[]{:S(2)}) collective-permute-start(bf16[64,2048]{1,0:T(8,128)(2,1)S(1)} %collective-permute-done.10.refs_4_), channel_id=1, source_target_pairs={{0,1},{1,0},{2,3},{3,2},{4,5},{5,4},{6,7},{7,6},{8,9},{9,8},{10,11... | collective-permute-start | bytes 786440 | tf_op jit(solution)/shard_map/ppermute | solution.py:20
  197.4 13.4 %collective-permute-start.13 = (bf16[64,2048]{1,0:T(8,128)(2,1)S(1)}, bf16[64,2048]{1,0:T(8,128)(2,1)S(1)}, u32[]{:S(2)}, u32[]{:S(2)}) collective-permute-start(bf16[64,2048]{1,0:T(8,128)(2,1)S(1)} %collective-permute-done.12.refs_6_), channel_id=1, source_target_pairs={{0,1},{1,0},{2,3},{3,2},{4,5},{5,4},{6,7},{7,6},{8,9},{9,8},{10,11... | collective-permute-start | bytes 786440 | tf_op jit(solution)/shard_map/ppermute | solution.py:20
  199.3 14.3 %collective-permute-start.9 = (bf16[64,2048]{1,0:T(8,128)(2,1)S(1)}, bf16[64,2048]{1,0:T(8,128)(2,1)S(1)}, u32[]{:S(2)}, u32[]{:S(2)}) collective-permute-start(bf16[64,2048]{1,0:T(8,128)(2,1)S(1)} %collective-permute-done.8.refs_2_), channel_id=1, source_target_pairs={{0,1},{1,0},{2,3},{3,2},{4,5},{5,4},{6,7},{7,6},{8,9},{9,8},{10,11... | collective-permute-start | bytes 786440 | tf_op jit(solution)/shard_map/ppermute | solution.py:20
  200.8 12.8 %copy-start = (bf16[1,256,2048]{2,1,0:T(8,128)(2,1)S(1)}, bf16[1,256,2048]{2,1,0:T(8,128)(2,1)}, u32[]{:S(2)}) copy-start(bf16[1,256,2048]{2,1,0:T(8,128)(2,1)} %param.10) | copy-start | bytes 3145732
  215.3 20.7 %copy-start.3 = (f32[256,512]{1,0:T(8,128)}, f32[256,512]{1,0:T(8,128)S(1)}, u32[]{:S(2)}) copy-start(f32[256,512]{1,0:T(8,128)S(1)} %get-tuple-element.15.coupling) | copy-start | bytes 1572868
  215.3 5.0 %collective-permute-start.18 = (bf16[4,64,256]{2,1,0:T(8,128)(2,1)S(1)}, bf16[4,64,256]{2,1,0:T(8,128)(2,1)S(1)}, u32[]{:S(2)}, u32[]{:S(2)}) collective-permute-start(bf16[4,64,256]{2,1,0:T(8,128)(2,1)S(1)} %get-tuple-element.17), channel_id=1, source_target_pairs={{0,1},{1,0},{2,3},{3,2},{4,5},{5,4},{6,7},{7,6},{8,9},{9,8},{10,11... | collective-permute-start | bytes 393224 | tf_op jit(solution)/shard_map/ppermute | solution.py:20
  220.3 6.2 %collective-permute-start.21 = (bf16[2,64,256]{2,1,0:T(8,128)(2,1)S(1)}, bf16[2,64,256]{2,1,0:T(8,128)(2,1)S(1)}, u32[]{:S(2)}, u32[]{:S(2)}) collective-permute-start(bf16[2,64,256]{2,1,0:T(8,128)(2,1)S(1)} %pad_maximum_fusion.6), channel_id=1, source_target_pairs={{0,6},{1,7},{2,4},{3,5},{4,2},{5,3},{6,0},{7,1},{8,14},{9,15},{10,... | collective-permute-start | bytes 196616 | tf_op jit(solution)/shard_map/ppermute | solution.py:20
  222.3 6.0 %collective-permute-start.20 = (bf16[2,64,256]{2,1,0:T(8,128)(2,1)S(1)}, bf16[2,64,256]{2,1,0:T(8,128)(2,1)S(1)}, u32[]{:S(2)}, u32[]{:S(2)}) collective-permute-start(bf16[2,64,256]{2,1,0:T(8,128)(2,1)S(1)} %pad_maximum_fusion.5), channel_id=1, source_target_pairs={{0,4},{1,5},{2,6},{3,7},{4,0},{5,1},{6,2},{7,3},{8,12},{9,13},{10,... | collective-permute-start | bytes 196616 | tf_op jit(solution)/shard_map/ppermute | solution.py:20
  223.9 4.5 %collective-permute-start.19 = (bf16[2,64,256]{2,1,0:T(8,128)(2,1)S(1)}, bf16[2,64,256]{2,1,0:T(8,128)(2,1)S(1)}, u32[]{:S(2)}, u32[]{:S(2)}) collective-permute-start(bf16[2,64,256]{2,1,0:T(8,128)(2,1)S(1)} %pad_maximum_fusion.4), channel_id=1, source_target_pairs={{0,2},{1,3},{2,0},{3,1},{4,6},{5,7},{6,4},{7,5},{8,10},{9,11},{10,... | collective-permute-start | bytes 196616 | tf_op jit(solution)/shard_map/ppermute | solution.py:20
  228.5 0.9 collective-permute-start.22
  236.1 67.3 %copy-start.1 = (bf16[1,256,2048]{2,1,0:T(8,128)(2,1)S(1)}, bf16[1,256,2048]{2,1,0:T(8,128)(2,1)}, u32[]{:S(2)}) copy-start(bf16[1,256,2048]{2,1,0:T(8,128)(2,1)} %param.9) | copy-start | bytes 3145732
  236.1 67.3 %copy-start.5 = (s32[2048]{0:T(1024)S(1)}, s32[2048]{0:T(1024)}, u32[]{:S(2)}) copy-start(s32[2048]{0:T(1024)} %param.17) | copy-start | bytes 24580
  236.1 10.8 %collective-permute-start.23 = (bf16[64,2048]{1,0:T(8,128)(2,1)S(1)}, bf16[64,2048]{1,0:T(8,128)(2,1)S(1)}, u32[]{:S(2)}, u32[]{:S(2)}) collective-permute-start(bf16[64,2048]{1,0:T(8,128)(2,1)S(1)} %shard_map.119), channel_id=1, source_target_pairs={{8,16},{9,17},{10,18},{11,19},{12,20},{13,21},{14,22},{15,23}} | collective-permute-start | bytes 786440 | tf_op jit(solution)/shard_map/ppermute | solution.py:26
  237.5 65.9 %copy-start.4 = (f32[256,512]{1,0:T(8,128)S(1)}, f32[256,512]{1,0:T(8,128)}, u32[]{:S(2)}) copy-start(f32[256,512]{1,0:T(8,128)} %copy-done.3) | copy-start | bytes 1572868
  253.6 2.4 collective-permute-start.24
  256.1 8.6 %collective-permute-start.26 = (bf16[64,2048]{1,0:T(8,128)(2,1)S(1)}, bf16[64,2048]{1,0:T(8,128)(2,1)S(1)}, u32[]{:S(2)}, u32[]{:S(2)}) collective-permute-start(bf16[64,2048]{1,0:T(8,128)(2,1)S(1)} %get-tuple-element.18.refs_0_), channel_id=1, source_target_pairs={{24,26},{25,27},{26,24},{27,25},{28,30},{29,31},{30,28},{31,29}} | collective-permute-start | bytes 786440 | tf_op jit(solution)/shard_map/ppermute | solution.py:20
  256.8 11.5 %collective-permute-start.28 = (bf16[64,2048]{1,0:T(8,128)(2,1)S(1)}, bf16[64,2048]{1,0:T(8,128)(2,1)S(1)}, u32[]{:S(2)}, u32[]{:S(2)}) collective-permute-start(bf16[64,2048]{1,0:T(8,128)(2,1)S(1)} %get-tuple-element.18.refs_0_), channel_id=1, source_target_pairs={{24,28},{25,29},{26,30},{27,31},{28,24},{29,25},{30,26},{31,27}} | collective-permute-start | bytes 786440 | tf_op jit(solution)/shard_map/ppermute | solution.py:20
  257.5 11.5 %collective-permute-start.30 = (bf16[64,2048]{1,0:T(8,128)(2,1)S(1)}, bf16[64,2048]{1,0:T(8,128)(2,1)S(1)}, u32[]{:S(2)}, u32[]{:S(2)}) collective-permute-start(bf16[64,2048]{1,0:T(8,128)(2,1)S(1)} %get-tuple-element.18.refs_0_), channel_id=1, source_target_pairs={{24,30},{25,31},{26,28},{27,29},{28,26},{29,27},{30,24},{31,25}} | collective-permute-start | bytes 786440 | tf_op jit(solution)/shard_map/ppermute | solution.py:20
  258.1 13.2 %collective-permute-start.33 = (bf16[64,2048]{1,0:T(8,128)(2,1)S(1)}, bf16[64,2048]{1,0:T(8,128)(2,1)S(1)}, u32[]{:S(2)}, u32[]{:S(2)}) collective-permute-start(bf16[64,2048]{1,0:T(8,128)(2,1)S(1)} %get-tuple-element.19), channel_id=1, source_target_pairs={{0,2},{1,3},{2,0},{3,1},{4,6},{5,7},{6,4},{7,5},{8,10},{9,11},{10,... | collective-permute-start | bytes 786440 | tf_op jit(solution)/shard_map/ppermute | solution.py:20
  260.1 22.5 %collective-permute-start.35 = (bf16[64,2048]{1,0:T(8,128)(2,1)S(1)}, bf16[64,2048]{1,0:T(8,128)(2,1)S(1)}, u32[]{:S(2)}, u32[]{:S(2)}) collective-permute-start(bf16[64,2048]{1,0:T(8,128)(2,1)S(1)} %get-tuple-element.19), channel_id=1, source_target_pairs={{0,4},{1,5},{2,6},{3,7},{4,0},{5,1},{6,2},{7,3},{8,12},{9,13},{10,... | collective-permute-start | bytes 786440 | tf_op jit(solution)/shard_map/ppermute | solution.py:20
  264.7 18.6 %collective-permute-start.37 = (bf16[64,2048]{1,0:T(8,128)(2,1)S(1)}, bf16[64,2048]{1,0:T(8,128)(2,1)S(1)}, u32[]{:S(2)}, u32[]{:S(2)}) collective-permute-start(bf16[64,2048]{1,0:T(8,128)(2,1)S(1)} %get-tuple-element.19), channel_id=1, source_target_pairs={{0,6},{1,7},{2,4},{3,5},{4,2},{5,3},{6,0},{7,1},{8,14},{9,15},{10,... | collective-permute-start | bytes 786440 | tf_op jit(solution)/shard_map/ppermute | solution.py:20
  268.3 15.7 %collective-permute-start.25 = (bf16[64,2048]{1,0:T(8,128)(2,1)S(1)}, bf16[64,2048]{1,0:T(8,128)(2,1)S(1)}, u32[]{:S(2)}, u32[]{:S(2)}) collective-permute-start(bf16[64,2048]{1,0:T(8,128)(2,1)S(1)} %get-tuple-element.18.refs_0_), channel_id=1, source_target_pairs={{24,25},{25,24},{26,27},{27,26},{28,29},{29,28},{30,31},{31,30}} | collective-permute-start | bytes 786440 | tf_op jit(solution)/shard_map/ppermute | solution.py:20
  269.0 17.6 %collective-permute-start.32 = (bf16[64,2048]{1,0:T(8,128)(2,1)S(1)}, bf16[64,2048]{1,0:T(8,128)(2,1)S(1)}, u32[]{:S(2)}, u32[]{:S(2)}) collective-permute-start(bf16[64,2048]{1,0:T(8,128)(2,1)S(1)} %get-tuple-element.19), channel_id=1, source_target_pairs={{0,1},{1,0},{2,3},{3,2},{4,5},{5,4},{6,7},{7,6},{8,9},{9,8},{10,11... | collective-permute-start | bytes 786440 | tf_op jit(solution)/shard_map/ppermute | solution.py:20
  271.4 18.5 %collective-permute-start.27 = (bf16[64,2048]{1,0:T(8,128)(2,1)S(1)}, bf16[64,2048]{1,0:T(8,128)(2,1)S(1)}, u32[]{:S(2)}, u32[]{:S(2)}) collective-permute-start(bf16[64,2048]{1,0:T(8,128)(2,1)S(1)} %collective-permute-done.26.refs_2_), channel_id=1, source_target_pairs={{24,25},{25,24},{26,27},{27,26},{28,29},{29,28},{30,31},{31,30}} | collective-permute-start | bytes 786440 | tf_op jit(solution)/shard_map/ppermute | solution.py:20
  282.6 9.9 %collective-permute-start.29 = (bf16[64,2048]{1,0:T(8,128)(2,1)S(1)}, bf16[64,2048]{1,0:T(8,128)(2,1)S(1)}, u32[]{:S(2)}, u32[]{:S(2)}) collective-permute-start(bf16[64,2048]{1,0:T(8,128)(2,1)S(1)} %collective-permute-done.28.refs_4_), channel_id=1, source_target_pairs={{24,25},{25,24},{26,27},{27,26},{28,29},{29,28},{30,31},{31,30}} | collective-permute-start | bytes 786440 | tf_op jit(solution)/shard_map/ppermute | solution.py:20
  283.3 9.2 %collective-permute-start.31 = (bf16[64,2048]{1,0:T(8,128)(2,1)S(1)}, bf16[64,2048]{1,0:T(8,128)(2,1)S(1)}, u32[]{:S(2)}, u32[]{:S(2)}) collective-permute-start(bf16[64,2048]{1,0:T(8,128)(2,1)S(1)} %collective-permute-done.30.refs_6_), channel_id=1, source_target_pairs={{24,25},{25,24},{26,27},{27,26},{28,29},{29,28},{30,31},{31,30}} | collective-permute-start | bytes 786440 | tf_op jit(solution)/shard_map/ppermute | solution.py:20
  284.0 11.1 %collective-permute-start.34 = (bf16[64,2048]{1,0:T(8,128)(2,1)S(1)}, bf16[64,2048]{1,0:T(8,128)(2,1)S(1)}, u32[]{:S(2)}, u32[]{:S(2)}) collective-permute-start(bf16[64,2048]{1,0:T(8,128)(2,1)S(1)} %collective-permute-done.33.refs_9_), channel_id=1, source_target_pairs={{0,1},{1,0},{2,3},{3,2},{4,5},{5,4},{6,7},{7,6},{8,9},{9,8},{10,11... | collective-permute-start | bytes 786440 | tf_op jit(solution)/shard_map/ppermute | solution.py:20
  286.6 14.0 %collective-permute-start.36 = (bf16[64,2048]{1,0:T(8,128)(2,1)S(1)}, bf16[64,2048]{1,0:T(8,128)(2,1)S(1)}, u32[]{:S(2)}, u32[]{:S(2)}) collective-permute-start(bf16[64,2048]{1,0:T(8,128)(2,1)S(1)} %collective-permute-done.35.refs_11_), channel_id=1, source_target_pairs={{0,1},{1,0},{2,3},{3,2},{4,5},{5,4},{6,7},{7,6},{8,9},{9,8},{10,11... | collective-permute-start | bytes 786440 | tf_op jit(solution)/shard_map/ppermute | solution.py:20
  289.9 13.5 %collective-permute-start.38 = (bf16[64,2048]{1,0:T(8,128)(2,1)S(1)}, bf16[64,2048]{1,0:T(8,128)(2,1)S(1)}, u32[]{:S(2)}, u32[]{:S(2)}) collective-permute-start(bf16[64,2048]{1,0:T(8,128)(2,1)S(1)} %collective-permute-done.37.refs_13_), channel_id=1, source_target_pairs={{0,1},{1,0},{2,3},{3,2},{4,5},{5,4},{6,7},{7,6},{8,9},{9,8},{10,11... | collective-permute-start | bytes 786440 | tf_op jit(solution)/shard_map/ppermute | solution.py:20
  (3 other events, 9.4 us)
Sparse Core Ops, SparseCore 0:
  10.1 142.5 all-gather.2

commit v2 on v1

--- a/solution.py
+++ b/solution.py
@@ -34,17 +34,38 @@
     return lax.dot_general(left, right, (((1,), (1,)), ((), ())), preferred_element_type=F32)
 
 
+def line_send(block, pairs, periods):
+    size = lax.axis_size("bus")
+    route = [
+        (p * size + 2 * source + y, p * size + 2 * target + y)
+        for p in periods
+        for source, target in pairs
+        for y in range(2)
+    ]
+    return lax.ppermute(block, BOTH, route)
+
+
+def across(block, periods):
+    return line_send(block, ((1, 2), (2, 1)), periods)
+
+
+def outwards(block, periods):
+    return line_send(block, ((1, 0), (2, 3)), periods)
+
+
+def together(*values):
+    return lax.optimization_barrier(values)
+
+
 def gather_parts(block, periods):
-    parts = {0: block}
-    for flip in (6, 4, 2):
-        parts[flip] = bus_send(block, flip, periods)
-    for flip in EVEN:
-        parts[flip ^ 1] = bus_send(parts[flip], 1, periods)
-    return [parts[flip] for flip in range(8)]
-
-
-def reduce_parts(keep, send, periods):
-    there = bus_send(send, 1, periods)
+    four, six = bus_send(block, 4, periods), bus_send(block, 6, periods)
+    two, one = together(bus_send(block, 2, periods), bus_send(block, 1, periods))
+    four, three = together(four, bus_send(two, 1, periods))
+    six, five = together(six, bus_send(four, 1, periods))
+    return [block, one, two, three, four, five, six, bus_send(six, 1, periods)]
+
+
+def reduce_z(keep, there, periods):
     total = None
     for place, flip in ((3, 6), (2, 4), (1, 2), (0, 0)):
         here = keep[place] + there[place].astype(F32)
@@ -61,8 +82,8 @@
         pair = jnp.stack([keep[place], there[place]])
         if flip:
             pair = bus_send(pair, flip, periods)
-        parts[flip], parts[flip ^ 1] = pair[0], pair[1]
-    return [parts[flip] for flip in range(8)]
+        parts[flip] = pair
+    return jnp.concatenate([parts[flip] for flip in EVEN])
 
 
 def in_vmem():
@@ -77,14 +98,14 @@
     return pl.BlockSpec(memory_space=pltpu.SMEM)
 
 
-def kernel_call(kernel, out_shape, in_specs, scratch, flops, bytes_accessed):
+def kernel_call(kernel, out_shape, in_specs, scratch, flops, bytes_accessed, mib):
     return pl.pallas_call(
         kernel,
         out_shape=out_shape,
         in_specs=in_specs,
         out_specs=jax.tree.map(lambda _: in_vmem(), out_shape),
         scratch_shapes=scratch,
-        compiler_params=pltpu.CompilerParams(vmem_limit_bytes=48 * MIB),
+        compiler_params=pltpu.CompilerParams(vmem_limit_bytes=mib * MIB),
         cost_estimate=pl.CostEstimate(
             flops=flops, bytes_accessed=bytes_accessed, transcendentals=0
         ),
@@ -157,79 +178,117 @@
         ],
         2 * buses * columns * (buses + units),
         24 * MIB,
+        48,
     )(rank, active, rhs, residual, inverse, sens)
 
 
-def weight_loads(rank, weights, held, sems):
-    units = held.shape[1]
-    loads = []
+def start_kernel(rank_ref, state, keep, send, whole):
+    whole[...] = state[...].T
+    deal(rank_ref[0], whole, keep, send)
+
+
+def start_pieces(rank, state):
+    units, columns = state.shape
+    piece = jax.ShapeDtypeStruct((4, columns // 8, units), BF16)
+    return kernel_call(
+        start_kernel,
+        [piece, piece],
+        [in_smem(), in_vmem()],
+        [pltpu.VMEM((columns, units), F32)],
+        state.size,
+        6 * state.size,
+        8,
+    )(rank, state)
+
+
+def join_kernel(rank_ref, pieces, out):
+    units = pieces.shape[2]
     for flip in range(8):
-        owner = pl.multiple_of((rank ^ flip) * units, units)
-        source = weights.at[pl.ds(owner, units)]
-        loads.append(pltpu.make_async_copy(source, held.at[flip], sems.at[flip]))
-    return loads
-
-
-def backward_kernel(rank_ref, vector, base, *refs):
-    weights, out, held, total, sems = refs
-    rank = rank_ref[0]
-    loads = weight_loads(rank, weights, held, sems)
+        own = pl.ds(pl.multiple_of((rank_ref[0] ^ flip) * units, units), units)
+        out[:, own] = pieces[flip]
+
+
+def join(rank, pieces):
+    _, rows, units = pieces.shape
+    return kernel_call(
+        join_kernel,
+        jax.ShapeDtypeStruct((rows, 8 * units), BF16),
+        [in_smem(), in_vmem()],
+        [],
+        pieces.size,
+        4 * pieces.size,
+        8,
+    )(rank, pieces)
+
+
+def pack_kernel(*refs):
+    parts, (out, sems) = refs[:7], refs[7:]
+    loads = [pltpu.make_async_copy(part, out.at[j], sems.at[j]) for j, part in enumerate(parts)]
     for load in loads:
         load.start()
-    units = held.shape[1]
+    for load in loads:
+        load.wait()
+
+
+def pack(parts):
+    return kernel_call(
+        pack_kernel,
+        jax.ShapeDtypeStruct((len(parts), *parts[0].shape), BF16),
+        [anywhere()] * len(parts),
+        [pltpu.SemaphoreType.DMA((len(parts),))],
+        0,
+        4 * len(parts) * parts[0].size,
+        48,
+    )(*parts)
+
+
+def backward_kernel(places, vector, base, packed, final_part, out, total):
+    units = final_part.shape[0]
     total[...] = base[...]
-    for flip, load in enumerate(loads):
-        load.wait()
-        own = pl.ds(pl.multiple_of((rank ^ flip) * units, units), units)
-        total[...] += times(vector[:, own], held[flip])
+    for place in range(8):
+        weight = packed[place] if place < 7 else final_part[...]
+        own = pl.ds(pl.multiple_of(places[place] * units, units), units)
+        total[...] += times(vector[:, own], weight)
     out[...] = total[...].astype(out.dtype)
 
 
-def forward_kernel(subtract, rank_ref, vector, *refs):
-    weights, refs = refs[0], refs[1:]
-    terms, (out, held, sems) = (refs[:8], refs[8:]) if subtract else (None, refs)
-    rank = rank_ref[0]
-    loads = weight_loads(rank, weights, held, sems)
-    for load in loads:
-        load.start()
-    units = held.shape[1]
-    for flip, load in enumerate(loads):
-        load.wait()
-        own = pl.ds(pl.multiple_of((rank ^ flip) * units, units), units)
-        product = times_t(vector[...], held[flip])
-        if subtract:
-            product = product - terms[flip][...].astype(F32)
+def forward_kernel(places, vector, packed, final_part, *refs):
+    terms, out = refs if len(refs) > 1 else (None, refs[0])
+    units = final_part.shape[0]
+    for place in range(8):
+        weight = packed[place] if place < 7 else final_part[...]
+        own = pl.ds(pl.multiple_of(places[place] * units, units), units)
+        product = times_t(vector[...], weight)
+        if terms is not None:
+            product = product - terms[places[place] ^ places[0]].astype(F32)
         out[:, own] = product.astype(out.dtype)
 
 
-def backward(rank, vector, base, weights):
+def backward(places, vector, base, weights):
     rows, whole = vector.shape
-    units = weights.shape[0] // 8
     return kernel_call(
         backward_kernel,
         jax.ShapeDtypeStruct((rows, whole), BF16),
-        [in_smem(), in_vmem(), in_vmem()] + [anywhere()],
-        [
-            pltpu.VMEM((8, units, whole), BF16),
-            pltpu.VMEM((rows, whole), F32),
-            pltpu.SemaphoreType.DMA((8,)),
-        ],
+        [in_smem()] + [in_vmem()] * 4,
+        [pltpu.VMEM((rows, whole), F32)],
         2 * rows * whole * whole,
         2 * whole * whole,
-    )(rank, vector, base, weights)
-
-
-def forward(rank, vector, weights, terms=()):
+        12,
+    )(places, vector, base, *weights)
+
+
+def forward(places, vector, weights, terms=None):
     rows, whole = vector.shape
-    units = weights.shape[0] // 8
-    return kernel_call(
-        functools.partial(forward_kernel, bool(terms)),
-        jax.ShapeDtypeStruct((rows, whole), BF16 if terms else F32),
-        [in_smem(), in_vmem()] + [anywhere()] + [in_vmem()] * len(terms),
-        [pltpu.VMEM((8, units, whole), BF16), pltpu.SemaphoreType.DMA((8,))],
+    extra = () if terms is None else (terms,)
+    return kernel_call(
+        forward_kernel,
+        jax.ShapeDtypeStruct((rows, whole), BF16 if extra else F32),
+        [in_smem()] + [in_vmem()] * (3 + len(extra)),
+        [],
         2 * rows * whole * whole,
         2 * whole * whole,
-    )(rank, vector, weights, *terms)
+        12,
+    )(places, vector, *weights, *extra)
 
 
 def assemble(rank, first, second, whole):
@@ -266,27 +325,27 @@
         [pltpu.VMEM((8 * rows, units), F32), pltpu.VMEM((8 * rows, whole), BF16)],
         16 * rows * whole * units,
         4 * MIB,
+        16,
     )(rank, schur, *parts)
 
 
-def finish_kernel(rank_ref, driven, *refs):
-    terms, out = refs[:8], refs[8]
-    rank = rank_ref[0]
-    units = terms[0].shape[1]
+def finish_kernel(rank_ref, driven, terms, out):
+    units = terms.shape[2]
     for flip in range(8):
-        own = pl.ds(pl.multiple_of((rank ^ flip) * units, units), units)
-        out[:, own] = (driven[:, own] - terms[flip][...].astype(F32)).astype(out.dtype)
+        own = pl.ds(pl.multiple_of((rank_ref[0] ^ flip) * units, units), units)
+        out[:, own] = (driven[:, own] - terms[flip].astype(F32)).astype(out.dtype)
 
 
 def finish(rank, driven, terms):
     return kernel_call(
         finish_kernel,
         jax.ShapeDtypeStruct(driven.shape, BF16),
-        [in_smem(), in_vmem()] + [in_vmem()] * 8,
+        [in_smem(), in_vmem(), in_vmem()],
         [],
         driven.size,
         8 * driven.size,
-    )(rank, driven, *terms)
+        8,
+    )(rank, driven, terms)
 
 
 def final_kernel(rank_ref, unit_bus, active, coupling, gain, residual_hbm, inverse_hbm, *refs):
@@ -340,6 +399,7 @@
         ],
         2 * columns * (buses * buses + (buses + units) * whole),
         24 * MIB,
+        48,
     )(rank, unit_bus, active, coupling, gain, residual, inverse, *first, *second[1:])
 
 
@@ -352,38 +412,54 @@
     everyone = tuple(range(last + 1))
     rows = residual.shape[1] // 8
 
-    gain_whole = lax.all_gather(gain, "bus", axis=0, tiled=True)
+    far_end = (rank[0] < 2) | (rank[0] >= 6)
+    order = jnp.where(
+        far_end,
+        jnp.array([0, 1, 2, 3, 4, 5, 6, 7], jnp.int32),
+        jnp.array([0, 1, 2, 3, 6, 7, 4, 5], jnp.int32),
+    )
+    places = rank ^ order
+
+    near, middle, own_y = (
+        bus_send(gain, 2, everyone), across(gain, everyone), bus_send(gain, 1, everyone)
+    )
     keep, send = front(rank, active, unit_rhs, residual, inverse, sens)
-    unit_right = reduce_parts(keep, send, everyone)
-
-    start_t = start_state.T.astype(BF16)
-
-    def start_piece(owner):
-        return lax.dynamic_slice_in_dim(start_t, owner * rows, rows, 0)
-
-    keep = jnp.stack([start_piece(rank[0] ^ flip) for flip in EVEN])
-    send = jnp.stack([start_piece(rank[0] ^ flip ^ 1) for flip in EVEN])
-    pieces = jnp.stack(swap_parts(keep, send, everyone))
-    ordered = jnp.take(pieces, jnp.arange(8, dtype=jnp.int32) ^ rank[0], axis=0)
-    start = jnp.transpose(ordered, (1, 0, 2)).reshape(rows, -1)
+    near, middle, own_y, keep, send = together(near, middle, own_y, keep, send)
+    there = bus_send(send, 1, everyone)
+    near_y = bus_send(near, 1, everyone)
+    middle2, third, near_y = together(
+        across(near, everyone), middle + outwards(middle, everyone), near_y
+    )
+    third_y = bus_send(third, 1, everyone)
+    fourth = middle2 + outwards(middle2, everyone)
+    fourth, third_y, there = together(fourth, third_y, there)
+    packed, fourth_y, unit_right = together(
+        pack([gain, own_y, near, near_y, third, third_y, fourth]),
+        bus_send(fourth, 1, everyone),
+        reduce_z(keep, there, everyone),
+    )
+    weights = [packed, fourth_y]
+    start = join(rank, swap_parts(*start_pieces(rank, start_state), everyone))
 
     costate = unit_right.astype(BF16)
     for target in range(last - 1, -1, -1):
         later = period_send(costate, target + 1, target)
-        costate = jnp.where(period == target, backward(rank, later, unit_right, gain_whole), costate)
+        costate = jnp.where(
+            period == target, backward(places, later, unit_right, weights), costate
+        )
     costates = gather_parts(costate, everyone)
     keep, send, costate_rows, coupling = couple(rank, schur, costates)
     coupled = swap_parts(keep, send, everyone)
 
     state = start
-    advanced = finish(rank, forward(rank, start, gain_whole), coupled)
+    advanced = finish(rank, forward(places, start, weights), coupled)
     for target in range(1, last + 1):
         arrived = period_send(advanced, target - 1, target)
         state = jnp.where(period == target, arrived, state)
         if target < last:
             early = state
-            advanced = forward(rank, arrived, gain_whole, coupled)
-    early, state = lax.optimization_barrier((early, state))
+            advanced = forward(places, arrived, weights, coupled)
+    early, state = together(early, state)
     last_states = gather_parts(state, (last,))
     early_states = gather_parts(early, everyone[:-1])
     storage, update = final(

time: 323 us -> 295 us (0.913)
  waiting for transfers between devices: 184 us -> 159 us
  between operations: 14.7 us -> 1.47 us
  starting transfers between devices: 56 us -> 69.2 us
  Pallas kernels: 53.7 us -> 44 us
  local copies, waits for them, and re-layouts: 6.63 us -> 13.4 us
    ppermute x0 -> x4, waiting for transfers between devices: none -> 44.2 us  [line_send(): return lax.ppermute(block, BOTH, route)]
    ppermute x33 -> x38, waiting for transfers between devices: 134 us -> 96.9 us  [bus_send(): return lax.ppermute(block, BOTH, route)]
    all_gather x1 -> x0, waiting for transfers between devices: 34.2 us -> none  [plane_body(): gain_whole = lax.all_gather(gain, 'bus', axis=0, tiled=True)]
    unnamed x25 -> x40, local copies, waits for them, and re-layouts: 2.19 us -> 12.4 us
    ppermute x33 -> x38, starting transfers between devices: 47.3 us -> 57.4 us  [bus_send(): return lax.ppermute(block, BOTH, route)]
    ppermute x0 -> x4, starting transfers between devices: none -> 5.08 us  [line_send(): return lax.ppermute(block, BOTH, route)]
    pallas_call x3, Pallas kernels: 11.3 us -> 6.3 us  [backward(): kernel_call(backward_kernel, jax.ShapeDtypeStruct((rows, whole), BF16), [...]
    pallas_call x3 -> x6, Pallas kernels: 20.2 us -> 15.4 us  [the longest x3 10.3 us: forward(): kernel_call(forward_kernel, jax.ShapeDtypeStruct((rows, whole), BF16 if e...]
  transfers between devices with their start and end apart: 40 -> 48, of which waited for: 19 -> 23; matrix products, arithmetic and copies ran while one was open for 3% -> 1% of each run, Pallas kernels for 8% -> 6%
where the time goes in v2:
time: 295 us; the launch traced here: 294 us
  waiting for transfers between devices  159 us (54%)
  starting transfers between devices  69.2 us (23%)
  Pallas kernels  44 us (15%)
  local copies, waits for them, and re-layouts  13.4 us (5%)
  other arithmetic  6.72 us (2%)
    ppermute x38, waiting for transfers between devices, bus_send(): return lax.ppermute(block, BOTH, route)  96.9 us
    ppermute x38, starting transfers between devices, bus_send(): return lax.ppermute(block, BOTH, route)  57.4 us
    ppermute x4, waiting for transfers between devices, line_send(): return lax.ppermute(block, BOTH, route)  44.2 us
    ppermute x6, waiting for transfers between devices, period_send(): return lax.ppermute(block, BOTH, route)  17.8 us
    unnamed x40, local copies, waits for them, and re-layouts  12.4 us
    pallas_call x3, Pallas kernels, forward(): kernel_call(forward_kernel, jax.ShapeDtypeStruct((rows, whole), BF16 if e...  10.3 us
    pallas_call x1, Pallas kernels, final(): kernel_call(final_kernel, [jax.ShapeDtypeStruct((units, columns), F32), j...  10.3 us
    pallas_call x1, Pallas kernels, front(): kernel_call(front_kernel, [keep, send], [in_smem(), in_vmem(), in_vmem(),...  10.2 us
  transfers between devices with their start and end apart: 48, of which 23 were waited for; matrix products, arithmetic and copies ran while one was open for 1% of the time, Pallas kernels for 6%

profile of v2, /device:TPU:2, one launch (start us, length us, event | category | flops | bytes accessed | tf_op | source)
XLA Modules:
  0.0 293.7 jit_solution(14466539562401194133)
XLA Ops:
  7.4 10.2 %shard_map.130 = (f32[4,64,2048]{2,1,0:T(8,128)S(1)}, bf16[4,64,2048]{2,1,0:T(8,128)(2,1)S(1)}) custom-call(s32[1]{0:T(128)} %bitcast.rank_ref, s32[1280,1]{1,0:T(8,128)S(1)} %copy.15.active, f32[256,512]{1,0:T(8,128)S(1)} %bitcast.25, f32[1280,512]{1,0:T(8,128)} %bitcast.30, bf16[1280,1280]{1,0:T(8,128)(2,1)} %bitcast.28, bf16[1280,2048]{1,0:T(8,128)(2,1)} %sens_hbm.1), custom_call_target="tpu_custom_call" | custom-call | flops 4362076160 | bytes 25165824 | tf_op jit(solution)/shard_map/pallas_call | solution.py:166
  17.6 8.2 %collective-permute-done.refs_2_ = bf16[256,2048]{1,0:T(8,128)(2,1)S(1)} collective-permute-done((bf16[256,2048]{1,0:T(8,128)(2,1)}, bf16[256,2048]{1,0:T(8,128)(2,1)S(1)}, u32[]{:S(2)}, u32[]{:S(2)}) %collective-permute-start) | collective-permute-done | bytes 1048608 | tf_op jit(solution)/shard_map/ppermute | solution.py:20
  25.8 2.9 %collective-permute-done.2.refs_1_ = bf16[256,2048]{1,0:T(8,128)(2,1)S(1)} collective-permute-done((bf16[256,2048]{1,0:T(8,128)(2,1)}, bf16[256,2048]{1,0:T(8,128)(2,1)S(1)}, u32[]{:S(2)}, u32[]{:S(2)}) %collective-permute-start.2) | collective-permute-done | bytes 1048608 | tf_op jit(solution)/shard_map/ppermute | solution.py:20
  33.3 22.8 %collective-permute-done.4 = bf16[256,2048]{1,0:T(8,128)(2,1)S(1)} collective-permute-done((bf16[256,2048]{1,0:T(8,128)(2,1)}, bf16[256,2048]{1,0:T(8,128)(2,1)S(1)}, u32[]{:S(2)}, u32[]{:S(2)}) %collective-permute-start.4) | collective-permute-done | bytes 1048608 | tf_op jit(solution)/shard_map/ppermute | solution.py:45
  61.4 21.4 %collective-permute-done.6 = bf16[256,2048]{1,0:T(8,128)(2,1)S(1)} collective-permute-done((bf16[256,2048]{1,0:T(8,128)(2,1)S(1)}, bf16[256,2048]{1,0:T(8,128)(2,1)S(1)}, u32[]{:S(2)}, u32[]{:S(2)}) %collective-permute-start.6) | collective-permute-done | bytes 1048608 | tf_op jit(solution)/shard_map/ppermute | solution.py:45
  83.1 2.3 collective-permute-done.8
  85.4 19.7 %collective-permute-done.7.refs_5_ = bf16[256,2048]{1,0:T(8,128)(2,1)S(1)} collective-permute-done((bf16[256,2048]{1,0:T(8,128)(2,1)S(1)}, bf16[256,2048]{1,0:T(8,128)(2,1)S(1)}, u32[]{:S(2)}, u32[]{:S(2)}) %collective-permute-start.7) | collective-permute-done | bytes 1048608 | tf_op jit(solution)/shard_map/ppermute | solution.py:20
  106.8 1.9 collective-permute-start.10
  108.7 2.3 collective-permute-start.11
  111.3 4.9 %shard_map.131.packed = bf16[7,256,2048]{2,1,0:T(8,128)(2,1)} custom-call(bf16[256,2048]{1,0:T(8,128)(2,1)S(1)} %bitcast.22, bf16[256,2048]{1,0:T(8,128)(2,1)S(1)} %copy-done.8, bf16[256,2048]{1,0:T(8,128)(2,1)S(1)} %copy-done.6, bf16[256,2048]{1,0:T(8,128)(2,1)S(1)} %collective-permute-done.5.refs_3_, bf16[256,2048]{1,0:T(8,128)(2,1)S(1)} %add.33.refs_4_, ...), custom_call_target="tpu_custom_call" | custom-call | bytes 14680064 | tf_op jit(solution)/shard_map/pallas_call | solution.py:234
  116.2 1.8 collective-permute-done.10
  117.9 11.8 %collective-permute-done.11 = bf16[64,2048]{1,0:T(8,128)(2,1)S(1)} collective-permute-done((bf16[64,2048]{1,0:T(8,128)(2,1)S(1)}, bf16[64,2048]{1,0:T(8,128)(2,1)S(1)}, u32[]{:S(2)}, u32[]{:S(2)}) %collective-permute-start.11) | collective-permute-done | bytes 262176 | tf_op jit(solution)/shard_map/ppermute | solution.py:20
  131.9 2.3 collective-permute-done.13.vector
  134.2 3.1 %copy-done = bf16[7,256,2048]{2,1,0:T(8,128)(2,1)S(1)} copy-done((bf16[7,256,2048]{2,1,0:T(8,128)(2,1)S(1)}, bf16[7,256,2048]{2,1,0:T(8,128)(2,1)}, u32[]{:S(2)}) %copy-start) | copy-done | bytes 7340056
  137.3 2.1 shard_map.132
  141.5 4.2 %collective-permute-done.14.vector = bf16[64,2048]{1,0:T(8,128)(2,1)S(1)} collective-permute-done((bf16[64,2048]{1,0:T(8,128)(2,1)}, bf16[64,2048]{1,0:T(8,128)(2,1)S(1)}, u32[]{:S(2)}, u32[]{:S(2)}) %collective-permute-start.14) | collective-permute-done | bytes 262176 | tf_op jit(solution)/shard_map/ppermute | solution.py:26
  145.6 3.1 %copy-done.1 = bf16[7,256,2048]{2,1,0:T(8,128)(2,1)S(1)} copy-done((bf16[7,256,2048]{2,1,0:T(8,128)(2,1)S(1)}, bf16[7,256,2048]{2,1,0:T(8,128)(2,1)}, u32[]{:S(2)}) %copy-start.1) | copy-done | bytes 7340056
  148.7 2.1 shard_map.133
  150.8 1.7 broadcast_select_fusion.2
  153.2 3.1 %copy-done.2 = bf16[7,256,2048]{2,1,0:T(8,128)(2,1)S(1)} copy-done((bf16[7,256,2048]{2,1,0:T(8,128)(2,1)S(1)}, bf16[7,256,2048]{2,1,0:T(8,128)(2,1)}, u32[]{:S(2)}) %copy-start.2) | copy-done | bytes 7340056
  156.3 2.1 shard_map.134
  162.0 2.2 collective-permute-start.18
  164.2 5.6 %collective-permute-done.16.refs_2_ = bf16[64,2048]{1,0:T(8,128)(2,1)S(1)} collective-permute-done((bf16[64,2048]{1,0:T(8,128)(2,1)S(1)}, bf16[64,2048]{1,0:T(8,128)(2,1)S(1)}, u32[]{:S(2)}, u32[]{:S(2)}) %collective-permute-start.16) | collective-permute-done | bytes 262176 | tf_op jit(solution)/shard_map/ppermute | solution.py:20
  173.3 8.8 %collective-permute-done.18.refs_4_ = bf16[64,2048]{1,0:T(8,128)(2,1)S(1)} collective-permute-done((bf16[64,2048]{1,0:T(8,128)(2,1)S(1)}, bf16[64,2048]{1,0:T(8,128)(2,1)S(1)}, u32[]{:S(2)}, u32[]{:S(2)}) %collective-permute-start.18) | collective-permute-done | bytes 262176 | tf_op jit(solution)/shard_map/ppermute | solution.py:20
  183.3 1.8 collective-permute-start.26
  185.1 3.3 %collective-permute-done.21.refs_5_ = bf16[64,2048]{1,0:T(8,128)(2,1)S(1)} collective-permute-done((bf16[64,2048]{1,0:T(8,128)(2,1)S(1)}, bf16[64,2048]{1,0:T(8,128)(2,1)S(1)}, u32[]{:S(2)}, u32[]{:S(2)}) %collective-permute-start.21) | collective-permute-done | bytes 262176 | tf_op jit(solution)/shard_map/ppermute | solution.py:20
  189.7 3.2 %shard_map.138.driven = f32[64,2048]{1,0:T(8,128)S(1)} custom-call(s32[8]{0:T(128)S(1)} %fusion.3.places, bf16[64,2048]{1,0:T(8,128)(2,1)S(1)} %shard_map.137.vector, bf16[7,256,2048]{2,1,0:T(8,128)(2,1)S(1)} %copy-done.3, bf16[256,2048]{1,0:T(8,128)(2,1)S(1)} %collective-permute-done.9.final_part), custom_call_target="tpu_custom_call" | custom-call | flops 536870912 | bytes 8388608 | tf_op jit(solution)/shard_map/pallas_call | solution.py:283
  192.9 1.9 collective-permute-done.22.refs_7_
  194.8 1.7 shard_map.135
  197.7 3.8 %collective-permute-done.27 = bf16[4,64,256]{2,1,0:T(8,128)(2,1)S(1)} collective-permute-done((bf16[4,64,256]{2,1,0:T(8,128)(2,1)S(1)}, bf16[4,64,256]{2,1,0:T(8,128)(2,1)S(1)}, u32[]{:S(2)}, u32[]{:S(2)}) %collective-permute-start.27) | collective-permute-done | bytes 131104 | tf_op jit(solution)/shard_map/ppermute | solution.py:20
  201.5 1.7 collective-permute-start.30
  206.1 2.2 collective-permute-done.28
  208.3 2.1 collective-permute-done.29
  211.4 3.2 %shard_map.140 = bf16[64,2048]{1,0:T(8,128)(2,1)S(1)} custom-call(s32[8]{0:T(128)S(1)} %fusion.3.places, bf16[64,2048]{1,0:T(8,128)(2,1)S(1)} %collective-permute-done.31.vector, bf16[7,256,2048]{2,1,0:T(8,128)(2,1)S(1)} %copy-done.3, bf16[256,2048]{1,0:T(8,128)(2,1)S(1)} %collective-permute-done.9.final_part, ...), custom_call_target="tpu_custom_call" | custom-call | flops 536870912 | bytes 8388608 | tf_op jit(solution)/shard_map/pallas_call | solution.py:283
  215.9 10.0 %collective-permute-done.32.vector = bf16[64,2048]{1,0:T(8,128)(2,1)S(1)} collective-permute-done((bf16[64,2048]{1,0:T(8,128)(2,1)S(1)}, bf16[64,2048]{1,0:T(8,128)(2,1)S(1)}, u32[]{:S(2)}, u32[]{:S(2)}) %collective-permute-start.32) | collective-permute-done | bytes 262176 | tf_op jit(solution)/shard_map/ppermute | solution.py:26
  225.9 3.9 %shard_map.141 = bf16[64,2048]{1,0:T(8,128)(2,1)} custom-call(s32[8]{0:T(128)S(1)} %fusion.3.places, bf16[64,2048]{1,0:T(8,128)(2,1)S(1)} %collective-permute-done.32.vector, bf16[7,256,2048]{2,1,0:T(8,128)(2,1)S(1)} %copy-done.3, bf16[256,2048]{1,0:T(8,128)(2,1)S(1)} %collective-permute-done.9.final_part, ...), custom_call_target="tpu_custom_call" | custom-call | flops 536870912 | bytes 8388608 | tf_op jit(solution)/shard_map/pallas_call | solution.py:283
  232.5 3.5 %collective-permute-start.41 = (bf16[64,2048]{1,0:T(8,128)(2,1)S(1)}, bf16[64,2048]{1,0:T(8,128)(2,1)S(1)}, u32[]{:S(2)}, u32[]{:S(2)}) collective-permute-start(bf16[64,2048]{1,0:T(8,128)(2,1)S(1)} %get-tuple-element.81), channel_id=1, source_target_pairs={{0,2},{1,3},{2,0},{3,1},{4,6},{5,7},{6,4},{7,5},{8,10},{9,11},{10,... | collective-permute-start | bytes 786440 | tf_op jit(solution)/shard_map/ppermute | solution.py:20
  236.0 3.5 %collective-permute-start.42 = (bf16[64,2048]{1,0:T(8,128)(2,1)S(1)}, bf16[64,2048]{1,0:T(8,128)(2,1)S(1)}, u32[]{:S(2)}, u32[]{:S(2)}) collective-permute-start(bf16[64,2048]{1,0:T(8,128)(2,1)S(1)} %get-tuple-element.81), channel_id=1, source_target_pairs={{0,1},{1,0},{2,3},{3,2},{4,5},{5,4},{6,7},{7,6},{8,9},{9,8},{10,11... | collective-permute-start | bytes 786440 | tf_op jit(solution)/shard_map/ppermute | solution.py:20
  240.8 2.7 collective-permute-start.43
  244.2 2.4 collective-permute-done.42.refs_8_
  246.6 3.5 %collective-permute-start.44 = (bf16[64,2048]{1,0:T(8,128)(2,1)S(1)}, bf16[64,2048]{1,0:T(8,128)(2,1)S(1)}, u32[]{:S(2)}, u32[]{:S(2)}) collective-permute-start(bf16[64,2048]{1,0:T(8,128)(2,1)S(1)} %collective-permute-done.41.refs_9_), channel_id=1, source_target_pairs={{0,1},{1,0},{2,3},{3,2},{4,5},{5,4},{6,7},{7,6},{8,9},{9,8},{10,11... | collective-permute-start | bytes 786440 | tf_op jit(solution)/shard_map/ppermute | solution.py:20
  250.8 4.1 %collective-permute-start.45 = (bf16[64,2048]{1,0:T(8,128)(2,1)S(1)}, bf16[64,2048]{1,0:T(8,128)(2,1)S(1)}, u32[]{:S(2)}, u32[]{:S(2)}) collective-permute-start(bf16[64,2048]{1,0:T(8,128)(2,1)S(1)} %get-tuple-element.81), channel_id=1, source_target_pairs={{0,6},{1,7},{2,4},{3,5},{4,2},{5,3},{6,0},{7,1},{8,14},{9,15},{10,... | collective-permute-start | bytes 786440 | tf_op jit(solution)/shard_map/ppermute | solution.py:20
  254.9 8.6 %collective-permute-done.43.refs_11_ = bf16[64,2048]{1,0:T(8,128)(2,1)S(1)} collective-permute-done((bf16[64,2048]{1,0:T(8,128)(2,1)S(1)}, bf16[64,2048]{1,0:T(8,128)(2,1)S(1)}, u32[]{:S(2)}, u32[]{:S(2)}) %collective-permute-start.43) | collective-permute-done | bytes 262176 | tf_op jit(solution)/shard_map/ppermute | solution.py:20
  264.2 2.7 collective-permute-start.46
  267.6 6.0 %collective-permute-done.46.refs_12_ = bf16[64,2048]{1,0:T(8,128)(2,1)S(1)} collective-permute-done((bf16[64,2048]{1,0:T(8,128)(2,1)S(1)}, bf16[64,2048]{1,0:T(8,128)(2,1)S(1)}, u32[]{:S(2)}, u32[]{:S(2)}) %collective-permute-start.46) | collective-permute-done | bytes 262176 | tf_op jit(solution)/shard_map/ppermute | solution.py:20
  273.7 2.2 collective-permute-start.47
  276.6 5.6 %collective-permute-done.47.refs_14_ = bf16[64,2048]{1,0:T(8,128)(2,1)S(1)} collective-permute-done((bf16[64,2048]{1,0:T(8,128)(2,1)S(1)}, bf16[64,2048]{1,0:T(8,128)(2,1)S(1)}, u32[]{:S(2)}, u32[]{:S(2)}) %collective-permute-start.47) | collective-permute-done | bytes 262176 | tf_op jit(solution)/shard_map/ppermute | solution.py:20
  283.2 10.3 %shard_map.142 = (f32[256,512]{1,0:T(8,128)}, f32[1280,512]{1,0:T(8,128)}) custom-call(s32[1]{0:T(128)} %bitcast.rank_ref, s32[1,2048]{1,0:T(1,128)S(1)} %bitcast.26, s32[1280,1]{1,0:T(8,128)S(1)} %copy.15.active, f32[256,512]{1,0:T(8,128)S(1)} %copy-done.13, bf16[256,2048]{1,0:T(8,128)(2,1)S(1)} %bitcast.23, f32[1280,512]{1,0:T(8,128)} %bitcast.31, ...), custom_call_target="tpu_custom_call" | custom-call | flops 4898947072 | bytes 25165824 | tf_op jit(solution)/shard_map/pallas_call | solution.py:386
  (124 shorter events, 48.0 us)
Async XLA Ops:
  0.6 25.2 %collective-permute-start = (bf16[256,2048]{1,0:T(8,128)(2,1)}, bf16[256,2048]{1,0:T(8,128)(2,1)S(1)}, u32[]{:S(2)}, u32[]{:S(2)}) collective-permute-start(bf16[256,2048]{1,0:T(8,128)(2,1)} %bitcast.19), channel_id=1, source_target_pairs={{0,2},{1,3},{2,0},{3,1},{4,6},{5,7},{6,4},{7,5},{8,10},{9,11},{10,... | collective-permute-start | bytes 3145736 | tf_op jit(solution)/shard_map/ppermute | solution.py:20
  2.3 23.5 %collective-permute-start.1 = (bf16[256,2048]{1,0:T(8,128)(2,1)}, bf16[256,2048]{1,0:T(8,128)(2,1)}, u32[]{:S(2)}, u32[]{:S(2)}) collective-permute-start(bf16[256,2048]{1,0:T(8,128)(2,1)} %bitcast.20), channel_id=1, source_target_pairs={{2,4},{3,5},{4,2},{5,3},{10,12},{11,13},{12,10},{13,11},{18,20},{1... | collective-permute-start | bytes 3145736 | tf_op jit(solution)/shard_map/ppermute | solution.py:45
  3.9 24.8 %collective-permute-start.2 = (bf16[256,2048]{1,0:T(8,128)(2,1)}, bf16[256,2048]{1,0:T(8,128)(2,1)S(1)}, u32[]{:S(2)}, u32[]{:S(2)}) collective-permute-start(bf16[256,2048]{1,0:T(8,128)(2,1)} %bitcast.21), channel_id=1, source_target_pairs={{0,1},{1,0},{2,3},{3,2},{4,5},{5,4},{6,7},{7,6},{8,9},{9,8},{10,11... | collective-permute-start | bytes 3145736 | tf_op jit(solution)/shard_map/ppermute | solution.py:20
  29.7 26.4 %collective-permute-start.4 = (bf16[256,2048]{1,0:T(8,128)(2,1)}, bf16[256,2048]{1,0:T(8,128)(2,1)S(1)}, u32[]{:S(2)}, u32[]{:S(2)}) collective-permute-start(bf16[256,2048]{1,0:T(8,128)(2,1)} %collective-permute-done.1), channel_id=1, source_target_pairs={{2,0},{3,1},{4,6},{5,7},{10,8},{11,9},{12,14},{13,15},{18,16},{19,... | collective-permute-start | bytes 3145736 | tf_op jit(solution)/shard_map/ppermute | solution.py:45
  31.0 26.8 %collective-permute-start.3 = (bf16[256,2048]{1,0:T(8,128)(2,1)S(1)}, bf16[256,2048]{1,0:T(8,128)(2,1)S(1)}, u32[]{:S(2)}, u32[]{:S(2)}) collective-permute-start(bf16[256,2048]{1,0:T(8,128)(2,1)S(1)} %collective-permute-done.refs_2_), channel_id=1, source_target_pairs={{2,4},{3,5},{4,2},{5,3},{10,12},{11,13},{12,10},{13,11},{18,20},{1... | collective-permute-start | bytes 3145736 | tf_op jit(solution)/shard_map/ppermute | solution.py:45
  31.7 26.1 %collective-permute-start.5 = (bf16[256,2048]{1,0:T(8,128)(2,1)S(1)}, bf16[256,2048]{1,0:T(8,128)(2,1)S(1)}, u32[]{:S(2)}, u32[]{:S(2)}) collective-permute-start(bf16[256,2048]{1,0:T(8,128)(2,1)S(1)} %collective-permute-done.refs_2_), channel_id=1, source_target_pairs={{0,1},{1,0},{2,3},{3,2},{4,5},{5,4},{6,7},{7,6},{8,9},{9,8},{10,11... | collective-permute-start | bytes 3145736 | tf_op jit(solution)/shard_map/ppermute | solution.py:20
  57.8 24.9 %collective-permute-start.6 = (bf16[256,2048]{1,0:T(8,128)(2,1)S(1)}, bf16[256,2048]{1,0:T(8,128)(2,1)S(1)}, u32[]{:S(2)}, u32[]{:S(2)}) collective-permute-start(bf16[256,2048]{1,0:T(8,128)(2,1)S(1)} %collective-permute-done.3), channel_id=1, source_target_pairs={{2,0},{3,1},{4,6},{5,7},{10,8},{11,9},{12,14},{13,15},{18,16},{19,... | collective-permute-start | bytes 3145736 | tf_op jit(solution)/shard_map/ppermute | solution.py:45
  59.3 26.2 %collective-permute-start.8 = (bf16[4,64,2048]{2,1,0:T(8,128)(2,1)S(1)}, bf16[4,64,2048]{2,1,0:T(8,128)(2,1)S(1)}, u32[]{:S(2)}, u32[]{:S(2)}) collective-permute-start(bf16[4,64,2048]{2,1,0:T(8,128)(2,1)S(1)} %get-tuple-element.55), channel_id=1, source_target_pairs={{0,1},{1,0},{2,3},{3,2},{4,5},{5,4},{6,7},{7,6},{8,9},{9,8},{10,11... | collective-permute-start | bytes 3145736 | tf_op jit(solution)/shard_map/ppermute | solution.py:20
  60.8 44.3 %collective-permute-start.7 = (bf16[256,2048]{1,0:T(8,128)(2,1)S(1)}, bf16[256,2048]{1,0:T(8,128)(2,1)S(1)}, u32[]{:S(2)}, u32[]{:S(2)}) collective-permute-start(bf16[256,2048]{1,0:T(8,128)(2,1)S(1)} %add.33.refs_4_), channel_id=1, source_target_pairs={{0,1},{1,0},{2,3},{3,2},{4,5},{5,4},{6,7},{7,6},{8,9},{9,8},{10,11... | collective-permute-start | bytes 3145736 | tf_op jit(solution)/shard_map/ppermute | solution.py:20
  105.1 24.7 %collective-permute-start.9 = (bf16[256,2048]{1,0:T(8,128)(2,1)S(1)}, bf16[256,2048]{1,0:T(8,128)(2,1)S(1)}, u32[]{:S(2)}, u32[]{:S(2)}) collective-permute-start(bf16[256,2048]{1,0:T(8,128)(2,1)S(1)} %add.34.refs_6_), channel_id=1, source_target_pairs={{0,1},{1,0},{2,3},{3,2},{4,5},{5,4},{6,7},{7,6},{8,9},{9,8},{10,11... | collective-permute-start | bytes 3145736 | tf_op jit(solution)/shard_map/ppermute | solution.py:20
  106.8 11.1 %collective-permute-start.10 = (bf16[64,2048]{1,0:T(8,128)(2,1)S(1)}, bf16[64,2048]{1,0:T(8,128)(2,1)S(1)}, u32[]{:S(2)}, u32[]{:S(2)}) collective-permute-start(bf16[64,2048]{1,0:T(8,128)(2,1)S(1)} %get-tuple-element.93), channel_id=1, source_target_pairs={{0,6},{1,7},{2,4},{3,5},{4,2},{5,3},{6,0},{7,1},{8,14},{9,15},{10,... | collective-permute-start | bytes 786440 | tf_op jit(solution)/shard_map/ppermute | solution.py:20
  108.7 21.0 %collective-permute-start.11 = (bf16[64,2048]{1,0:T(8,128)(2,1)S(1)}, bf16[64,2048]{1,0:T(8,128)(2,1)S(1)}, u32[]{:S(2)}, u32[]{:S(2)}) collective-permute-start(bf16[64,2048]{1,0:T(8,128)(2,1)S(1)} %get-tuple-element.95), channel_id=1, source_target_pairs={{0,4},{1,5},{2,6},{3,7},{4,0},{5,1},{6,2},{7,3},{8,12},{9,13},{10,... | collective-permute-start | bytes 786440 | tf_op jit(solution)/shard_map/ppermute | solution.py:20
  111.1 18.6 %collective-permute-start.12 = (bf16[64,2048]{1,0:T(8,128)(2,1)S(1)}, bf16[64,2048]{1,0:T(8,128)(2,1)S(1)}, u32[]{:S(2)}, u32[]{:S(2)}) collective-permute-start(bf16[64,2048]{1,0:T(8,128)(2,1)S(1)} %get-tuple-element.94), channel_id=1, source_target_pairs={{0,2},{1,3},{2,0},{3,1},{4,6},{5,7},{6,4},{7,5},{8,10},{9,11},{10,... | collective-permute-start | bytes 786440 | tf_op jit(solution)/shard_map/ppermute | solution.py:20
  130.6 3.6 %collective-permute-start.13 = (bf16[64,2048]{1,0:T(8,128)(2,1)}, bf16[64,2048]{1,0:T(8,128)(2,1)S(1)}, u32[]{:S(2)}, u32[]{:S(2)}) collective-permute-start(bf16[64,2048]{1,0:T(8,128)(2,1)} %convert_element_type.59), channel_id=1, source_target_pairs={{24,16},{25,17},{26,18},{27,19},{28,20},{29,21},{30,22},{31,23}} | collective-permute-start | bytes 786440 | tf_op jit(solution)/shard_map/ppermute | solution.py:26
  140.2 5.5 %collective-permute-start.14 = (bf16[64,2048]{1,0:T(8,128)(2,1)}, bf16[64,2048]{1,0:T(8,128)(2,1)S(1)}, u32[]{:S(2)}, u32[]{:S(2)}) collective-permute-start(bf16[64,2048]{1,0:T(8,128)(2,1)} %broadcast_select_fusion.1), channel_id=1, source_target_pairs={{16,8},{17,9},{18,10},{19,11},{20,12},{21,13},{22,14},{23,15}} | collective-permute-start | bytes 786440 | tf_op jit(solution)/shard_map/ppermute | solution.py:26
  152.5 0.7 collective-permute-start.15
  159.5 10.3 %collective-permute-start.16 = (bf16[64,2048]{1,0:T(8,128)(2,1)S(1)}, bf16[64,2048]{1,0:T(8,128)(2,1)S(1)}, u32[]{:S(2)}, u32[]{:S(2)}) collective-permute-start(bf16[64,2048]{1,0:T(8,128)(2,1)S(1)} %broadcast_select_fusion.3.refs_0_), channel_id=1, source_target_pairs={{0,2},{1,3},{2,0},{3,1},{4,6},{5,7},{6,4},{7,5},{8,10},{9,11},{10,... | collective-permute-start | bytes 786440 | tf_op jit(solution)/shard_map/ppermute | solution.py:20
  159.6 10.2 %collective-permute-start.17 = (bf16[64,2048]{1,0:T(8,128)(2,1)S(1)}, bf16[64,2048]{1,0:T(8,128)(2,1)S(1)}, u32[]{:S(2)}, u32[]{:S(2)}) collective-permute-start(bf16[64,2048]{1,0:T(8,128)(2,1)S(1)} %broadcast_select_fusion.3.refs_0_), channel_id=1, source_target_pairs={{0,1},{1,0},{2,3},{3,2},{4,5},{5,4},{6,7},{7,6},{8,9},{9,8},{10,11... | collective-permute-start | bytes 786440 | tf_op jit(solution)/shard_map/ppermute | solution.py:20
  161.1 9.7 %collective-permute-start.23 = (bf16[4,64,256]{2,1,0:T(8,128)(2,1)S(1)}, bf16[4,64,256]{2,1,0:T(8,128)(2,1)S(1)}, u32[]{:S(2)}, u32[]{:S(2)}) collective-permute-start(bf16[4,64,256]{2,1,0:T(8,128)(2,1)S(1)} %get-tuple-element.71), channel_id=1, source_target_pairs={{0,1},{1,0},{2,3},{3,2},{4,5},{5,4},{6,7},{7,6},{8,9},{9,8},{10,11... | collective-permute-start | bytes 393224 | tf_op jit(solution)/shard_map/ppermute | solution.py:20
  162.0 20.0 %collective-permute-start.18 = (bf16[64,2048]{1,0:T(8,128)(2,1)S(1)}, bf16[64,2048]{1,0:T(8,128)(2,1)S(1)}, u32[]{:S(2)}, u32[]{:S(2)}) collective-permute-start(bf16[64,2048]{1,0:T(8,128)(2,1)S(1)} %broadcast_select_fusion.3.refs_0_), channel_id=1, source_target_pairs={{0,4},{1,5},{2,6},{3,7},{4,0},{5,1},{6,2},{7,3},{8,12},{9,13},{10,... | collective-permute-start | bytes 786440 | tf_op jit(solution)/shard_map/ppermute | solution.py:20
  169.8 12.2 %collective-permute-start.19 = (bf16[64,2048]{1,0:T(8,128)(2,1)S(1)}, bf16[64,2048]{1,0:T(8,128)(2,1)S(1)}, u32[]{:S(2)}, u32[]{:S(2)}) collective-permute-start(bf16[64,2048]{1,0:T(8,128)(2,1)S(1)} %collective-permute-done.16.refs_2_), channel_id=1, source_target_pairs={{0,1},{1,0},{2,3},{3,2},{4,5},{5,4},{6,7},{7,6},{8,9},{9,8},{10,11... | collective-permute-start | bytes 786440 | tf_op jit(solution)/shard_map/ppermute | solution.py:20
  170.8 14.3 %collective-permute-start.24 = (bf16[2,64,256]{2,1,0:T(8,128)(2,1)S(1)}, bf16[2,64,256]{2,1,0:T(8,128)(2,1)S(1)}, u32[]{:S(2)}, u32[]{:S(2)}) collective-permute-start(bf16[2,64,256]{2,1,0:T(8,128)(2,1)S(1)} %pad_maximum_fusion), channel_id=1, source_target_pairs={{0,2},{1,3},{2,0},{3,1},{4,6},{5,7},{6,4},{7,5},{8,10},{9,11},{10,... | collective-permute-start | bytes 196616 | tf_op jit(solution)/shard_map/ppermute | solution.py:20
  171.6 13.5 %collective-permute-start.20 = (bf16[64,2048]{1,0:T(8,128)(2,1)S(1)}, bf16[64,2048]{1,0:T(8,128)(2,1)S(1)}, u32[]{:S(2)}, u32[]{:S(2)}) collective-permute-start(bf16[64,2048]{1,0:T(8,128)(2,1)S(1)} %broadcast_select_fusion.3.refs_0_), channel_id=1, source_target_pairs={{0,6},{1,7},{2,4},{3,5},{4,2},{5,3},{6,0},{7,1},{8,14},{9,15},{10,... | collective-permute-start | bytes 786440 | tf_op jit(solution)/shard_map/ppermute | solution.py:20
  182.1 6.4 %collective-permute-start.21 = (bf16[64,2048]{1,0:T(8,128)(2,1)S(1)}, bf16[64,2048]{1,0:T(8,128)(2,1)S(1)}, u32[]{:S(2)}, u32[]{:S(2)}) collective-permute-start(bf16[64,2048]{1,0:T(8,128)(2,1)S(1)} %collective-permute-done.18.refs_4_), channel_id=1, source_target_pairs={{0,1},{1,0},{2,3},{3,2},{4,5},{5,4},{6,7},{7,6},{8,9},{9,8},{10,11... | collective-permute-start | bytes 786440 | tf_op jit(solution)/shard_map/ppermute | solution.py:20
  183.2 6.4 %collective-permute-start.25 = (bf16[2,64,256]{2,1,0:T(8,128)(2,1)S(1)}, bf16[2,64,256]{2,1,0:T(8,128)(2,1)S(1)}, u32[]{:S(2)}, u32[]{:S(2)}) collective-permute-start(bf16[2,64,256]{2,1,0:T(8,128)(2,1)S(1)} %pad_maximum_fusion.1), channel_id=1, source_target_pairs={{0,4},{1,5},{2,6},{3,7},{4,0},{5,1},{6,2},{7,3},{8,12},{9,13},{10,... | collective-permute-start | bytes 196616 | tf_op jit(solution)/shard_map/ppermute | solution.py:20
  183.3 6.3 %collective-permute-start.26 = (bf16[2,64,256]{2,1,0:T(8,128)(2,1)S(1)}, bf16[2,64,256]{2,1,0:T(8,128)(2,1)S(1)}, u32[]{:S(2)}, u32[]{:S(2)}) collective-permute-start(bf16[2,64,256]{2,1,0:T(8,128)(2,1)S(1)} %pad_maximum_fusion.2), channel_id=1, source_target_pairs={{0,6},{1,7},{2,4},{3,5},{4,2},{5,3},{6,0},{7,1},{8,14},{9,15},{10,... | collective-permute-start | bytes 196616 | tf_op jit(solution)/shard_map/ppermute | solution.py:20
  188.4 6.4 %collective-permute-start.22 = (bf16[64,2048]{1,0:T(8,128)(2,1)S(1)}, bf16[64,2048]{1,0:T(8,128)(2,1)S(1)}, u32[]{:S(2)}, u32[]{:S(2)}) collective-permute-start(bf16[64,2048]{1,0:T(8,128)(2,1)S(1)} %collective-permute-done.20.refs_6_), channel_id=1, source_target_pairs={{0,1},{1,0},{2,3},{3,2},{4,5},{5,4},{6,7},{7,6},{8,9},{9,8},{10,11... | collective-permute-start | bytes 786440 | tf_op jit(solution)/shard_map/ppermute | solution.py:20
  196.5 5.0 %collective-permute-start.27 = (bf16[4,64,256]{2,1,0:T(8,128)(2,1)S(1)}, bf16[4,64,256]{2,1,0:T(8,128)(2,1)S(1)}, u32[]{:S(2)}, u32[]{:S(2)}) collective-permute-start(bf16[4,64,256]{2,1,0:T(8,128)(2,1)S(1)} %get-tuple-element.73), channel_id=1, source_target_pairs={{0,1},{1,0},{2,3},{3,2},{4,5},{5,4},{6,7},{7,6},{8,9},{9,8},{10,11... | collective-permute-start | bytes 393224 | tf_op jit(solution)/shard_map/ppermute | solution.py:20
  201.5 8.9 %collective-permute-start.30 = (bf16[2,64,256]{2,1,0:T(8,128)(2,1)S(1)}, bf16[2,64,256]{2,1,0:T(8,128)(2,1)S(1)}, u32[]{:S(2)}, u32[]{:S(2)}) collective-permute-start(bf16[2,64,256]{2,1,0:T(8,128)(2,1)S(1)} %pad_maximum_fusion.5), channel_id=1, source_target_pairs={{0,6},{1,7},{2,4},{3,5},{4,2},{5,3},{6,0},{7,1},{8,14},{9,15},{10,... | collective-permute-start | bytes 196616 | tf_op jit(solution)/shard_map/ppermute | solution.py:20
  203.3 5.0 %collective-permute-start.28 = (bf16[2,64,256]{2,1,0:T(8,128)(2,1)S(1)}, bf16[2,64,256]{2,1,0:T(8,128)(2,1)S(1)}, u32[]{:S(2)}, u32[]{:S(2)}) collective-permute-start(bf16[2,64,256]{2,1,0:T(8,128)(2,1)S(1)} %pad_maximum_fusion.3), channel_id=1, source_target_pairs={{0,2},{1,3},{2,0},{3,1},{4,6},{5,7},{6,4},{7,5},{8,10},{9,11},{10,... | collective-permute-start | bytes 196616 | tf_op jit(solution)/shard_map/ppermute | solution.py:20
  204.5 5.9 %collective-permute-start.29 = (bf16[2,64,256]{2,1,0:T(8,128)(2,1)S(1)}, bf16[2,64,256]{2,1,0:T(8,128)(2,1)S(1)}, u32[]{:S(2)}, u32[]{:S(2)}) collective-permute-start(bf16[2,64,256]{2,1,0:T(8,128)(2,1)S(1)} %pad_maximum_fusion.4), channel_id=1, source_target_pairs={{0,4},{1,5},{2,6},{3,7},{4,0},{5,1},{6,2},{7,3},{8,12},{9,13},{10,... | collective-permute-start | bytes 196616 | tf_op jit(solution)/shard_map/ppermute | solution.py:20
  210.5 0.9 collective-permute-start.31
  214.6 11.3 %collective-permute-start.32 = (bf16[64,2048]{1,0:T(8,128)(2,1)S(1)}, bf16[64,2048]{1,0:T(8,128)(2,1)S(1)}, u32[]{:S(2)}, u32[]{:S(2)}) collective-permute-start(bf16[64,2048]{1,0:T(8,128)(2,1)S(1)} %shard_map.140), channel_id=1, source_target_pairs={{8,16},{9,17},{10,18},{11,19},{12,20},{13,21},{14,22},{15,23}} | collective-permute-start | bytes 786440 | tf_op jit(solution)/shard_map/ppermute | solution.py:26
  229.8 2.6 collective-permute-start.33
  232.5 11.0 %collective-permute-start.41 = (bf16[64,2048]{1,0:T(8,128)(2,1)S(1)}, bf16[64,2048]{1,0:T(8,128)(2,1)S(1)}, u32[]{:S(2)}, u32[]{:S(2)}) collective-permute-start(bf16[64,2048]{1,0:T(8,128)(2,1)S(1)} %get-tuple-element.81), channel_id=1, source_target_pairs={{0,2},{1,3},{2,0},{3,1},{4,6},{5,7},{6,4},{7,5},{8,10},{9,11},{10,... | collective-permute-start | bytes 786440 | tf_op jit(solution)/shard_map/ppermute | solution.py:20
  236.0 10.6 %collective-permute-start.42 = (bf16[64,2048]{1,0:T(8,128)(2,1)S(1)}, bf16[64,2048]{1,0:T(8,128)(2,1)S(1)}, u32[]{:S(2)}, u32[]{:S(2)}) collective-permute-start(bf16[64,2048]{1,0:T(8,128)(2,1)S(1)} %get-tuple-element.81), channel_id=1, source_target_pairs={{0,1},{1,0},{2,3},{3,2},{4,5},{5,4},{6,7},{7,6},{8,9},{9,8},{10,11... | collective-permute-start | bytes 786440 | tf_op jit(solution)/shard_map/ppermute | solution.py:20
  239.5 10.6 %collective-permute-start.34 = (bf16[64,2048]{1,0:T(8,128)(2,1)S(1)}, bf16[64,2048]{1,0:T(8,128)(2,1)S(1)}, u32[]{:S(2)}, u32[]{:S(2)}) collective-permute-start(bf16[64,2048]{1,0:T(8,128)(2,1)S(1)} %get-tuple-element.74.refs_0_), channel_id=1, source_target_pairs={{24,26},{25,27},{26,24},{27,25},{28,30},{29,31},{30,28},{31,29}} | collective-permute-start | bytes 786440 | tf_op jit(solution)/shard_map/ppermute | solution.py:20
  240.2 10.0 %collective-permute-start.35 = (bf16[64,2048]{1,0:T(8,128)(2,1)S(1)}, bf16[64,2048]{1,0:T(8,128)(2,1)S(1)}, u32[]{:S(2)}, u32[]{:S(2)}) collective-permute-start(bf16[64,2048]{1,0:T(8,128)(2,1)S(1)} %get-tuple-element.74.refs_0_), channel_id=1, source_target_pairs={{24,25},{25,24},{26,27},{27,26},{28,29},{29,28},{30,31},{31,30}} | collective-permute-start | bytes 786440 | tf_op jit(solution)/shard_map/ppermute | solution.py:20
  240.8 22.7 %collective-permute-start.43 = (bf16[64,2048]{1,0:T(8,128)(2,1)S(1)}, bf16[64,2048]{1,0:T(8,128)(2,1)S(1)}, u32[]{:S(2)}, u32[]{:S(2)}) collective-permute-start(bf16[64,2048]{1,0:T(8,128)(2,1)S(1)} %get-tuple-element.81), channel_id=1, source_target_pairs={{0,4},{1,5},{2,6},{3,7},{4,0},{5,1},{6,2},{7,3},{8,12},{9,13},{10,... | collective-permute-start | bytes 786440 | tf_op jit(solution)/shard_map/ppermute | solution.py:20
  243.5 23.4 %collective-permute-start.36 = (bf16[64,2048]{1,0:T(8,128)(2,1)S(1)}, bf16[64,2048]{1,0:T(8,128)(2,1)S(1)}, u32[]{:S(2)}, u32[]{:S(2)}) collective-permute-start(bf16[64,2048]{1,0:T(8,128)(2,1)S(1)} %get-tuple-element.74.refs_0_), channel_id=1, source_target_pairs={{24,28},{25,29},{26,30},{27,31},{28,24},{29,25},{30,26},{31,27}} | collective-permute-start | bytes 786440 | tf_op jit(solution)/shard_map/ppermute | solution.py:20
  246.6 17.6 %collective-permute-start.44 = (bf16[64,2048]{1,0:T(8,128)(2,1)S(1)}, bf16[64,2048]{1,0:T(8,128)(2,1)S(1)}, u32[]{:S(2)}, u32[]{:S(2)}) collective-permute-start(bf16[64,2048]{1,0:T(8,128)(2,1)S(1)} %collective-permute-done.41.refs_9_), channel_id=1, source_target_pairs={{0,1},{1,0},{2,3},{3,2},{4,5},{5,4},{6,7},{7,6},{8,9},{9,8},{10,11... | collective-permute-start | bytes 786440 | tf_op jit(solution)/shard_map/ppermute | solution.py:20
  250.1 16.8 %collective-permute-start.37 = (bf16[64,2048]{1,0:T(8,128)(2,1)S(1)}, bf16[64,2048]{1,0:T(8,128)(2,1)S(1)}, u32[]{:S(2)}, u32[]{:S(2)}) collective-permute-start(bf16[64,2048]{1,0:T(8,128)(2,1)S(1)} %collective-permute-done.34.refs_2_), channel_id=1, source_target_pairs={{24,25},{25,24},{26,27},{27,26},{28,29},{29,28},{30,31},{31,30}} | collective-permute-start | bytes 786440 | tf_op jit(solution)/shard_map/ppermute | solution.py:20
  250.8 16.8 %collective-permute-start.45 = (bf16[64,2048]{1,0:T(8,128)(2,1)S(1)}, bf16[64,2048]{1,0:T(8,128)(2,1)S(1)}, u32[]{:S(2)}, u32[]{:S(2)}) collective-permute-start(bf16[64,2048]{1,0:T(8,128)(2,1)S(1)} %get-tuple-element.81), channel_id=1, source_target_pairs={{0,6},{1,7},{2,4},{3,5},{4,2},{5,3},{6,0},{7,1},{8,14},{9,15},{10,... | collective-permute-start | bytes 786440 | tf_op jit(solution)/shard_map/ppermute | solution.py:20
  263.5 12.4 %collective-permute-start.38 = (bf16[64,2048]{1,0:T(8,128)(2,1)S(1)}, bf16[64,2048]{1,0:T(8,128)(2,1)S(1)}, u32[]{:S(2)}, u32[]{:S(2)}) collective-permute-start(bf16[64,2048]{1,0:T(8,128)(2,1)S(1)} %get-tuple-element.74.refs_0_), channel_id=1, source_target_pairs={{24,30},{25,31},{26,28},{27,29},{28,26},{29,27},{30,24},{31,25}} | collective-permute-start | bytes 786440 | tf_op jit(solution)/shard_map/ppermute | solution.py:20
  264.2 9.4 %collective-permute-start.46 = (bf16[64,2048]{1,0:T(8,128)(2,1)S(1)}, bf16[64,2048]{1,0:T(8,128)(2,1)S(1)}, u32[]{:S(2)}, u32[]{:S(2)}) collective-permute-start(bf16[64,2048]{1,0:T(8,128)(2,1)S(1)} %collective-permute-done.43.refs_11_), channel_id=1, source_target_pairs={{0,1},{1,0},{2,3},{3,2},{4,5},{5,4},{6,7},{7,6},{8,9},{9,8},{10,11... | collective-permute-start | bytes 786440 | tf_op jit(solution)/shard_map/ppermute | solution.py:20
  266.9 9.0 %collective-permute-start.39 = (bf16[64,2048]{1,0:T(8,128)(2,1)S(1)}, bf16[64,2048]{1,0:T(8,128)(2,1)S(1)}, u32[]{:S(2)}, u32[]{:S(2)}) collective-permute-start(bf16[64,2048]{1,0:T(8,128)(2,1)S(1)} %collective-permute-done.36.refs_4_), channel_id=1, source_target_pairs={{24,25},{25,24},{26,27},{27,26},{28,29},{29,28},{30,31},{31,30}} | collective-permute-start | bytes 786440 | tf_op jit(solution)/shard_map/ppermute | solution.py:20
  273.7 8.5 %collective-permute-start.47 = (bf16[64,2048]{1,0:T(8,128)(2,1)S(1)}, bf16[64,2048]{1,0:T(8,128)(2,1)S(1)}, u32[]{:S(2)}, u32[]{:S(2)}) collective-permute-start(bf16[64,2048]{1,0:T(8,128)(2,1)S(1)} %collective-permute-done.45.refs_13_), channel_id=1, source_target_pairs={{0,1},{1,0},{2,3},{3,2},{4,5},{5,4},{6,7},{7,6},{8,9},{9,8},{10,11... | collective-permute-start | bytes 786440 | tf_op jit(solution)/shard_map/ppermute | solution.py:20
  275.9 6.3 %collective-permute-start.40 = (bf16[64,2048]{1,0:T(8,128)(2,1)S(1)}, bf16[64,2048]{1,0:T(8,128)(2,1)S(1)}, u32[]{:S(2)}, u32[]{:S(2)}) collective-permute-start(bf16[64,2048]{1,0:T(8,128)(2,1)S(1)} %collective-permute-done.38.refs_6_), channel_id=1, source_target_pairs={{24,25},{25,24},{26,27},{27,26},{28,29},{29,28},{30,31},{31,30}} | collective-permute-start | bytes 786440 | tf_op jit(solution)/shard_map/ppermute | solution.py:20
  (18 other events, 381.2 us)

commit v3 on v2

--- a/solution.py
+++ b/solution.py
@@ -75,15 +75,14 @@
     return total
 
 
+def swap_z(pairs, periods):
+    others = [bus_send(pairs[flip // 2], flip, periods) for flip in (2, 4, 6)]
+    return jnp.concatenate([pairs[0], *others])
+
+
 def swap_parts(keep, send, periods):
     there = bus_send(send, 1, periods)
-    parts = {}
-    for place, flip in enumerate(EVEN):
-        pair = jnp.stack([keep[place], there[place]])
-        if flip:
-            pair = bus_send(pair, flip, periods)
-        parts[flip] = pair
-    return jnp.concatenate([parts[flip] for flip in EVEN])
+    return swap_z([jnp.stack([keep[place], there[place]]) for place in range(4)], periods)
 
 
 def in_vmem():
@@ -301,32 +300,71 @@
         whole[pl.ds(owner, rows), :] = block
 
 
-def couple_kernel(rank_ref, schur, *refs):
-    parts, (keep, send, costate, coupling, product, whole) = refs[:8], refs[8:]
+def couple_kernel(rank_ref, schur, schur_y, *refs):
+    parts, (p0, p2, p4, p6, own, cross, whole, product) = refs[:4], refs[4:]
     rank = rank_ref[0]
-    assemble(rank, parts, (), whole)
-    product[...] = times_t(whole[...], schur[...])
-    deal(rank, product, keep, send)
-    coupling[...] = product[...].T
-    units = schur.shape[0]
-    own = pl.ds(pl.multiple_of(rank * units, units), units)
-    costate[...] = whole[:, own].astype(F32).T
-
-
-def couple(rank, schur, parts):
+    rows, units = p0.shape[1:]
+
+    def along_z(flip):
+        return pl.ds(pl.multiple_of(((rank ^ flip) // 2) * rows, rows), rows)
+
+    for part, flip in zip(parts, EVEN, strict=True):
+        whole[along_z(flip), :] = part[...]
+    product[0] = times_t(whole[...], schur[...])
+    product[1] = times_t(whole[...], schur_y[...])
+    for out, flip in zip((p0, p2, p4, p6), EVEN, strict=True):
+        for place in range(2):
+            out[place] = product[place, along_z(flip), :].astype(BF16)
+    own[0] = product[0]
+    cross[0] = product[1].astype(BF16)
+    for place, out in enumerate((own, cross)):
+        place_units = pl.ds(pl.multiple_of((rank ^ place) * units, units), units)
+        out[1] = whole[:, place_units].astype(out.dtype)
+
+
+def couple(rank, schur, schur_y, parts):
     units, whole = schur.shape
     rows = parts[0].shape[0]
-    piece = jax.ShapeDtypeStruct((4, rows, units), BF16)
-    out = jax.ShapeDtypeStruct((units, 8 * rows), F32)
+    pair = jax.ShapeDtypeStruct((2, rows, units), BF16)
     return kernel_call(
         couple_kernel,
-        [piece, piece, out, out],
-        [in_smem(), in_vmem()] + [in_vmem()] * 8,
-        [pltpu.VMEM((8 * rows, units), F32), pltpu.VMEM((8 * rows, whole), BF16)],
+        [pair] * 4
+        + [
+            jax.ShapeDtypeStruct((2, 4 * rows, units), F32),
+            jax.ShapeDtypeStruct((2, 4 * rows, units), BF16),
+        ],
+        [in_smem()] + [in_vmem()] * 6,
+        [pltpu.VMEM((4 * rows, whole), BF16), pltpu.VMEM((2, 4 * rows, units), F32)],
         16 * rows * whole * units,
         4 * MIB,
         16,
-    )(rank, schur, *parts)
+    )(rank, schur, schur_y, *parts)
+
+
+def rows_kernel(rank_ref, own, cross, coupling, costate, whole):
+    y = rank_ref[0] % 2
+    rows = whole.shape[0] // 8
+    for place, out in enumerate((coupling, costate)):
+        for z in range(4):
+            here = pl.ds(z * rows, rows)
+            whole[pl.ds(pl.multiple_of((2 * z + y) * rows, rows), rows), :] = own[place, here, :]
+            other = pl.ds(pl.multiple_of((2 * z + 1 - y) * rows, rows), rows)
+            whole[other, :] = cross[place, here, :].astype(F32)
+        out[...] = whole[...].T
+
+
+def rows_out(rank, own, cross):
+    columns, units = 2 * own.shape[1], own.shape[2]
+    out = jax.ShapeDtypeStruct((units, columns), F32)
+    return kernel_call(
+        rows_kernel,
+        [out, out],
+        [in_smem(), in_vmem(), in_vmem()],
+        [pltpu.VMEM((columns, units), F32)],
+        own.size,
+        12 * own.size,
+        12,
+    )(rank, own, cross)
 
 
 def finish_kernel(rank_ref, driven, terms, out):
@@ -433,10 +471,11 @@
     third_y = bus_send(third, 1, everyone)
     fourth = middle2 + outwards(middle2, everyone)
     fourth, third_y, there = together(fourth, third_y, there)
-    packed, fourth_y, unit_right = together(
+    packed, fourth_y, unit_right, schur_in = together(
         pack([gain, own_y, near, near_y, third, third_y, fourth]),
         bus_send(fourth, 1, everyone),
         reduce_z(keep, there, everyone),
+        schur,
     )
     weights = [packed, fourth_y]
     start = join(rank, swap_parts(*start_pieces(rank, start_state), everyone))
@@ -447,9 +486,10 @@
         costate = jnp.where(
             period == target, backward(places, later, unit_right, weights), costate
         )
-    costates = gather_parts(costate, everyone)
-    keep, send, costate_rows, coupling = couple(rank, schur, costates)
-    coupled = swap_parts(keep, send, everyone)
+    schur_y = bus_send(schur_in, 1, everyone)
+    others = [bus_send(costate, flip, everyone) for flip in (2, 4, 6)]
+    *pairs, own, cross = couple(rank, schur, schur_y, [costate, *others])
+    coupled = swap_z(pairs, everyone)
 
     state = start
     advanced = finish(rank, forward(places, start, weights), coupled)
@@ -459,6 +499,8 @@
         if target < last:
             early = state
             advanced = forward(places, arrived, weights, coupled)
+    cross = bus_send(cross, 1, everyone)
+    coupling, costate_rows = rows_out(rank, own, cross)
     early, state = together(early, state)
     last_states = gather_parts(state, (last,))
     early_states = gather_parts(early, everyone[:-1])

time: 295 us -> 273 us (0.925)
  waiting for transfers between devices: 159 us -> 142 us
  starting transfers between devices: 69.2 us -> 64.9 us
    ppermute x38 -> x35, waiting for transfers between devices: 96.9 us -> 81.9 us  [bus_send(): return lax.ppermute(block, BOTH, route)]
    ppermute x38 -> x35, starting transfers between devices: 57.4 us -> 52.9 us  [bus_send(): return lax.ppermute(block, BOTH, route)]
    select_n x3, other arithmetic: 3.56 us -> 0.1 us  [plane_body(): jnp.where(period == target, backward(places, later, unit_right, weights),...]
    unnamed x40 -> x47, local copies, waits for them, and re-layouts: 12.4 us -> 11.3 us
  transfers between devices with their start and end apart: 48 -> 45, of which waited for: 23 -> 21; matrix products, arithmetic and copies ran while one was open for 1% -> 3% of each run, Pallas kernels for 6% -> 10%
where the time goes in v3:
time: 273 us; the launch traced here: 272 us
  waiting for transfers between devices  142 us (52%)
  starting transfers between devices  64.9 us (24%)
  Pallas kernels  44.2 us (16%)
  local copies, waits for them, and re-layouts  13 us (5%)
  other arithmetic  5.75 us (2%)
    ppermute x35, waiting for transfers between devices, bus_send(): return lax.ppermute(block, BOTH, route)  81.9 us
    ppermute x35, starting transfers between devices, bus_send(): return lax.ppermute(block, BOTH, route)  52.9 us
    ppermute x4, waiting for transfers between devices, line_send(): return lax.ppermute(block, BOTH, route)  44.2 us
    ppermute x6, waiting for transfers between devices, period_send(): return lax.ppermute(block, BOTH, route)  16.1 us
    unnamed x47, local copies, waits for them, and re-layouts  11.3 us
    pallas_call x1, Pallas kernels, final(): kernel_call(final_kernel, [jax.ShapeDtypeStruct((units, columns), F32), j...  10.3 us
    pallas_call x1, Pallas kernels, front(): kernel_call(front_kernel, [keep, send], [in_smem(), in_vmem(), in_vmem(),...  10.2 us
    pallas_call x3, Pallas kernels, forward(): kernel_call(forward_kernel, jax.ShapeDtypeStruct((rows, whole), BF16 if e...  9.6 us
  transfers between devices with their start and end apart: 45, of which 21 were waited for; matrix products, arithmetic and copies ran while one was open for 3% of the time, Pallas kernels for 10%

profile of v3, /device:TPU:2, one launch (start us, length us, event | category | flops | bytes accessed | tf_op | source)
XLA Modules:
  0.0 271.6 jit_solution(2656132268208744130)
XLA Ops:
  0.6 1.6 collective-permute-start
  2.3 1.6 collective-permute-start.1
  3.9 1.5 collective-permute-start.2
  7.7 10.2 %shard_map.130 = (f32[4,64,2048]{2,1,0:T(8,128)S(1)}, bf16[4,64,2048]{2,1,0:T(8,128)(2,1)S(1)}) custom-call(s32[1]{0:T(128)} %bitcast.rank_ref, s32[1280,1]{1,0:T(8,128)S(1)} %copy.15.active, f32[256,512]{1,0:T(8,128)S(1)} %bitcast.26, f32[1280,512]{1,0:T(8,128)} %bitcast.31, bf16[1280,1280]{1,0:T(8,128)(2,1)} %bitcast.29, bf16[1280,2048]{1,0:T(8,128)(2,1)} %sens_hbm.1), custom_call_target="tpu_custom_call" | custom-call | flops 4362076160 | bytes 25165824 | tf_op jit(solution)/shard_map/pallas_call | solution.py:165
  17.9 7.9 %collective-permute-done.refs_2_ = bf16[256,2048]{1,0:T(8,128)(2,1)S(1)} collective-permute-done((bf16[256,2048]{1,0:T(8,128)(2,1)}, bf16[256,2048]{1,0:T(8,128)(2,1)S(1)}, u32[]{:S(2)}, u32[]{:S(2)}) %collective-permute-start) | collective-permute-done | bytes 1048608 | tf_op jit(solution)/shard_map/ppermute | solution.py:20
  25.8 2.9 %collective-permute-done.2.refs_1_ = bf16[256,2048]{1,0:T(8,128)(2,1)S(1)} collective-permute-done((bf16[256,2048]{1,0:T(8,128)(2,1)}, bf16[256,2048]{1,0:T(8,128)(2,1)S(1)}, u32[]{:S(2)}, u32[]{:S(2)}) %collective-permute-start.2) | collective-permute-done | bytes 1048608 | tf_op jit(solution)/shard_map/ppermute | solution.py:20
  31.8 1.6 collective-permute-start.5
  33.4 22.8 %collective-permute-done.4 = bf16[256,2048]{1,0:T(8,128)(2,1)S(1)} collective-permute-done((bf16[256,2048]{1,0:T(8,128)(2,1)}, bf16[256,2048]{1,0:T(8,128)(2,1)S(1)}, u32[]{:S(2)}, u32[]{:S(2)}) %collective-permute-start.4) | collective-permute-done | bytes 1048608 | tf_op jit(solution)/shard_map/ppermute | solution.py:45
  56.2 1.6 add.33.refs_4_
  59.3 1.6 collective-permute-start.8
  61.4 21.4 %collective-permute-done.6 = bf16[256,2048]{1,0:T(8,128)(2,1)S(1)} collective-permute-done((bf16[256,2048]{1,0:T(8,128)(2,1)S(1)}, bf16[256,2048]{1,0:T(8,128)(2,1)S(1)}, u32[]{:S(2)}, u32[]{:S(2)}) %collective-permute-start.6) | collective-permute-done | bytes 1048608 | tf_op jit(solution)/shard_map/ppermute | solution.py:45
  85.5 19.5 %collective-permute-done.7.refs_5_ = bf16[256,2048]{1,0:T(8,128)(2,1)S(1)} collective-permute-done((bf16[256,2048]{1,0:T(8,128)(2,1)S(1)}, bf16[256,2048]{1,0:T(8,128)(2,1)S(1)}, u32[]{:S(2)}, u32[]{:S(2)}) %collective-permute-start.7) | collective-permute-done | bytes 1048608 | tf_op jit(solution)/shard_map/ppermute | solution.py:20
  105.0 1.5 collective-permute-start.9
  107.5 1.8 collective-permute-start.10
  109.3 2.3 collective-permute-start.11
  116.9 4.9 %shard_map.131.packed = bf16[7,256,2048]{2,1,0:T(8,128)(2,1)} custom-call(bf16[256,2048]{1,0:T(8,128)(2,1)S(1)} %bitcast.22, bf16[256,2048]{1,0:T(8,128)(2,1)S(1)} %copy-done.7, bf16[256,2048]{1,0:T(8,128)(2,1)S(1)} %copy-done.5, bf16[256,2048]{1,0:T(8,128)(2,1)S(1)} %copy-done.9, bf16[256,2048]{1,0:T(8,128)(2,1)S(1)} %add.33.refs_4_, ...), custom_call_target="tpu_custom_call" | custom-call | bytes 14680064 | tf_op jit(solution)/shard_map/pallas_call | solution.py:233
  121.8 9.0 %collective-permute-done.11 = bf16[64,2048]{1,0:T(8,128)(2,1)} collective-permute-done((bf16[64,2048]{1,0:T(8,128)(2,1)}, bf16[64,2048]{1,0:T(8,128)(2,1)}, u32[]{:S(2)}, u32[]{:S(2)}) %collective-permute-start.11) | collective-permute-done | bytes 262176 | tf_op jit(solution)/shard_map/ppermute | solution.py:20
  133.7 2.1 collective-permute-done.14.vector
  135.8 3.1 %copy-done = bf16[7,256,2048]{2,1,0:T(8,128)(2,1)S(1)} copy-done((bf16[7,256,2048]{2,1,0:T(8,128)(2,1)S(1)}, bf16[7,256,2048]{2,1,0:T(8,128)(2,1)}, u32[]{:S(2)}) %copy-start) | copy-done | bytes 7340056
  138.9 2.1 shard_map.132
  144.0 2.3 collective-permute-done.15.vector
  146.3 2.1 shard_map.133
  149.3 2.0 collective-permute-start.24
  151.3 2.1 shard_map.134
  153.4 1.6 collective-permute-start.17
  155.9 1.9 collective-permute-start.19
  157.9 3.2 %shard_map.139.driven = f32[64,2048]{1,0:T(8,128)S(1)} custom-call(s32[8]{0:T(128)S(1)} %fusion.3.places, bf16[64,2048]{1,0:T(8,128)(2,1)S(1)} %shard_map.138.vector, bf16[7,256,2048]{2,1,0:T(8,128)(2,1)S(1)} %copy-done.1, bf16[256,2048]{1,0:T(8,128)(2,1)S(1)} %collective-permute-done.9.final_part), custom_call_target="tpu_custom_call" | custom-call | flops 536870912 | bytes 8388608 | tf_op jit(solution)/shard_map/pallas_call | solution.py:282
  161.1 6.9 %collective-permute-done.13.schur_y = bf16[256,2048]{1,0:T(8,128)(2,1)S(1)} collective-permute-done((bf16[256,2048]{1,0:T(8,128)(2,1)S(1)}, bf16[256,2048]{1,0:T(8,128)(2,1)S(1)}, u32[]{:S(2)}, u32[]{:S(2)}) %collective-permute-start.13) | collective-permute-done | bytes 1048608 | tf_op jit(solution)/shard_map/ppermute | solution.py:20
  168.0 7.4 %collective-permute-done.18.refs_2_ = bf16[64,2048]{1,0:T(8,128)(2,1)S(1)} collective-permute-done((bf16[64,2048]{1,0:T(8,128)(2,1)S(1)}, bf16[64,2048]{1,0:T(8,128)(2,1)S(1)}, u32[]{:S(2)}, u32[]{:S(2)}) %collective-permute-start.18) | collective-permute-done | bytes 262176 | tf_op jit(solution)/shard_map/ppermute | solution.py:20
  176.3 3.6 %collective-permute-start.25 = (bf16[2,64,256]{2,1,0:T(8,128)(2,1)S(1)}, bf16[2,64,256]{2,1,0:T(8,128)(2,1)S(1)}, u32[]{:S(2)}, u32[]{:S(2)}) collective-permute-start(bf16[2,64,256]{2,1,0:T(8,128)(2,1)S(1)} %get-tuple-element.69), channel_id=1, source_target_pairs={{0,2},{1,3},{2,0},{3,1},{4,6},{5,7},{6,4},{7,5},{8,10},{9,11},{10,... | collective-permute-start | bytes 196616 | tf_op jit(solution)/shard_map/ppermute | solution.py:20
  180.6 1.7 collective-permute-start.27
  182.3 3.3 %collective-permute-done.26 = bf16[2,64,256]{2,1,0:T(8,128)(2,1)S(1)} collective-permute-done((bf16[2,64,256]{2,1,0:T(8,128)(2,1)S(1)}, bf16[2,64,256]{2,1,0:T(8,128)(2,1)S(1)}, u32[]{:S(2)}, u32[]{:S(2)}) %collective-permute-start.26) | collective-permute-done | bytes 65568 | tf_op jit(solution)/shard_map/ppermute | solution.py:20
  187.7 3.2 %shard_map.141 = bf16[64,2048]{1,0:T(8,128)(2,1)S(1)} custom-call(s32[8]{0:T(128)S(1)} %fusion.3.places, bf16[64,2048]{1,0:T(8,128)(2,1)S(1)} %collective-permute-done.28.vector, bf16[7,256,2048]{2,1,0:T(8,128)(2,1)S(1)} %copy-done.1, bf16[256,2048]{1,0:T(8,128)(2,1)S(1)} %collective-permute-done.9.final_part, ...), custom_call_target="tpu_custom_call" | custom-call | flops 536870912 | bytes 8388608 | tf_op jit(solution)/shard_map/pallas_call | solution.py:282
  192.2 10.6 %collective-permute-done.29.vector = bf16[64,2048]{1,0:T(8,128)(2,1)S(1)} collective-permute-done((bf16[64,2048]{1,0:T(8,128)(2,1)S(1)}, bf16[64,2048]{1,0:T(8,128)(2,1)S(1)}, u32[]{:S(2)}, u32[]{:S(2)}) %collective-permute-start.29) | collective-permute-done | bytes 262176 | tf_op jit(solution)/shard_map/ppermute | solution.py:26
  202.8 3.2 %shard_map.142 = bf16[64,2048]{1,0:T(8,128)(2,1)S(1)} custom-call(s32[8]{0:T(128)S(1)} %fusion.3.places, bf16[64,2048]{1,0:T(8,128)(2,1)S(1)} %collective-permute-done.29.vector, bf16[7,256,2048]{2,1,0:T(8,128)(2,1)S(1)} %copy-done.1, bf16[256,2048]{1,0:T(8,128)(2,1)S(1)} %collective-permute-done.9.final_part, ...), custom_call_target="tpu_custom_call" | custom-call | flops 536870912 | bytes 8388608 | tf_op jit(solution)/shard_map/pallas_call | solution.py:282
  208.5 3.9 %collective-permute-start.38 = (bf16[64,2048]{1,0:T(8,128)(2,1)S(1)}, bf16[64,2048]{1,0:T(8,128)(2,1)S(1)}, u32[]{:S(2)}, u32[]{:S(2)}) collective-permute-start(bf16[64,2048]{1,0:T(8,128)(2,1)S(1)} %get-tuple-element.79), channel_id=1, source_target_pairs={{0,2},{1,3},{2,0},{3,1},{4,6},{5,7},{6,4},{7,5},{8,10},{9,11},{10,... | collective-permute-start | bytes 786440 | tf_op jit(solution)/shard_map/ppermute | solution.py:20
  212.4 2.4 collective-permute-start.39
  216.2 2.3 collective-permute-start.40
  219.3 3.7 %collective-permute-done.39.refs_8_ = bf16[64,2048]{1,0:T(8,128)(2,1)S(1)} collective-permute-done((bf16[64,2048]{1,0:T(8,128)(2,1)S(1)}, bf16[64,2048]{1,0:T(8,128)(2,1)S(1)}, u32[]{:S(2)}, u32[]{:S(2)}) %collective-permute-start.39) | collective-permute-done | bytes 262176 | tf_op jit(solution)/shard_map/ppermute | solution.py:20
  223.0 2.4 collective-permute-start.41
  226.1 3.3 %collective-permute-start.42 = (bf16[64,2048]{1,0:T(8,128)(2,1)S(1)}, bf16[64,2048]{1,0:T(8,128)(2,1)S(1)}, u32[]{:S(2)}, u32[]{:S(2)}) collective-permute-start(bf16[64,2048]{1,0:T(8,128)(2,1)S(1)} %get-tuple-element.79), channel_id=1, source_target_pairs={{0,6},{1,7},{2,4},{3,5},{4,2},{5,3},{6,0},{7,1},{8,14},{9,15},{10,... | collective-permute-start | bytes 786440 | tf_op jit(solution)/shard_map/ppermute | solution.py:20
  229.5 9.2 %collective-permute-done.40.refs_11_ = bf16[64,2048]{1,0:T(8,128)(2,1)S(1)} collective-permute-done((bf16[64,2048]{1,0:T(8,128)(2,1)S(1)}, bf16[64,2048]{1,0:T(8,128)(2,1)S(1)}, u32[]{:S(2)}, u32[]{:S(2)}) %collective-permute-start.40) | collective-permute-done | bytes 262176 | tf_op jit(solution)/shard_map/ppermute | solution.py:20
  239.4 3.4 %collective-permute-start.43 = (bf16[64,2048]{1,0:T(8,128)(2,1)S(1)}, bf16[64,2048]{1,0:T(8,128)(2,1)S(1)}, u32[]{:S(2)}, u32[]{:S(2)}) collective-permute-start(bf16[64,2048]{1,0:T(8,128)(2,1)S(1)} %collective-permute-done.40.refs_11_), channel_id=1, source_target_pairs={{0,1},{1,0},{2,3},{3,2},{4,5},{5,4},{6,7},{7,6},{8,9},{9,8},{10,11... | collective-permute-start | bytes 786440 | tf_op jit(solution)/shard_map/ppermute | solution.py:20
  244.1 6.4 %collective-permute-done.43.refs_12_ = bf16[64,2048]{1,0:T(8,128)(2,1)S(1)} collective-permute-done((bf16[64,2048]{1,0:T(8,128)(2,1)S(1)}, bf16[64,2048]{1,0:T(8,128)(2,1)S(1)}, u32[]{:S(2)}, u32[]{:S(2)}) %collective-permute-start.43) | collective-permute-done | bytes 262176 | tf_op jit(solution)/shard_map/ppermute | solution.py:20
  250.5 3.4 %collective-permute-start.44 = (bf16[64,2048]{1,0:T(8,128)(2,1)S(1)}, bf16[64,2048]{1,0:T(8,128)(2,1)S(1)}, u32[]{:S(2)}, u32[]{:S(2)}) collective-permute-start(bf16[64,2048]{1,0:T(8,128)(2,1)S(1)} %collective-permute-done.42.refs_13_), channel_id=1, source_target_pairs={{0,1},{1,0},{2,3},{3,2},{4,5},{5,4},{6,7},{7,6},{8,9},{9,8},{10,11... | collective-permute-start | bytes 786440 | tf_op jit(solution)/shard_map/ppermute | solution.py:20
  254.6 1.5 collective-permute-done.20.cross
  258.4 1.6 collective-permute-done.44.refs_14_
  261.1 10.3 %shard_map.143 = (f32[256,512]{1,0:T(8,128)}, f32[1280,512]{1,0:T(8,128)}) custom-call(s32[1]{0:T(128)} %bitcast.rank_ref, s32[1,2048]{1,0:T(1,128)S(1)} %bitcast.27, s32[1280,1]{1,0:T(8,128)S(1)} %copy-done.12, f32[256,512]{1,0:T(8,128)S(1)} %get-tuple-element.65.coupling, bf16[256,2048]{1,0:T(8,128)(2,1)S(1)} %bitcast.23, f32[1280,512]{1,0:T(8,128)} %bitcast.32, ...), custom_call_target="tpu_custom_call" | custom-call | flops 4898947072 | bytes 25165824 | tf_op jit(solution)/shard_map/pallas_call | solution.py:424
  (121 shorter events, 40.0 us)
Async XLA Ops:
  0.6 25.2 %collective-permute-start = (bf16[256,2048]{1,0:T(8,128)(2,1)}, bf16[256,2048]{1,0:T(8,128)(2,1)S(1)}, u32[]{:S(2)}, u32[]{:S(2)}) collective-permute-start(bf16[256,2048]{1,0:T(8,128)(2,1)} %bitcast.19), channel_id=1, source_target_pairs={{0,2},{1,3},{2,0},{3,1},{4,6},{5,7},{6,4},{7,5},{8,10},{9,11},{10,... | collective-permute-start | bytes 3145736 | tf_op jit(solution)/shard_map/ppermute | solution.py:20
  2.3 23.5 %collective-permute-start.1 = (bf16[256,2048]{1,0:T(8,128)(2,1)}, bf16[256,2048]{1,0:T(8,128)(2,1)}, u32[]{:S(2)}, u32[]{:S(2)}) collective-permute-start(bf16[256,2048]{1,0:T(8,128)(2,1)} %bitcast.20), channel_id=1, source_target_pairs={{2,4},{3,5},{4,2},{5,3},{10,12},{11,13},{12,10},{13,11},{18,20},{1... | collective-permute-start | bytes 3145736 | tf_op jit(solution)/shard_map/ppermute | solution.py:45
  3.9 24.8 %collective-permute-start.2 = (bf16[256,2048]{1,0:T(8,128)(2,1)}, bf16[256,2048]{1,0:T(8,128)(2,1)S(1)}, u32[]{:S(2)}, u32[]{:S(2)}) collective-permute-start(bf16[256,2048]{1,0:T(8,128)(2,1)} %bitcast.21), channel_id=1, source_target_pairs={{0,1},{1,0},{2,3},{3,2},{4,5},{5,4},{6,7},{7,6},{8,9},{9,8},{10,11... | collective-permute-start | bytes 3145736 | tf_op jit(solution)/shard_map/ppermute | solution.py:20
  17.9 88.6 %copy-start.2 = (f32[4,64,2048]{2,1,0:T(8,128)}, f32[4,64,2048]{2,1,0:T(8,128)S(1)}, u32[]{:S(2)}) copy-start(f32[4,64,2048]{2,1,0:T(8,128)S(1)} %get-tuple-element.57) | copy-start | bytes 6291460
  25.8 58.4 %copy-start.4 = (bf16[256,2048]{1,0:T(8,128)(2,1)}, bf16[256,2048]{1,0:T(8,128)(2,1)S(1)}, u32[]{:S(2)}) copy-start(bf16[256,2048]{1,0:T(8,128)(2,1)S(1)} %collective-permute-done.refs_2_) | copy-start | bytes 3145732
  29.8 26.4 %collective-permute-start.4 = (bf16[256,2048]{1,0:T(8,128)(2,1)}, bf16[256,2048]{1,0:T(8,128)(2,1)S(1)}, u32[]{:S(2)}, u32[]{:S(2)}) collective-permute-start(bf16[256,2048]{1,0:T(8,128)(2,1)} %collective-permute-done.1), channel_id=1, source_target_pairs={{2,0},{3,1},{4,6},{5,7},{10,8},{11,9},{12,14},{13,15},{18,16},{19,... | collective-permute-start | bytes 3145736 | tf_op jit(solution)/shard_map/ppermute | solution.py:45
  31.1 26.8 %collective-permute-start.3 = (bf16[256,2048]{1,0:T(8,128)(2,1)S(1)}, bf16[256,2048]{1,0:T(8,128)(2,1)S(1)}, u32[]{:S(2)}, u32[]{:S(2)}) collective-permute-start(bf16[256,2048]{1,0:T(8,128)(2,1)S(1)} %collective-permute-done.refs_2_), channel_id=1, source_target_pairs={{2,4},{3,5},{4,2},{5,3},{10,12},{11,13},{12,10},{13,11},{18,20},{1... | collective-permute-start | bytes 3145736 | tf_op jit(solution)/shard_map/ppermute | solution.py:45
  31.8 26.1 %collective-permute-start.5 = (bf16[256,2048]{1,0:T(8,128)(2,1)S(1)}, bf16[256,2048]{1,0:T(8,128)(2,1)S(1)}, u32[]{:S(2)}, u32[]{:S(2)}) collective-permute-start(bf16[256,2048]{1,0:T(8,128)(2,1)S(1)} %collective-permute-done.refs_2_), channel_id=1, source_target_pairs={{0,1},{1,0},{2,3},{3,2},{4,5},{5,4},{6,7},{7,6},{8,9},{9,8},{10,11... | collective-permute-start | bytes 3145736 | tf_op jit(solution)/shard_map/ppermute | solution.py:20
  57.9 24.9 %collective-permute-start.6 = (bf16[256,2048]{1,0:T(8,128)(2,1)S(1)}, bf16[256,2048]{1,0:T(8,128)(2,1)S(1)}, u32[]{:S(2)}, u32[]{:S(2)}) collective-permute-start(bf16[256,2048]{1,0:T(8,128)(2,1)S(1)} %collective-permute-done.3), channel_id=1, source_target_pairs={{2,0},{3,1},{4,6},{5,7},{10,8},{11,9},{12,14},{13,15},{18,16},{19,... | collective-permute-start | bytes 3145736 | tf_op jit(solution)/shard_map/ppermute | solution.py:45
  59.3 26.2 %collective-permute-start.8 = (bf16[4,64,2048]{2,1,0:T(8,128)(2,1)S(1)}, bf16[4,64,2048]{2,1,0:T(8,128)(2,1)S(1)}, u32[]{:S(2)}, u32[]{:S(2)}) collective-permute-start(bf16[4,64,2048]{2,1,0:T(8,128)(2,1)S(1)} %get-tuple-element.54), channel_id=1, source_target_pairs={{0,1},{1,0},{2,3},{3,2},{4,5},{5,4},{6,7},{7,6},{8,9},{9,8},{10,11... | collective-permute-start | bytes 3145736 | tf_op jit(solution)/shard_map/ppermute | solution.py:20
  60.9 44.1 %collective-permute-start.7 = (bf16[256,2048]{1,0:T(8,128)(2,1)S(1)}, bf16[256,2048]{1,0:T(8,128)(2,1)S(1)}, u32[]{:S(2)}, u32[]{:S(2)}) collective-permute-start(bf16[256,2048]{1,0:T(8,128)(2,1)S(1)} %add.33.refs_4_), channel_id=1, source_target_pairs={{0,1},{1,0},{2,3},{3,2},{4,5},{5,4},{6,7},{7,6},{8,9},{9,8},{10,11... | collective-permute-start | bytes 3145736 | tf_op jit(solution)/shard_map/ppermute | solution.py:20
  105.0 27.3 %collective-permute-start.9 = (bf16[256,2048]{1,0:T(8,128)(2,1)}, bf16[256,2048]{1,0:T(8,128)(2,1)S(1)}, u32[]{:S(2)}, u32[]{:S(2)}) collective-permute-start(bf16[256,2048]{1,0:T(8,128)(2,1)} %add.34.refs_6_), channel_id=1, source_target_pairs={{0,1},{1,0},{2,3},{3,2},{4,5},{5,4},{6,7},{7,6},{8,9},{9,8},{10,11... | collective-permute-start | bytes 3145736 | tf_op jit(solution)/shard_map/ppermute | solution.py:20
  107.5 14.3 %collective-permute-start.10 = (bf16[64,2048]{1,0:T(8,128)(2,1)}, bf16[64,2048]{1,0:T(8,128)(2,1)}, u32[]{:S(2)}, u32[]{:S(2)}) collective-permute-start(bf16[64,2048]{1,0:T(8,128)(2,1)} %get-tuple-element.91), channel_id=1, source_target_pairs={{0,6},{1,7},{2,4},{3,5},{4,2},{5,3},{6,0},{7,1},{8,14},{9,15},{10,... | collective-permute-start | bytes 786440 | tf_op jit(solution)/shard_map/ppermute | solution.py:20
  109.3 21.5 %collective-permute-start.11 = (bf16[64,2048]{1,0:T(8,128)(2,1)}, bf16[64,2048]{1,0:T(8,128)(2,1)}, u32[]{:S(2)}, u32[]{:S(2)}) collective-permute-start(bf16[64,2048]{1,0:T(8,128)(2,1)} %get-tuple-element.93), channel_id=1, source_target_pairs={{0,4},{1,5},{2,6},{3,7},{4,0},{5,1},{6,2},{7,3},{8,12},{9,13},{10,... | collective-permute-start | bytes 786440 | tf_op jit(solution)/shard_map/ppermute | solution.py:20
  111.6 19.2 %collective-permute-start.12 = (bf16[64,2048]{1,0:T(8,128)(2,1)S(1)}, bf16[64,2048]{1,0:T(8,128)(2,1)}, u32[]{:S(2)}, u32[]{:S(2)}) collective-permute-start(bf16[64,2048]{1,0:T(8,128)(2,1)S(1)} %get-tuple-element.92), channel_id=1, source_target_pairs={{0,2},{1,3},{2,0},{3,1},{4,6},{5,7},{6,4},{7,5},{8,10},{9,11},{10,... | collective-permute-start | bytes 786440 | tf_op jit(solution)/shard_map/ppermute | solution.py:20
  112.7 29.7 %collective-permute-start.21 = (bf16[4,64,256]{2,1,0:T(8,128)(2,1)}, bf16[4,64,256]{2,1,0:T(8,128)(2,1)}, u32[]{:S(2)}, u32[]{:S(2)}) collective-permute-start(bf16[4,64,256]{2,1,0:T(8,128)(2,1)} %get-tuple-element.67), channel_id=1, source_target_pairs={{0,1},{1,0},{2,3},{3,2},{4,5},{5,4},{6,7},{7,6},{8,9},{9,8},{10,11... | collective-permute-start | bytes 393224 | tf_op jit(solution)/shard_map/ppermute | solution.py:20
  132.3 3.4 %collective-permute-start.14 = (bf16[64,2048]{1,0:T(8,128)(2,1)S(1)}, bf16[64,2048]{1,0:T(8,128)(2,1)S(1)}, u32[]{:S(2)}, u32[]{:S(2)}) collective-permute-start(bf16[64,2048]{1,0:T(8,128)(2,1)S(1)} %convert_element_type.59), channel_id=1, source_target_pairs={{24,16},{25,17},{26,18},{27,19},{28,20},{29,21},{30,22},{31,23}} | collective-permute-start | bytes 786440 | tf_op jit(solution)/shard_map/ppermute | solution.py:26
  141.0 5.3 %collective-permute-start.15 = (bf16[64,2048]{1,0:T(8,128)(2,1)S(1)}, bf16[64,2048]{1,0:T(8,128)(2,1)S(1)}, u32[]{:S(2)}, u32[]{:S(2)}) collective-permute-start(bf16[64,2048]{1,0:T(8,128)(2,1)S(1)} %broadcast_select_fusion.1), channel_id=1, source_target_pairs={{16,8},{17,9},{18,10},{19,11},{20,12},{21,13},{22,14},{23,15}} | collective-permute-start | bytes 786440 | tf_op jit(solution)/shard_map/ppermute | solution.py:26
  143.3 8.0 %collective-permute-start.22 = (bf16[2,64,256]{2,1,0:T(8,128)(2,1)S(1)}, bf16[2,64,256]{2,1,0:T(8,128)(2,1)S(1)}, u32[]{:S(2)}, u32[]{:S(2)}) collective-permute-start(bf16[2,64,256]{2,1,0:T(8,128)(2,1)S(1)} %pad_maximum_fusion), channel_id=1, source_target_pairs={{0,2},{1,3},{2,0},{3,1},{4,6},{5,7},{6,4},{7,5},{8,10},{9,11},{10,... | collective-permute-start | bytes 196616 | tf_op jit(solution)/shard_map/ppermute | solution.py:20
  143.4 24.6 %collective-permute-start.13 = (bf16[256,2048]{1,0:T(8,128)(2,1)S(1)}, bf16[256,2048]{1,0:T(8,128)(2,1)S(1)}, u32[]{:S(2)}, u32[]{:S(2)}) collective-permute-start(bf16[256,2048]{1,0:T(8,128)(2,1)S(1)} %bitcast.24), channel_id=1, source_target_pairs={{0,1},{1,0},{2,3},{3,2},{4,5},{5,4},{6,7},{7,6},{8,9},{9,8},{10,11... | collective-permute-start | bytes 3145736 | tf_op jit(solution)/shard_map/ppermute | solution.py:20
  148.5 2.8 %collective-permute-start.16 = (bf16[64,2048]{1,0:T(8,128)(2,1)S(1)}, bf16[64,2048]{1,0:T(8,128)(2,1)S(1)}, u32[]{:S(2)}, u32[]{:S(2)}) collective-permute-start(bf16[64,2048]{1,0:T(8,128)(2,1)S(1)} %broadcast_select_fusion.2), channel_id=1, source_target_pairs={{8,0},{9,1},{10,2},{11,3},{12,4},{13,5},{14,6},{15,7}} | collective-permute-start | bytes 786440 | tf_op jit(solution)/shard_map/ppermute | solution.py:26
  149.2 6.8 %collective-permute-start.23 = (bf16[2,64,256]{2,1,0:T(8,128)(2,1)S(1)}, bf16[2,64,256]{2,1,0:T(8,128)(2,1)S(1)}, u32[]{:S(2)}, u32[]{:S(2)}) collective-permute-start(bf16[2,64,256]{2,1,0:T(8,128)(2,1)S(1)} %pad_maximum_fusion.1), channel_id=1, source_target_pairs={{0,4},{1,5},{2,6},{3,7},{4,0},{5,1},{6,2},{7,3},{8,12},{9,13},{10,... | collective-permute-start | bytes 196616 | tf_op jit(solution)/shard_map/ppermute | solution.py:20
  149.3 8.6 %collective-permute-start.24 = (bf16[2,64,256]{2,1,0:T(8,128)(2,1)S(1)}, bf16[2,64,256]{2,1,0:T(8,128)(2,1)S(1)}, u32[]{:S(2)}, u32[]{:S(2)}) collective-permute-start(bf16[2,64,256]{2,1,0:T(8,128)(2,1)S(1)} %pad_maximum_fusion.2), channel_id=1, source_target_pairs={{0,6},{1,7},{2,4},{3,5},{4,2},{5,3},{6,0},{7,1},{8,14},{9,15},{10,... | collective-permute-start | bytes 196616 | tf_op jit(solution)/shard_map/ppermute | solution.py:20
  153.4 14.6 %collective-permute-start.17 = (bf16[64,2048]{1,0:T(8,128)(2,1)S(1)}, bf16[64,2048]{1,0:T(8,128)(2,1)S(1)}, u32[]{:S(2)}, u32[]{:S(2)}) collective-permute-start(bf16[64,2048]{1,0:T(8,128)(2,1)S(1)} %broadcast_select_fusion.3.refs_0_), channel_id=1, source_target_pairs={{0,2},{1,3},{2,0},{3,1},{4,6},{5,7},{6,4},{7,5},{8,10},{9,11},{10,... | collective-permute-start | bytes 786440 | tf_op jit(solution)/shard_map/ppermute | solution.py:20
  155.0 20.4 %collective-permute-start.18 = (bf16[64,2048]{1,0:T(8,128)(2,1)S(1)}, bf16[64,2048]{1,0:T(8,128)(2,1)S(1)}, u32[]{:S(2)}, u32[]{:S(2)}) collective-permute-start(bf16[64,2048]{1,0:T(8,128)(2,1)S(1)} %broadcast_select_fusion.3.refs_0_), channel_id=1, source_target_pairs={{0,4},{1,5},{2,6},{3,7},{4,0},{5,1},{6,2},{7,3},{8,12},{9,13},{10,... | collective-permute-start | bytes 786440 | tf_op jit(solution)/shard_map/ppermute | solution.py:20
  155.9 19.5 %collective-permute-start.19 = (bf16[64,2048]{1,0:T(8,128)(2,1)S(1)}, bf16[64,2048]{1,0:T(8,128)(2,1)S(1)}, u32[]{:S(2)}, u32[]{:S(2)}) collective-permute-start(bf16[64,2048]{1,0:T(8,128)(2,1)S(1)} %broadcast_select_fusion.3.refs_0_), channel_id=1, source_target_pairs={{0,6},{1,7},{2,4},{3,5},{4,2},{5,3},{6,0},{7,1},{8,14},{9,15},{10,... | collective-permute-start | bytes 786440 | tf_op jit(solution)/shard_map/ppermute | solution.py:20
  176.3 6.1 %collective-permute-start.25 = (bf16[2,64,256]{2,1,0:T(8,128)(2,1)S(1)}, bf16[2,64,256]{2,1,0:T(8,128)(2,1)S(1)}, u32[]{:S(2)}, u32[]{:S(2)}) collective-permute-start(bf16[2,64,256]{2,1,0:T(8,128)(2,1)S(1)} %get-tuple-element.69), channel_id=1, source_target_pairs={{0,2},{1,3},{2,0},{3,1},{4,6},{5,7},{6,4},{7,5},{8,10},{9,11},{10,... | collective-permute-start | bytes 196616 | tf_op jit(solution)/shard_map/ppermute | solution.py:20
  179.9 5.8 %collective-permute-start.26 = (bf16[2,64,256]{2,1,0:T(8,128)(2,1)S(1)}, bf16[2,64,256]{2,1,0:T(8,128)(2,1)S(1)}, u32[]{:S(2)}, u32[]{:S(2)}) collective-permute-start(bf16[2,64,256]{2,1,0:T(8,128)(2,1)S(1)} %get-tuple-element.70), channel_id=1, source_target_pairs={{0,4},{1,5},{2,6},{3,7},{4,0},{5,1},{6,2},{7,3},{8,12},{9,13},{10,... | collective-permute-start | bytes 196616 | tf_op jit(solution)/shard_map/ppermute | solution.py:20
  180.6 6.2 %collective-permute-start.27 = (bf16[2,64,256]{2,1,0:T(8,128)(2,1)S(1)}, bf16[2,64,256]{2,1,0:T(8,128)(2,1)S(1)}, u32[]{:S(2)}, u32[]{:S(2)}) collective-permute-start(bf16[2,64,256]{2,1,0:T(8,128)(2,1)S(1)} %get-tuple-element.71), channel_id=1, source_target_pairs={{0,6},{1,7},{2,4},{3,5},{4,2},{5,3},{6,0},{7,1},{8,14},{9,15},{10,... | collective-permute-start | bytes 196616 | tf_op jit(solution)/shard_map/ppermute | solution.py:20
  186.8 0.9 collective-permute-start.28
  190.9 69.1 %copy-start.17 = (s32[2048]{0:T(1024)S(1)}, s32[2048]{0:T(1024)}, u32[]{:S(2)}) copy-start(s32[2048]{0:T(1024)} %param.19) | copy-start | bytes 24580
  190.9 11.9 %collective-permute-start.29 = (bf16[64,2048]{1,0:T(8,128)(2,1)S(1)}, bf16[64,2048]{1,0:T(8,128)(2,1)S(1)}, u32[]{:S(2)}, u32[]{:S(2)}) collective-permute-start(bf16[64,2048]{1,0:T(8,128)(2,1)S(1)} %shard_map.141), channel_id=1, source_target_pairs={{8,16},{9,17},{10,18},{11,19},{12,20},{13,21},{14,22},{15,23}} | collective-permute-start | bytes 786440 | tf_op jit(solution)/shard_map/ppermute | solution.py:26
  206.0 2.4 collective-permute-start.30
  208.5 10.1 %collective-permute-start.38 = (bf16[64,2048]{1,0:T(8,128)(2,1)S(1)}, bf16[64,2048]{1,0:T(8,128)(2,1)S(1)}, u32[]{:S(2)}, u32[]{:S(2)}) collective-permute-start(bf16[64,2048]{1,0:T(8,128)(2,1)S(1)} %get-tuple-element.79), channel_id=1, source_target_pairs={{0,2},{1,3},{2,0},{3,1},{4,6},{5,7},{6,4},{7,5},{8,10},{9,11},{10,... | collective-permute-start | bytes 786440 | tf_op jit(solution)/shard_map/ppermute | solution.py:20
  212.4 10.6 %collective-permute-start.39 = (bf16[64,2048]{1,0:T(8,128)(2,1)S(1)}, bf16[64,2048]{1,0:T(8,128)(2,1)S(1)}, u32[]{:S(2)}, u32[]{:S(2)}) collective-permute-start(bf16[64,2048]{1,0:T(8,128)(2,1)S(1)} %get-tuple-element.79), channel_id=1, source_target_pairs={{0,1},{1,0},{2,3},{3,2},{4,5},{5,4},{6,7},{7,6},{8,9},{9,8},{10,11... | collective-permute-start | bytes 786440 | tf_op jit(solution)/shard_map/ppermute | solution.py:20
  214.8 10.6 %collective-permute-start.31 = (bf16[64,2048]{1,0:T(8,128)(2,1)S(1)}, bf16[64,2048]{1,0:T(8,128)(2,1)S(1)}, u32[]{:S(2)}, u32[]{:S(2)}) collective-permute-start(bf16[64,2048]{1,0:T(8,128)(2,1)S(1)} %get-tuple-element.72.refs_0_), channel_id=1, source_target_pairs={{24,26},{25,27},{26,24},{27,25},{28,30},{29,31},{30,28},{31,29}} | collective-permute-start | bytes 786440 | tf_op jit(solution)/shard_map/ppermute | solution.py:20
  215.5 10.0 %collective-permute-start.32 = (bf16[64,2048]{1,0:T(8,128)(2,1)S(1)}, bf16[64,2048]{1,0:T(8,128)(2,1)S(1)}, u32[]{:S(2)}, u32[]{:S(2)}) collective-permute-start(bf16[64,2048]{1,0:T(8,128)(2,1)S(1)} %get-tuple-element.72.refs_0_), channel_id=1, source_target_pairs={{24,25},{25,24},{26,27},{27,26},{28,29},{29,28},{30,31},{31,30}} | collective-permute-start | bytes 786440 | tf_op jit(solution)/shard_map/ppermute | solution.py:20
  216.2 22.5 %collective-permute-start.40 = (bf16[64,2048]{1,0:T(8,128)(2,1)S(1)}, bf16[64,2048]{1,0:T(8,128)(2,1)S(1)}, u32[]{:S(2)}, u32[]{:S(2)}) collective-permute-start(bf16[64,2048]{1,0:T(8,128)(2,1)S(1)} %get-tuple-element.79), channel_id=1, source_target_pairs={{0,4},{1,5},{2,6},{3,7},{4,0},{5,1},{6,2},{7,3},{8,12},{9,13},{10,... | collective-permute-start | bytes 786440 | tf_op jit(solution)/shard_map/ppermute | solution.py:20
  218.6 24.2 %collective-permute-start.33 = (bf16[64,2048]{1,0:T(8,128)(2,1)S(1)}, bf16[64,2048]{1,0:T(8,128)(2,1)S(1)}, u32[]{:S(2)}, u32[]{:S(2)}) collective-permute-start(bf16[64,2048]{1,0:T(8,128)(2,1)S(1)} %get-tuple-element.72.refs_0_), channel_id=1, source_target_pairs={{24,28},{25,29},{26,30},{27,31},{28,24},{29,25},{30,26},{31,27}} | collective-permute-start | bytes 786440 | tf_op jit(solution)/shard_map/ppermute | solution.py:20
  223.0 16.4 %collective-permute-start.41 = (bf16[64,2048]{1,0:T(8,128)(2,1)S(1)}, bf16[64,2048]{1,0:T(8,128)(2,1)S(1)}, u32[]{:S(2)}, u32[]{:S(2)}) collective-permute-start(bf16[64,2048]{1,0:T(8,128)(2,1)S(1)} %collective-permute-done.38.refs_9_), channel_id=1, source_target_pairs={{0,1},{1,0},{2,3},{3,2},{4,5},{5,4},{6,7},{7,6},{8,9},{9,8},{10,11... | collective-permute-start | bytes 786440 | tf_op jit(solution)/shard_map/ppermute | solution.py:20
  225.5 17.3 %collective-permute-start.34 = (bf16[64,2048]{1,0:T(8,128)(2,1)S(1)}, bf16[64,2048]{1,0:T(8,128)(2,1)S(1)}, u32[]{:S(2)}, u32[]{:S(2)}) collective-permute-start(bf16[64,2048]{1,0:T(8,128)(2,1)S(1)} %collective-permute-done.31.refs_2_), channel_id=1, source_target_pairs={{24,25},{25,24},{26,27},{27,26},{28,29},{29,28},{30,31},{31,30}} | collective-permute-start | bytes 786440 | tf_op jit(solution)/shard_map/ppermute | solution.py:20
  226.1 17.9 %collective-permute-start.42 = (bf16[64,2048]{1,0:T(8,128)(2,1)S(1)}, bf16[64,2048]{1,0:T(8,128)(2,1)S(1)}, u32[]{:S(2)}, u32[]{:S(2)}) collective-permute-start(bf16[64,2048]{1,0:T(8,128)(2,1)S(1)} %get-tuple-element.79), channel_id=1, source_target_pairs={{0,6},{1,7},{2,4},{3,5},{4,2},{5,3},{6,0},{7,1},{8,14},{9,15},{10,... | collective-permute-start | bytes 786440 | tf_op jit(solution)/shard_map/ppermute | solution.py:20
  238.7 15.2 %collective-permute-start.35 = (bf16[64,2048]{1,0:T(8,128)(2,1)S(1)}, bf16[64,2048]{1,0:T(8,128)(2,1)S(1)}, u32[]{:S(2)}, u32[]{:S(2)}) collective-permute-start(bf16[64,2048]{1,0:T(8,128)(2,1)S(1)} %get-tuple-element.72.refs_0_), channel_id=1, source_target_pairs={{24,30},{25,31},{26,28},{27,29},{28,26},{29,27},{30,24},{31,25}} | collective-permute-start | bytes 786440 | tf_op jit(solution)/shard_map/ppermute | solution.py:20
  239.4 11.1 %collective-permute-start.43 = (bf16[64,2048]{1,0:T(8,128)(2,1)S(1)}, bf16[64,2048]{1,0:T(8,128)(2,1)S(1)}, u32[]{:S(2)}, u32[]{:S(2)}) collective-permute-start(bf16[64,2048]{1,0:T(8,128)(2,1)S(1)} %collective-permute-done.40.refs_11_), channel_id=1, source_target_pairs={{0,1},{1,0},{2,3},{3,2},{4,5},{5,4},{6,7},{7,6},{8,9},{9,8},{10,11... | collective-permute-start | bytes 786440 | tf_op jit(solution)/shard_map/ppermute | solution.py:20
  242.8 11.1 %collective-permute-start.36 = (bf16[64,2048]{1,0:T(8,128)(2,1)S(1)}, bf16[64,2048]{1,0:T(8,128)(2,1)S(1)}, u32[]{:S(2)}, u32[]{:S(2)}) collective-permute-start(bf16[64,2048]{1,0:T(8,128)(2,1)S(1)} %collective-permute-done.33.refs_4_), channel_id=1, source_target_pairs={{24,25},{25,24},{26,27},{27,26},{28,29},{29,28},{30,31},{31,30}} | collective-permute-start | bytes 786440 | tf_op jit(solution)/shard_map/ppermute | solution.py:20
  243.5 12.6 %collective-permute-start.20 = (bf16[2,256,256]{2,1,0:T(8,128)(2,1)S(1)}, bf16[2,256,256]{2,1,0:T(8,128)(2,1)S(1)}, u32[]{:S(2)}, u32[]{:S(2)}) collective-permute-start(bf16[2,256,256]{2,1,0:T(8,128)(2,1)S(1)} %get-tuple-element.64), channel_id=1, source_target_pairs={{0,1},{1,0},{2,3},{3,2},{4,5},{5,4},{6,7},{7,6},{8,9},{9,8},{10,11... | collective-permute-start | bytes 786440 | tf_op jit(solution)/shard_map/ppermute | solution.py:20
  250.5 9.5 %collective-permute-start.44 = (bf16[64,2048]{1,0:T(8,128)(2,1)S(1)}, bf16[64,2048]{1,0:T(8,128)(2,1)S(1)}, u32[]{:S(2)}, u32[]{:S(2)}) collective-permute-start(bf16[64,2048]{1,0:T(8,128)(2,1)S(1)} %collective-permute-done.42.refs_13_), channel_id=1, source_target_pairs={{0,1},{1,0},{2,3},{3,2},{4,5},{5,4},{6,7},{7,6},{8,9},{9,8},{10,11... | collective-permute-start | bytes 786440 | tf_op jit(solution)/shard_map/ppermute | solution.py:20
  253.9 6.1 %collective-permute-start.37 = (bf16[64,2048]{1,0:T(8,128)(2,1)S(1)}, bf16[64,2048]{1,0:T(8,128)(2,1)S(1)}, u32[]{:S(2)}, u32[]{:S(2)}) collective-permute-start(bf16[64,2048]{1,0:T(8,128)(2,1)S(1)} %collective-permute-done.35.refs_6_), channel_id=1, source_target_pairs={{24,25},{25,24},{26,27},{27,26},{28,29},{29,28},{30,31},{31,30}} | collective-permute-start | bytes 786440 | tf_op jit(solution)/shard_map/ppermute | solution.py:20
  (18 other events, 228.8 us)

commit v4 on v2

v4 whole, which is shorter than its diff:
```python
import functools

import jax
import jax.numpy as jnp
from jax import lax
from jax.experimental import pallas as pl
from jax.experimental.pallas import tpu as pltpu
from jax.sharding import PartitionSpec as P

BOTH = ("period", "bus")
F32 = jnp.float32
BF16 = jnp.bfloat16
MIB = 1 << 20


def bus_send(block, flip, periods):
    size = lax.axis_size("bus")
    route = [(p * size + b, p * size + (b ^ flip)) for p in periods for b in range(size)]
    return lax.ppermute(block, BOTH, route)


def period_send(block, source, target, flip=0):
    size = lax.axis_size("bus")
    route = [(source * size + b, target * size + (b ^ flip)) for b in range(size)]
    return lax.ppermute(block, BOTH, route)


def times(left, right):
    return jnp.dot(left, right, preferred_element_type=F32)


def times_t(left, right):
    return lax.dot_general(left, right, (((1,), (1,)), ((), ())), preferred_element_type=F32)


def together(*values):
    return lax.optimization_barrier(values)


def line_send(block, pairs, periods):
    size = lax.axis_size("bus")
    route = [
        (p * size + 2 * source + y, p * size + 2 * target + y)
        for p in periods
        for source, target in pairs
        for y in range(2)
    ]
    return lax.ppermute(block, BOTH, route)


def across(block, periods):
    return line_send(block, ((1, 2), (2, 1)), periods)


def outwards(block, periods):
    return line_send(block, ((1, 0), (2, 3)), periods)


def swap_z(pieces, periods):
    return [pieces[0]] + [bus_send(pieces[flip // 2], flip, periods) for flip in (2, 4, 6)]


def in_vmem():
    return pl.BlockSpec(memory_space=pltpu.VMEM)


def anywhere():
    return pl.BlockSpec(memory_space=pl.ANY)


def in_smem():
    return pl.BlockSpec(memory_space=pltpu.SMEM)


def kernel_call(kernel, out_shape, in_specs, scratch, flops, bytes_accessed, mib, out_specs=None):
    return pl.pallas_call(
        kernel,
        out_shape=out_shape,
        in_specs=in_specs,
        out_specs=out_specs or jax.tree.map(lambda _: in_vmem(), out_shape),
        scratch_shapes=scratch,
        compiler_params=pltpu.CompilerParams(vmem_limit_bytes=mib * MIB),
        cost_estimate=pl.CostEstimate(
            flops=flops, bytes_accessed=bytes_accessed, transcendentals=0
        ),
    )


def at(index, size):
    return pl.ds(pl.multiple_of(index * size, size), size)


def front_kernel(
    rank_ref, active, rhs, residual_hbm, inverse_hbm, sens_hbm,
    k0, k2, k4, k6, send, solved,
    residual, inverse, sens, net, solve_t, partial, sems,
):
    rank = rank_ref[0]
    z, y = rank // 2, rank % 2
    loads = [
        pltpu.make_async_copy(residual_hbm, residual, sems.at[0]),
        pltpu.make_async_copy(inverse_hbm, inverse, sems.at[1]),
        pltpu.make_async_copy(sens_hbm, sens, sems.at[2]),
    ]
    for load in loads:
        load.start()
    loads[0].wait()
    net[...] = (residual[...] * (1.0 + 3.0 * active[...].astype(F32))).astype(BF16)
    loads[1].wait()
    blocks = inverse.shape[0] // 256

    @pl.loop(0, blocks)
    def _(i):
        rows = pl.ds(pl.multiple_of(i * 256, 256), 256)
        product = times(inverse[rows, :], net[...])
        solved[rows, :] = product
        solve_t[:, rows] = product.T.astype(BF16)

    loads[2].wait()

    @pl.loop(0, sens.shape[1] // 256)
    def _(i):
        columns = pl.ds(pl.multiple_of(i * 256, 256), 256)
        partial[:, columns] = times(solve_t[...], sens[:, columns])

    units = rhs.shape[0]
    partial[:, at(rank, units)] += rhs[...].T
    rows = k0.shape[0]
    for turn, out in enumerate((k0, k2, k4, k6)):
        here = at(z ^ turn, rows)
        for block in range(4):
            lanes = pl.ds(block * units, units)
            out[:, lanes] = partial[here, at(2 * block + y, units)]
            send[turn, :, lanes] = partial[here, at(2 * block + 1 - y, units)].astype(BF16)


def front(rank, active, rhs, residual, inverse, sens):
    buses, columns = residual.shape
    units = sens.shape[1]
    keep = jax.ShapeDtypeStruct((columns // 4, units // 2), F32)
    send = jax.ShapeDtypeStruct((4, columns // 4, units // 2), BF16)
    return kernel_call(
        front_kernel,
        [keep] * 4 + [send, jax.ShapeDtypeStruct((buses, columns), F32)],
        [in_smem(), in_vmem(), in_vmem(), anywhere(), anywhere(), anywhere()],
        [
            pltpu.VMEM((buses, columns), F32),
            pltpu.VMEM((buses, buses), BF16),
            pltpu.VMEM((buses, units), BF16),
            pltpu.VMEM((buses, columns), BF16),
            pltpu.VMEM((columns, buses), BF16),
            pltpu.VMEM((columns, units), F32),
            pltpu.SemaphoreType.DMA((3,)),
        ],
        2 * buses * columns * (buses + units),
        24 * MIB,
        48,
    )(rank, active, rhs, residual, inverse, sens)


def start_kernel(rank_ref, state, p0, p2, p4, p6):
    for turn, out in enumerate((p0, p2, p4, p6)):
        out[...] = state[:, at((rank_ref[0] // 2) ^ turn, out.shape[1])].astype(BF16)


def start_pieces(rank, state):
    units, columns = state.shape
    return kernel_call(
        start_kernel,
        [jax.ShapeDtypeStruct((units, columns // 4), BF16)] * 4,
        [in_smem(), in_vmem()],
        [],
        state.size,
        6 * state.size,
        8,
    )(rank, state)


def join_kernel(rank_ref, p0, p2, p4, p6, out):
    for turn, piece in enumerate((p0, p2, p4, p6)):
        out[at((rank_ref[0] // 2) ^ turn, piece.shape[0]), :] = piece[...]


def join(rank, pieces):
    units, rights = pieces[0].shape
    return kernel_call(
        join_kernel,
        jax.ShapeDtypeStruct((4 * units, rights), BF16),
        [in_smem()] + [in_vmem()] * 4,
        [],
        units * rights,
        16 * units * rights,
        8,
    )(rank, *pieces)


def pack_kernel(*refs):
    parts, (out, sems) = refs[:3], refs[3:]
    loads = [pltpu.make_async_copy(part, out.at[j], sems.at[j]) for j, part in enumerate(parts)]
    for load in loads:
        load.start()
    for load in loads:
        load.wait()


def pack(parts):
    return kernel_call(
        pack_kernel,
        jax.ShapeDtypeStruct((3, *parts[0].shape), BF16),
        [anywhere()] * 3,
        [pltpu.SemaphoreType.DMA((3,))],
        0,
        12 * parts[0].size,
        48,
    )(*parts)


def backward_kernel(places, turn, own, other, base, former_sums, former_cross, packed, fourth, sums, cross, total):
    units = fourth.shape[0]
    y = places[4]

    def step():
        vector = (own[...].astype(F32) + other[...].astype(F32)).astype(BF16)
        cross_like = jnp.zeros(total.shape, F32)
        total[...] = cross_like
        whole = packed.shape[2]
        for width in range(0, whole, 1024):
            lanes = pl.ds(width, 1024)
            product = None
            for place in range(4):
                weight = packed[place, :, lanes] if place < 3 else fourth[:, lanes]
                blocks = [
                    vector[:, z * units : (z + 1) * units] for z in range(4)
                ]
                chosen = blocks[0]
                for z in range(1, 4):
                    chosen = jnp.where(places[place] == z, blocks[z], chosen)
                term = times(chosen, weight)
                product = term if product is None else product + term
            total[:, lanes] = product
        for block in range(4):
            lanes = pl.ds(block * units, units)
            sums[:, lanes] = (base[:, lanes] + total[:, at(2 * block + y, units)]).astype(BF16)
            cross[:, lanes] = total[:, at(2 * block + 1 - y, units)].astype(BF16)

    def skip():
        sums[...] = former_sums[...]
        cross[...] = former_cross[...]

    pl.when(turn[0] == 1)(step)
    pl.when(turn[0] == 0)(skip)


def backward(places, turn, vector, base, former, weights):
    rows, half = base.shape
    out = jax.ShapeDtypeStruct((rows, half), BF16)
    return kernel_call(
        backward_kernel,
        [out, out],
        [in_smem()] * 2 + [in_vmem()] * 7,
        [pltpu.VMEM((rows, 2 * half), F32)],
        4 * rows * half * half,
        4 * half * half,
        12,
    )(places, turn.astype(jnp.int32).reshape(1), *vector, base, *former, *weights)


def forward_kernel(places, own, other, packed, fourth, *refs):
    subtracted, (out, state) = (refs[0], refs[1:]) if len(refs) > 2 else (None, refs)
    units = fourth.shape[0]
    y = places[4]
    for block in range(4):
        here = pl.ds(block * units, units)
        state[at(2 * block + y, units), :] = own[here, :]
        state[at(2 * block + 1 - y, units), :] = other[here, :]
    for place in range(4):
        weight = packed[place] if place < 3 else fourth[...]
        here = at(places[place], units)
        product = times(weight, state[...])
        if subtracted is not None:
            product = product - subtracted[here, :].astype(F32)
        out[here, :] = product.astype(out.dtype)


def forward(places, state, weights, subtracted=None):
    half, rights = state[0].shape
    extra = () if subtracted is None else (subtracted,)
    return kernel_call(
        forward_kernel,
        jax.ShapeDtypeStruct((half, rights), BF16 if extra else F32),
        [in_smem()] + [in_vmem()] * (4 + len(extra)),
        [pltpu.VMEM((2 * half, rights), BF16)],
        4 * rights * half * half,
        4 * half * half,
        12,
    )(places, *state, *weights, *extra)


def couple_kernel(rank_ref, schur, schur_y, c0, c2, c4, c6, product, cross, costate, whole, mine):
    z, y = rank_ref[0] // 2, rank_ref[0] % 2
    rows, units = c0.shape[0], schur.shape[0]
    for turn, part in enumerate((c0, c2, c4, c6)):
        whole[at(z ^ turn, rows), :] = part[...]
    for block in range(4):
        mine[:, pl.ds(block * units, units)] = schur[:, at(2 * block + y, units)]
    product[...] = times_t(whole[...], mine[...])
    cross[...] = times_t(whole[...], schur_y[...]).astype(BF16)
    costate[...] = whole[:, at(z, units)].astype(F32).T


def couple(rank, schur, schur_y, parts):
    units, half = schur_y.shape
    rows = parts[0].shape[0]
    return kernel_call(
        couple_kernel,
        [
            jax.ShapeDtypeStruct((4 * rows, units), F32),
            jax.ShapeDtypeStruct((4 * rows, units), BF16),
            jax.ShapeDtypeStruct((units, 4 * rows), F32),
        ],
        [in_smem()] + [in_vmem()] * 6,
        [pltpu.VMEM((4 * rows, half), BF16), pltpu.VMEM((units, half), BF16)],
        16 * rows * half * units,
        4 * MIB,
        16,
    )(rank, schur, schur_y, *parts)


def schur_kernel(rank_ref, schur, out):
    units = schur.shape[0]
    for block in range(4):
        out[:, pl.ds(block * units, units)] = schur[:, at(2 * block + 1 - rank_ref[0] % 2, units)]


def schur_cross(rank, schur):
    units, whole = schur.shape
    return kernel_call(
        schur_kernel,
        jax.ShapeDtypeStruct((units, whole // 2), BF16),
        [in_smem(), in_vmem()],
        [],
        units * whole,
        3 * units * whole,
        8,
    )(rank, schur)


def settle_kernel(rank_ref, product, cross, p0, p2, p4, p6, coupling):
    coupling[...] = (product[...] + cross[...].astype(F32)).T
    for turn, out in enumerate((p0, p2, p4, p6)):
        out[...] = coupling[:, at((rank_ref[0] // 2) ^ turn, out.shape[1])].astype(BF16)


def settle(rank, product, cross):
    columns, units = product.shape
    piece = jax.ShapeDtypeStruct((units, columns // 4), BF16)
    return kernel_call(
        settle_kernel,
        [piece] * 4 + [jax.ShapeDtypeStruct((units, columns), F32)],
        [in_smem()] + [in_vmem()] * 2,
        [],
        product.size,
        12 * product.size,
        8,
    )(rank, product, cross)


def finish_kernel(rank_ref, driven, p0, p2, p4, p6, out, terms):
    for turn, piece in enumerate((p0, p2, p4, p6)):
        here = at((rank_ref[0] // 2) ^ turn, piece.shape[0])
        out[here, :] = (driven[here, :] - piece[...].astype(F32)).astype(out.dtype)
        terms[here, :] = piece[...]


def finish(rank, driven, pieces):
    out = jax.ShapeDtypeStruct(driven.shape, BF16)
    return kernel_call(
        finish_kernel,
        [out, out],
        [in_smem()] + [in_vmem()] * 5,
        [],
        driven.size,
        10 * driven.size,
        8,
    )(rank, driven, *pieces)


def picked_kernel(rank_ref, unit_bus, inverse, out):
    buses = inverse.shape[0]
    ids = rank_ref[0] * buses + lax.broadcasted_iota(jnp.int32, (buses, 1), 0)

    @pl.loop(0, out.shape[1] // 256)
    def _(i):
        lanes = at(i, 256)
        placed = (unit_bus[:, lanes] == ids).astype(BF16)
        out[:, lanes] = times(inverse[...], placed).astype(BF16)


def picked(rank, unit_bus, inverse):
    buses, whole = inverse.shape[0], unit_bus.shape[1]
    return kernel_call(
        picked_kernel,
        jax.ShapeDtypeStruct((buses, whole), BF16),
        [in_smem(), in_vmem(), in_vmem()],
        [],
        2 * buses * buses * whole,
        12 * MIB,
        24,
    )(rank, unit_bus, inverse)


def final_kernel(
    rank_ref, coupling, gain, solved_hbm, columns_hbm,
    own, other, near, own4, other4, own6, other6,
    storage, update, solved, columns, whole, sems,
):
    rank = rank_ref[0]
    z, y = rank // 2, rank % 2
    blocks = columns.shape[0] // 256
    sources = ((columns_hbm, columns), (solved_hbm, solved))

    def transfer(i, kind):
        here = at(i, 256)
        if kind == 2:
            return pltpu.make_async_copy(solved.at[here], update.at[here], sems.at[2, i])
        source, target = sources[kind]
        return pltpu.make_async_copy(source.at[here], target.at[here], sems.at[kind, i])

    @pl.loop(0, blocks)
    def _(i):
        for kind in range(2):
            transfer(i, kind).start()

    rights, units = own.shape[1], gain.shape[0]

    def put(turn, halves):
        for block in range(4):
            lanes = slice(block * units, (block + 1) * units)
            for place, half in enumerate(halves):
                which = y if place == 0 else 1 - y
                whole[at(2 * block + which, units), at(z ^ turn, rights)] = half[lanes, :]

    put(0, (own[...], other[...]))
    put(1, (near[0], near[1]))
    put(2, (own4[...], other4[...]))
    put(3, (own6[...], other6[...]))
    storage[...] = times(gain[...], whole[...]) - coupling[...]

    @pl.loop(0, blocks)
    def _(i):
        here = at(i, 256)
        for kind in range(2):
            transfer(i, kind).wait()
        solved[here, :] = solved[here, :] - times(columns[here, :], whole[...])
        transfer(i, 2).start()

    @pl.loop(0, blocks)
    def _(i):
        transfer(i, 2).wait()


def final(rank, coupling, gain, solved, columns, parts):
    buses, rights = solved.shape
    units, whole = gain.shape
    return kernel_call(
        final_kernel,
        [
            jax.ShapeDtypeStruct((units, rights), F32),
            jax.ShapeDtypeStruct((buses, rights), F32),
        ],
        [in_smem()] + [in_vmem()] * 2 + [anywhere()] * 2 + [in_vmem()] * 7,
        [
            pltpu.VMEM((buses, rights), F32),
            pltpu.VMEM((buses, whole), BF16),
            pltpu.VMEM((whole, rights), BF16),
            pltpu.SemaphoreType.DMA((3, buses // 256)),
        ],
        2 * rights * (buses + units) * whole,
        24 * MIB,
        48,
        [in_vmem(), anywhere()],
    )(rank, coupling, gain, solved, columns, *parts)


def plane_body(
    gain, schur, inverse, sens, residual, unit_rhs, start_state, active, unit_bus
):
    period = lax.axis_index("period")
    rank = lax.axis_index("bus").reshape(1)
    last = lax.axis_size("period") - 1
    everyone = tuple(range(last + 1))
    z, y = rank // 2, rank % 2
    far_end = (z == 0) | (z == 3)
    places = jnp.concatenate(
        [z, z ^ 1, jnp.where(far_end, z ^ 2, z ^ 3), jnp.where(far_end, z ^ 3, z ^ 2), y]
    )

    near, middle = bus_send(gain, 2, everyone), across(gain, everyone)
    *keep, send, solved = front(rank, active, unit_rhs, residual, inverse, sens)
    send, start_in = together(send, start_state)
    pieces = swap_z(start_pieces(rank, start_in), everyone)
    near, middle, send, keep, schur_in, pieces = together(
        near, middle, send, keep, schur, pieces
    )
    there = bus_send(send, 1, everyone)
    start = join(rank, pieces)
    middle2, third, there = together(
        across(near, everyone), middle + outwards(middle, everyone), there
    )
    fourth = middle2 + outwards(middle2, everyone)
    schur_y = bus_send(schur_cross(rank, schur_in), 1, everyone)
    unit_right = None
    for turn, flip in ((3, 6), (2, 4), (1, 2), (0, 0)):
        here = keep[turn] + there[turn].astype(F32)
        if flip:
            here = bus_send(here.astype(BF16), flip, everyone).astype(F32)
        unit_right = here if unit_right is None else unit_right + here
    packed, fourth, unit_right, schur_y, columns, start, start_y = together(
        pack([gain, near, third]),
        fourth,
        unit_right,
        schur_y,
        picked(rank, unit_bus, inverse),
        start,
        bus_send(start, 1, everyone),
    )
    weights = [packed, fourth]

    sums, cross = unit_right.astype(BF16), jnp.zeros(unit_right.shape, BF16)
    for target in range(last - 1, -1, -1):
        vector = (
            period_send(sums, target + 1, target),
            cross if target == last - 1 else period_send(cross, target + 1, target, 1),
        )
        sums, cross = backward(places, period == target, vector, unit_right, (sums, cross), weights)
    costate = (sums.astype(F32) + bus_send(cross, 1, everyone).astype(F32)).astype(BF16)
    product, cross, costate_rows = couple(
        rank, schur, schur_y, swap_z([costate] * 4, everyone)
    )
    *pieces, coupling = settle(rank, product, bus_send(cross, 1, everyone))
    driven = forward(places, (start, start_y), weights)
    advanced, coupled = finish(rank, driven, swap_z(pieces, everyone))

    state = (start, start_y)
    for target in range(1, last + 1):
        arrived = (
            period_send(advanced, target - 1, target),
            period_send(advanced, target - 1, target, 1),
        )
        state = tuple(
            jnp.where(period == target, new, old) for new, old in zip(arrived, state, strict=True)
        )
        if target < last:
            advanced = forward(places, arrived, weights, coupled)
    near = bus_send(jnp.stack(state), 2, everyone)
    own4, own6 = bus_send(state[0], 4, everyone), bus_send(state[0], 6, everyone)
    other4, other6 = bus_send(own4, 1, everyone), bus_send(own6, 1, everyone)
    storage, update = final(
        rank, coupling, gain, solved, columns, [*state, near, own4, other4, own6, other6]
    )
    return storage, costate_rows, update


def plain_body(
    gain, schur, inverse, sens, residual, unit_rhs, start_state, active, unit_bus
):
    period = lax.axis_index("period")
    rank = lax.axis_index("bus")
    size = lax.axis_size("bus")
    groups = lax.axis_size("period")
    units, whole = gain.shape
    buses, columns = residual.shape
    rows = columns // size

    def gathered(block):
        return lax.all_gather(block, "bus", axis=0, tiled=True)

    def to_columns(block):
        swapped = lax.all_to_all(block.reshape(size, rows, units), "bus", 0, 0)
        return jnp.transpose(swapped, (1, 0, 2)).reshape(rows, whole)

    weighted = residual * (1.0 + 3.0 * active.astype(F32))
    solve = times(inverse, weighted.astype(BF16)).astype(BF16)
    partial = lax.dot_general(solve, sens, (((0,), (0,)), ((), ())), preferred_element_type=F32)
    place = (0, rank * units)
    own = lax.dynamic_slice(partial, place, (columns, units)) + unit_rhs.T
    partial = lax.dynamic_update_slice(partial, own, place).astype(BF16)
    unit_right = lax.psum_scatter(partial, "bus", scatter_dimension=0, tiled=True).astype(F32)
    gain_whole = gathered(gain)
    costate = unit_right.astype(BF16)
    for target in range(groups - 2, -1, -1):
        later = period_send(costate, target + 1, target)
        current = (unit_right + times(later, gain_whole)).astype(BF16)
        costate = jnp.where(period == target, current, costate)
    costate_whole = gathered(costate)
    coupling = times_t(costate_whole, schur)
    coupled = to_columns(coupling.astype(BF16)).astype(F32)
    state = to_columns(start_state.T.astype(BF16))
    advanced = times_t(state, gain_whole) - coupled
    for target in range(1, groups):
        arrived = period_send(advanced.astype(BF16), target - 1, target)
        state = jnp.where(period == target, arrived, state)
        advanced = times_t(arrived, gain_whole) - coupled
    state_whole = gathered(state)
    storage = times_t(gain, state_whole) - coupling.T
    costate_rows = lax.dynamic_slice_in_dim(costate_whole, rank * units, units, 1).T.astype(F32)
    ids = rank * buses + jnp.arange(buses, dtype=jnp.int32)
    placement = (unit_bus == ids[:, None]).astype(BF16)
    network = (weighted - times_t(placement, state_whole)).astype(BF16)
    return storage, costate_rows, times(inverse, network)


def body(
    gain, schur, inverse_blocks, sensitivity, residual_bus, unit_rhs, start_state, active_set, unit_bus
):
    in_planes = lax.axis_size("bus") == 8 and lax.axis_size("period") > 2
    storage, costate, update = (plane_body if in_planes else plain_body)(
        gain[0],
        schur[0],
        inverse_blocks[0],
        sensitivity,
        residual_bus[0],
        unit_rhs[0],
        start_state,
        active_set[0][:, None],
        unit_bus[None, :],
    )
    return storage[None], costate[None], update[None]


def solution(mesh):
    by_period = P("period", "bus", None)
    placed = (
        by_period,
        by_period,
        by_period,
        P("bus", None),
        by_period,
        by_period,
        P("bus", None),
        P("period", "bus"),
        P(),
    )
    return jax.shard_map(
        body,
        mesh=mesh,
        in_specs=placed,
        out_specs=(by_period, by_period, by_period),
        check_vma=False,
    )
```

time: 295 us -> 250 us (0.85)
  waiting for transfers between devices: 159 us -> 131 us
  starting transfers between devices: 69.2 us -> 53.2 us
    ppermute x38 -> x23, starting transfers between devices: 57.4 us -> 33.5 us  [bus_send(): return lax.ppermute(block, BOTH, route)]
    ppermute x4, waiting for transfers between devices: 44.2 us -> 21.1 us  [line_send(): return lax.ppermute(block, BOTH, route)]
    ppermute x38 -> x23, waiting for transfers between devices: 96.9 us -> 77.2 us  [bus_send(): return lax.ppermute(block, BOTH, route)]
    ppermute x6 -> x11, waiting for transfers between devices: 17.8 us -> 32.4 us  [period_send(): return lax.ppermute(block, BOTH, route)]
    ppermute x6 -> x11, starting transfers between devices: 6.68 us -> 14.8 us  [period_send(): return lax.ppermute(block, BOTH, route)]
    pallas_call x13 -> x16, Pallas kernels: 44 us -> 43 us  [the longest x1 11.9 us: front(): kernel_call(front_kernel, [keep] * 4 + [send, jax.ShapeDtypeStruct((buses...]
    unnamed x40 -> x58, local copies, waits for them, and re-layouts: 12.4 us -> 12.1 us
  transfers between devices with their start and end apart: 48 -> 38, of which waited for: 23 -> 20; matrix products, arithmetic and copies ran while one was open for 1% -> 3% of each run, Pallas kernels for 6% -> 10%
where the time goes in v4:
time: 250 us; the launch traced here: 249 us
  waiting for transfers between devices  131 us (52%)
  starting transfers between devices  53.2 us (21%)
  Pallas kernels  43 us (17%)
  local copies, waits for them, and re-layouts  14 us (6%)
  other arithmetic  6.44 us (3%)
    ppermute x23, waiting for transfers between devices, bus_send(): return lax.ppermute(block, BOTH, route)  77.2 us
    ppermute x23, starting transfers between devices, bus_send(): return lax.ppermute(block, BOTH, route)  33.5 us
    ppermute x11, waiting for transfers between devices, period_send(): return lax.ppermute(block, BOTH, route)  32.4 us
    ppermute x4, waiting for transfers between devices, line_send(): return lax.ppermute(block, BOTH, route)  21.1 us
    ppermute x11, starting transfers between devices, period_send(): return lax.ppermute(block, BOTH, route)  14.8 us
    unnamed x58, local copies, waits for them, and re-layouts  12.1 us
    pallas_call x1, Pallas kernels, front(): kernel_call(front_kernel, [keep] * 4 + [send, jax.ShapeDtypeStruct((buses...  11.9 us
    pallas_call x1, Pallas kernels, picked(): kernel_call(picked_kernel, jax.ShapeDtypeStruct((buses, whole), BF16), [i...  8.32 us
  transfers between devices with their start and end apart: 38, of which 20 were waited for; matrix products, arithmetic and copies ran while one was open for 3% of the time, Pallas kernels for 10%

profile of v4, /device:TPU:2, one launch (start us, length us, event | category | flops | bytes accessed | tf_op | source)
XLA Modules:
  0.0 248.7 jit_solution(4603328381727384554)
XLA Ops:
  0.6 1.7 collective-permute-start.1
  2.3 3.5 %collective-permute-start = (bf16[256,2048]{1,0:T(8,128)(2,1)}, bf16[256,2048]{1,0:T(8,128)(2,1)S(1)}, u32[]{:S(2)}, u32[]{:S(2)}) collective-permute-start(bf16[256,2048]{1,0:T(8,128)(2,1)} %bitcast.31), channel_id=1, source_target_pairs={{0,2},{1,3},{2,0},{3,1},{4,6},{5,7},{6,4},{7,5},{8,10},{9,11},{10,... | collective-permute-start | bytes 3145736 | tf_op jit(solution)/shard_map/ppermute | solution.py:19
  5.8 1.8 copy.12.active
  9.7 11.9 %shard_map.112 = (f32[128,1024]{1,0:T(8,128)S(1)}, f32[128,1024]{1,0:T(8,128)S(1)}, f32[128,1024]{1,0:T(8,128)S(1)}, f32[128,1024]{1,0:T(8,128)S(1)}, bf16[4,128...) custom-call(s32[1]{0:T(128)} %bitcast.rank_ref, s32[1280,1]{1,0:T(8,128)S(1)} %copy-done.19, f32[256,512]{1,0:T(8,128)S(1)} %bitcast.38, ...), custom_call_target="tpu_custom_call" | custom-call | flops 4362076160 | bytes 25165824 | tf_op jit(solution)/shard_map/pallas_call | solution.py:142
  21.7 1.9 collective-permute-start.3
  23.6 2.5 collective-permute-start.4
  26.1 6.0 %collective-permute-done.2.p2 = bf16[256,128]{1,0:T(8,128)(2,1)S(1)} collective-permute-done((bf16[256,128]{1,0:T(8,128)(2,1)S(1)}, bf16[256,128]{1,0:T(8,128)(2,1)S(1)}, u32[]{:S(2)}, u32[]{:S(2)}) %collective-permute-start.2) | collective-permute-done | bytes 65568 | tf_op jit(solution)/shard_map/ppermute | solution.py:19
  32.1 2.2 collective-permute-done.4.p6
  35.5 1.6 collective-permute-start.7
  38.5 21.1 %collective-permute-done.6 = bf16[256,2048]{1,0:T(8,128)(2,1)S(1)} collective-permute-done((bf16[256,2048]{1,0:T(8,128)(2,1)}, bf16[256,2048]{1,0:T(8,128)(2,1)S(1)}, u32[]{:S(2)}, u32[]{:S(2)}) %collective-permute-start.6) | collective-permute-done | bytes 1048608 | tf_op jit(solution)/shard_map/ppermute | solution.py:48
  59.7 1.6 add.37.refs_2_
  63.3 2.5 %collective-permute-start.9 = (bf16[128,1024]{1,0:T(8,128)(2,1)S(1)}, bf16[128,1024]{1,0:T(8,128)(2,1)S(1)}, u32[]{:S(2)}, u32[]{:S(2)}) collective-permute-start(bf16[128,1024]{1,0:T(8,128)(2,1)S(1)} %get-tuple-element.107), channel_id=1, source_target_pairs={{0,6},{1,7},{2,4},{3,5},{4,2},{5,3},{6,0},{7,1},{8,14},{9,15},{10,... | collective-permute-start | bytes 786440 | tf_op jit(solution)/shard_map/ppermute | solution.py:19
  65.8 1.9 collective-permute-start.11
  67.7 8.3 %shard_map.116.columns_hbm = bf16[1280,2048]{1,0:T(8,128)(2,1)S(1)} custom-call(s32[1]{0:T(128)} %bitcast.rank_ref, s32[1,2048]{1,0:T(1,128)S(1)} %bitcast.39, bf16[1280,1280]{1,0:T(8,128)(2,1)S(1)} %bitcast.37), custom_call_target="tpu_custom_call" | custom-call | flops 6710886400 | bytes 12582912 | tf_op jit(solution)/shard_map/pallas_call | solution.py:401
  76.1 2.3 copy-done.28
  78.4 2.0 shard_map.114.packed
  80.4 1.6 collective-permute-start.13
  82.0 20.7 %collective-permute-done.11 = bf16[128,1024]{1,0:T(8,128)(2,1)S(1)} collective-permute-done((bf16[128,1024]{1,0:T(8,128)(2,1)S(1)}, bf16[128,1024]{1,0:T(8,128)(2,1)S(1)}, u32[]{:S(2)}, u32[]{:S(2)}) %collective-permute-start.11) | collective-permute-done | bytes 262176 | tf_op jit(solution)/shard_map/ppermute | solution.py:19
  106.5 2.3 collective-permute-done.14.own
  111.2 2.7 %shard_map.118 = (bf16[128,1024]{1,0:T(8,128)(2,1)}, bf16[128,1024]{1,0:T(8,128)(2,1)}) custom-call(s32[5]{0:T(128)S(1)} %concatenate.3.places, s32[1]{0:T(128)} %bitcast.14.turn, bf16[128,1024]{1,0:T(8,128)(2,1)} %collective-permute-done.14.own, bf16[128,1024]{1,0:T(8,128)(2,1)S(1)} %broadcast_in_dim.16.other.former_cross, f32[128,1024]{1,0:T(8,128)S(1)} %copy-done.6, ...), custom_call_target="tpu_custom_call" | custom-call | flops 536870912 | bytes 4194304 | tf_op jit(solution)/shard_map/pallas_call | solution.py:257
  113.9 2.0 collective-permute-start.15
  115.8 2.0 collective-permute-start.16
  117.8 1.5 collective-permute-done.15.own
  119.3 2.8 %collective-permute-done.16.other = bf16[128,1024]{1,0:T(8,128)(2,1)} collective-permute-done((bf16[128,1024]{1,0:T(8,128)(2,1)}, bf16[128,1024]{1,0:T(8,128)(2,1)}, u32[]{:S(2)}, u32[]{:S(2)}) %collective-permute-start.16) | collective-permute-done | bytes 262176 | tf_op jit(solution)/shard_map/ppermute | solution.py:25
  124.4 2.0 shard_map.119
  134.2 5.1 %collective-permute-done.19 = bf16[128,1024]{1,0:T(8,128)(2,1)S(1)} collective-permute-done((bf16[128,1024]{1,0:T(8,128)(2,1)S(1)}, bf16[128,1024]{1,0:T(8,128)(2,1)S(1)}, u32[]{:S(2)}, u32[]{:S(2)}) %collective-permute-start.19) | collective-permute-done | bytes 262176 | tf_op jit(solution)/shard_map/ppermute | solution.py:19
  139.3 2.5 %collective-permute-start.22 = (bf16[128,1024]{1,0:T(8,128)(2,1)S(1)}, bf16[128,1024]{1,0:T(8,128)(2,1)S(1)}, u32[]{:S(2)}, u32[]{:S(2)}) collective-permute-start(bf16[128,1024]{1,0:T(8,128)(2,1)S(1)} %add_convert_fusion.c0), channel_id=1, source_target_pairs={{0,6},{1,7},{2,4},{3,5},{4,2},{5,3},{6,0},{7,1},{8,14},{9,15},{10,... | collective-permute-start | bytes 786440 | tf_op jit(solution)/shard_map/ppermute | solution.py:19
  141.9 1.9 collective-permute-start.20
  143.8 4.1 %collective-permute-done.22.c6 = bf16[128,1024]{1,0:T(8,128)(2,1)S(1)} collective-permute-done((bf16[128,1024]{1,0:T(8,128)(2,1)S(1)}, bf16[128,1024]{1,0:T(8,128)(2,1)S(1)}, u32[]{:S(2)}, u32[]{:S(2)}) %collective-permute-start.22) | collective-permute-done | bytes 262176 | tf_op jit(solution)/shard_map/ppermute | solution.py:19
  147.9 8.2 %collective-permute-done.21.c4 = bf16[128,1024]{1,0:T(8,128)(2,1)S(1)} collective-permute-done((bf16[128,1024]{1,0:T(8,128)(2,1)S(1)}, bf16[128,1024]{1,0:T(8,128)(2,1)S(1)}, u32[]{:S(2)}, u32[]{:S(2)}) %collective-permute-start.21) | collective-permute-done | bytes 262176 | tf_op jit(solution)/shard_map/ppermute | solution.py:19
  156.2 1.5 shard_map.121
  158.9 5.1 %collective-permute-done.23.cross = bf16[512,256]{1,0:T(8,128)(2,1)S(1)} collective-permute-done((bf16[512,256]{1,0:T(8,128)(2,1)S(1)}, bf16[512,256]{1,0:T(8,128)(2,1)S(1)}, u32[]{:S(2)}, u32[]{:S(2)}) %collective-permute-start.23) | collective-permute-done | bytes 262176 | tf_op jit(solution)/shard_map/ppermute | solution.py:19
  165.1 3.0 %collective-permute-start.25 = (bf16[256,128]{1,0:T(8,128)(2,1)S(1)}, bf16[256,128]{1,0:T(8,128)(2,1)S(1)}, u32[]{:S(2)}, u32[]{:S(2)}) collective-permute-start(bf16[256,128]{1,0:T(8,128)(2,1)S(1)} %get-tuple-element.100), channel_id=1, source_target_pairs={{0,4},{1,5},{2,6},{3,7},{4,0},{5,1},{6,2},{7,3},{8,12},{9,13},{10,... | collective-permute-start | bytes 196616 | tf_op jit(solution)/shard_map/ppermute | solution.py:19
  169.5 1.8 shard_map.123.driven
  171.3 2.9 %collective-permute-done.26.p6 = bf16[256,128]{1,0:T(8,128)(2,1)S(1)} collective-permute-done((bf16[256,128]{1,0:T(8,128)(2,1)S(1)}, bf16[256,128]{1,0:T(8,128)(2,1)S(1)}, u32[]{:S(2)}, u32[]{:S(2)}) %collective-permute-start.26) | collective-permute-done | bytes 65568 | tf_op jit(solution)/shard_map/ppermute | solution.py:19
  175.9 1.8 shard_map.125
  180.3 21.9 %collective-permute-done.30.other = bf16[1024,128]{1,0:T(8,128)(2,1)S(1)} collective-permute-done((bf16[1024,128]{1,0:T(8,128)(2,1)S(1)}, bf16[1024,128]{1,0:T(8,128)(2,1)S(1)}, u32[]{:S(2)}, u32[]{:S(2)}) %collective-permute-start.30) | collective-permute-done | bytes 262176 | tf_op jit(solution)/shard_map/ppermute | solution.py:25
  202.2 2.1 collective-permute-done.29.own
  204.2 2.5 %shard_map.126 = bf16[1024,128]{1,0:T(8,128)(2,1)} custom-call(s32[5]{0:T(128)S(1)} %concatenate.3.places, bf16[1024,128]{1,0:T(8,128)(2,1)S(1)} %collective-permute-done.29.own, bf16[1024,128]{1,0:T(8,128)(2,1)S(1)} %collective-permute-done.30.other, bf16[3,256,2048]{2,1,0:T(8,128)(2,1)S(1)} %copy-done, bf16[256,2048]{1,0:T(8,128)(2,1)S(1)} %copy-done.4, ...), custom_call_target="tpu_custom_call" | custom-call | flops 536870912 | bytes 4194304 | tf_op jit(solution)/shard_map/pallas_call | solution.py:288
  206.8 1.4 collective-permute-start.31
  210.6 1.4 collective-permute-start.36
  212.0 1.8 collective-permute-done.32
  214.9 1.9 collective-permute-start.34
  216.8 4.9 %collective-permute-done.36.own6 = bf16[1024,128]{1,0:T(8,128)(2,1)S(1)} collective-permute-done((bf16[1024,128]{1,0:T(8,128)(2,1)S(1)}, bf16[1024,128]{1,0:T(8,128)(2,1)S(1)}, u32[]{:S(2)}, u32[]{:S(2)}) %collective-permute-start.36) | collective-permute-done | bytes 262176 | tf_op jit(solution)/shard_map/ppermute | solution.py:19
  223.0 11.0 %collective-permute-done.34.own4 = bf16[1024,128]{1,0:T(8,128)(2,1)S(1)} collective-permute-done((bf16[1024,128]{1,0:T(8,128)(2,1)S(1)}, bf16[1024,128]{1,0:T(8,128)(2,1)S(1)}, u32[]{:S(2)}, u32[]{:S(2)}) %collective-permute-start.34) | collective-permute-done | bytes 262176 | tf_op jit(solution)/shard_map/ppermute | solution.py:19
  235.3 1.6 collective-permute-done.33.near
  236.9 5.1 %collective-permute-done.35.other4 = bf16[1024,128]{1,0:T(8,128)(2,1)S(1)} collective-permute-done((bf16[1024,128]{1,0:T(8,128)(2,1)S(1)}, bf16[1024,128]{1,0:T(8,128)(2,1)S(1)}, u32[]{:S(2)}, u32[]{:S(2)}) %collective-permute-start.35) | collective-permute-done | bytes 262176 | tf_op jit(solution)/shard_map/ppermute | solution.py:19
  241.9 6.6 %shard_map.127 = (f32[256,512]{1,0:T(8,128)}, f32[1280,512]{1,0:T(8,128)}) custom-call(s32[1]{0:T(128)} %bitcast.rank_ref, f32[256,512]{1,0:T(8,128)S(1)} %copy-done.26, bf16[256,2048]{1,0:T(8,128)(2,1)S(1)} %bitcast.33, f32[1280,512]{1,0:T(8,128)} %get-tuple-element.94.solved_hbm, bf16[1280,2048]{1,0:T(8,128)(2,1)} %copy-done.28, ...), custom_call_target="tpu_custom_call" | custom-call | flops 3221225472 | bytes 25165824 | tf_op jit(solution)/shard_map/pallas_call | solution.py:465
  (114 shorter events, 37.1 us)
Async XLA Ops:
  0.6 33.6 %collective-permute-start.1 = (bf16[256,2048]{1,0:T(8,128)(2,1)}, bf16[256,2048]{1,0:T(8,128)(2,1)}, u32[]{:S(2)}, u32[]{:S(2)}) collective-permute-start(bf16[256,2048]{1,0:T(8,128)(2,1)} %bitcast.30), channel_id=1, source_target_pairs={{2,4},{3,5},{4,2},{5,3},{10,12},{11,13},{12,10},{13,11},{18,20},{1... | collective-permute-start | bytes 3145736 | tf_op jit(solution)/shard_map/ppermute | solution.py:48
  2.3 31.9 %collective-permute-start = (bf16[256,2048]{1,0:T(8,128)(2,1)}, bf16[256,2048]{1,0:T(8,128)(2,1)S(1)}, u32[]{:S(2)}, u32[]{:S(2)}) collective-permute-start(bf16[256,2048]{1,0:T(8,128)(2,1)} %bitcast.31), channel_id=1, source_target_pairs={{0,2},{1,3},{2,0},{3,1},{4,6},{5,7},{6,4},{7,5},{8,10},{9,11},{10,... | collective-permute-start | bytes 3145736 | tf_op jit(solution)/shard_map/ppermute | solution.py:19
  9.7 28.2 %copy-start.9 = (bf16[1,256,2048]{2,1,0:T(8,128)(2,1)S(1)}, bf16[1,256,2048]{2,1,0:T(8,128)(2,1)}, u32[]{:S(2)}) copy-start(bf16[1,256,2048]{2,1,0:T(8,128)(2,1)} %param.10) | copy-start | bytes 3145732
  21.7 10.4 %collective-permute-start.2 = (bf16[256,128]{1,0:T(8,128)(2,1)S(1)}, bf16[256,128]{1,0:T(8,128)(2,1)S(1)}, u32[]{:S(2)}, u32[]{:S(2)}) collective-permute-start(bf16[256,128]{1,0:T(8,128)(2,1)S(1)} %get-tuple-element.63), channel_id=1, source_target_pairs={{0,2},{1,3},{2,0},{3,1},{4,6},{5,7},{6,4},{7,5},{8,10},{9,11},{10,... | collective-permute-start | bytes 196616 | tf_op jit(solution)/shard_map/ppermute | solution.py:19
  21.7 10.3 %collective-permute-start.3 = (bf16[256,128]{1,0:T(8,128)(2,1)S(1)}, bf16[256,128]{1,0:T(8,128)(2,1)S(1)}, u32[]{:S(2)}, u32[]{:S(2)}) collective-permute-start(bf16[256,128]{1,0:T(8,128)(2,1)S(1)} %get-tuple-element.64), channel_id=1, source_target_pairs={{0,4},{1,5},{2,6},{3,7},{4,0},{5,1},{6,2},{7,3},{8,12},{9,13},{10,... | collective-permute-start | bytes 196616 | tf_op jit(solution)/shard_map/ppermute | solution.py:19
  23.6 10.6 %collective-permute-start.4 = (bf16[256,128]{1,0:T(8,128)(2,1)S(1)}, bf16[256,128]{1,0:T(8,128)(2,1)S(1)}, u32[]{:S(2)}, u32[]{:S(2)}) collective-permute-start(bf16[256,128]{1,0:T(8,128)(2,1)S(1)} %get-tuple-element.65), channel_id=1, source_target_pairs={{0,6},{1,7},{2,4},{3,5},{4,2},{5,3},{6,0},{7,1},{8,14},{9,15},{10,... | collective-permute-start | bytes 196616 | tf_op jit(solution)/shard_map/ppermute | solution.py:19
  34.2 25.4 %collective-permute-start.6 = (bf16[256,2048]{1,0:T(8,128)(2,1)}, bf16[256,2048]{1,0:T(8,128)(2,1)S(1)}, u32[]{:S(2)}, u32[]{:S(2)}) collective-permute-start(bf16[256,2048]{1,0:T(8,128)(2,1)} %collective-permute-done.1), channel_id=1, source_target_pairs={{2,0},{3,1},{4,6},{5,7},{10,8},{11,9},{12,14},{13,15},{18,16},{19,... | collective-permute-start | bytes 3145736 | tf_op jit(solution)/shard_map/ppermute | solution.py:48
  35.5 26.2 %collective-permute-start.7 = (bf16[4,128,1024]{2,1,0:T(8,128)(2,1)S(1)}, bf16[4,128,1024]{2,1,0:T(8,128)(2,1)S(1)}, u32[]{:S(2)}, u32[]{:S(2)}) collective-permute-start(bf16[4,128,1024]{2,1,0:T(8,128)(2,1)S(1)} %get-tuple-element.68), channel_id=1, source_target_pairs={{0,1},{1,0},{2,3},{3,2},{4,5},{5,4},{6,7},{7,6},{8,9},{9,8},{10,11... | collective-permute-start | bytes 3145736 | tf_op jit(solution)/shard_map/ppermute | solution.py:19
  37.1 24.6 %collective-permute-start.5 = (bf16[256,2048]{1,0:T(8,128)(2,1)S(1)}, bf16[256,2048]{1,0:T(8,128)(2,1)S(1)}, u32[]{:S(2)}, u32[]{:S(2)}) collective-permute-start(bf16[256,2048]{1,0:T(8,128)(2,1)S(1)} %collective-permute-done.refs_1_), channel_id=1, source_target_pairs={{2,4},{3,5},{4,2},{5,3},{10,12},{11,13},{12,10},{13,11},{18,20},{1... | collective-permute-start | bytes 3145736 | tf_op jit(solution)/shard_map/ppermute | solution.py:48
  37.9 29.8 %copy-start.23 = (bf16[1,1280,1280]{2,1,0:T(8,128)(2,1)S(1)}, bf16[1,1280,1280]{2,1,0:T(8,128)(2,1)}, u32[]{:S(2)}) copy-start(bf16[1,1280,1280]{2,1,0:T(8,128)(2,1)} %param.11) | copy-start | bytes 9830404
  38.0 29.8 %copy-start.27 = (s32[2048]{0:T(1024)S(1)}, s32[2048]{0:T(1024)}, u32[]{:S(2)}) copy-start(s32[2048]{0:T(1024)} %param.17) | copy-start | bytes 24580
  38.0 66.3 %collective-permute-start.12 = (bf16[256,1024]{1,0:T(8,128)(2,1)S(1)}, bf16[256,1024]{1,0:T(8,128)(2,1)S(1)}, u32[]{:S(2)}, u32[]{:S(2)}) collective-permute-start(bf16[256,1024]{1,0:T(8,128)(2,1)S(1)} %shard_map.115), channel_id=1, source_target_pairs={{0,1},{1,0},{2,3},{3,2},{4,5},{5,4},{6,7},{7,6},{8,9},{9,8},{10,11... | collective-permute-start | bytes 1572872 | tf_op jit(solution)/shard_map/ppermute | solution.py:19
  61.7 41.2 %collective-permute-start.8 = (bf16[256,2048]{1,0:T(8,128)(2,1)S(1)}, bf16[256,2048]{1,0:T(8,128)(2,1)S(1)}, u32[]{:S(2)}, u32[]{:S(2)}) collective-permute-start(bf16[256,2048]{1,0:T(8,128)(2,1)S(1)} %collective-permute-done.5), channel_id=1, source_target_pairs={{2,0},{3,1},{4,6},{5,7},{10,8},{11,9},{12,14},{13,15},{18,16},{19,... | collective-permute-start | bytes 3145736 | tf_op jit(solution)/shard_map/ppermute | solution.py:48
  63.3 17.2 %collective-permute-start.9 = (bf16[128,1024]{1,0:T(8,128)(2,1)S(1)}, bf16[128,1024]{1,0:T(8,128)(2,1)S(1)}, u32[]{:S(2)}, u32[]{:S(2)}) collective-permute-start(bf16[128,1024]{1,0:T(8,128)(2,1)S(1)} %get-tuple-element.107), channel_id=1, source_target_pairs={{0,6},{1,7},{2,4},{3,5},{4,2},{5,3},{6,0},{7,1},{8,14},{9,15},{10,... | collective-permute-start | bytes 786440 | tf_op jit(solution)/shard_map/ppermute | solution.py:19
  65.8 36.9 %collective-permute-start.11 = (bf16[128,1024]{1,0:T(8,128)(2,1)S(1)}, bf16[128,1024]{1,0:T(8,128)(2,1)S(1)}, u32[]{:S(2)}, u32[]{:S(2)}) collective-permute-start(bf16[128,1024]{1,0:T(8,128)(2,1)S(1)} %get-tuple-element.108), channel_id=1, source_target_pairs={{0,2},{1,3},{2,0},{3,1},{4,6},{5,7},{6,4},{7,5},{8,10},{9,11},{10,... | collective-permute-start | bytes 786440 | tf_op jit(solution)/shard_map/ppermute | solution.py:19
  67.7 35.0 %collective-permute-start.10 = (bf16[128,1024]{1,0:T(8,128)(2,1)S(1)}, bf16[128,1024]{1,0:T(8,128)(2,1)S(1)}, u32[]{:S(2)}, u32[]{:S(2)}) collective-permute-start(bf16[128,1024]{1,0:T(8,128)(2,1)S(1)} %get-tuple-element.109), channel_id=1, source_target_pairs={{0,4},{1,5},{2,6},{3,7},{4,0},{5,1},{6,2},{7,3},{8,12},{9,13},{10,... | collective-permute-start | bytes 786440 | tf_op jit(solution)/shard_map/ppermute | solution.py:19
  80.4 28.5 %copy-start = (bf16[3,256,2048]{2,1,0:T(8,128)(2,1)S(1)}, bf16[3,256,2048]{2,1,0:T(8,128)(2,1)}, u32[]{:S(2)}) copy-start(bf16[3,256,2048]{2,1,0:T(8,128)(2,1)} %shard_map.114.packed) | copy-start | bytes 9437188
  80.4 23.8 %collective-permute-start.13 = (bf16[1024,128]{1,0:T(8,128)(2,1)S(1)}, bf16[1024,128]{1,0:T(8,128)(2,1)S(1)}, u32[]{:S(2)}, u32[]{:S(2)}) collective-permute-start(bf16[1024,128]{1,0:T(8,128)(2,1)S(1)} %shard_map.117.own), channel_id=1, source_target_pairs={{0,1},{1,0},{2,3},{3,2},{4,5},{5,4},{6,7},{7,6},{8,9},{9,8},{10,11... | collective-permute-start | bytes 786440 | tf_op jit(solution)/shard_map/ppermute | solution.py:19
  105.1 3.8 %collective-permute-start.14 = (bf16[128,1024]{1,0:T(8,128)(2,1)}, bf16[128,1024]{1,0:T(8,128)(2,1)}, u32[]{:S(2)}, u32[]{:S(2)}) collective-permute-start(bf16[128,1024]{1,0:T(8,128)(2,1)} %convert_element_type.71.former_sums), channel_id=1, source_target_pairs={{24,16},{25,17},{26,18},{27,19},{28,20},{29,21},{30,22},{31,23}} | collective-permute-start | bytes 786440 | tf_op jit(solution)/shard_map/ppermute | solution.py:25
  113.9 5.5 %collective-permute-start.15 = (bf16[128,1024]{1,0:T(8,128)(2,1)}, bf16[128,1024]{1,0:T(8,128)(2,1)}, u32[]{:S(2)}, u32[]{:S(2)}) collective-permute-start(bf16[128,1024]{1,0:T(8,128)(2,1)} %get-tuple-element.85.former_sums), channel_id=1, source_target_pairs={{16,8},{17,9},{18,10},{19,11},{20,12},{21,13},{22,14},{23,15}} | collective-permute-start | bytes 786440 | tf_op jit(solution)/shard_map/ppermute | solution.py:25
  115.8 6.3 %collective-permute-start.16 = (bf16[128,1024]{1,0:T(8,128)(2,1)}, bf16[128,1024]{1,0:T(8,128)(2,1)}, u32[]{:S(2)}, u32[]{:S(2)}) collective-permute-start(bf16[128,1024]{1,0:T(8,128)(2,1)} %get-tuple-element.86.former_cross), channel_id=1, source_target_pairs={{16,9},{17,8},{18,11},{19,10},{20,13},{21,12},{22,15},{23,14}} | collective-permute-start | bytes 786440 | tf_op jit(solution)/shard_map/ppermute | solution.py:25
  126.4 2.7 %collective-permute-start.17 = (bf16[128,1024]{1,0:T(8,128)(2,1)}, bf16[128,1024]{1,0:T(8,128)(2,1)}, u32[]{:S(2)}, u32[]{:S(2)}) collective-permute-start(bf16[128,1024]{1,0:T(8,128)(2,1)} %get-tuple-element.87.former_sums), channel_id=1, source_target_pairs={{8,0},{9,1},{10,2},{11,3},{12,4},{13,5},{14,6},{15,7}} | collective-permute-start | bytes 786440 | tf_op jit(solution)/shard_map/ppermute | solution.py:25
  127.8 1.4 collective-permute-start.18
  132.8 36.7 %copy-start.4 = (bf16[256,2048]{1,0:T(8,128)(2,1)S(1)}, bf16[256,2048]{1,0:T(8,128)(2,1)}, u32[]{:S(2)}) copy-start(bf16[256,2048]{1,0:T(8,128)(2,1)} %add.38.fourth) | copy-start | bytes 3145732
  132.8 36.7 %copy-start.14 = (bf16[1024,128]{1,0:T(8,128)(2,1)S(1)}, bf16[1024,128]{1,0:T(8,128)(2,1)}, u32[]{:S(2)}) copy-start(bf16[1024,128]{1,0:T(8,128)(2,1)} %copy-done.13) | copy-start | bytes 786436
  132.8 6.4 %collective-permute-start.19 = (bf16[128,1024]{1,0:T(8,128)(2,1)S(1)}, bf16[128,1024]{1,0:T(8,128)(2,1)S(1)}, u32[]{:S(2)}, u32[]{:S(2)}) collective-permute-start(bf16[128,1024]{1,0:T(8,128)(2,1)S(1)} %get-tuple-element.90), channel_id=1, source_target_pairs={{0,1},{1,0},{2,3},{3,2},{4,5},{5,4},{6,7},{7,6},{8,9},{9,8},{10,11... | collective-permute-start | bytes 786440 | tf_op jit(solution)/shard_map/ppermute | solution.py:19
  139.3 8.6 %collective-permute-start.22 = (bf16[128,1024]{1,0:T(8,128)(2,1)S(1)}, bf16[128,1024]{1,0:T(8,128)(2,1)S(1)}, u32[]{:S(2)}, u32[]{:S(2)}) collective-permute-start(bf16[128,1024]{1,0:T(8,128)(2,1)S(1)} %add_convert_fusion.c0), channel_id=1, source_target_pairs={{0,6},{1,7},{2,4},{3,5},{4,2},{5,3},{6,0},{7,1},{8,14},{9,15},{10,... | collective-permute-start | bytes 786440 | tf_op jit(solution)/shard_map/ppermute | solution.py:19
  141.9 14.3 %collective-permute-start.21 = (bf16[128,1024]{1,0:T(8,128)(2,1)S(1)}, bf16[128,1024]{1,0:T(8,128)(2,1)S(1)}, u32[]{:S(2)}, u32[]{:S(2)}) collective-permute-start(bf16[128,1024]{1,0:T(8,128)(2,1)S(1)} %add_convert_fusion.c0), channel_id=1, source_target_pairs={{0,4},{1,5},{2,6},{3,7},{4,0},{5,1},{6,2},{7,3},{8,12},{9,13},{10,... | collective-permute-start | bytes 786440 | tf_op jit(solution)/shard_map/ppermute | solution.py:19
  141.9 14.3 %collective-permute-start.20 = (bf16[128,1024]{1,0:T(8,128)(2,1)S(1)}, bf16[128,1024]{1,0:T(8,128)(2,1)S(1)}, u32[]{:S(2)}, u32[]{:S(2)}) collective-permute-start(bf16[128,1024]{1,0:T(8,128)(2,1)S(1)} %add_convert_fusion.c0), channel_id=1, source_target_pairs={{0,2},{1,3},{2,0},{3,1},{4,6},{5,7},{6,4},{7,5},{8,10},{9,11},{10,... | collective-permute-start | bytes 786440 | tf_op jit(solution)/shard_map/ppermute | solution.py:19
  157.7 6.4 %collective-permute-start.23 = (bf16[512,256]{1,0:T(8,128)(2,1)S(1)}, bf16[512,256]{1,0:T(8,128)(2,1)S(1)}, u32[]{:S(2)}, u32[]{:S(2)}) collective-permute-start(bf16[512,256]{1,0:T(8,128)(2,1)S(1)} %get-tuple-element.92), channel_id=1, source_target_pairs={{0,1},{1,0},{2,3},{3,2},{4,5},{5,4},{6,7},{7,6},{8,9},{9,8},{10,11... | collective-permute-start | bytes 786440 | tf_op jit(solution)/shard_map/ppermute | solution.py:19
  165.1 6.2 %collective-permute-start.24 = (bf16[256,128]{1,0:T(8,128)(2,1)S(1)}, bf16[256,128]{1,0:T(8,128)(2,1)S(1)}, u32[]{:S(2)}, u32[]{:S(2)}) collective-permute-start(bf16[256,128]{1,0:T(8,128)(2,1)S(1)} %get-tuple-element.99), channel_id=1, source_target_pairs={{0,2},{1,3},{2,0},{3,1},{4,6},{5,7},{6,4},{7,5},{8,10},{9,11},{10,... | collective-permute-start | bytes 196616 | tf_op jit(solution)/shard_map/ppermute | solution.py:19
  165.1 6.2 %collective-permute-start.25 = (bf16[256,128]{1,0:T(8,128)(2,1)S(1)}, bf16[256,128]{1,0:T(8,128)(2,1)S(1)}, u32[]{:S(2)}, u32[]{:S(2)}) collective-permute-start(bf16[256,128]{1,0:T(8,128)(2,1)S(1)} %get-tuple-element.100), channel_id=1, source_target_pairs={{0,4},{1,5},{2,6},{3,7},{4,0},{5,1},{6,2},{7,3},{8,12},{9,13},{10,... | collective-permute-start | bytes 196616 | tf_op jit(solution)/shard_map/ppermute | solution.py:19
  168.1 6.1 %collective-permute-start.26 = (bf16[256,128]{1,0:T(8,128)(2,1)S(1)}, bf16[256,128]{1,0:T(8,128)(2,1)S(1)}, u32[]{:S(2)}, u32[]{:S(2)}) collective-permute-start(bf16[256,128]{1,0:T(8,128)(2,1)S(1)} %get-tuple-element.101), channel_id=1, source_target_pairs={{0,6},{1,7},{2,4},{3,5},{4,2},{5,3},{6,0},{7,1},{8,14},{9,15},{10,... | collective-permute-start | bytes 196616 | tf_op jit(solution)/shard_map/ppermute | solution.py:19
  174.3 1.6 collective-permute-start.28
  175.0 0.9 collective-permute-start.27
  175.8 30.9 %copy-start.15 = (bf16[1024,128]{1,0:T(8,128)(2,1)}, bf16[1024,128]{1,0:T(8,128)(2,1)S(1)}, u32[]{:S(2)}) copy-start(bf16[1024,128]{1,0:T(8,128)(2,1)S(1)} %collective-permute-done.28.other) | copy-start | bytes 786436
  175.8 26.3 %copy-start.17 = (bf16[1024,128]{1,0:T(8,128)(2,1)}, bf16[1024,128]{1,0:T(8,128)(2,1)S(1)}, u32[]{:S(2)}) copy-start(bf16[1024,128]{1,0:T(8,128)(2,1)S(1)} %collective-permute-done.27.own) | copy-start | bytes 786436
  177.7 24.5 %collective-permute-start.30 = (bf16[1024,128]{1,0:T(8,128)(2,1)S(1)}, bf16[1024,128]{1,0:T(8,128)(2,1)S(1)}, u32[]{:S(2)}, u32[]{:S(2)}) collective-permute-start(bf16[1024,128]{1,0:T(8,128)(2,1)S(1)} %shard_map.125), channel_id=1, source_target_pairs={{8,17},{9,16},{10,19},{11,18},{12,21},{13,20},{14,23},{15,22}} | collective-permute-start | bytes 786440 | tf_op jit(solution)/shard_map/ppermute | solution.py:25
  179.0 25.2 %collective-permute-start.29 = (bf16[1024,128]{1,0:T(8,128)(2,1)S(1)}, bf16[1024,128]{1,0:T(8,128)(2,1)S(1)}, u32[]{:S(2)}, u32[]{:S(2)}) collective-permute-start(bf16[1024,128]{1,0:T(8,128)(2,1)S(1)} %shard_map.125), channel_id=1, source_target_pairs={{8,16},{9,17},{10,18},{11,19},{12,20},{13,21},{14,22},{15,23}} | collective-permute-start | bytes 786440 | tf_op jit(solution)/shard_map/ppermute | solution.py:25
  206.8 35.2 %copy-start.12 = (bf16[1,256,2048]{2,1,0:T(8,128)(2,1)S(1)}, bf16[1,256,2048]{2,1,0:T(8,128)(2,1)}, u32[]{:S(2)}) copy-start(bf16[1,256,2048]{2,1,0:T(8,128)(2,1)} %param.9) | copy-start | bytes 3145732
  206.8 35.2 %copy-start.26 = (f32[256,512]{1,0:T(8,128)S(1)}, f32[256,512]{1,0:T(8,128)}, u32[]{:S(2)}) copy-start(f32[256,512]{1,0:T(8,128)} %copy-done.25) | copy-start | bytes 1572868
  206.8 2.8 %collective-permute-start.31 = (bf16[1024,128]{1,0:T(8,128)(2,1)}, bf16[1024,128]{1,0:T(8,128)(2,1)S(1)}, u32[]{:S(2)}, u32[]{:S(2)}) collective-permute-start(bf16[1024,128]{1,0:T(8,128)(2,1)} %shard_map.126), channel_id=1, source_target_pairs={{16,24},{17,25},{18,26},{19,27},{20,28},{21,29},{22,30},{23,31}} | collective-permute-start | bytes 786440 | tf_op jit(solution)/shard_map/ppermute | solution.py:25
  208.2 5.5 %collective-permute-start.32 = (bf16[1024,128]{1,0:T(8,128)(2,1)}, bf16[1024,128]{1,0:T(8,128)(2,1)S(1)}, u32[]{:S(2)}, u32[]{:S(2)}) collective-permute-start(bf16[1024,128]{1,0:T(8,128)(2,1)} %shard_map.126), channel_id=1, source_target_pairs={{16,25},{17,24},{18,27},{19,26},{20,29},{21,28},{22,31},{23,30}} | collective-permute-start | bytes 786440 | tf_op jit(solution)/shard_map/ppermute | solution.py:25
  210.6 11.1 %collective-permute-start.36 = (bf16[1024,128]{1,0:T(8,128)(2,1)S(1)}, bf16[1024,128]{1,0:T(8,128)(2,1)S(1)}, u32[]{:S(2)}, u32[]{:S(2)}) collective-permute-start(bf16[1024,128]{1,0:T(8,128)(2,1)S(1)} %select_select_fusion.1.own), channel_id=1, source_target_pairs={{0,6},{1,7},{2,4},{3,5},{4,2},{5,3},{6,0},{7,1},{8,14},{9,15},{10,... | collective-permute-start | bytes 786440 | tf_op jit(solution)/shard_map/ppermute | solution.py:19
  214.9 22.0 %collective-permute-start.33 = (bf16[2,1024,128]{2,1,0:T(8,128)(2,1)S(1)}, bf16[2,1024,128]{2,1,0:T(8,128)(2,1)S(1)}, u32[]{:S(2)}, u32[]{:S(2)}) collective-permute-start(bf16[2,1024,128]{2,1,0:T(8,128)(2,1)S(1)} %pad_maximum_fusion), channel_id=1, source_target_pairs={{0,2},{1,3},{2,0},{3,1},{4,6},{5,7},{6,4},{7,5},{8,10},{9,11},{10,... | collective-permute-start | bytes 1572872 | tf_op jit(solution)/shard_map/ppermute | solution.py:19
  214.9 19.1 %collective-permute-start.34 = (bf16[1024,128]{1,0:T(8,128)(2,1)S(1)}, bf16[1024,128]{1,0:T(8,128)(2,1)S(1)}, u32[]{:S(2)}, u32[]{:S(2)}) collective-permute-start(bf16[1024,128]{1,0:T(8,128)(2,1)S(1)} %select_select_fusion.1.own), channel_id=1, source_target_pairs={{0,4},{1,5},{2,6},{3,7},{4,0},{5,1},{6,2},{7,3},{8,12},{9,13},{10,... | collective-permute-start | bytes 786440 | tf_op jit(solution)/shard_map/ppermute | solution.py:19
  221.7 15.2 %collective-permute-start.37 = (bf16[1024,128]{1,0:T(8,128)(2,1)S(1)}, bf16[1024,128]{1,0:T(8,128)(2,1)S(1)}, u32[]{:S(2)}, u32[]{:S(2)}) collective-permute-start(bf16[1024,128]{1,0:T(8,128)(2,1)S(1)} %collective-permute-done.36.own6), channel_id=1, source_target_pairs={{0,1},{1,0},{2,3},{3,2},{4,5},{5,4},{6,7},{7,6},{8,9},{9,8},{10,11... | collective-permute-start | bytes 786440 | tf_op jit(solution)/shard_map/ppermute | solution.py:19
  234.0 7.9 %collective-permute-start.35 = (bf16[1024,128]{1,0:T(8,128)(2,1)S(1)}, bf16[1024,128]{1,0:T(8,128)(2,1)S(1)}, u32[]{:S(2)}, u32[]{:S(2)}) collective-permute-start(bf16[1024,128]{1,0:T(8,128)(2,1)S(1)} %collective-permute-done.34.own4), channel_id=1, source_target_pairs={{0,1},{1,0},{2,3},{3,2},{4,5},{5,4},{6,7},{7,6},{8,9},{9,8},{10,11... | collective-permute-start | bytes 786440 | tf_op jit(solution)/shard_map/ppermute | solution.py:19
  (19 other events, 98.5 us)

commit v5 on v4

--- a/solution.py
+++ b/solution.py
@@ -211,7 +211,7 @@
         [pltpu.SemaphoreType.DMA((3,))],
         0,
         12 * parts[0].size,
-        48,
+        8,
     )(*parts)
 
 
@@ -515,8 +515,10 @@
         if flip:
             here = bus_send(here.astype(BF16), flip, everyone).astype(F32)
         unit_right = here if unit_right is None else unit_right + here
-    packed, fourth, unit_right, schur_y, columns, start, start_y = together(
-        pack([gain, near, third]),
+    gain, near, third, fourth, unit_right, schur_y, columns, start, start_y = together(
+        gain,
+        near,
+        third,
         fourth,
         unit_right,
         schur_y,
@@ -524,7 +526,6 @@
         start,
         bus_send(start, 1, everyone),
     )
-    weights = [packed, fourth]
 
     sums, cross = unit_right.astype(BF16), jnp.zeros(unit_right.shape, BF16)
     for target in range(last - 1, -1, -1):
@@ -532,6 +533,8 @@
             period_send(sums, target + 1, target),
             cross if target == last - 1 else period_send(cross, target + 1, target, 1),
         )
+        gain, near, third, fourth, sums, cross = together(gain, near, third, fourth, sums, cross)
+        weights = [pack([gain, near, third]), fourth]
         sums, cross = backward(places, period == target, vector, unit_right, (sums, cross), weights)
     costate = (sums.astype(F32) + bus_send(cross, 1, everyone).astype(F32)).astype(BF16)
     product, cross, costate_rows = couple(

time: 250 us -> 246 us (0.984)
  starting transfers between devices: 53.2 us -> 58.2 us
  other arithmetic: 6.44 us -> 1.5 us
    ppermute x23, waiting for transfers between devices: 77.2 us -> 88.1 us  [bus_send(): return lax.ppermute(block, BOTH, route)]
    ppermute x11, waiting for transfers between devices: 32.4 us -> 22.7 us  [period_send(): return lax.ppermute(block, BOTH, route)]
    ppermute x23, starting transfers between devices: 33.5 us -> 38.5 us  [bus_send(): return lax.ppermute(block, BOTH, route)]
    unnamed x58 -> x38, local copies, waits for them, and re-layouts: 12.1 us -> 10.9 us
  transfers between devices with their start and end apart: 38 -> 38, of which waited for: 20 -> 20; matrix products, arithmetic and copies ran while one was open for 3% -> 1% of each run, Pallas kernels for 10% -> 9%
where the time goes in v5:
time: 246 us; the launch traced here: 245 us
  waiting for transfers between devices  131 us (53%)
  starting transfers between devices  58.2 us (24%)
  Pallas kernels  41 us (17%)
  local copies, waits for them, and re-layouts  11.9 us (5%)
    ppermute x23, waiting for transfers between devices, bus_send(): return lax.ppermute(block, BOTH, route)  88.1 us
    ppermute x23, starting transfers between devices, bus_send(): return lax.ppermute(block, BOTH, route)  38.5 us
    ppermute x11, waiting for transfers between devices, period_send(): return lax.ppermute(block, BOTH, route)  22.7 us
    ppermute x4, waiting for transfers between devices, line_send(): return lax.ppermute(block, BOTH, route)  20.6 us
    ppermute x11, starting transfers between devices, period_send(): return lax.ppermute(block, BOTH, route)  15.7 us
    pallas_call x1, Pallas kernels, front(): kernel_call(front_kernel, [keep] * 4 + [send, jax.ShapeDtypeStruct((buses...  11.9 us
    unnamed x38, local copies, waits for them, and re-layouts  10.9 us
    pallas_call x1, Pallas kernels, picked(): kernel_call(picked_kernel, jax.ShapeDtypeStruct((buses, whole), BF16), [i...  8.48 us
  transfers between devices with their start and end apart: 38, of which 20 were waited for; matrix products, arithmetic and copies ran while one was open for 1% of the time, Pallas kernels for 9%

profile of v5, /device:TPU:2, one launch (start us, length us, event | category | flops | bytes accessed | tf_op | source)
XLA Modules:
  0.0 245.4 jit_solution(322203377558980469)
XLA Ops:
  0.6 1.6 collective-permute-start
  5.0 11.9 %shard_map.112 = (f32[128,1024]{1,0:T(8,128)S(1)}, f32[128,1024]{1,0:T(8,128)S(1)}, f32[128,1024]{1,0:T(8,128)S(1)}, f32[128,1024]{1,0:T(8,128)S(1)}, bf16[4,128...) custom-call(s32[1]{0:T(128)} %bitcast.rank_ref, s32[1280,1]{1,0:T(8,128)S(1)} %copy.12.active, f32[256,512]{1,0:T(8,128)S(1)} %bitcast.40, ...), custom_call_target="tpu_custom_call" | custom-call | flops 4362076160 | bytes 25165824 | tf_op jit(solution)/shard_map/pallas_call | solution.py:142
  17.0 4.4 %collective-permute-start.2 = (bf16[256,128]{1,0:T(8,128)(2,1)S(1)}, bf16[256,128]{1,0:T(8,128)(2,1)S(1)}, u32[]{:S(2)}, u32[]{:S(2)}) collective-permute-start(bf16[256,128]{1,0:T(8,128)(2,1)S(1)} %get-tuple-element.83), channel_id=1, source_target_pairs={{0,2},{1,3},{2,0},{3,1},{4,6},{5,7},{6,4},{7,5},{8,10},{9,11},{10,... | collective-permute-start | bytes 196616 | tf_op jit(solution)/shard_map/ppermute | solution.py:19
  21.4 2.4 collective-permute-start.4
  23.9 3.6 %collective-permute-done.2.p2 = bf16[256,128]{1,0:T(8,128)(2,1)S(1)} collective-permute-done((bf16[256,128]{1,0:T(8,128)(2,1)S(1)}, bf16[256,128]{1,0:T(8,128)(2,1)S(1)}, u32[]{:S(2)}, u32[]{:S(2)}) %collective-permute-start.2) | collective-permute-done | bytes 65568 | tf_op jit(solution)/shard_map/ppermute | solution.py:19
  27.5 7.3 %collective-permute-done.3.p4 = bf16[256,128]{1,0:T(8,128)(2,1)S(1)} collective-permute-done((bf16[256,128]{1,0:T(8,128)(2,1)S(1)}, bf16[256,128]{1,0:T(8,128)(2,1)S(1)}, u32[]{:S(2)}, u32[]{:S(2)}) %collective-permute-start.3) | collective-permute-done | bytes 65568 | tf_op jit(solution)/shard_map/ppermute | solution.py:19
  36.8 1.6 collective-permute-start.7
  39.1 20.6 %collective-permute-done.6 = bf16[256,2048]{1,0:T(8,128)(2,1)S(1)} collective-permute-done((bf16[256,2048]{1,0:T(8,128)(2,1)S(1)}, bf16[256,2048]{1,0:T(8,128)(2,1)S(1)}, u32[]{:S(2)}, u32[]{:S(2)}) %collective-permute-start.6) | collective-permute-done | bytes 1048608 | tf_op jit(solution)/shard_map/ppermute | solution.py:48
  60.1 2.9 %collective-permute-done.7 = bf16[4,128,1024]{2,1,0:T(8,128)(2,1)S(1)} collective-permute-done((bf16[4,128,1024]{2,1,0:T(8,128)(2,1)S(1)}, bf16[4,128,1024]{2,1,0:T(8,128)(2,1)S(1)}, u32[]{:S(2)}, u32[]{:S(2)}) %collective-permute-start.7) | collective-permute-done | bytes 1048608 | tf_op jit(solution)/shard_map/ppermute | solution.py:19
  64.6 5.5 %collective-permute-start.10 = (bf16[128,1024]{1,0:T(8,128)(2,1)S(1)}, bf16[128,1024]{1,0:T(8,128)(2,1)S(1)}, u32[]{:S(2)}, u32[]{:S(2)}) collective-permute-start(bf16[128,1024]{1,0:T(8,128)(2,1)S(1)} %get-tuple-element.149), channel_id=1, source_target_pairs={{0,4},{1,5},{2,6},{3,7},{4,0},{5,1},{6,2},{7,3},{8,12},{9,13},{10,... | collective-permute-start | bytes 786440 | tf_op jit(solution)/shard_map/ppermute | solution.py:19
  70.4 2.3 collective-permute-start.9
  72.7 8.5 %shard_map.115.columns_hbm = bf16[1280,2048]{1,0:T(8,128)(2,1)S(1)} custom-call(s32[1]{0:T(128)} %bitcast.rank_ref, s32[1,2048]{1,0:T(1,128)S(1)} %bitcast.41, bf16[1280,1280]{1,0:T(8,128)(2,1)S(1)} %bitcast.39), custom_call_target="tpu_custom_call" | custom-call | flops 6710886400 | bytes 12582912 | tf_op jit(solution)/shard_map/pallas_call | solution.py:401
  81.2 2.4 collective-permute-done.10
  83.6 1.5 collective-permute-start.13
  85.1 17.1 %collective-permute-done.11 = bf16[128,1024]{1,0:T(8,128)(2,1)S(1)} collective-permute-done((bf16[128,1024]{1,0:T(8,128)(2,1)S(1)}, bf16[128,1024]{1,0:T(8,128)(2,1)S(1)}, u32[]{:S(2)}, u32[]{:S(2)}) %collective-permute-start.11) | collective-permute-done | bytes 262176 | tf_op jit(solution)/shard_map/ppermute | solution.py:19
  107.9 2.6 %shard_map.118 = (bf16[128,1024]{1,0:T(8,128)(2,1)}, bf16[128,1024]{1,0:T(8,128)(2,1)}) custom-call(s32[5]{0:T(128)S(1)} %concatenate.3.places, s32[1]{0:T(128)} %bitcast.14.turn, bf16[128,1024]{1,0:T(8,128)(2,1)} %collective-permute-done.14.own, bf16[128,1024]{1,0:T(8,128)(2,1)S(1)} %broadcast_in_dim.16.other.former_cross, f32[128,1024]{1,0:T(8,128)S(1)} %fusion.base, ...), custom_call_target="tpu_custom_call" | custom-call | flops 536870912 | bytes 4194304 | tf_op jit(solution)/shard_map/pallas_call | solution.py:257
  110.5 1.3 collective-permute-start.15
  111.8 2.0 collective-permute-start.16
  117.2 1.5 collective-permute-done.16.other
  119.7 1.9 shard_map.120
  121.6 1.4 collective-permute-start.17
  123.0 1.4 collective-permute-start.18
  128.4 1.6 collective-permute-start.19
  130.0 4.9 %collective-permute-done.19 = bf16[128,1024]{1,0:T(8,128)(2,1)S(1)} collective-permute-done((bf16[128,1024]{1,0:T(8,128)(2,1)S(1)}, bf16[128,1024]{1,0:T(8,128)(2,1)S(1)}, u32[]{:S(2)}, u32[]{:S(2)}) %collective-permute-start.19) | collective-permute-done | bytes 262176 | tf_op jit(solution)/shard_map/ppermute | solution.py:19
  135.0 2.4 collective-permute-start.21
  137.4 2.0 collective-permute-start.22
  139.4 6.7 %collective-permute-done.20.c2 = bf16[128,1024]{1,0:T(8,128)(2,1)S(1)} collective-permute-done((bf16[128,1024]{1,0:T(8,128)(2,1)S(1)}, bf16[128,1024]{1,0:T(8,128)(2,1)S(1)}, u32[]{:S(2)}, u32[]{:S(2)}) %collective-permute-start.20) | collective-permute-done | bytes 262176 | tf_op jit(solution)/shard_map/ppermute | solution.py:19
  146.1 8.9 %collective-permute-done.21.c4 = bf16[128,1024]{1,0:T(8,128)(2,1)S(1)} collective-permute-done((bf16[128,1024]{1,0:T(8,128)(2,1)S(1)}, bf16[128,1024]{1,0:T(8,128)(2,1)S(1)}, u32[]{:S(2)}, u32[]{:S(2)}) %collective-permute-start.21) | collective-permute-done | bytes 262176 | tf_op jit(solution)/shard_map/ppermute | solution.py:19
  155.0 1.5 shard_map.123
  156.5 1.5 collective-permute-start.23
  158.0 4.9 %collective-permute-done.23.cross = bf16[512,256]{1,0:T(8,128)(2,1)S(1)} collective-permute-done((bf16[512,256]{1,0:T(8,128)(2,1)S(1)}, bf16[512,256]{1,0:T(8,128)(2,1)S(1)}, u32[]{:S(2)}, u32[]{:S(2)}) %collective-permute-start.23) | collective-permute-done | bytes 262176 | tf_op jit(solution)/shard_map/ppermute | solution.py:19
  163.1 3.7 %collective-permute-start.24 = (bf16[256,128]{1,0:T(8,128)(2,1)S(1)}, bf16[256,128]{1,0:T(8,128)(2,1)S(1)}, u32[]{:S(2)}, u32[]{:S(2)}) collective-permute-start(bf16[256,128]{1,0:T(8,128)(2,1)S(1)} %get-tuple-element.139), channel_id=1, source_target_pairs={{0,2},{1,3},{2,0},{3,1},{4,6},{5,7},{6,4},{7,5},{8,10},{9,11},{10,... | collective-permute-start | bytes 196616 | tf_op jit(solution)/shard_map/ppermute | solution.py:19
  167.3 2.0 collective-permute-start.26
  169.3 1.8 shard_map.125.driven
  175.1 1.8 shard_map.127
  179.6 15.3 %collective-permute-done.29.own = bf16[1024,128]{1,0:T(8,128)(2,1)S(1)} collective-permute-done((bf16[1024,128]{1,0:T(8,128)(2,1)S(1)}, bf16[1024,128]{1,0:T(8,128)(2,1)S(1)}, u32[]{:S(2)}, u32[]{:S(2)}) %collective-permute-start.29) | collective-permute-done | bytes 262176 | tf_op jit(solution)/shard_map/ppermute | solution.py:25
  194.9 4.2 %collective-permute-done.30.other = bf16[1024,128]{1,0:T(8,128)(2,1)S(1)} collective-permute-done((bf16[1024,128]{1,0:T(8,128)(2,1)S(1)}, bf16[1024,128]{1,0:T(8,128)(2,1)S(1)}, u32[]{:S(2)}, u32[]{:S(2)}) %collective-permute-start.30) | collective-permute-done | bytes 262176 | tf_op jit(solution)/shard_map/ppermute | solution.py:25
  199.0 1.8 shard_map.128
  200.9 2.1 collective-permute-start.31
  203.0 2.0 collective-permute-start.32
  205.1 1.5 collective-permute-start.34
  206.6 1.6 collective-permute-done.32
  209.2 2.0 collective-permute-start.36
  211.2 9.0 %collective-permute-done.34.own4 = bf16[1024,128]{1,0:T(8,128)(2,1)S(1)} collective-permute-done((bf16[1024,128]{1,0:T(8,128)(2,1)S(1)}, bf16[1024,128]{1,0:T(8,128)(2,1)S(1)}, u32[]{:S(2)}, u32[]{:S(2)}) %collective-permute-start.34) | collective-permute-done | bytes 262176 | tf_op jit(solution)/shard_map/ppermute | solution.py:19
  220.3 11.1 %collective-permute-done.36.own6 = bf16[1024,128]{1,0:T(8,128)(2,1)S(1)} collective-permute-done((bf16[1024,128]{1,0:T(8,128)(2,1)S(1)}, bf16[1024,128]{1,0:T(8,128)(2,1)S(1)}, u32[]{:S(2)}, u32[]{:S(2)}) %collective-permute-start.36) | collective-permute-done | bytes 262176 | tf_op jit(solution)/shard_map/ppermute | solution.py:19
  231.4 2.2 collective-permute-done.33.near
  233.7 4.9 %collective-permute-done.37.other6 = bf16[1024,128]{1,0:T(8,128)(2,1)S(1)} collective-permute-done((bf16[1024,128]{1,0:T(8,128)(2,1)S(1)}, bf16[1024,128]{1,0:T(8,128)(2,1)S(1)}, u32[]{:S(2)}, u32[]{:S(2)}) %collective-permute-start.37) | collective-permute-done | bytes 262176 | tf_op jit(solution)/shard_map/ppermute | solution.py:19
  238.6 6.6 %shard_map.129 = (f32[256,512]{1,0:T(8,128)}, f32[1280,512]{1,0:T(8,128)}) custom-call(s32[1]{0:T(128)} %bitcast.rank_ref, f32[256,512]{1,0:T(8,128)S(1)} %get-tuple-element.133.coupling, bf16[256,2048]{1,0:T(8,128)(2,1)S(1)} %bitcast.33, f32[1280,512]{1,0:T(8,128)} %get-tuple-element.134.solved_hbm, bf16[1280,2048]{1,0:T(8,128)(2,1)} %copy-done.18, ...), custom_call_target="tpu_custom_call" | custom-call | flops 3221225472 | bytes 25165824 | tf_op jit(solution)/shard_map/pallas_call | solution.py:465
  (96 shorter events, 30.2 us)
Async XLA Ops:
  0.6 34.1 %collective-permute-start = (bf16[256,2048]{1,0:T(8,128)(2,1)}, bf16[256,2048]{1,0:T(8,128)(2,1)S(1)}, u32[]{:S(2)}, u32[]{:S(2)}) collective-permute-start(bf16[256,2048]{1,0:T(8,128)(2,1)} %bitcast.28), channel_id=1, source_target_pairs={{0,2},{1,3},{2,0},{3,1},{4,6},{5,7},{6,4},{7,5},{8,10},{9,11},{10,... | collective-permute-start | bytes 3145736 | tf_op jit(solution)/shard_map/ppermute | solution.py:19
  2.3 32.5 %collective-permute-start.1 = (bf16[256,2048]{1,0:T(8,128)(2,1)}, bf16[256,2048]{1,0:T(8,128)(2,1)S(1)}, u32[]{:S(2)}, u32[]{:S(2)}) collective-permute-start(bf16[256,2048]{1,0:T(8,128)(2,1)} %bitcast.29), channel_id=1, source_target_pairs={{2,4},{3,5},{4,2},{5,3},{10,12},{11,13},{12,10},{13,11},{18,20},{1... | collective-permute-start | bytes 3145736 | tf_op jit(solution)/shard_map/ppermute | solution.py:48
  5.0 11.9 %copy-start.10 = (f32[256,512]{1,0:T(8,128)S(1)}, f32[256,512]{1,0:T(8,128)}, u32[]{:S(2)}) copy-start(f32[256,512]{1,0:T(8,128)} %state) | copy-start | bytes 1572868
  5.0 33.4 %copy-start.8 = (bf16[1,256,2048]{2,1,0:T(8,128)(2,1)S(1)}, bf16[1,256,2048]{2,1,0:T(8,128)(2,1)}, u32[]{:S(2)}) copy-start(bf16[1,256,2048]{2,1,0:T(8,128)(2,1)} %param.10) | copy-start | bytes 3145732
  17.0 10.4 %collective-permute-start.2 = (bf16[256,128]{1,0:T(8,128)(2,1)S(1)}, bf16[256,128]{1,0:T(8,128)(2,1)S(1)}, u32[]{:S(2)}, u32[]{:S(2)}) collective-permute-start(bf16[256,128]{1,0:T(8,128)(2,1)S(1)} %get-tuple-element.83), channel_id=1, source_target_pairs={{0,2},{1,3},{2,0},{3,1},{4,6},{5,7},{6,4},{7,5},{8,10},{9,11},{10,... | collective-permute-start | bytes 196616 | tf_op jit(solution)/shard_map/ppermute | solution.py:19
  21.4 13.3 %collective-permute-start.3 = (bf16[256,128]{1,0:T(8,128)(2,1)S(1)}, bf16[256,128]{1,0:T(8,128)(2,1)S(1)}, u32[]{:S(2)}, u32[]{:S(2)}) collective-permute-start(bf16[256,128]{1,0:T(8,128)(2,1)S(1)} %get-tuple-element.84), channel_id=1, source_target_pairs={{0,4},{1,5},{2,6},{3,7},{4,0},{5,1},{6,2},{7,3},{8,12},{9,13},{10,... | collective-permute-start | bytes 196616 | tf_op jit(solution)/shard_map/ppermute | solution.py:19
  21.4 13.3 %collective-permute-start.4 = (bf16[256,128]{1,0:T(8,128)(2,1)S(1)}, bf16[256,128]{1,0:T(8,128)(2,1)S(1)}, u32[]{:S(2)}, u32[]{:S(2)}) collective-permute-start(bf16[256,128]{1,0:T(8,128)(2,1)S(1)} %get-tuple-element.85), channel_id=1, source_target_pairs={{0,6},{1,7},{2,4},{3,5},{4,2},{5,3},{6,0},{7,1},{8,14},{9,15},{10,... | collective-permute-start | bytes 196616 | tf_op jit(solution)/shard_map/ppermute | solution.py:19
  34.8 29.8 %copy-start.4 = (bf16[256,2048]{1,0:T(8,128)(2,1)}, bf16[256,2048]{1,0:T(8,128)(2,1)S(1)}, u32[]{:S(2)}) copy-start(bf16[256,2048]{1,0:T(8,128)(2,1)S(1)} %collective-permute-done.refs_1_) | copy-start | bytes 3145732
  34.8 24.9 %collective-permute-start.6 = (bf16[256,2048]{1,0:T(8,128)(2,1)S(1)}, bf16[256,2048]{1,0:T(8,128)(2,1)S(1)}, u32[]{:S(2)}, u32[]{:S(2)}) collective-permute-start(bf16[256,2048]{1,0:T(8,128)(2,1)S(1)} %collective-permute-done.1), channel_id=1, source_target_pairs={{2,0},{3,1},{4,6},{5,7},{10,8},{11,9},{12,14},{13,15},{18,16},{19,... | collective-permute-start | bytes 3145736 | tf_op jit(solution)/shard_map/ppermute | solution.py:48
  36.1 24.0 %collective-permute-start.5 = (bf16[256,2048]{1,0:T(8,128)(2,1)S(1)}, bf16[256,2048]{1,0:T(8,128)(2,1)S(1)}, u32[]{:S(2)}, u32[]{:S(2)}) collective-permute-start(bf16[256,2048]{1,0:T(8,128)(2,1)S(1)} %collective-permute-done.refs_1_), channel_id=1, source_target_pairs={{2,4},{3,5},{4,2},{5,3},{10,12},{11,13},{12,10},{13,11},{18,20},{1... | collective-permute-start | bytes 3145736 | tf_op jit(solution)/shard_map/ppermute | solution.py:48
  36.8 26.2 %collective-permute-start.7 = (bf16[4,128,1024]{2,1,0:T(8,128)(2,1)S(1)}, bf16[4,128,1024]{2,1,0:T(8,128)(2,1)S(1)}, u32[]{:S(2)}, u32[]{:S(2)}) collective-permute-start(bf16[4,128,1024]{2,1,0:T(8,128)(2,1)S(1)} %get-tuple-element.88), channel_id=1, source_target_pairs={{0,1},{1,0},{2,3},{3,2},{4,5},{5,4},{6,7},{7,6},{8,9},{9,8},{10,11... | collective-permute-start | bytes 3145736 | tf_op jit(solution)/shard_map/ppermute | solution.py:19
  38.5 34.2 %copy-start.15 = (bf16[1,1280,1280]{2,1,0:T(8,128)(2,1)S(1)}, bf16[1,1280,1280]{2,1,0:T(8,128)(2,1)}, u32[]{:S(2)}) copy-start(bf16[1,1280,1280]{2,1,0:T(8,128)(2,1)} %param.11) | copy-start | bytes 9830404
  38.5 34.2 %copy-start.17 = (s32[2048]{0:T(1024)S(1)}, s32[2048]{0:T(1024)}, u32[]{:S(2)}) copy-start(s32[2048]{0:T(1024)} %param.17) | copy-start | bytes 24580
  38.5 64.4 %collective-permute-start.12 = (bf16[256,1024]{1,0:T(8,128)(2,1)S(1)}, bf16[256,1024]{1,0:T(8,128)(2,1)S(1)}, u32[]{:S(2)}, u32[]{:S(2)}) collective-permute-start(bf16[256,1024]{1,0:T(8,128)(2,1)S(1)} %shard_map.114), channel_id=1, source_target_pairs={{0,1},{1,0},{2,3},{3,2},{4,5},{5,4},{6,7},{7,6},{8,9},{9,8},{10,11... | collective-permute-start | bytes 1572872 | tf_op jit(solution)/shard_map/ppermute | solution.py:19
  63.0 39.5 %collective-permute-start.8 = (bf16[256,2048]{1,0:T(8,128)(2,1)S(1)}, bf16[256,2048]{1,0:T(8,128)(2,1)S(1)}, u32[]{:S(2)}, u32[]{:S(2)}) collective-permute-start(bf16[256,2048]{1,0:T(8,128)(2,1)S(1)} %collective-permute-done.5), channel_id=1, source_target_pairs={{2,0},{3,1},{4,6},{5,7},{10,8},{11,9},{12,14},{13,15},{18,16},{19,... | collective-permute-start | bytes 3145736 | tf_op jit(solution)/shard_map/ppermute | solution.py:48
  64.6 19.0 %collective-permute-start.10 = (bf16[128,1024]{1,0:T(8,128)(2,1)S(1)}, bf16[128,1024]{1,0:T(8,128)(2,1)S(1)}, u32[]{:S(2)}, u32[]{:S(2)}) collective-permute-start(bf16[128,1024]{1,0:T(8,128)(2,1)S(1)} %get-tuple-element.149), channel_id=1, source_target_pairs={{0,4},{1,5},{2,6},{3,7},{4,0},{5,1},{6,2},{7,3},{8,12},{9,13},{10,... | collective-permute-start | bytes 786440 | tf_op jit(solution)/shard_map/ppermute | solution.py:19
  70.0 32.2 %collective-permute-start.11 = (bf16[128,1024]{1,0:T(8,128)(2,1)S(1)}, bf16[128,1024]{1,0:T(8,128)(2,1)S(1)}, u32[]{:S(2)}, u32[]{:S(2)}) collective-permute-start(bf16[128,1024]{1,0:T(8,128)(2,1)S(1)} %get-tuple-element.148), channel_id=1, source_target_pairs={{0,2},{1,3},{2,0},{3,1},{4,6},{5,7},{6,4},{7,5},{8,10},{9,11},{10,... | collective-permute-start | bytes 786440 | tf_op jit(solution)/shard_map/ppermute | solution.py:19
  70.4 31.9 %collective-permute-start.9 = (bf16[128,1024]{1,0:T(8,128)(2,1)S(1)}, bf16[128,1024]{1,0:T(8,128)(2,1)S(1)}, u32[]{:S(2)}, u32[]{:S(2)}) collective-permute-start(bf16[128,1024]{1,0:T(8,128)(2,1)S(1)} %get-tuple-element.147), channel_id=1, source_target_pairs={{0,6},{1,7},{2,4},{3,5},{4,2},{5,3},{6,0},{7,1},{8,14},{9,15},{10,... | collective-permute-start | bytes 786440 | tf_op jit(solution)/shard_map/ppermute | solution.py:19
  81.2 22.5 %copy-start.18 = (bf16[1280,2048]{1,0:T(8,128)(2,1)}, bf16[1280,2048]{1,0:T(8,128)(2,1)S(1)}, u32[]{:S(2)}) copy-start(bf16[1280,2048]{1,0:T(8,128)(2,1)S(1)} %shard_map.115.columns_hbm) | copy-start | bytes 15728644
  83.6 19.2 %collective-permute-start.13 = (bf16[1024,128]{1,0:T(8,128)(2,1)S(1)}, bf16[1024,128]{1,0:T(8,128)(2,1)S(1)}, u32[]{:S(2)}, u32[]{:S(2)}) collective-permute-start(bf16[1024,128]{1,0:T(8,128)(2,1)S(1)} %shard_map.116.own), channel_id=1, source_target_pairs={{0,1},{1,0},{2,3},{3,2},{4,5},{5,4},{6,7},{7,6},{8,9},{9,8},{10,11... | collective-permute-start | bytes 786440 | tf_op jit(solution)/shard_map/ppermute | solution.py:19
  103.7 4.1 %collective-permute-start.14 = (bf16[128,1024]{1,0:T(8,128)(2,1)S(1)}, bf16[128,1024]{1,0:T(8,128)(2,1)}, u32[]{:S(2)}, u32[]{:S(2)}) collective-permute-start(bf16[128,1024]{1,0:T(8,128)(2,1)S(1)} %convert_element_type.71.former_sums), channel_id=1, source_target_pairs={{24,16},{25,17},{26,18},{27,19},{28,20},{29,21},{30,22},{31,23}} | collective-permute-start | bytes 786440 | tf_op jit(solution)/shard_map/ppermute | solution.py:25
  105.1 1.2 copy-start
  110.5 6.0 %collective-permute-start.15 = (bf16[128,1024]{1,0:T(8,128)(2,1)}, bf16[128,1024]{1,0:T(8,128)(2,1)S(1)}, u32[]{:S(2)}, u32[]{:S(2)}) collective-permute-start(bf16[128,1024]{1,0:T(8,128)(2,1)} %get-tuple-element.115.former_sums), channel_id=1, source_target_pairs={{16,8},{17,9},{18,10},{19,11},{20,12},{21,13},{22,14},{23,15}} | collective-permute-start | bytes 786440 | tf_op jit(solution)/shard_map/ppermute | solution.py:25
  111.8 7.0 %collective-permute-start.16 = (bf16[128,1024]{1,0:T(8,128)(2,1)}, bf16[128,1024]{1,0:T(8,128)(2,1)}, u32[]{:S(2)}, u32[]{:S(2)}) collective-permute-start(bf16[128,1024]{1,0:T(8,128)(2,1)} %get-tuple-element.116.former_cross), channel_id=1, source_target_pairs={{16,9},{17,8},{18,11},{19,10},{20,13},{21,12},{22,15},{23,14}} | collective-permute-start | bytes 786440 | tf_op jit(solution)/shard_map/ppermute | solution.py:25
  121.6 5.5 %collective-permute-start.17 = (bf16[128,1024]{1,0:T(8,128)(2,1)S(1)}, bf16[128,1024]{1,0:T(8,128)(2,1)}, u32[]{:S(2)}, u32[]{:S(2)}) collective-permute-start(bf16[128,1024]{1,0:T(8,128)(2,1)S(1)} %get-tuple-element.123.former_sums), channel_id=1, source_target_pairs={{8,0},{9,1},{10,2},{11,3},{12,4},{13,5},{14,6},{15,7}} | collective-permute-start | bytes 786440 | tf_op jit(solution)/shard_map/ppermute | solution.py:25
  123.0 4.1 %collective-permute-start.18 = (bf16[128,1024]{1,0:T(8,128)(2,1)}, bf16[128,1024]{1,0:T(8,128)(2,1)}, u32[]{:S(2)}, u32[]{:S(2)}) collective-permute-start(bf16[128,1024]{1,0:T(8,128)(2,1)} %get-tuple-element.124.former_cross), channel_id=1, source_target_pairs={{8,1},{9,0},{10,3},{11,2},{12,5},{13,4},{14,7},{15,6}} | collective-permute-start | bytes 786440 | tf_op jit(solution)/shard_map/ppermute | solution.py:25
  127.1 27.9 %copy-start.9 = (bf16[1,256,2048]{2,1,0:T(8,128)(2,1)S(1)}, bf16[1,256,2048]{2,1,0:T(8,128)(2,1)}, u32[]{:S(2)}) copy-start(bf16[1,256,2048]{2,1,0:T(8,128)(2,1)} %param.10) | copy-start | bytes 3145732
  127.1 27.9 %copy-start.12 = (bf16[256,1024]{1,0:T(8,128)(2,1)S(1)}, bf16[256,1024]{1,0:T(8,128)(2,1)}, u32[]{:S(2)}) copy-start(bf16[256,1024]{1,0:T(8,128)(2,1)} %copy-done.11) | copy-start | bytes 1572868
  128.4 6.5 %collective-permute-start.19 = (bf16[128,1024]{1,0:T(8,128)(2,1)S(1)}, bf16[128,1024]{1,0:T(8,128)(2,1)S(1)}, u32[]{:S(2)}, u32[]{:S(2)}) collective-permute-start(bf16[128,1024]{1,0:T(8,128)(2,1)S(1)} %get-tuple-element.130), channel_id=1, source_target_pairs={{0,1},{1,0},{2,3},{3,2},{4,5},{5,4},{6,7},{7,6},{8,9},{9,8},{10,11... | collective-permute-start | bytes 786440 | tf_op jit(solution)/shard_map/ppermute | solution.py:19
  134.9 11.1 %collective-permute-start.20 = (bf16[128,1024]{1,0:T(8,128)(2,1)S(1)}, bf16[128,1024]{1,0:T(8,128)(2,1)S(1)}, u32[]{:S(2)}, u32[]{:S(2)}) collective-permute-start(bf16[128,1024]{1,0:T(8,128)(2,1)S(1)} %add_convert_fusion.c0), channel_id=1, source_target_pairs={{0,2},{1,3},{2,0},{3,1},{4,6},{5,7},{6,4},{7,5},{8,10},{9,11},{10,... | collective-permute-start | bytes 786440 | tf_op jit(solution)/shard_map/ppermute | solution.py:19
  135.0 20.0 %collective-permute-start.21 = (bf16[128,1024]{1,0:T(8,128)(2,1)S(1)}, bf16[128,1024]{1,0:T(8,128)(2,1)S(1)}, u32[]{:S(2)}, u32[]{:S(2)}) collective-permute-start(bf16[128,1024]{1,0:T(8,128)(2,1)S(1)} %add_convert_fusion.c0), channel_id=1, source_target_pairs={{0,4},{1,5},{2,6},{3,7},{4,0},{5,1},{6,2},{7,3},{8,12},{9,13},{10,... | collective-permute-start | bytes 786440 | tf_op jit(solution)/shard_map/ppermute | solution.py:19
  137.4 17.6 %collective-permute-start.22 = (bf16[128,1024]{1,0:T(8,128)(2,1)S(1)}, bf16[128,1024]{1,0:T(8,128)(2,1)S(1)}, u32[]{:S(2)}, u32[]{:S(2)}) collective-permute-start(bf16[128,1024]{1,0:T(8,128)(2,1)S(1)} %add_convert_fusion.c0), channel_id=1, source_target_pairs={{0,6},{1,7},{2,4},{3,5},{4,2},{5,3},{6,0},{7,1},{8,14},{9,15},{10,... | collective-permute-start | bytes 786440 | tf_op jit(solution)/shard_map/ppermute | solution.py:19
  156.5 6.4 %collective-permute-start.23 = (bf16[512,256]{1,0:T(8,128)(2,1)S(1)}, bf16[512,256]{1,0:T(8,128)(2,1)S(1)}, u32[]{:S(2)}, u32[]{:S(2)}) collective-permute-start(bf16[512,256]{1,0:T(8,128)(2,1)S(1)} %get-tuple-element.132), channel_id=1, source_target_pairs={{0,1},{1,0},{2,3},{3,2},{4,5},{5,4},{6,7},{7,6},{8,9},{9,8},{10,11... | collective-permute-start | bytes 786440 | tf_op jit(solution)/shard_map/ppermute | solution.py:19
  163.1 8.0 %collective-permute-start.24 = (bf16[256,128]{1,0:T(8,128)(2,1)S(1)}, bf16[256,128]{1,0:T(8,128)(2,1)S(1)}, u32[]{:S(2)}, u32[]{:S(2)}) collective-permute-start(bf16[256,128]{1,0:T(8,128)(2,1)S(1)} %get-tuple-element.139), channel_id=1, source_target_pairs={{0,2},{1,3},{2,0},{3,1},{4,6},{5,7},{6,4},{7,5},{8,10},{9,11},{10,... | collective-permute-start | bytes 196616 | tf_op jit(solution)/shard_map/ppermute | solution.py:19
  166.9 5.5 %collective-permute-start.25 = (bf16[256,128]{1,0:T(8,128)(2,1)S(1)}, bf16[256,128]{1,0:T(8,128)(2,1)S(1)}, u32[]{:S(2)}, u32[]{:S(2)}) collective-permute-start(bf16[256,128]{1,0:T(8,128)(2,1)S(1)} %get-tuple-element.140), channel_id=1, source_target_pairs={{0,4},{1,5},{2,6},{3,7},{4,0},{5,1},{6,2},{7,3},{8,12},{9,13},{10,... | collective-permute-start | bytes 196616 | tf_op jit(solution)/shard_map/ppermute | solution.py:19
  167.3 6.2 %collective-permute-start.26 = (bf16[256,128]{1,0:T(8,128)(2,1)S(1)}, bf16[256,128]{1,0:T(8,128)(2,1)S(1)}, u32[]{:S(2)}, u32[]{:S(2)}) collective-permute-start(bf16[256,128]{1,0:T(8,128)(2,1)S(1)} %get-tuple-element.141), channel_id=1, source_target_pairs={{0,6},{1,7},{2,4},{3,5},{4,2},{5,3},{6,0},{7,1},{8,14},{9,15},{10,... | collective-permute-start | bytes 196616 | tf_op jit(solution)/shard_map/ppermute | solution.py:19
  173.6 1.6 collective-permute-start.27
  174.2 0.9 collective-permute-start.28
  177.0 17.9 %collective-permute-start.29 = (bf16[1024,128]{1,0:T(8,128)(2,1)S(1)}, bf16[1024,128]{1,0:T(8,128)(2,1)S(1)}, u32[]{:S(2)}, u32[]{:S(2)}) collective-permute-start(bf16[1024,128]{1,0:T(8,128)(2,1)S(1)} %shard_map.127), channel_id=1, source_target_pairs={{8,16},{9,17},{10,18},{11,19},{12,20},{13,21},{14,22},{15,23}} | collective-permute-start | bytes 786440 | tf_op jit(solution)/shard_map/ppermute | solution.py:25
  178.3 20.8 %collective-permute-start.30 = (bf16[1024,128]{1,0:T(8,128)(2,1)S(1)}, bf16[1024,128]{1,0:T(8,128)(2,1)S(1)}, u32[]{:S(2)}, u32[]{:S(2)}) collective-permute-start(bf16[1024,128]{1,0:T(8,128)(2,1)S(1)} %shard_map.127), channel_id=1, source_target_pairs={{8,17},{9,16},{10,19},{11,18},{12,21},{13,20},{14,23},{15,22}} | collective-permute-start | bytes 786440 | tf_op jit(solution)/shard_map/ppermute | solution.py:25
  200.9 37.7 %copy-start.3 = (bf16[1,256,2048]{2,1,0:T(8,128)(2,1)S(1)}, bf16[1,256,2048]{2,1,0:T(8,128)(2,1)}, u32[]{:S(2)}) copy-start(bf16[1,256,2048]{2,1,0:T(8,128)(2,1)} %param.9) | copy-start | bytes 3145732
  200.9 4.2 %collective-permute-start.31 = (bf16[1024,128]{1,0:T(8,128)(2,1)S(1)}, bf16[1024,128]{1,0:T(8,128)(2,1)}, u32[]{:S(2)}, u32[]{:S(2)}) collective-permute-start(bf16[1024,128]{1,0:T(8,128)(2,1)S(1)} %shard_map.128), channel_id=1, source_target_pairs={{16,24},{17,25},{18,26},{19,27},{20,28},{21,29},{22,30},{23,31}} | collective-permute-start | bytes 786440 | tf_op jit(solution)/shard_map/ppermute | solution.py:25
  203.0 5.2 %collective-permute-start.32 = (bf16[1024,128]{1,0:T(8,128)(2,1)S(1)}, bf16[1024,128]{1,0:T(8,128)(2,1)}, u32[]{:S(2)}, u32[]{:S(2)}) collective-permute-start(bf16[1024,128]{1,0:T(8,128)(2,1)S(1)} %shard_map.128), channel_id=1, source_target_pairs={{16,25},{17,24},{18,27},{19,26},{20,29},{21,28},{22,31},{23,30}} | collective-permute-start | bytes 786440 | tf_op jit(solution)/shard_map/ppermute | solution.py:25
  205.1 15.1 %collective-permute-start.34 = (bf16[1024,128]{1,0:T(8,128)(2,1)S(1)}, bf16[1024,128]{1,0:T(8,128)(2,1)S(1)}, u32[]{:S(2)}, u32[]{:S(2)}) collective-permute-start(bf16[1024,128]{1,0:T(8,128)(2,1)S(1)} %select_select_fusion.1.own), channel_id=1, source_target_pairs={{0,4},{1,5},{2,6},{3,7},{4,0},{5,1},{6,2},{7,3},{8,12},{9,13},{10,... | collective-permute-start | bytes 786440 | tf_op jit(solution)/shard_map/ppermute | solution.py:19
  208.3 25.3 %collective-permute-start.33 = (bf16[2,1024,128]{2,1,0:T(8,128)(2,1)S(1)}, bf16[2,1024,128]{2,1,0:T(8,128)(2,1)S(1)}, u32[]{:S(2)}, u32[]{:S(2)}) collective-permute-start(bf16[2,1024,128]{2,1,0:T(8,128)(2,1)S(1)} %pad_maximum_fusion), channel_id=1, source_target_pairs={{0,2},{1,3},{2,0},{3,1},{4,6},{5,7},{6,4},{7,5},{8,10},{9,11},{10,... | collective-permute-start | bytes 1572872 | tf_op jit(solution)/shard_map/ppermute | solution.py:19
  209.2 22.2 %collective-permute-start.36 = (bf16[1024,128]{1,0:T(8,128)(2,1)S(1)}, bf16[1024,128]{1,0:T(8,128)(2,1)S(1)}, u32[]{:S(2)}, u32[]{:S(2)}) collective-permute-start(bf16[1024,128]{1,0:T(8,128)(2,1)S(1)} %select_select_fusion.1.own), channel_id=1, source_target_pairs={{0,6},{1,7},{2,4},{3,5},{4,2},{5,3},{6,0},{7,1},{8,14},{9,15},{10,... | collective-permute-start | bytes 786440 | tf_op jit(solution)/shard_map/ppermute | solution.py:19
  220.2 13.5 %collective-permute-start.35 = (bf16[1024,128]{1,0:T(8,128)(2,1)S(1)}, bf16[1024,128]{1,0:T(8,128)(2,1)S(1)}, u32[]{:S(2)}, u32[]{:S(2)}) collective-permute-start(bf16[1024,128]{1,0:T(8,128)(2,1)S(1)} %collective-permute-done.34.own4), channel_id=1, source_target_pairs={{0,1},{1,0},{2,3},{3,2},{4,5},{5,4},{6,7},{7,6},{8,9},{9,8},{10,11... | collective-permute-start | bytes 786440 | tf_op jit(solution)/shard_map/ppermute | solution.py:19
  231.4 7.1 %collective-permute-start.37 = (bf16[1024,128]{1,0:T(8,128)(2,1)S(1)}, bf16[1024,128]{1,0:T(8,128)(2,1)S(1)}, u32[]{:S(2)}, u32[]{:S(2)}) collective-permute-start(bf16[1024,128]{1,0:T(8,128)(2,1)S(1)} %collective-permute-done.36.own6), channel_id=1, source_target_pairs={{0,1},{1,0},{2,3},{3,2},{4,5},{5,4},{6,7},{7,6},{8,9},{9,8},{10,11... | collective-permute-start | bytes 786440 | tf_op jit(solution)/shard_map/ppermute | solution.py:19
  (9 other events, 9.6 us)

commit v6 on v5

--- a/solution.py
+++ b/solution.py
@@ -504,17 +504,33 @@
     )
     there = bus_send(send, 1, everyone)
     start = join(rank, pieces)
-    middle2, third, there = together(
-        across(near, everyone), middle + outwards(middle, everyone), there
+    middle2, third, there, columns = together(
+        across(near, everyone),
+        middle + outwards(middle, everyone),
+        there,
+        picked(rank, unit_bus, inverse),
     )
     fourth = middle2 + outwards(middle2, everyone)
     schur_y = bus_send(schur_cross(rank, schur_in), 1, everyone)
-    unit_right = None
-    for turn, flip in ((3, 6), (2, 4), (1, 2), (0, 0)):
-        here = keep[turn] + there[turn].astype(F32)
-        if flip:
-            here = bus_send(here.astype(BF16), flip, everyone).astype(F32)
-        unit_right = here if unit_right is None else unit_right + here
+    terms = [mine + theirs.astype(F32) for mine, theirs in zip(keep, there, strict=True)]
+    sent = [term.astype(BF16) for term in terms]
+    start_y, fourth, from_end, from_middle, from_far = together(
+        bus_send(start, 1, everyone),
+        fourth,
+        line_send(sent[1], ((0, 1), (3, 2)), everyone),
+        across(jnp.stack([sent[3], sent[2]]), everyone),
+        line_send(jnp.stack([sent[2], sent[3]]), ((0, 2), (3, 1)), everyone),
+    )
+    passed = outwards(
+        (terms[1] + from_middle[1].astype(F32) + from_far[1].astype(F32)).astype(BF16), everyone
+    )
+    unit_right = (
+        terms[0]
+        + from_middle[0].astype(F32)
+        + from_far[0].astype(F32)
+        + from_end.astype(F32)
+        + passed.astype(F32)
+    )
     gain, near, third, fourth, unit_right, schur_y, columns, start, start_y = together(
         gain,
         near,
@@ -522,9 +538,9 @@
         fourth,
         unit_right,
         schur_y,
-        picked(rank, unit_bus, inverse),
+        columns,
         start,
-        bus_send(start, 1, everyone),
+        start_y,
     )
 
     sums, cross = unit_right.astype(BF16), jnp.zeros(unit_right.shape, BF16)

time: 246 us -> 245 us (level)
  waiting for transfers between devices: 131 us -> 121 us
  starting transfers between devices: 58.2 us -> 66.7 us
    ppermute x23 -> x20, waiting for transfers between devices: 88.1 us -> 68.1 us  [bus_send(): return lax.ppermute(block, BOTH, route)]
    ppermute x4 -> x8, starting transfers between devices: 4.02 us -> 16.6 us  [line_send(): return lax.ppermute(block, BOTH, route)]
    ppermute x4 -> x8, waiting for transfers between devices: 20.6 us -> 29.9 us  [line_send(): return lax.ppermute(block, BOTH, route)]
    ppermute x23 -> x20, starting transfers between devices: 38.5 us -> 34.6 us  [bus_send(): return lax.ppermute(block, BOTH, route)]
  transfers between devices with their start and end apart: 38 -> 39, of which waited for: 20 -> 20; matrix products, arithmetic and copies ran while one was open for 1% -> 1% of each run, Pallas kernels for 9% -> 10%
where the time goes in v6:
time: 245 us; the launch traced here: 244 us
  waiting for transfers between devices  121 us (49%)
  starting transfers between devices  66.7 us (27%)
  Pallas kernels  41.3 us (17%)
  local copies, waits for them, and re-layouts  11.9 us (5%)
    ppermute x20, waiting for transfers between devices, bus_send(): return lax.ppermute(block, BOTH, route)  68.1 us
    ppermute x20, starting transfers between devices, bus_send(): return lax.ppermute(block, BOTH, route)  34.6 us
    ppermute x8, waiting for transfers between devices, line_send(): return lax.ppermute(block, BOTH, route)  29.9 us
    ppermute x11, waiting for transfers between devices, period_send(): return lax.ppermute(block, BOTH, route)  22.8 us
    ppermute x8, starting transfers between devices, line_send(): return lax.ppermute(block, BOTH, route)  16.6 us
    ppermute x11, starting transfers between devices, period_send(): return lax.ppermute(block, BOTH, route)  15.4 us
    pallas_call x1, Pallas kernels, front(): kernel_call(front_kernel, [keep] * 4 + [send, jax.ShapeDtypeStruct((buses...  12 us
    unnamed x38, local copies, waits for them, and re-layouts  10.9 us
  transfers between devices with their start and end apart: 39, of which 20 were waited for; matrix products, arithmetic and copies ran while one was open for 1% of the time, Pallas kernels for 10%

profile of v6, /device:TPU:2, one launch (start us, length us, event | category | flops | bytes accessed | tf_op | source)
XLA Modules:
  0.0 243.8 jit_solution(12032653250065246244)
XLA Ops:
  0.6 1.6 collective-permute-start
  5.0 12.0 %shard_map.112 = (f32[128,1024]{1,0:T(8,128)S(1)}, f32[128,1024]{1,0:T(8,128)S(1)}, f32[128,1024]{1,0:T(8,128)S(1)}, f32[128,1024]{1,0:T(8,128)S(1)}, bf16[4,128...) custom-call(s32[1]{0:T(128)} %bitcast.rank_ref, s32[1280,1]{1,0:T(8,128)S(1)} %copy.12.active, f32[256,512]{1,0:T(8,128)S(1)} %bitcast.57, ...), custom_call_target="tpu_custom_call" | custom-call | flops 4362076160 | bytes 25165824 | tf_op jit(solution)/shard_map/pallas_call | solution.py:142
  17.1 4.4 %collective-permute-start.2 = (bf16[256,128]{1,0:T(8,128)(2,1)S(1)}, bf16[256,128]{1,0:T(8,128)(2,1)S(1)}, u32[]{:S(2)}, u32[]{:S(2)}) collective-permute-start(bf16[256,128]{1,0:T(8,128)(2,1)S(1)} %get-tuple-element.89), channel_id=1, source_target_pairs={{0,2},{1,3},{2,0},{3,1},{4,6},{5,7},{6,4},{7,5},{8,10},{9,11},{10,... | collective-permute-start | bytes 196616 | tf_op jit(solution)/shard_map/ppermute | solution.py:19
  21.5 2.4 collective-permute-start.4
  23.9 3.5 %collective-permute-done.2.p2 = bf16[256,128]{1,0:T(8,128)(2,1)S(1)} collective-permute-done((bf16[256,128]{1,0:T(8,128)(2,1)S(1)}, bf16[256,128]{1,0:T(8,128)(2,1)S(1)}, u32[]{:S(2)}, u32[]{:S(2)}) %collective-permute-start.2) | collective-permute-done | bytes 65568 | tf_op jit(solution)/shard_map/ppermute | solution.py:19
  27.5 7.3 %collective-permute-done.3.p4 = bf16[256,128]{1,0:T(8,128)(2,1)S(1)} collective-permute-done((bf16[256,128]{1,0:T(8,128)(2,1)S(1)}, bf16[256,128]{1,0:T(8,128)(2,1)S(1)}, u32[]{:S(2)}, u32[]{:S(2)}) %collective-permute-start.3) | collective-permute-done | bytes 65568 | tf_op jit(solution)/shard_map/ppermute | solution.py:19
  36.8 1.6 collective-permute-start.7
  38.4 8.5 %shard_map.114.columns_hbm = bf16[1280,2048]{1,0:T(8,128)(2,1)S(1)} custom-call(s32[1]{0:T(128)} %bitcast.rank_ref, s32[1,2048]{1,0:T(1,128)S(1)} %bitcast.58, bf16[1280,1280]{1,0:T(8,128)(2,1)S(1)} %bitcast.56), custom_call_target="tpu_custom_call" | custom-call | flops 6710886400 | bytes 12582912 | tf_op jit(solution)/shard_map/pallas_call | solution.py:401
  46.9 12.8 %collective-permute-done.6 = bf16[256,2048]{1,0:T(8,128)(2,1)S(1)} collective-permute-done((bf16[256,2048]{1,0:T(8,128)(2,1)S(1)}, bf16[256,2048]{1,0:T(8,128)(2,1)S(1)}, u32[]{:S(2)}, u32[]{:S(2)}) %collective-permute-start.6) | collective-permute-done | bytes 1048608 | tf_op jit(solution)/shard_map/ppermute | solution.py:48
  62.6 9.2 %collective-permute-start.12 = (bf16[2,128,1024]{2,1,0:T(8,128)(2,1)S(1)}, bf16[2,128,1024]{2,1,0:T(8,128)(2,1)S(1)}, u32[]{:S(2)}, u32[]{:S(2)}) collective-permute-start(bf16[2,128,1024]{2,1,0:T(8,128)(2,1)S(1)} %get-tuple-element.162), channel_id=1, source_target_pairs={{0,4},{1,5},{6,2},{7,3},{8,12},{9,13},{14,10},{15,11},{16,20},{17,... | collective-permute-start | bytes 1572872 | tf_op jit(solution)/shard_map/ppermute | solution.py:48
  71.9 1.6 collective-permute-start.8
  73.5 1.3 collective-permute-start.10
  74.8 10.6 %collective-permute-done.9 = bf16[256,2048]{1,0:T(8,128)(2,1)S(1)} collective-permute-done((bf16[256,2048]{1,0:T(8,128)(2,1)S(1)}, bf16[256,2048]{1,0:T(8,128)(2,1)S(1)}, u32[]{:S(2)}, u32[]{:S(2)}) %collective-permute-start.9) | collective-permute-done | bytes 1048608 | tf_op jit(solution)/shard_map/ppermute | solution.py:48
  87.4 1.6 collective-permute-start.14
  89.0 6.4 %collective-permute-done.13 = bf16[128,1024]{1,0:T(8,128)(2,1)S(1)} collective-permute-done((bf16[128,1024]{1,0:T(8,128)(2,1)S(1)}, bf16[128,1024]{1,0:T(8,128)(2,1)S(1)}, u32[]{:S(2)}, u32[]{:S(2)}) %collective-permute-start.13) | collective-permute-done | bytes 262176 | tf_op jit(solution)/shard_map/ppermute | solution.py:48
  101.8 2.6 %shard_map.118 = (bf16[128,1024]{1,0:T(8,128)(2,1)}, bf16[128,1024]{1,0:T(8,128)(2,1)}) custom-call(s32[5]{0:T(128)S(1)} %concatenate.3.places, s32[1]{0:T(128)} %bitcast.20.turn, bf16[128,1024]{1,0:T(8,128)(2,1)} %collective-permute-done.15.own, bf16[128,1024]{1,0:T(8,128)(2,1)S(1)} %broadcast_in_dim.16.other.former_cross, f32[128,1024]{1,0:T(8,128)S(1)} %fusion.2.base, ...), custom_call_target="tpu_custom_call" | custom-call | flops 536870912 | bytes 4194304 | tf_op jit(solution)/shard_map/pallas_call | solution.py:257
  105.8 2.0 collective-permute-start.17
  111.2 1.6 collective-permute-done.17.other
  113.7 1.9 shard_map.120
  115.5 1.4 collective-permute-start.18
  116.9 1.4 collective-permute-start.19
  121.0 1.5 shard_map.122
  122.5 1.6 collective-permute-start.20
  124.1 4.9 %collective-permute-done.20 = bf16[128,1024]{1,0:T(8,128)(2,1)S(1)} collective-permute-done((bf16[128,1024]{1,0:T(8,128)(2,1)S(1)}, bf16[128,1024]{1,0:T(8,128)(2,1)S(1)}, u32[]{:S(2)}, u32[]{:S(2)}) %collective-permute-start.20) | collective-permute-done | bytes 262176 | tf_op jit(solution)/shard_map/ppermute | solution.py:19
  129.0 4.8 %collective-permute-start.21 = (bf16[128,1024]{1,0:T(8,128)(2,1)S(1)}, bf16[128,1024]{1,0:T(8,128)(2,1)S(1)}, u32[]{:S(2)}, u32[]{:S(2)}) collective-permute-start(bf16[128,1024]{1,0:T(8,128)(2,1)S(1)} %add_convert_fusion.c0), channel_id=1, source_target_pairs={{0,2},{1,3},{2,0},{3,1},{4,6},{5,7},{6,4},{7,5},{8,10},{9,11},{10,... | collective-permute-start | bytes 786440 | tf_op jit(solution)/shard_map/ppermute | solution.py:19
  134.1 2.2 collective-permute-start.23
  136.3 5.1 %collective-permute-done.21.c2 = bf16[128,1024]{1,0:T(8,128)(2,1)S(1)} collective-permute-done((bf16[128,1024]{1,0:T(8,128)(2,1)S(1)}, bf16[128,1024]{1,0:T(8,128)(2,1)S(1)}, u32[]{:S(2)}, u32[]{:S(2)}) %collective-permute-start.21) | collective-permute-done | bytes 262176 | tf_op jit(solution)/shard_map/ppermute | solution.py:19
  141.4 12.1 %collective-permute-done.22.c4 = bf16[128,1024]{1,0:T(8,128)(2,1)S(1)} collective-permute-done((bf16[128,1024]{1,0:T(8,128)(2,1)S(1)}, bf16[128,1024]{1,0:T(8,128)(2,1)S(1)}, u32[]{:S(2)}, u32[]{:S(2)}) %collective-permute-start.22) | collective-permute-done | bytes 262176 | tf_op jit(solution)/shard_map/ppermute | solution.py:19
  153.5 1.5 shard_map.123
  155.0 1.5 collective-permute-start.24
  156.5 4.9 %collective-permute-done.24.cross = bf16[512,256]{1,0:T(8,128)(2,1)S(1)} collective-permute-done((bf16[512,256]{1,0:T(8,128)(2,1)S(1)}, bf16[512,256]{1,0:T(8,128)(2,1)S(1)}, u32[]{:S(2)}, u32[]{:S(2)}) %collective-permute-start.24) | collective-permute-done | bytes 262176 | tf_op jit(solution)/shard_map/ppermute | solution.py:19
  161.6 3.8 %collective-permute-start.25 = (bf16[256,128]{1,0:T(8,128)(2,1)S(1)}, bf16[256,128]{1,0:T(8,128)(2,1)S(1)}, u32[]{:S(2)}, u32[]{:S(2)}) collective-permute-start(bf16[256,128]{1,0:T(8,128)(2,1)S(1)} %get-tuple-element.151), channel_id=1, source_target_pairs={{0,2},{1,3},{2,0},{3,1},{4,6},{5,7},{6,4},{7,5},{8,10},{9,11},{10,... | collective-permute-start | bytes 196616 | tf_op jit(solution)/shard_map/ppermute | solution.py:19
  165.7 2.2 collective-permute-start.27
  167.8 1.8 shard_map.125.driven
  173.3 1.8 shard_map.127
  177.7 15.5 %collective-permute-done.30.own = bf16[1024,128]{1,0:T(8,128)(2,1)S(1)} collective-permute-done((bf16[1024,128]{1,0:T(8,128)(2,1)S(1)}, bf16[1024,128]{1,0:T(8,128)(2,1)S(1)}, u32[]{:S(2)}, u32[]{:S(2)}) %collective-permute-start.30) | collective-permute-done | bytes 262176 | tf_op jit(solution)/shard_map/ppermute | solution.py:25
  193.3 4.2 %collective-permute-done.31.other = bf16[1024,128]{1,0:T(8,128)(2,1)S(1)} collective-permute-done((bf16[1024,128]{1,0:T(8,128)(2,1)S(1)}, bf16[1024,128]{1,0:T(8,128)(2,1)S(1)}, u32[]{:S(2)}, u32[]{:S(2)}) %collective-permute-start.31) | collective-permute-done | bytes 262176 | tf_op jit(solution)/shard_map/ppermute | solution.py:25
  197.4 1.8 shard_map.128
  199.3 2.2 collective-permute-start.32
  201.5 2.0 collective-permute-start.33
  203.5 1.6 collective-permute-start.35
  205.1 1.5 collective-permute-done.33
  207.7 2.1 collective-permute-start.37
  209.8 8.9 %collective-permute-done.35.own4 = bf16[1024,128]{1,0:T(8,128)(2,1)S(1)} collective-permute-done((bf16[1024,128]{1,0:T(8,128)(2,1)S(1)}, bf16[1024,128]{1,0:T(8,128)(2,1)S(1)}, u32[]{:S(2)}, u32[]{:S(2)}) %collective-permute-start.35) | collective-permute-done | bytes 262176 | tf_op jit(solution)/shard_map/ppermute | solution.py:19
  218.8 11.1 %collective-permute-done.37.own6 = bf16[1024,128]{1,0:T(8,128)(2,1)S(1)} collective-permute-done((bf16[1024,128]{1,0:T(8,128)(2,1)S(1)}, bf16[1024,128]{1,0:T(8,128)(2,1)S(1)}, u32[]{:S(2)}, u32[]{:S(2)}) %collective-permute-start.37) | collective-permute-done | bytes 262176 | tf_op jit(solution)/shard_map/ppermute | solution.py:19
  229.9 2.1 collective-permute-done.34.near
  232.0 5.0 %collective-permute-done.38.other6 = bf16[1024,128]{1,0:T(8,128)(2,1)S(1)} collective-permute-done((bf16[1024,128]{1,0:T(8,128)(2,1)S(1)}, bf16[1024,128]{1,0:T(8,128)(2,1)S(1)}, u32[]{:S(2)}, u32[]{:S(2)}) %collective-permute-start.38) | collective-permute-done | bytes 262176 | tf_op jit(solution)/shard_map/ppermute | solution.py:19
  237.0 6.6 %shard_map.129 = (f32[256,512]{1,0:T(8,128)}, f32[1280,512]{1,0:T(8,128)}) custom-call(s32[1]{0:T(128)} %bitcast.rank_ref, f32[256,512]{1,0:T(8,128)S(1)} %get-tuple-element.145.coupling, bf16[256,2048]{1,0:T(8,128)(2,1)S(1)} %bitcast.50, f32[1280,512]{1,0:T(8,128)} %get-tuple-element.146.solved_hbm, bf16[1280,2048]{1,0:T(8,128)(2,1)} %copy-done.18, ...), custom_call_target="tpu_custom_call" | custom-call | flops 3221225472 | bytes 25165824 | tf_op jit(solution)/shard_map/pallas_call | solution.py:465
  (100 shorter events, 32.6 us)
Async XLA Ops:
  0.6 34.1 %collective-permute-start = (bf16[256,2048]{1,0:T(8,128)(2,1)}, bf16[256,2048]{1,0:T(8,128)(2,1)S(1)}, u32[]{:S(2)}, u32[]{:S(2)}) collective-permute-start(bf16[256,2048]{1,0:T(8,128)(2,1)} %bitcast.45), channel_id=1, source_target_pairs={{0,2},{1,3},{2,0},{3,1},{4,6},{5,7},{6,4},{7,5},{8,10},{9,11},{10,... | collective-permute-start | bytes 3145736 | tf_op jit(solution)/shard_map/ppermute | solution.py:19
  2.3 32.5 %collective-permute-start.1 = (bf16[256,2048]{1,0:T(8,128)(2,1)}, bf16[256,2048]{1,0:T(8,128)(2,1)S(1)}, u32[]{:S(2)}, u32[]{:S(2)}) collective-permute-start(bf16[256,2048]{1,0:T(8,128)(2,1)} %bitcast.46), channel_id=1, source_target_pairs={{2,4},{3,5},{4,2},{5,3},{10,12},{11,13},{12,10},{13,11},{18,20},{1... | collective-permute-start | bytes 3145736 | tf_op jit(solution)/shard_map/ppermute | solution.py:48
  5.0 12.0 %copy-start.10 = (f32[256,512]{1,0:T(8,128)S(1)}, f32[256,512]{1,0:T(8,128)}, u32[]{:S(2)}) copy-start(f32[256,512]{1,0:T(8,128)} %state) | copy-start | bytes 1572868
  5.0 33.4 %copy-start.15 = (bf16[1,1280,1280]{2,1,0:T(8,128)(2,1)S(1)}, bf16[1,1280,1280]{2,1,0:T(8,128)(2,1)}, u32[]{:S(2)}) copy-start(bf16[1,1280,1280]{2,1,0:T(8,128)(2,1)} %param.11) | copy-start | bytes 9830404
  5.0 33.4 %copy-start.17 = (s32[2048]{0:T(1024)S(1)}, s32[2048]{0:T(1024)}, u32[]{:S(2)}) copy-start(s32[2048]{0:T(1024)} %param.17) | copy-start | bytes 24580
  17.1 10.4 %collective-permute-start.2 = (bf16[256,128]{1,0:T(8,128)(2,1)S(1)}, bf16[256,128]{1,0:T(8,128)(2,1)S(1)}, u32[]{:S(2)}, u32[]{:S(2)}) collective-permute-start(bf16[256,128]{1,0:T(8,128)(2,1)S(1)} %get-tuple-element.89), channel_id=1, source_target_pairs={{0,2},{1,3},{2,0},{3,1},{4,6},{5,7},{6,4},{7,5},{8,10},{9,11},{10,... | collective-permute-start | bytes 196616 | tf_op jit(solution)/shard_map/ppermute | solution.py:19
  21.5 13.3 %collective-permute-start.3 = (bf16[256,128]{1,0:T(8,128)(2,1)S(1)}, bf16[256,128]{1,0:T(8,128)(2,1)S(1)}, u32[]{:S(2)}, u32[]{:S(2)}) collective-permute-start(bf16[256,128]{1,0:T(8,128)(2,1)S(1)} %get-tuple-element.90), channel_id=1, source_target_pairs={{0,4},{1,5},{2,6},{3,7},{4,0},{5,1},{6,2},{7,3},{8,12},{9,13},{10,... | collective-permute-start | bytes 196616 | tf_op jit(solution)/shard_map/ppermute | solution.py:19
  21.5 13.3 %collective-permute-start.4 = (bf16[256,128]{1,0:T(8,128)(2,1)S(1)}, bf16[256,128]{1,0:T(8,128)(2,1)S(1)}, u32[]{:S(2)}, u32[]{:S(2)}) collective-permute-start(bf16[256,128]{1,0:T(8,128)(2,1)S(1)} %get-tuple-element.91), channel_id=1, source_target_pairs={{0,6},{1,7},{2,4},{3,5},{4,2},{5,3},{6,0},{7,1},{8,14},{9,15},{10,... | collective-permute-start | bytes 196616 | tf_op jit(solution)/shard_map/ppermute | solution.py:19
  34.8 12.1 %copy-start.4 = (bf16[256,2048]{1,0:T(8,128)(2,1)}, bf16[256,2048]{1,0:T(8,128)(2,1)S(1)}, u32[]{:S(2)}) copy-start(bf16[256,2048]{1,0:T(8,128)(2,1)S(1)} %collective-permute-done.refs_1_) | copy-start | bytes 3145732
  34.8 24.9 %collective-permute-start.6 = (bf16[256,2048]{1,0:T(8,128)(2,1)S(1)}, bf16[256,2048]{1,0:T(8,128)(2,1)S(1)}, u32[]{:S(2)}, u32[]{:S(2)}) collective-permute-start(bf16[256,2048]{1,0:T(8,128)(2,1)S(1)} %collective-permute-done.1), channel_id=1, source_target_pairs={{2,0},{3,1},{4,6},{5,7},{10,8},{11,9},{12,14},{13,15},{18,16},{19,... | collective-permute-start | bytes 3145736 | tf_op jit(solution)/shard_map/ppermute | solution.py:48
  36.1 24.0 %collective-permute-start.5 = (bf16[256,2048]{1,0:T(8,128)(2,1)S(1)}, bf16[256,2048]{1,0:T(8,128)(2,1)S(1)}, u32[]{:S(2)}, u32[]{:S(2)}) collective-permute-start(bf16[256,2048]{1,0:T(8,128)(2,1)S(1)} %collective-permute-done.refs_1_), channel_id=1, source_target_pairs={{2,4},{3,5},{4,2},{5,3},{10,12},{11,13},{12,10},{13,11},{18,20},{1... | collective-permute-start | bytes 3145736 | tf_op jit(solution)/shard_map/ppermute | solution.py:48
  36.8 23.3 %collective-permute-start.7 = (bf16[4,128,1024]{2,1,0:T(8,128)(2,1)S(1)}, bf16[4,128,1024]{2,1,0:T(8,128)(2,1)S(1)}, u32[]{:S(2)}, u32[]{:S(2)}) collective-permute-start(bf16[4,128,1024]{2,1,0:T(8,128)(2,1)S(1)} %get-tuple-element.94), channel_id=1, source_target_pairs={{0,1},{1,0},{2,3},{3,2},{4,5},{5,4},{6,7},{7,6},{8,9},{9,8},{10,11... | collective-permute-start | bytes 3145736 | tf_op jit(solution)/shard_map/ppermute | solution.py:19
  46.9 14.8 %copy-start.18 = (bf16[1280,2048]{1,0:T(8,128)(2,1)}, bf16[1280,2048]{1,0:T(8,128)(2,1)S(1)}, u32[]{:S(2)}) copy-start(bf16[1280,2048]{1,0:T(8,128)(2,1)S(1)} %shard_map.114.columns_hbm) | copy-start | bytes 15728644
  60.1 25.3 %collective-permute-start.9 = (bf16[256,2048]{1,0:T(8,128)(2,1)S(1)}, bf16[256,2048]{1,0:T(8,128)(2,1)S(1)}, u32[]{:S(2)}, u32[]{:S(2)}) collective-permute-start(bf16[256,2048]{1,0:T(8,128)(2,1)S(1)} %collective-permute-done.5), channel_id=1, source_target_pairs={{2,0},{3,1},{4,6},{5,7},{10,8},{11,9},{12,14},{13,15},{18,16},{19,... | collective-permute-start | bytes 3145736 | tf_op jit(solution)/shard_map/ppermute | solution.py:48
  61.7 25.6 %copy-start.8 = (bf16[1,256,2048]{2,1,0:T(8,128)(2,1)S(1)}, bf16[1,256,2048]{2,1,0:T(8,128)(2,1)}, u32[]{:S(2)}) copy-start(bf16[1,256,2048]{2,1,0:T(8,128)(2,1)} %param.10) | copy-start | bytes 3145732
  61.8 24.0 %collective-permute-start.11 = (bf16[2,128,1024]{2,1,0:T(8,128)(2,1)S(1)}, bf16[2,128,1024]{2,1,0:T(8,128)(2,1)S(1)}, u32[]{:S(2)}, u32[]{:S(2)}) collective-permute-start(bf16[2,128,1024]{2,1,0:T(8,128)(2,1)S(1)} %get-tuple-element.163), channel_id=1, source_target_pairs={{2,4},{3,5},{4,2},{5,3},{10,12},{11,13},{12,10},{13,11},{18,20},{1... | collective-permute-start | bytes 1572872 | tf_op jit(solution)/shard_map/ppermute | solution.py:48
  62.6 23.2 %collective-permute-start.12 = (bf16[2,128,1024]{2,1,0:T(8,128)(2,1)S(1)}, bf16[2,128,1024]{2,1,0:T(8,128)(2,1)S(1)}, u32[]{:S(2)}, u32[]{:S(2)}) collective-permute-start(bf16[2,128,1024]{2,1,0:T(8,128)(2,1)S(1)} %get-tuple-element.162), channel_id=1, source_target_pairs={{0,4},{1,5},{6,2},{7,3},{8,12},{9,13},{14,10},{15,11},{16,20},{17,... | collective-permute-start | bytes 1572872 | tf_op jit(solution)/shard_map/ppermute | solution.py:48
  71.9 13.9 %collective-permute-start.8 = (bf16[1024,128]{1,0:T(8,128)(2,1)S(1)}, bf16[1024,128]{1,0:T(8,128)(2,1)S(1)}, u32[]{:S(2)}, u32[]{:S(2)}) collective-permute-start(bf16[1024,128]{1,0:T(8,128)(2,1)S(1)} %shard_map.115.own), channel_id=1, source_target_pairs={{0,1},{1,0},{2,3},{3,2},{4,5},{5,4},{6,7},{7,6},{8,9},{9,8},{10,11... | collective-permute-start | bytes 786440 | tf_op jit(solution)/shard_map/ppermute | solution.py:19
  73.5 12.4 %collective-permute-start.10 = (bf16[128,1024]{1,0:T(8,128)(2,1)S(1)}, bf16[128,1024]{1,0:T(8,128)(2,1)S(1)}, u32[]{:S(2)}, u32[]{:S(2)}) collective-permute-start(bf16[128,1024]{1,0:T(8,128)(2,1)S(1)} %get-tuple-element.161), channel_id=1, source_target_pairs={{0,2},{1,3},{6,4},{7,5},{8,10},{9,11},{14,12},{15,13},{16,18},{17,... | collective-permute-start | bytes 786440 | tf_op jit(solution)/shard_map/ppermute | solution.py:48
  86.0 9.4 %collective-permute-start.13 = (bf16[128,1024]{1,0:T(8,128)(2,1)S(1)}, bf16[128,1024]{1,0:T(8,128)(2,1)S(1)}, u32[]{:S(2)}, u32[]{:S(2)}) collective-permute-start(bf16[128,1024]{1,0:T(8,128)(2,1)S(1)} %fusion), channel_id=1, source_target_pairs={{2,0},{3,1},{4,6},{5,7},{10,8},{11,9},{12,14},{13,15},{18,16},{19,... | collective-permute-start | bytes 786440 | tf_op jit(solution)/shard_map/ppermute | solution.py:48
  87.4 9.4 %collective-permute-start.14 = (bf16[256,1024]{1,0:T(8,128)(2,1)S(1)}, bf16[256,1024]{1,0:T(8,128)(2,1)S(1)}, u32[]{:S(2)}, u32[]{:S(2)}) collective-permute-start(bf16[256,1024]{1,0:T(8,128)(2,1)S(1)} %shard_map.116), channel_id=1, source_target_pairs={{0,1},{1,0},{2,3},{3,2},{4,5},{5,4},{6,7},{7,6},{8,9},{9,8},{10,11... | collective-permute-start | bytes 1572872 | tf_op jit(solution)/shard_map/ppermute | solution.py:19
  97.7 4.1 %collective-permute-start.15 = (bf16[128,1024]{1,0:T(8,128)(2,1)S(1)}, bf16[128,1024]{1,0:T(8,128)(2,1)}, u32[]{:S(2)}, u32[]{:S(2)}) collective-permute-start(bf16[128,1024]{1,0:T(8,128)(2,1)S(1)} %convert_element_type.103.former_sums), channel_id=1, source_target_pairs={{24,16},{25,17},{26,18},{27,19},{28,20},{29,21},{30,22},{31,23}} | collective-permute-start | bytes 786440 | tf_op jit(solution)/shard_map/ppermute | solution.py:25
  104.5 6.0 %collective-permute-start.16 = (bf16[128,1024]{1,0:T(8,128)(2,1)}, bf16[128,1024]{1,0:T(8,128)(2,1)S(1)}, u32[]{:S(2)}, u32[]{:S(2)}) collective-permute-start(bf16[128,1024]{1,0:T(8,128)(2,1)} %get-tuple-element.127.former_sums), channel_id=1, source_target_pairs={{16,8},{17,9},{18,10},{19,11},{20,12},{21,13},{22,14},{23,15}} | collective-permute-start | bytes 786440 | tf_op jit(solution)/shard_map/ppermute | solution.py:25
  105.8 7.0 %collective-permute-start.17 = (bf16[128,1024]{1,0:T(8,128)(2,1)}, bf16[128,1024]{1,0:T(8,128)(2,1)}, u32[]{:S(2)}, u32[]{:S(2)}) collective-permute-start(bf16[128,1024]{1,0:T(8,128)(2,1)} %get-tuple-element.128.former_cross), channel_id=1, source_target_pairs={{16,9},{17,8},{18,11},{19,10},{20,13},{21,12},{22,15},{23,14}} | collective-permute-start | bytes 786440 | tf_op jit(solution)/shard_map/ppermute | solution.py:25
  115.5 5.5 %collective-permute-start.18 = (bf16[128,1024]{1,0:T(8,128)(2,1)S(1)}, bf16[128,1024]{1,0:T(8,128)(2,1)}, u32[]{:S(2)}, u32[]{:S(2)}) collective-permute-start(bf16[128,1024]{1,0:T(8,128)(2,1)S(1)} %get-tuple-element.135.former_sums), channel_id=1, source_target_pairs={{8,0},{9,1},{10,2},{11,3},{12,4},{13,5},{14,6},{15,7}} | collective-permute-start | bytes 786440 | tf_op jit(solution)/shard_map/ppermute | solution.py:25
  116.9 4.1 %collective-permute-start.19 = (bf16[128,1024]{1,0:T(8,128)(2,1)}, bf16[128,1024]{1,0:T(8,128)(2,1)}, u32[]{:S(2)}, u32[]{:S(2)}) collective-permute-start(bf16[128,1024]{1,0:T(8,128)(2,1)} %get-tuple-element.136.former_cross), channel_id=1, source_target_pairs={{8,1},{9,0},{10,3},{11,2},{12,5},{13,4},{14,7},{15,6}} | collective-permute-start | bytes 786440 | tf_op jit(solution)/shard_map/ppermute | solution.py:25
  121.0 32.5 %copy-start.9 = (bf16[1,256,2048]{2,1,0:T(8,128)(2,1)S(1)}, bf16[1,256,2048]{2,1,0:T(8,128)(2,1)}, u32[]{:S(2)}) copy-start(bf16[1,256,2048]{2,1,0:T(8,128)(2,1)} %param.10) | copy-start | bytes 3145732
  121.0 32.5 %copy-start.12 = (bf16[256,1024]{1,0:T(8,128)(2,1)S(1)}, bf16[256,1024]{1,0:T(8,128)(2,1)}, u32[]{:S(2)}) copy-start(bf16[256,1024]{1,0:T(8,128)(2,1)} %copy-done.11) | copy-start | bytes 1572868
  122.5 6.4 %collective-permute-start.20 = (bf16[128,1024]{1,0:T(8,128)(2,1)S(1)}, bf16[128,1024]{1,0:T(8,128)(2,1)S(1)}, u32[]{:S(2)}, u32[]{:S(2)}) collective-permute-start(bf16[128,1024]{1,0:T(8,128)(2,1)S(1)} %get-tuple-element.142), channel_id=1, source_target_pairs={{0,1},{1,0},{2,3},{3,2},{4,5},{5,4},{6,7},{7,6},{8,9},{9,8},{10,11... | collective-permute-start | bytes 786440 | tf_op jit(solution)/shard_map/ppermute | solution.py:19
  129.0 12.3 %collective-permute-start.21 = (bf16[128,1024]{1,0:T(8,128)(2,1)S(1)}, bf16[128,1024]{1,0:T(8,128)(2,1)S(1)}, u32[]{:S(2)}, u32[]{:S(2)}) collective-permute-start(bf16[128,1024]{1,0:T(8,128)(2,1)S(1)} %add_convert_fusion.c0), channel_id=1, source_target_pairs={{0,2},{1,3},{2,0},{3,1},{4,6},{5,7},{6,4},{7,5},{8,10},{9,11},{10,... | collective-permute-start | bytes 786440 | tf_op jit(solution)/shard_map/ppermute | solution.py:19
  133.9 19.6 %collective-permute-start.22 = (bf16[128,1024]{1,0:T(8,128)(2,1)S(1)}, bf16[128,1024]{1,0:T(8,128)(2,1)S(1)}, u32[]{:S(2)}, u32[]{:S(2)}) collective-permute-start(bf16[128,1024]{1,0:T(8,128)(2,1)S(1)} %add_convert_fusion.c0), channel_id=1, source_target_pairs={{0,4},{1,5},{2,6},{3,7},{4,0},{5,1},{6,2},{7,3},{8,12},{9,13},{10,... | collective-permute-start | bytes 786440 | tf_op jit(solution)/shard_map/ppermute | solution.py:19
  134.1 19.3 %collective-permute-start.23 = (bf16[128,1024]{1,0:T(8,128)(2,1)S(1)}, bf16[128,1024]{1,0:T(8,128)(2,1)S(1)}, u32[]{:S(2)}, u32[]{:S(2)}) collective-permute-start(bf16[128,1024]{1,0:T(8,128)(2,1)S(1)} %add_convert_fusion.c0), channel_id=1, source_target_pairs={{0,6},{1,7},{2,4},{3,5},{4,2},{5,3},{6,0},{7,1},{8,14},{9,15},{10,... | collective-permute-start | bytes 786440 | tf_op jit(solution)/shard_map/ppermute | solution.py:19
  155.0 6.4 %collective-permute-start.24 = (bf16[512,256]{1,0:T(8,128)(2,1)S(1)}, bf16[512,256]{1,0:T(8,128)(2,1)S(1)}, u32[]{:S(2)}, u32[]{:S(2)}) collective-permute-start(bf16[512,256]{1,0:T(8,128)(2,1)S(1)} %get-tuple-element.144), channel_id=1, source_target_pairs={{0,1},{1,0},{2,3},{3,2},{4,5},{5,4},{6,7},{7,6},{8,9},{9,8},{10,11... | collective-permute-start | bytes 786440 | tf_op jit(solution)/shard_map/ppermute | solution.py:19
  161.6 8.0 %collective-permute-start.25 = (bf16[256,128]{1,0:T(8,128)(2,1)S(1)}, bf16[256,128]{1,0:T(8,128)(2,1)S(1)}, u32[]{:S(2)}, u32[]{:S(2)}) collective-permute-start(bf16[256,128]{1,0:T(8,128)(2,1)S(1)} %get-tuple-element.151), channel_id=1, source_target_pairs={{0,2},{1,3},{2,0},{3,1},{4,6},{5,7},{6,4},{7,5},{8,10},{9,11},{10,... | collective-permute-start | bytes 196616 | tf_op jit(solution)/shard_map/ppermute | solution.py:19
  165.4 5.4 %collective-permute-start.26 = (bf16[256,128]{1,0:T(8,128)(2,1)S(1)}, bf16[256,128]{1,0:T(8,128)(2,1)S(1)}, u32[]{:S(2)}, u32[]{:S(2)}) collective-permute-start(bf16[256,128]{1,0:T(8,128)(2,1)S(1)} %get-tuple-element.152), channel_id=1, source_target_pairs={{0,4},{1,5},{2,6},{3,7},{4,0},{5,1},{6,2},{7,3},{8,12},{9,13},{10,... | collective-permute-start | bytes 196616 | tf_op jit(solution)/shard_map/ppermute | solution.py:19
  165.7 6.2 %collective-permute-start.27 = (bf16[256,128]{1,0:T(8,128)(2,1)S(1)}, bf16[256,128]{1,0:T(8,128)(2,1)S(1)}, u32[]{:S(2)}, u32[]{:S(2)}) collective-permute-start(bf16[256,128]{1,0:T(8,128)(2,1)S(1)} %get-tuple-element.153), channel_id=1, source_target_pairs={{0,6},{1,7},{2,4},{3,5},{4,2},{5,3},{6,0},{7,1},{8,14},{9,15},{10,... | collective-permute-start | bytes 196616 | tf_op jit(solution)/shard_map/ppermute | solution.py:19
  171.9 1.4 collective-permute-start.28
  172.6 0.7 collective-permute-start.29
  175.1 18.1 %collective-permute-start.30 = (bf16[1024,128]{1,0:T(8,128)(2,1)S(1)}, bf16[1024,128]{1,0:T(8,128)(2,1)S(1)}, u32[]{:S(2)}, u32[]{:S(2)}) collective-permute-start(bf16[1024,128]{1,0:T(8,128)(2,1)S(1)} %shard_map.127), channel_id=1, source_target_pairs={{8,16},{9,17},{10,18},{11,19},{12,20},{13,21},{14,22},{15,23}} | collective-permute-start | bytes 786440 | tf_op jit(solution)/shard_map/ppermute | solution.py:25
  176.4 21.0 %collective-permute-start.31 = (bf16[1024,128]{1,0:T(8,128)(2,1)S(1)}, bf16[1024,128]{1,0:T(8,128)(2,1)S(1)}, u32[]{:S(2)}, u32[]{:S(2)}) collective-permute-start(bf16[1024,128]{1,0:T(8,128)(2,1)S(1)} %shard_map.127), channel_id=1, source_target_pairs={{8,17},{9,16},{10,19},{11,18},{12,21},{13,20},{14,23},{15,22}} | collective-permute-start | bytes 786440 | tf_op jit(solution)/shard_map/ppermute | solution.py:25
  199.3 37.8 %copy-start.3 = (bf16[1,256,2048]{2,1,0:T(8,128)(2,1)S(1)}, bf16[1,256,2048]{2,1,0:T(8,128)(2,1)}, u32[]{:S(2)}) copy-start(bf16[1,256,2048]{2,1,0:T(8,128)(2,1)} %param.9) | copy-start | bytes 3145732
  199.3 4.2 %collective-permute-start.32 = (bf16[1024,128]{1,0:T(8,128)(2,1)S(1)}, bf16[1024,128]{1,0:T(8,128)(2,1)}, u32[]{:S(2)}, u32[]{:S(2)}) collective-permute-start(bf16[1024,128]{1,0:T(8,128)(2,1)S(1)} %shard_map.128), channel_id=1, source_target_pairs={{16,24},{17,25},{18,26},{19,27},{20,28},{21,29},{22,30},{23,31}} | collective-permute-start | bytes 786440 | tf_op jit(solution)/shard_map/ppermute | solution.py:25
  201.5 5.2 %collective-permute-start.33 = (bf16[1024,128]{1,0:T(8,128)(2,1)S(1)}, bf16[1024,128]{1,0:T(8,128)(2,1)}, u32[]{:S(2)}, u32[]{:S(2)}) collective-permute-start(bf16[1024,128]{1,0:T(8,128)(2,1)S(1)} %shard_map.128), channel_id=1, source_target_pairs={{16,25},{17,24},{18,27},{19,26},{20,29},{21,28},{22,31},{23,30}} | collective-permute-start | bytes 786440 | tf_op jit(solution)/shard_map/ppermute | solution.py:25
  203.5 15.1 %collective-permute-start.35 = (bf16[1024,128]{1,0:T(8,128)(2,1)S(1)}, bf16[1024,128]{1,0:T(8,128)(2,1)S(1)}, u32[]{:S(2)}, u32[]{:S(2)}) collective-permute-start(bf16[1024,128]{1,0:T(8,128)(2,1)S(1)} %select_select_fusion.1.own), channel_id=1, source_target_pairs={{0,4},{1,5},{2,6},{3,7},{4,0},{5,1},{6,2},{7,3},{8,12},{9,13},{10,... | collective-permute-start | bytes 786440 | tf_op jit(solution)/shard_map/ppermute | solution.py:19
  206.7 25.3 %collective-permute-start.34 = (bf16[2,1024,128]{2,1,0:T(8,128)(2,1)S(1)}, bf16[2,1024,128]{2,1,0:T(8,128)(2,1)S(1)}, u32[]{:S(2)}, u32[]{:S(2)}) collective-permute-start(bf16[2,1024,128]{2,1,0:T(8,128)(2,1)S(1)} %pad_maximum_fusion.2), channel_id=1, source_target_pairs={{0,2},{1,3},{2,0},{3,1},{4,6},{5,7},{6,4},{7,5},{8,10},{9,11},{10,... | collective-permute-start | bytes 1572872 | tf_op jit(solution)/shard_map/ppermute | solution.py:19
  207.7 22.2 %collective-permute-start.37 = (bf16[1024,128]{1,0:T(8,128)(2,1)S(1)}, bf16[1024,128]{1,0:T(8,128)(2,1)S(1)}, u32[]{:S(2)}, u32[]{:S(2)}) collective-permute-start(bf16[1024,128]{1,0:T(8,128)(2,1)S(1)} %select_select_fusion.1.own), channel_id=1, source_target_pairs={{0,6},{1,7},{2,4},{3,5},{4,2},{5,3},{6,0},{7,1},{8,14},{9,15},{10,... | collective-permute-start | bytes 786440 | tf_op jit(solution)/shard_map/ppermute | solution.py:19
  218.7 13.3 %collective-permute-start.36 = (bf16[1024,128]{1,0:T(8,128)(2,1)S(1)}, bf16[1024,128]{1,0:T(8,128)(2,1)S(1)}, u32[]{:S(2)}, u32[]{:S(2)}) collective-permute-start(bf16[1024,128]{1,0:T(8,128)(2,1)S(1)} %collective-permute-done.35.own4), channel_id=1, source_target_pairs={{0,1},{1,0},{2,3},{3,2},{4,5},{5,4},{6,7},{7,6},{8,9},{9,8},{10,11... | collective-permute-start | bytes 786440 | tf_op jit(solution)/shard_map/ppermute | solution.py:19
  229.9 7.1 %collective-permute-start.38 = (bf16[1024,128]{1,0:T(8,128)(2,1)S(1)}, bf16[1024,128]{1,0:T(8,128)(2,1)S(1)}, u32[]{:S(2)}, u32[]{:S(2)}) collective-permute-start(bf16[1024,128]{1,0:T(8,128)(2,1)S(1)} %collective-permute-done.37.own6), channel_id=1, source_target_pairs={{0,1},{1,0},{2,3},{3,2},{4,5},{5,4},{6,7},{7,6},{8,9},{9,8},{10,11... | collective-permute-start | bytes 786440 | tf_op jit(solution)/shard_map/ppermute | solution.py:19
  (10 other events, 10.8 us)

commit v7 on v6

--- a/solution.py
+++ b/solution.py
@@ -498,7 +498,7 @@
     near, middle = bus_send(gain, 2, everyone), across(gain, everyone)
     *keep, send, solved = front(rank, active, unit_rhs, residual, inverse, sens)
     send, start_in = together(send, start_state)
-    pieces = swap_z(start_pieces(rank, start_in), everyone)
+    pieces = swap_z(start_pieces(rank, start_in), (0,))
     near, middle, send, keep, schur_in, pieces = together(
         near, middle, send, keep, schur, pieces
     )
@@ -515,7 +515,7 @@
     terms = [mine + theirs.astype(F32) for mine, theirs in zip(keep, there, strict=True)]
     sent = [term.astype(BF16) for term in terms]
     start_y, fourth, from_end, from_middle, from_far = together(
-        bus_send(start, 1, everyone),
+        bus_send(start, 1, (0,)),
         fourth,
         line_send(sent[1], ((0, 1), (3, 2)), everyone),
         across(jnp.stack([sent[3], sent[2]]), everyone),

time: 245 us -> 241 us (0.984)
  starting transfers between devices: 66.7 us -> 58.6 us
  waiting for transfers between devices: 121 us -> 125 us
    ppermute x20, starting transfers between devices: 34.6 us -> 26.5 us  [bus_send(): return lax.ppermute(block, BOTH, route)]
    ppermute x8, waiting for transfers between devices: 29.9 us -> 35.3 us  [line_send(): return lax.ppermute(block, BOTH, route)]
  transfers between devices with their start and end apart: 39 -> 39, of which waited for: 20 -> 19; matrix products, arithmetic and copies ran while one was open for 1% -> 1% of each run, Pallas kernels for 10% -> 10%
where the time goes in v7:
time: 241 us; the launch traced here: 240 us
  waiting for transfers between devices  125 us (52%)
  starting transfers between devices  58.6 us (24%)
  Pallas kernels  41.3 us (17%)
  local copies, waits for them, and re-layouts  11.9 us (5%)
    ppermute x20, waiting for transfers between devices, bus_send(): return lax.ppermute(block, BOTH, route)  66.3 us
    ppermute x8, waiting for transfers between devices, line_send(): return lax.ppermute(block, BOTH, route)  35.3 us
    ppermute x20, starting transfers between devices, bus_send(): return lax.ppermute(block, BOTH, route)  26.5 us
    ppermute x11, waiting for transfers between devices, period_send(): return lax.ppermute(block, BOTH, route)  23.2 us
    ppermute x8, starting transfers between devices, line_send(): return lax.ppermute(block, BOTH, route)  16.6 us
    ppermute x11, starting transfers between devices, period_send(): return lax.ppermute(block, BOTH, route)  15.4 us
    pallas_call x1, Pallas kernels, front(): kernel_call(front_kernel, [keep] * 4 + [send, jax.ShapeDtypeStruct((buses...  12 us
    unnamed x38, local copies, waits for them, and re-layouts  10.9 us
  transfers between devices with their start and end apart: 39, of which 19 were waited for; matrix products, arithmetic and copies ran while one was open for 1% of the time, Pallas kernels for 10%

profile of v7, /device:TPU:2, one launch (start us, length us, event | category | flops | bytes accessed | tf_op | source)
XLA Modules:
  0.0 239.8 jit_solution(12606547623161413779)
XLA Ops:
  0.6 1.6 collective-permute-start
  5.0 12.0 %shard_map.112 = (f32[128,1024]{1,0:T(8,128)S(1)}, f32[128,1024]{1,0:T(8,128)S(1)}, f32[128,1024]{1,0:T(8,128)S(1)}, f32[128,1024]{1,0:T(8,128)S(1)}, bf16[4,128...) custom-call(s32[1]{0:T(128)} %bitcast.rank_ref, s32[1280,1]{1,0:T(8,128)S(1)} %copy.12.active, f32[256,512]{1,0:T(8,128)S(1)} %bitcast.57, ...), custom_call_target="tpu_custom_call" | custom-call | flops 4362076160 | bytes 25165824 | tf_op jit(solution)/shard_map/pallas_call | solution.py:142
  19.1 6.7 %collective-permute-done.refs_1_ = bf16[256,2048]{1,0:T(8,128)(2,1)S(1)} collective-permute-done((bf16[256,2048]{1,0:T(8,128)(2,1)}, bf16[256,2048]{1,0:T(8,128)(2,1)S(1)}, u32[]{:S(2)}, u32[]{:S(2)}) %collective-permute-start) | collective-permute-done | bytes 1048608 | tf_op jit(solution)/shard_map/ppermute | solution.py:19
  27.8 1.6 collective-permute-start.7
  29.4 8.5 %shard_map.114.columns_hbm = bf16[1280,2048]{1,0:T(8,128)(2,1)S(1)} custom-call(s32[1]{0:T(128)} %bitcast.rank_ref, s32[1,2048]{1,0:T(1,128)S(1)} %bitcast.58, bf16[1280,1280]{1,0:T(8,128)(2,1)S(1)} %bitcast.56), custom_call_target="tpu_custom_call" | custom-call | flops 6710886400 | bytes 12582912 | tf_op jit(solution)/shard_map/pallas_call | solution.py:401
  37.9 16.0 %collective-permute-done.6 = bf16[256,2048]{1,0:T(8,128)(2,1)S(1)} collective-permute-done((bf16[256,2048]{1,0:T(8,128)(2,1)S(1)}, bf16[256,2048]{1,0:T(8,128)(2,1)S(1)}, u32[]{:S(2)}, u32[]{:S(2)}) %collective-permute-start.6) | collective-permute-done | bytes 1048608 | tf_op jit(solution)/shard_map/ppermute | solution.py:48
  56.9 9.2 %collective-permute-start.12 = (bf16[2,128,1024]{2,1,0:T(8,128)(2,1)S(1)}, bf16[2,128,1024]{2,1,0:T(8,128)(2,1)S(1)}, u32[]{:S(2)}, u32[]{:S(2)}) collective-permute-start(bf16[2,128,1024]{2,1,0:T(8,128)(2,1)S(1)} %get-tuple-element.162), channel_id=1, source_target_pairs={{0,4},{1,5},{6,2},{7,3},{8,12},{9,13},{14,10},{15,11},{16,20},{17,... | collective-permute-start | bytes 1572872 | tf_op jit(solution)/shard_map/ppermute | solution.py:48
  66.8 1.3 collective-permute-start.10
  68.1 12.8 %collective-permute-done.9 = bf16[256,2048]{1,0:T(8,128)(2,1)S(1)} collective-permute-done((bf16[256,2048]{1,0:T(8,128)(2,1)S(1)}, bf16[256,2048]{1,0:T(8,128)(2,1)S(1)}, u32[]{:S(2)}, u32[]{:S(2)}) %collective-permute-start.9) | collective-permute-done | bytes 1048608 | tf_op jit(solution)/shard_map/ppermute | solution.py:48
  81.5 1.3 collective-permute-start.13
  82.9 1.6 collective-permute-start.14
  84.5 6.4 %collective-permute-done.13 = bf16[128,1024]{1,0:T(8,128)(2,1)S(1)} collective-permute-done((bf16[128,1024]{1,0:T(8,128)(2,1)S(1)}, bf16[128,1024]{1,0:T(8,128)(2,1)S(1)}, u32[]{:S(2)}, u32[]{:S(2)}) %collective-permute-start.13) | collective-permute-done | bytes 262176 | tf_op jit(solution)/shard_map/ppermute | solution.py:48
  91.2 2.4 %collective-permute-done.14.schur_y = bf16[256,1024]{1,0:T(8,128)(2,1)S(1)} collective-permute-done((bf16[256,1024]{1,0:T(8,128)(2,1)S(1)}, bf16[256,1024]{1,0:T(8,128)(2,1)S(1)}, u32[]{:S(2)}, u32[]{:S(2)}) %collective-permute-start.14) | collective-permute-done | bytes 524320 | tf_op jit(solution)/shard_map/ppermute | solution.py:19
  94.5 1.3 collective-permute-start.15
  98.6 2.6 %shard_map.118 = (bf16[128,1024]{1,0:T(8,128)(2,1)}, bf16[128,1024]{1,0:T(8,128)(2,1)}) custom-call(s32[5]{0:T(128)S(1)} %concatenate.3.places, s32[1]{0:T(128)} %bitcast.20.turn, bf16[128,1024]{1,0:T(8,128)(2,1)} %collective-permute-done.15.own, bf16[128,1024]{1,0:T(8,128)(2,1)S(1)} %broadcast_in_dim.16.other.former_cross, f32[128,1024]{1,0:T(8,128)S(1)} %fusion.2.base, ...), custom_call_target="tpu_custom_call" | custom-call | flops 536870912 | bytes 4194304 | tf_op jit(solution)/shard_map/pallas_call | solution.py:257
  101.3 1.3 collective-permute-start.16
  102.6 2.0 collective-permute-start.17
  108.0 1.6 collective-permute-done.17.other
  110.5 1.9 shard_map.120
  112.4 1.4 collective-permute-start.18
  113.7 1.4 collective-permute-start.19
  117.9 1.5 shard_map.122
  119.3 1.6 collective-permute-start.20
  120.9 4.9 %collective-permute-done.20 = bf16[128,1024]{1,0:T(8,128)(2,1)S(1)} collective-permute-done((bf16[128,1024]{1,0:T(8,128)(2,1)S(1)}, bf16[128,1024]{1,0:T(8,128)(2,1)S(1)}, u32[]{:S(2)}, u32[]{:S(2)}) %collective-permute-start.20) | collective-permute-done | bytes 262176 | tf_op jit(solution)/shard_map/ppermute | solution.py:19
  125.8 3.6 %collective-permute-start.21 = (bf16[128,1024]{1,0:T(8,128)(2,1)S(1)}, bf16[128,1024]{1,0:T(8,128)(2,1)S(1)}, u32[]{:S(2)}, u32[]{:S(2)}) collective-permute-start(bf16[128,1024]{1,0:T(8,128)(2,1)S(1)} %add_convert_fusion.c0), channel_id=1, source_target_pairs={{0,2},{1,3},{2,0},{3,1},{4,6},{5,7},{6,4},{7,5},{8,10},{9,11},{10,... | collective-permute-start | bytes 786440 | tf_op jit(solution)/shard_map/ppermute | solution.py:19
  130.2 1.7 collective-permute-start.23
  131.9 4.4 %collective-permute-done.21.c2 = bf16[128,1024]{1,0:T(8,128)(2,1)S(1)} collective-permute-done((bf16[128,1024]{1,0:T(8,128)(2,1)S(1)}, bf16[128,1024]{1,0:T(8,128)(2,1)S(1)}, u32[]{:S(2)}, u32[]{:S(2)}) %collective-permute-start.21) | collective-permute-done | bytes 262176 | tf_op jit(solution)/shard_map/ppermute | solution.py:19
  136.3 13.0 %collective-permute-done.22.c4 = bf16[128,1024]{1,0:T(8,128)(2,1)S(1)} collective-permute-done((bf16[128,1024]{1,0:T(8,128)(2,1)S(1)}, bf16[128,1024]{1,0:T(8,128)(2,1)S(1)}, u32[]{:S(2)}, u32[]{:S(2)}) %collective-permute-start.22) | collective-permute-done | bytes 262176 | tf_op jit(solution)/shard_map/ppermute | solution.py:19
  149.3 1.5 shard_map.123
  150.8 1.5 collective-permute-start.24
  152.3 4.9 %collective-permute-done.24.cross = bf16[512,256]{1,0:T(8,128)(2,1)S(1)} collective-permute-done((bf16[512,256]{1,0:T(8,128)(2,1)S(1)}, bf16[512,256]{1,0:T(8,128)(2,1)S(1)}, u32[]{:S(2)}, u32[]{:S(2)}) %collective-permute-start.24) | collective-permute-done | bytes 262176 | tf_op jit(solution)/shard_map/ppermute | solution.py:19
  157.5 3.5 %collective-permute-start.25 = (bf16[256,128]{1,0:T(8,128)(2,1)S(1)}, bf16[256,128]{1,0:T(8,128)(2,1)S(1)}, u32[]{:S(2)}, u32[]{:S(2)}) collective-permute-start(bf16[256,128]{1,0:T(8,128)(2,1)S(1)} %get-tuple-element.151), channel_id=1, source_target_pairs={{0,2},{1,3},{2,0},{3,1},{4,6},{5,7},{6,4},{7,5},{8,10},{9,11},{10,... | collective-permute-start | bytes 196616 | tf_op jit(solution)/shard_map/ppermute | solution.py:19
  161.7 1.7 collective-permute-start.27
  163.4 1.8 shard_map.125.driven
  165.3 1.5 collective-permute-done.26.p4
  169.3 1.8 shard_map.127
  173.8 15.6 %collective-permute-done.30.own = bf16[1024,128]{1,0:T(8,128)(2,1)S(1)} collective-permute-done((bf16[1024,128]{1,0:T(8,128)(2,1)S(1)}, bf16[1024,128]{1,0:T(8,128)(2,1)S(1)}, u32[]{:S(2)}, u32[]{:S(2)}) %collective-permute-start.30) | collective-permute-done | bytes 262176 | tf_op jit(solution)/shard_map/ppermute | solution.py:25
  189.4 4.1 %collective-permute-done.31.other = bf16[1024,128]{1,0:T(8,128)(2,1)S(1)} collective-permute-done((bf16[1024,128]{1,0:T(8,128)(2,1)S(1)}, bf16[1024,128]{1,0:T(8,128)(2,1)S(1)}, u32[]{:S(2)}, u32[]{:S(2)}) %collective-permute-start.31) | collective-permute-done | bytes 262176 | tf_op jit(solution)/shard_map/ppermute | solution.py:25
  193.5 1.8 shard_map.128
  195.3 2.2 collective-permute-start.32
  197.5 2.0 collective-permute-start.33
  200.7 1.9 collective-permute-done.33
  203.7 1.7 collective-permute-start.37
  205.4 9.2 %collective-permute-done.35.own4 = bf16[1024,128]{1,0:T(8,128)(2,1)S(1)} collective-permute-done((bf16[1024,128]{1,0:T(8,128)(2,1)S(1)}, bf16[1024,128]{1,0:T(8,128)(2,1)S(1)}, u32[]{:S(2)}, u32[]{:S(2)}) %collective-permute-start.35) | collective-permute-done | bytes 262176 | tf_op jit(solution)/shard_map/ppermute | solution.py:19
  214.8 11.1 %collective-permute-done.37.own6 = bf16[1024,128]{1,0:T(8,128)(2,1)S(1)} collective-permute-done((bf16[1024,128]{1,0:T(8,128)(2,1)S(1)}, bf16[1024,128]{1,0:T(8,128)(2,1)S(1)}, u32[]{:S(2)}, u32[]{:S(2)}) %collective-permute-start.37) | collective-permute-done | bytes 262176 | tf_op jit(solution)/shard_map/ppermute | solution.py:19
  225.9 2.2 collective-permute-done.34.near
  228.1 5.0 %collective-permute-done.38.other6 = bf16[1024,128]{1,0:T(8,128)(2,1)S(1)} collective-permute-done((bf16[1024,128]{1,0:T(8,128)(2,1)S(1)}, bf16[1024,128]{1,0:T(8,128)(2,1)S(1)}, u32[]{:S(2)}, u32[]{:S(2)}) %collective-permute-start.38) | collective-permute-done | bytes 262176 | tf_op jit(solution)/shard_map/ppermute | solution.py:19
  233.0 6.6 %shard_map.129 = (f32[256,512]{1,0:T(8,128)}, f32[1280,512]{1,0:T(8,128)}) custom-call(s32[1]{0:T(128)} %bitcast.rank_ref, f32[256,512]{1,0:T(8,128)S(1)} %get-tuple-element.145.coupling, bf16[256,2048]{1,0:T(8,128)(2,1)S(1)} %bitcast.50, f32[1280,512]{1,0:T(8,128)} %get-tuple-element.146.solved_hbm, bf16[1280,2048]{1,0:T(8,128)(2,1)} %copy-done.18, ...), custom_call_target="tpu_custom_call" | custom-call | flops 3221225472 | bytes 25165824 | tf_op jit(solution)/shard_map/pallas_call | solution.py:465
  (100 shorter events, 31.3 us)
Async XLA Ops:
  0.6 25.2 %collective-permute-start = (bf16[256,2048]{1,0:T(8,128)(2,1)}, bf16[256,2048]{1,0:T(8,128)(2,1)S(1)}, u32[]{:S(2)}, u32[]{:S(2)}) collective-permute-start(bf16[256,2048]{1,0:T(8,128)(2,1)} %bitcast.45), channel_id=1, source_target_pairs={{0,2},{1,3},{2,0},{3,1},{4,6},{5,7},{6,4},{7,5},{8,10},{9,11},{10,... | collective-permute-start | bytes 3145736 | tf_op jit(solution)/shard_map/ppermute | solution.py:19
  2.3 23.5 %collective-permute-start.1 = (bf16[256,2048]{1,0:T(8,128)(2,1)}, bf16[256,2048]{1,0:T(8,128)(2,1)S(1)}, u32[]{:S(2)}, u32[]{:S(2)}) collective-permute-start(bf16[256,2048]{1,0:T(8,128)(2,1)} %bitcast.46), channel_id=1, source_target_pairs={{2,4},{3,5},{4,2},{5,3},{10,12},{11,13},{12,10},{13,11},{18,20},{1... | collective-permute-start | bytes 3145736 | tf_op jit(solution)/shard_map/ppermute | solution.py:48
  5.0 12.0 %copy-start.10 = (f32[256,512]{1,0:T(8,128)S(1)}, f32[256,512]{1,0:T(8,128)}, u32[]{:S(2)}) copy-start(f32[256,512]{1,0:T(8,128)} %state) | copy-start | bytes 1572868
  5.0 24.4 %copy-start.15 = (bf16[1,1280,1280]{2,1,0:T(8,128)(2,1)S(1)}, bf16[1,1280,1280]{2,1,0:T(8,128)(2,1)}, u32[]{:S(2)}) copy-start(bf16[1,1280,1280]{2,1,0:T(8,128)(2,1)} %param.11) | copy-start | bytes 9830404
  5.0 24.4 %copy-start.17 = (s32[2048]{0:T(1024)S(1)}, s32[2048]{0:T(1024)}, u32[]{:S(2)}) copy-start(s32[2048]{0:T(1024)} %param.17) | copy-start | bytes 24580
  17.1 2.0 collective-permute-start.2
  17.7 1.4 collective-permute-start.3
  18.4 0.7 collective-permute-start.4
  25.8 12.1 %copy-start.4 = (bf16[256,2048]{1,0:T(8,128)(2,1)}, bf16[256,2048]{1,0:T(8,128)(2,1)S(1)}, u32[]{:S(2)}) copy-start(bf16[256,2048]{1,0:T(8,128)(2,1)S(1)} %collective-permute-done.refs_1_) | copy-start | bytes 3145732
  25.8 28.1 %collective-permute-start.6 = (bf16[256,2048]{1,0:T(8,128)(2,1)S(1)}, bf16[256,2048]{1,0:T(8,128)(2,1)S(1)}, u32[]{:S(2)}, u32[]{:S(2)}) collective-permute-start(bf16[256,2048]{1,0:T(8,128)(2,1)S(1)} %collective-permute-done.1), channel_id=1, source_target_pairs={{2,0},{3,1},{4,6},{5,7},{10,8},{11,9},{12,14},{13,15},{18,16},{19,... | collective-permute-start | bytes 3145736 | tf_op jit(solution)/shard_map/ppermute | solution.py:48
  27.1 27.2 %collective-permute-start.5 = (bf16[256,2048]{1,0:T(8,128)(2,1)S(1)}, bf16[256,2048]{1,0:T(8,128)(2,1)S(1)}, u32[]{:S(2)}, u32[]{:S(2)}) collective-permute-start(bf16[256,2048]{1,0:T(8,128)(2,1)S(1)} %collective-permute-done.refs_1_), channel_id=1, source_target_pairs={{2,4},{3,5},{4,2},{5,3},{10,12},{11,13},{12,10},{13,11},{18,20},{1... | collective-permute-start | bytes 3145736 | tf_op jit(solution)/shard_map/ppermute | solution.py:48
  27.8 26.5 %collective-permute-start.7 = (bf16[4,128,1024]{2,1,0:T(8,128)(2,1)S(1)}, bf16[4,128,1024]{2,1,0:T(8,128)(2,1)S(1)}, u32[]{:S(2)}, u32[]{:S(2)}) collective-permute-start(bf16[4,128,1024]{2,1,0:T(8,128)(2,1)S(1)} %get-tuple-element.94), channel_id=1, source_target_pairs={{0,1},{1,0},{2,3},{3,2},{4,5},{5,4},{6,7},{7,6},{8,9},{9,8},{10,11... | collective-permute-start | bytes 3145736 | tf_op jit(solution)/shard_map/ppermute | solution.py:19
  37.9 18.0 %copy-start.18 = (bf16[1280,2048]{1,0:T(8,128)(2,1)}, bf16[1280,2048]{1,0:T(8,128)(2,1)S(1)}, u32[]{:S(2)}) copy-start(bf16[1280,2048]{1,0:T(8,128)(2,1)S(1)} %shard_map.114.columns_hbm) | copy-start | bytes 15728644
  54.4 26.6 %collective-permute-start.9 = (bf16[256,2048]{1,0:T(8,128)(2,1)S(1)}, bf16[256,2048]{1,0:T(8,128)(2,1)S(1)}, u32[]{:S(2)}, u32[]{:S(2)}) collective-permute-start(bf16[256,2048]{1,0:T(8,128)(2,1)S(1)} %collective-permute-done.5), channel_id=1, source_target_pairs={{2,0},{3,1},{4,6},{5,7},{10,8},{11,9},{12,14},{13,15},{18,16},{19,... | collective-permute-start | bytes 3145736 | tf_op jit(solution)/shard_map/ppermute | solution.py:48
  55.9 26.9 %copy-start.8 = (bf16[1,256,2048]{2,1,0:T(8,128)(2,1)S(1)}, bf16[1,256,2048]{2,1,0:T(8,128)(2,1)}, u32[]{:S(2)}) copy-start(bf16[1,256,2048]{2,1,0:T(8,128)(2,1)} %param.10) | copy-start | bytes 3145732
  56.0 25.3 %collective-permute-start.11 = (bf16[2,128,1024]{2,1,0:T(8,128)(2,1)S(1)}, bf16[2,128,1024]{2,1,0:T(8,128)(2,1)S(1)}, u32[]{:S(2)}, u32[]{:S(2)}) collective-permute-start(bf16[2,128,1024]{2,1,0:T(8,128)(2,1)S(1)} %get-tuple-element.163), channel_id=1, source_target_pairs={{2,4},{3,5},{4,2},{5,3},{10,12},{11,13},{12,10},{13,11},{18,20},{1... | collective-permute-start | bytes 1572872 | tf_op jit(solution)/shard_map/ppermute | solution.py:48
  56.9 24.5 %collective-permute-start.12 = (bf16[2,128,1024]{2,1,0:T(8,128)(2,1)S(1)}, bf16[2,128,1024]{2,1,0:T(8,128)(2,1)S(1)}, u32[]{:S(2)}, u32[]{:S(2)}) collective-permute-start(bf16[2,128,1024]{2,1,0:T(8,128)(2,1)S(1)} %get-tuple-element.162), channel_id=1, source_target_pairs={{0,4},{1,5},{6,2},{7,3},{8,12},{9,13},{14,10},{15,11},{16,20},{17,... | collective-permute-start | bytes 1572872 | tf_op jit(solution)/shard_map/ppermute | solution.py:48
  66.1 15.2 %collective-permute-start.8 = (bf16[1024,128]{1,0:T(8,128)(2,1)S(1)}, bf16[1024,128]{1,0:T(8,128)(2,1)S(1)}, u32[]{:S(2)}, u32[]{:S(2)}) collective-permute-start(bf16[1024,128]{1,0:T(8,128)(2,1)S(1)} %shard_map.115.own), channel_id=1, source_target_pairs={{0,1},{1,0},{2,3},{3,2},{4,5},{5,4},{6,7},{7,6}} | collective-permute-start | bytes 786440 | tf_op jit(solution)/shard_map/ppermute | solution.py:19
  66.8 14.5 %collective-permute-start.10 = (bf16[128,1024]{1,0:T(8,128)(2,1)S(1)}, bf16[128,1024]{1,0:T(8,128)(2,1)S(1)}, u32[]{:S(2)}, u32[]{:S(2)}) collective-permute-start(bf16[128,1024]{1,0:T(8,128)(2,1)S(1)} %get-tuple-element.161), channel_id=1, source_target_pairs={{0,2},{1,3},{6,4},{7,5},{8,10},{9,11},{14,12},{15,13},{16,18},{17,... | collective-permute-start | bytes 786440 | tf_op jit(solution)/shard_map/ppermute | solution.py:48
  81.5 9.4 %collective-permute-start.13 = (bf16[128,1024]{1,0:T(8,128)(2,1)S(1)}, bf16[128,1024]{1,0:T(8,128)(2,1)S(1)}, u32[]{:S(2)}, u32[]{:S(2)}) collective-permute-start(bf16[128,1024]{1,0:T(8,128)(2,1)S(1)} %fusion), channel_id=1, source_target_pairs={{2,0},{3,1},{4,6},{5,7},{10,8},{11,9},{12,14},{13,15},{18,16},{19,... | collective-permute-start | bytes 786440 | tf_op jit(solution)/shard_map/ppermute | solution.py:48
  82.9 10.7 %collective-permute-start.14 = (bf16[256,1024]{1,0:T(8,128)(2,1)S(1)}, bf16[256,1024]{1,0:T(8,128)(2,1)S(1)}, u32[]{:S(2)}, u32[]{:S(2)}) collective-permute-start(bf16[256,1024]{1,0:T(8,128)(2,1)S(1)} %shard_map.116), channel_id=1, source_target_pairs={{0,1},{1,0},{2,3},{3,2},{4,5},{5,4},{6,7},{7,6},{8,9},{9,8},{10,11... | collective-permute-start | bytes 1572872 | tf_op jit(solution)/shard_map/ppermute | solution.py:19
  94.5 4.1 %collective-permute-start.15 = (bf16[128,1024]{1,0:T(8,128)(2,1)S(1)}, bf16[128,1024]{1,0:T(8,128)(2,1)}, u32[]{:S(2)}, u32[]{:S(2)}) collective-permute-start(bf16[128,1024]{1,0:T(8,128)(2,1)S(1)} %convert_element_type.103.former_sums), channel_id=1, source_target_pairs={{24,16},{25,17},{26,18},{27,19},{28,20},{29,21},{30,22},{31,23}} | collective-permute-start | bytes 786440 | tf_op jit(solution)/shard_map/ppermute | solution.py:25
  101.3 6.0 %collective-permute-start.16 = (bf16[128,1024]{1,0:T(8,128)(2,1)}, bf16[128,1024]{1,0:T(8,128)(2,1)S(1)}, u32[]{:S(2)}, u32[]{:S(2)}) collective-permute-start(bf16[128,1024]{1,0:T(8,128)(2,1)} %get-tuple-element.127.former_sums), channel_id=1, source_target_pairs={{16,8},{17,9},{18,10},{19,11},{20,12},{21,13},{22,14},{23,15}} | collective-permute-start | bytes 786440 | tf_op jit(solution)/shard_map/ppermute | solution.py:25
  102.6 7.0 %collective-permute-start.17 = (bf16[128,1024]{1,0:T(8,128)(2,1)}, bf16[128,1024]{1,0:T(8,128)(2,1)}, u32[]{:S(2)}, u32[]{:S(2)}) collective-permute-start(bf16[128,1024]{1,0:T(8,128)(2,1)} %get-tuple-element.128.former_cross), channel_id=1, source_target_pairs={{16,9},{17,8},{18,11},{19,10},{20,13},{21,12},{22,15},{23,14}} | collective-permute-start | bytes 786440 | tf_op jit(solution)/shard_map/ppermute | solution.py:25
  112.4 5.5 %collective-permute-start.18 = (bf16[128,1024]{1,0:T(8,128)(2,1)S(1)}, bf16[128,1024]{1,0:T(8,128)(2,1)}, u32[]{:S(2)}, u32[]{:S(2)}) collective-permute-start(bf16[128,1024]{1,0:T(8,128)(2,1)S(1)} %get-tuple-element.135.former_sums), channel_id=1, source_target_pairs={{8,0},{9,1},{10,2},{11,3},{12,4},{13,5},{14,6},{15,7}} | collective-permute-start | bytes 786440 | tf_op jit(solution)/shard_map/ppermute | solution.py:25
  113.7 4.1 %collective-permute-start.19 = (bf16[128,1024]{1,0:T(8,128)(2,1)}, bf16[128,1024]{1,0:T(8,128)(2,1)}, u32[]{:S(2)}, u32[]{:S(2)}) collective-permute-start(bf16[128,1024]{1,0:T(8,128)(2,1)} %get-tuple-element.136.former_cross), channel_id=1, source_target_pairs={{8,1},{9,0},{10,3},{11,2},{12,5},{13,4},{14,7},{15,6}} | collective-permute-start | bytes 786440 | tf_op jit(solution)/shard_map/ppermute | solution.py:25
  117.8 31.5 %copy-start.9 = (bf16[1,256,2048]{2,1,0:T(8,128)(2,1)S(1)}, bf16[1,256,2048]{2,1,0:T(8,128)(2,1)}, u32[]{:S(2)}) copy-start(bf16[1,256,2048]{2,1,0:T(8,128)(2,1)} %param.10) | copy-start | bytes 3145732
  117.8 31.5 %copy-start.12 = (bf16[256,1024]{1,0:T(8,128)(2,1)S(1)}, bf16[256,1024]{1,0:T(8,128)(2,1)}, u32[]{:S(2)}) copy-start(bf16[256,1024]{1,0:T(8,128)(2,1)} %copy-done.11) | copy-start | bytes 1572868
  119.3 6.4 %collective-permute-start.20 = (bf16[128,1024]{1,0:T(8,128)(2,1)S(1)}, bf16[128,1024]{1,0:T(8,128)(2,1)S(1)}, u32[]{:S(2)}, u32[]{:S(2)}) collective-permute-start(bf16[128,1024]{1,0:T(8,128)(2,1)S(1)} %get-tuple-element.142), channel_id=1, source_target_pairs={{0,1},{1,0},{2,3},{3,2},{4,5},{5,4},{6,7},{7,6},{8,9},{9,8},{10,11... | collective-permute-start | bytes 786440 | tf_op jit(solution)/shard_map/ppermute | solution.py:19
  125.8 10.5 %collective-permute-start.21 = (bf16[128,1024]{1,0:T(8,128)(2,1)S(1)}, bf16[128,1024]{1,0:T(8,128)(2,1)S(1)}, u32[]{:S(2)}, u32[]{:S(2)}) collective-permute-start(bf16[128,1024]{1,0:T(8,128)(2,1)S(1)} %add_convert_fusion.c0), channel_id=1, source_target_pairs={{0,2},{1,3},{2,0},{3,1},{4,6},{5,7},{6,4},{7,5},{8,10},{9,11},{10,... | collective-permute-start | bytes 786440 | tf_op jit(solution)/shard_map/ppermute | solution.py:19
  129.4 19.8 %collective-permute-start.22 = (bf16[128,1024]{1,0:T(8,128)(2,1)S(1)}, bf16[128,1024]{1,0:T(8,128)(2,1)S(1)}, u32[]{:S(2)}, u32[]{:S(2)}) collective-permute-start(bf16[128,1024]{1,0:T(8,128)(2,1)S(1)} %add_convert_fusion.c0), channel_id=1, source_target_pairs={{0,4},{1,5},{2,6},{3,7},{4,0},{5,1},{6,2},{7,3},{8,12},{9,13},{10,... | collective-permute-start | bytes 786440 | tf_op jit(solution)/shard_map/ppermute | solution.py:19
  130.2 19.1 %collective-permute-start.23 = (bf16[128,1024]{1,0:T(8,128)(2,1)S(1)}, bf16[128,1024]{1,0:T(8,128)(2,1)S(1)}, u32[]{:S(2)}, u32[]{:S(2)}) collective-permute-start(bf16[128,1024]{1,0:T(8,128)(2,1)S(1)} %add_convert_fusion.c0), channel_id=1, source_target_pairs={{0,6},{1,7},{2,4},{3,5},{4,2},{5,3},{6,0},{7,1},{8,14},{9,15},{10,... | collective-permute-start | bytes 786440 | tf_op jit(solution)/shard_map/ppermute | solution.py:19
  150.8 6.4 %collective-permute-start.24 = (bf16[512,256]{1,0:T(8,128)(2,1)S(1)}, bf16[512,256]{1,0:T(8,128)(2,1)S(1)}, u32[]{:S(2)}, u32[]{:S(2)}) collective-permute-start(bf16[512,256]{1,0:T(8,128)(2,1)S(1)} %get-tuple-element.144), channel_id=1, source_target_pairs={{0,1},{1,0},{2,3},{3,2},{4,5},{5,4},{6,7},{7,6},{8,9},{9,8},{10,11... | collective-permute-start | bytes 786440 | tf_op jit(solution)/shard_map/ppermute | solution.py:19
  157.5 7.8 %collective-permute-start.25 = (bf16[256,128]{1,0:T(8,128)(2,1)S(1)}, bf16[256,128]{1,0:T(8,128)(2,1)S(1)}, u32[]{:S(2)}, u32[]{:S(2)}) collective-permute-start(bf16[256,128]{1,0:T(8,128)(2,1)S(1)} %get-tuple-element.151), channel_id=1, source_target_pairs={{0,2},{1,3},{2,0},{3,1},{4,6},{5,7},{6,4},{7,5},{8,10},{9,11},{10,... | collective-permute-start | bytes 196616 | tf_op jit(solution)/shard_map/ppermute | solution.py:19
  161.0 5.8 %collective-permute-start.26 = (bf16[256,128]{1,0:T(8,128)(2,1)S(1)}, bf16[256,128]{1,0:T(8,128)(2,1)S(1)}, u32[]{:S(2)}, u32[]{:S(2)}) collective-permute-start(bf16[256,128]{1,0:T(8,128)(2,1)S(1)} %get-tuple-element.152), channel_id=1, source_target_pairs={{0,4},{1,5},{2,6},{3,7},{4,0},{5,1},{6,2},{7,3},{8,12},{9,13},{10,... | collective-permute-start | bytes 196616 | tf_op jit(solution)/shard_map/ppermute | solution.py:19
  161.7 6.2 %collective-permute-start.27 = (bf16[256,128]{1,0:T(8,128)(2,1)S(1)}, bf16[256,128]{1,0:T(8,128)(2,1)S(1)}, u32[]{:S(2)}, u32[]{:S(2)}) collective-permute-start(bf16[256,128]{1,0:T(8,128)(2,1)S(1)} %get-tuple-element.153), channel_id=1, source_target_pairs={{0,6},{1,7},{2,4},{3,5},{4,2},{5,3},{6,0},{7,1},{8,14},{9,15},{10,... | collective-permute-start | bytes 196616 | tf_op jit(solution)/shard_map/ppermute | solution.py:19
  167.9 1.4 collective-permute-start.28
  168.6 0.7 collective-permute-start.29
  171.2 18.2 %collective-permute-start.30 = (bf16[1024,128]{1,0:T(8,128)(2,1)S(1)}, bf16[1024,128]{1,0:T(8,128)(2,1)S(1)}, u32[]{:S(2)}, u32[]{:S(2)}) collective-permute-start(bf16[1024,128]{1,0:T(8,128)(2,1)S(1)} %shard_map.127), channel_id=1, source_target_pairs={{8,16},{9,17},{10,18},{11,19},{12,20},{13,21},{14,22},{15,23}} | collective-permute-start | bytes 786440 | tf_op jit(solution)/shard_map/ppermute | solution.py:25
  172.5 21.0 %collective-permute-start.31 = (bf16[1024,128]{1,0:T(8,128)(2,1)S(1)}, bf16[1024,128]{1,0:T(8,128)(2,1)S(1)}, u32[]{:S(2)}, u32[]{:S(2)}) collective-permute-start(bf16[1024,128]{1,0:T(8,128)(2,1)S(1)} %shard_map.127), channel_id=1, source_target_pairs={{8,17},{9,16},{10,19},{11,18},{12,21},{13,20},{14,23},{15,22}} | collective-permute-start | bytes 786440 | tf_op jit(solution)/shard_map/ppermute | solution.py:25
  195.3 37.7 %copy-start.3 = (bf16[1,256,2048]{2,1,0:T(8,128)(2,1)S(1)}, bf16[1,256,2048]{2,1,0:T(8,128)(2,1)}, u32[]{:S(2)}) copy-start(bf16[1,256,2048]{2,1,0:T(8,128)(2,1)} %param.9) | copy-start | bytes 3145732
  195.3 4.2 %collective-permute-start.32 = (bf16[1024,128]{1,0:T(8,128)(2,1)S(1)}, bf16[1024,128]{1,0:T(8,128)(2,1)}, u32[]{:S(2)}, u32[]{:S(2)}) collective-permute-start(bf16[1024,128]{1,0:T(8,128)(2,1)S(1)} %shard_map.128), channel_id=1, source_target_pairs={{16,24},{17,25},{18,26},{19,27},{20,28},{21,29},{22,30},{23,31}} | collective-permute-start | bytes 786440 | tf_op jit(solution)/shard_map/ppermute | solution.py:25
  197.5 5.2 %collective-permute-start.33 = (bf16[1024,128]{1,0:T(8,128)(2,1)S(1)}, bf16[1024,128]{1,0:T(8,128)(2,1)}, u32[]{:S(2)}, u32[]{:S(2)}) collective-permute-start(bf16[1024,128]{1,0:T(8,128)(2,1)S(1)} %shard_map.128), channel_id=1, source_target_pairs={{16,25},{17,24},{18,27},{19,26},{20,29},{21,28},{22,31},{23,30}} | collective-permute-start | bytes 786440 | tf_op jit(solution)/shard_map/ppermute | solution.py:25
  199.6 15.1 %collective-permute-start.35 = (bf16[1024,128]{1,0:T(8,128)(2,1)S(1)}, bf16[1024,128]{1,0:T(8,128)(2,1)S(1)}, u32[]{:S(2)}, u32[]{:S(2)}) collective-permute-start(bf16[1024,128]{1,0:T(8,128)(2,1)S(1)} %select_select_fusion.1.own), channel_id=1, source_target_pairs={{0,4},{1,5},{2,6},{3,7},{4,0},{5,1},{6,2},{7,3},{8,12},{9,13},{10,... | collective-permute-start | bytes 786440 | tf_op jit(solution)/shard_map/ppermute | solution.py:19
  202.8 25.3 %collective-permute-start.34 = (bf16[2,1024,128]{2,1,0:T(8,128)(2,1)S(1)}, bf16[2,1024,128]{2,1,0:T(8,128)(2,1)S(1)}, u32[]{:S(2)}, u32[]{:S(2)}) collective-permute-start(bf16[2,1024,128]{2,1,0:T(8,128)(2,1)S(1)} %pad_maximum_fusion.2), channel_id=1, source_target_pairs={{0,2},{1,3},{2,0},{3,1},{4,6},{5,7},{6,4},{7,5},{8,10},{9,11},{10,... | collective-permute-start | bytes 1572872 | tf_op jit(solution)/shard_map/ppermute | solution.py:19
  203.7 22.2 %collective-permute-start.37 = (bf16[1024,128]{1,0:T(8,128)(2,1)S(1)}, bf16[1024,128]{1,0:T(8,128)(2,1)S(1)}, u32[]{:S(2)}, u32[]{:S(2)}) collective-permute-start(bf16[1024,128]{1,0:T(8,128)(2,1)S(1)} %select_select_fusion.1.own), channel_id=1, source_target_pairs={{0,6},{1,7},{2,4},{3,5},{4,2},{5,3},{6,0},{7,1},{8,14},{9,15},{10,... | collective-permute-start | bytes 786440 | tf_op jit(solution)/shard_map/ppermute | solution.py:19
  214.6 13.4 %collective-permute-start.36 = (bf16[1024,128]{1,0:T(8,128)(2,1)S(1)}, bf16[1024,128]{1,0:T(8,128)(2,1)S(1)}, u32[]{:S(2)}, u32[]{:S(2)}) collective-permute-start(bf16[1024,128]{1,0:T(8,128)(2,1)S(1)} %collective-permute-done.35.own4), channel_id=1, source_target_pairs={{0,1},{1,0},{2,3},{3,2},{4,5},{5,4},{6,7},{7,6},{8,9},{9,8},{10,11... | collective-permute-start | bytes 786440 | tf_op jit(solution)/shard_map/ppermute | solution.py:19
  225.9 7.1 %collective-permute-start.38 = (bf16[1024,128]{1,0:T(8,128)(2,1)S(1)}, bf16[1024,128]{1,0:T(8,128)(2,1)S(1)}, u32[]{:S(2)}, u32[]{:S(2)}) collective-permute-start(bf16[1024,128]{1,0:T(8,128)(2,1)S(1)} %collective-permute-done.37.own6), channel_id=1, source_target_pairs={{0,1},{1,0},{2,3},{3,2},{4,5},{5,4},{6,7},{7,6},{8,9},{9,8},{10,11... | collective-permute-start | bytes 786440 | tf_op jit(solution)/shard_map/ppermute | solution.py:19
  (10 other events, 10.8 us)
